TPU v7x, 32 devices: a whole 2x2x4 slice. The times are simulated.
32 devices in a mesh: sta: 2 (over x), gx: 4 (over z), gy: 4 (over y, core).
Axes of the slice: x: 2, y: 2, z: 4, core: 2. Of those that a mesh axis runs over, the one named last changes fastest.
Arguments:
- rec_state: float32 [2, 4, 9, 32, 32, 128], P('sta', None, None, 'gx', 'gy'), may hold values from -6 to 6
- source_strain: bfloat16 [2, 8, 6, 32, 32, 128], P('sta', None, None, 'gx', 'gy'), may hold values from -6 to 6
- material: int32 [32, 32, 128], P('gx', 'gy'), may hold values from 0 to 15
- material_table: float32 [16, 3], replicated, may hold values from 0.5 to 1.5
- residual: float32 [2, 4, 8], P('sta'), may hold values from -4 to 4
- rec_cell: int32 [2, 4], P('sta'), may hold values from 0 to 1023
- listed: int32 [2, 8, 2], replicated, may hold values 0 or 1
- src_pick: int32 [2, 8], replicated, may hold values from 0 to 1
Outputs:
- kernels: float32 [2, 32, 32, 128], P(None, ('gx', 'sta'), 'gy')
All inputs are finite; a program needn't handle non-finite values.
Results may differ from a plain program's by a relative error of at most 0.0003.
Values may be sent and summed in bfloat16 or wider, within the bound.
No kernel may reach another device: no remote copies, remote signals or barrier semaphores. Data moves between devices by JAX's collectives and lax.ppermute only.
A program may use at most 128 MiB of HBM per device.

v0:
```python
import functools

import jax
import jax.numpy as jnp
from jax import lax
from jax.experimental import pallas as pl
from jax.experimental.pallas import tpu as pltpu
from jax.sharding import PartitionSpec as P

C_NEAR = 8.0 / 12.0
C_FAR = 1.0 / 12.0
TIME_STEP = 0.25
AMPLITUDE = 4.0
KERNEL_SCALE = 0.0625
STIFFNESS = 0.3
REACH = 2
DEEP = 2 * REACH
ALONG_X = (0, 3, 4)

VMEM = pl.BlockSpec(memory_space=pltpu.VMEM)
SMEM = pl.BlockSpec(memory_space=pltpu.SMEM)
F32 = jnp.float32


def call(body, outs, ins, aliases=None, flops=2_000_000):
    return pl.pallas_call(
        body,
        out_shape=[jax.ShapeDtypeStruct(shape, F32) for shape in outs],
        in_specs=[SMEM if small else VMEM for _, small in ins],
        out_specs=[VMEM] * len(outs),
        input_output_aliases=aliases or {},
        compiler_params=pltpu.CompilerParams(vmem_limit_bytes=32 * 1024 * 1024),
        cost_estimate=pl.CostEstimate(flops=flops, bytes_accessed=4_000_000, transcendentals=0),
    )(*[array for array, _ in ins])


def edge_coefs(shape, axis):
    at = lax.broadcasted_iota(jnp.int32, shape, axis)
    size = shape[axis]
    return (
        jnp.where(at < size - 1, C_NEAR, 0.0).astype(F32),
        jnp.where(at >= 1, C_NEAR, 0.0).astype(F32),
        jnp.where(at < size - 2, C_FAR, 0.0).astype(F32),
        jnp.where(at >= 2, C_FAR, 0.0).astype(F32),
    )


def in_row(row, coefs, axis):
    size = row.shape[axis]
    near = coefs[0] * pltpu.roll(row, size - 1, axis) - coefs[1] * pltpu.roll(row, 1, axis)
    far = coefs[2] * pltpu.roll(row, size - 2, axis) - coefs[3] * pltpu.roll(row, 2, axis)
    return near - far


def across(rows, x):
    return C_NEAR * (rows(x + 1) - rows(x - 1)) - C_FAR * (rows(x + 2) - rows(x - 2))


def assemble(place, *refs):
    count = len(refs) - 5
    tiles, (vel, stress, cells, low, high) = refs[:count], refs[count:]
    tile_x, tile_y = tiles[0].shape[1:3]
    for turn, tile in enumerate(tiles):
        spot = pl.ds(pl.multiple_of((place[0] ^ turn) * tile_y, tile_y), tile_y)
        vel[:, :, spot, :] = tile[0:3]
        stress[:, :, spot, :] = tile[3:9]
        cells[:, spot, :] = tile[9]
        for at, comp in enumerate(ALONG_X):
            low[at, :, spot, :] = tile[3 + comp, :REACH]
            high[at, :, spot, :] = tile[3 + comp, tile_x - REACH :]
        low[len(ALONG_X), :, spot, :] = tile[9, :REACH]
        high[len(ALONG_X), :, spot, :] = tile[9, tile_x - REACH :]


def push(place, amount, stress, vel, low_stress, high_stress, buoyancy, vel_out, low_out, high_out):
    _, tile_x, size_y, depth = vel.shape
    shape = (size_y, depth)
    coef_y, coef_z = edge_coefs(shape, 0), edge_coefs(shape, 1)
    spot = (lax.broadcasted_iota(jnp.int32, shape, 0) == place[4]) & (
        lax.broadcasted_iota(jnp.int32, shape, 1) == 0
    )
    spot = jnp.where(spot, amount, 0.0)

    def rows(at):
        def row(x):
            if x < 0:
                return low_stress[at, x + REACH]
            if x >= tile_x:
                return high_stress[at, x - tile_x]
            return stress[ALONG_X[at], x]

        return row

    for x in range(tile_x):
        xy, xz, yz = stress[3, x], stress[4, x], stress[5, x]
        force_x = across(rows(0), x) + in_row(xy, coef_y, 0) + in_row(xz, coef_z, 1)
        force_y = across(rows(1), x) + in_row(stress[1, x], coef_y, 0) + in_row(yz, coef_z, 1)
        force_z = across(rows(2), x) + in_row(yz, coef_y, 0) + in_row(stress[2, x], coef_z, 1)
        force_z = force_z + jnp.where(place[3] == x, 1.0, 0.0) * spot
        light = buoyancy[x]
        for comp, force in enumerate((force_x, force_y, force_z)):
            fresh = vel[comp, x] + light * force
            vel_out[comp, x] = fresh
            if x < DEEP:
                low_out[comp, x] = fresh
            if x >= tile_x - DEEP:
                high_out[comp, x - (tile_x - DEEP)] = fresh


def first(place, table, residual, vel, stress, cells, low, high, vel_out, low_out, high_out, light, lame, shear):
    tile_x = vel.shape[1]
    count = table.shape[0]
    for x in range(-REACH, tile_x + REACH):
        if x < 0:
            number, inside = low[len(ALONG_X), x + REACH], place[1] > 0
        elif x >= tile_x:
            number, inside = high[len(ALONG_X), x - tile_x], place[1] < place[2] - 1
        else:
            number, inside = cells[x], None
        parts = [jnp.full(number.shape, table[0, c], F32) for c in range(3)]
        for m in range(1, count):
            hit = number == float(m)
            parts = [jnp.where(hit, table[m, c], parts[c]) for c in range(3)]
        half_step = 1.0 if inside is None else jnp.where(inside, 1.0, 0.0)
        lame[x + REACH] = (TIME_STEP * STIFFNESS * half_step) * parts[1]
        shear[x + REACH] = (2.0 * TIME_STEP * STIFFNESS * half_step) * parts[2]
        if inside is None:
            light[x] = TIME_STEP / parts[0]
    amount = AMPLITUDE * residual[place[0], 0]
    push(place, amount, stress, vel, low, high, light, vel_out, low_out, high_out)


def advance(moment, last, *refs):
    place, residual, vel, low, high, stress, low_stress, high_stress, light, lame, shear = refs[:11]
    if last:
        (rates,) = refs[11:]
    else:
        rates, stress_out, low_stress_out, high_stress_out, vel_out, low_out, high_out = refs[11:]
    _, tile_x, size_y, depth = vel.shape
    shape = (size_y, depth)
    coef_y, coef_z = edge_coefs(shape, 0), edge_coefs(shape, 1)

    def rows(comp):
        def row(x):
            if x < 0:
                return low[comp, x + DEEP]
            if x >= tile_x:
                return high[comp, x - tile_x]
            return vel[comp, x]

        return row

    vx, vy, vz = rows(0), rows(1), rows(2)
    reach = 0 if last else REACH
    for x in range(-reach, tile_x + reach):
        own = 0 <= x < tile_x
        xx = across(vx, x)
        yy = in_row(vy(x), coef_y, 0)
        zz = in_row(vz(x), coef_z, 1)
        xy = 0.5 * (in_row(vx(x), coef_y, 0) + across(vy, x))
        xz = 0.5 * (in_row(vx(x), coef_z, 1) + across(vz, x))
        if own:
            yz = 0.5 * (in_row(vy(x), coef_z, 1) + in_row(vz(x), coef_y, 0))
            for comp, rate in enumerate((xx, yy, zz, xy, xz, yz)):
                rates[comp, x] = rate
        if last:
            continue
        stiff = shear[x + REACH]
        bulk = lame[x + REACH] * (xx + yy + zz)
        if own:
            for comp, rate in enumerate((xx, yy, zz)):
                stress_out[comp, x] = stress[comp, x] + (bulk + stiff * rate)
            for comp, rate in enumerate((xy, xz, yz)):
                stress_out[3 + comp, x] = stress[3 + comp, x] + stiff * rate
        else:
            source, target, row = (
                (low_stress, low_stress_out, x + REACH) if x < 0 else (high_stress, high_stress_out, x - tile_x)
            )
            target[0, row] = source[0, row] + (bulk + stiff * xx)
            target[1, row] = source[1, row] + stiff * xy
            target[2, row] = source[2, row] + stiff * xz
    if not last:
        amount = AMPLITUDE * residual[place[0], moment + 1]
        push(place, amount, stress_out, vel, low_stress_out, high_stress_out, light, vel_out, low_out, high_out)


def correlate(moments, pieces, *refs):
    place, residual = refs[:2]
    rates = refs[2 : 2 + moments]
    sources = refs[2 + moments : 2 + moments + pieces]
    (terms,) = refs[2 + moments + pieces :]
    tile_x, tile_y = sources[0].shape[2:4]
    for turn in range(pieces):
        spot = pl.ds(pl.multiple_of((place[0] ^ turn) * tile_y, tile_y), tile_y)
        for x in range(tile_x):
            lam = mu = None
            for moment in range(moments):
                weight = KERNEL_SCALE * residual[place[0], moment]
                rate = [rates[moment][c, x, spot, :] for c in range(6)]
                source = [sources[turn][moment, c, x] for c in range(6)]
                bulk = (source[0] + source[1] + source[2]) * (rate[0] + rate[1] + rate[2])
                diag = source[0] * rate[0] + source[1] * rate[1] + source[2] * rate[2]
                off = source[3] * rate[3] + source[4] * rate[4] + source[5] * rate[5]
                bulk, both = weight * bulk, (2.0 * weight) * (diag + 2.0 * off)
                lam = bulk if lam is None else lam + bulk
                mu = both if mu is None else mu + both
            terms[turn, 0, x] = lam
            terms[turn, 1, x] = mu


def swap(array, axis, turn):
    count = lax.axis_size(axis)
    return lax.ppermute(array, axis, [(i, i ^ turn) for i in range(count)])


def to_neighbours(low, high, axis):
    count = lax.axis_size(axis)
    up = [(i, i + 1) for i in range(count - 1)]
    down = [(i + 1, i) for i in range(count - 1)]
    return lax.ppermute(high, axis, up), lax.ppermute(low, axis, down)


def local(rec_state, source_strain, material, material_table, residual, rec_cell, listed, src_pick):
    state = rec_state[0]
    receivers, _, tile_x, tile_y, depth = state.shape
    pieces = lax.axis_size("gy")
    groups = lax.axis_size("sta")
    assert receivers == pieces and pieces & (pieces - 1) == 0 and groups & (groups - 1) == 0
    size_y = pieces * tile_y
    group, slab, me = lax.axis_index("sta"), lax.axis_index("gx"), lax.axis_index("gy")
    moments = residual.shape[2]

    numbers = material.astype(F32)[None]
    chunks = []
    for turn in range(pieces):
        mine = lax.dynamic_index_in_dim(state, me ^ turn, 0, keepdims=False)
        mine = jnp.concatenate([mine, numbers], 0)
        chunks.append(swap(mine, "gy", turn) if turn else mine)

    weights = lax.dynamic_slice_in_dim(listed, group, 1, 2)[:, :, 0].astype(F32)
    combined = 0.0
    for turn in range(groups):
        piece = swap(source_strain[0], "sta", turn) if turn else source_strain[0]
        factor = jnp.sum(weights * (src_pick == (group ^ turn)).astype(F32), 0)
        combined = combined + factor[:, None, None, None, None] * piece.astype(F32)

    cell = lax.dynamic_index_in_dim(rec_cell[0], me, 0, keepdims=False)
    place = jnp.stack(
        [me, slab, jnp.full((), lax.axis_size("gx")), cell // size_y - slab * tile_x, cell % size_y]
    ).astype(jnp.int32)
    rows = residual[0]
    whole, halo, face = (size_y, depth), (3, REACH, size_y, depth), (3, DEEP, size_y, depth)
    vel_shape, stress_shape = (3, tile_x) + whole, (6, tile_x) + whole
    ends = (4, REACH) + whole

    vel, stress, cells, low, high = call(
        assemble,
        [vel_shape, stress_shape, (tile_x,) + whole, ends, ends],
        [(place, True)] + [(chunk, False) for chunk in chunks],
    )
    low_stress, high_stress = to_neighbours(low, high, "gx")
    vel, low, high, light, lame, shear = call(
        first,
        [vel_shape, face, face, (tile_x,) + whole, (tile_x + 2 * REACH,) + whole, (tile_x + 2 * REACH,) + whole],
        [(place, True), (material_table, True), (rows, True)]
        + [(array, False) for array in (vel, stress, cells, low_stress, high_stress)],
    )
    low_stress, high_stress = low_stress[:3], high_stress[:3]

    rates = []
    for moment in range(moments):
        last = moment == moments - 1
        low, high = to_neighbours(low, high, "gx")
        outs = [stress_shape]
        if not last:
            outs += [stress_shape, halo, halo, vel_shape, face, face]
        results = call(
            functools.partial(advance, moment, last),
            outs,
            [(place, True), (rows, True)]
            + [
                (array, False)
                for array in (vel, low, high, stress, low_stress, high_stress, light, lame, shear)
            ],
        )
        rates.append(results[0])
        if not last:
            stress, low_stress, high_stress, vel, low, high = results[1:]

    sources = [combined]
    width = pieces // 2
    found = {0: combined}
    while width:
        for turn in list(found):
            found[turn ^ width] = swap(found[turn], "gy", width)
        width //= 2
    sources = [found[turn] for turn in range(pieces)]

    (terms,) = call(
        functools.partial(correlate, moments, pieces),
        [(pieces, 2, tile_x, tile_y, depth)],
        [(place, True), (rows, True)] + [(array, False) for array in rates + sources],
    )
    held = {turn: terms[turn] for turn in range(pieces)}
    width = 1
    while width < pieces:
        keep = [turn for turn in held if not turn & width]
        sent = swap(jnp.stack([held[turn ^ width] for turn in keep]), "gy", width)
        held = {turn: held[turn] + sent[at] for at, turn in enumerate(keep)}
        width *= 2
    total = held[0]
    share = tile_x // groups
    result = lax.dynamic_slice_in_dim(total, group * share, share, 1)
    for turn in range(1, groups):
        part = lax.dynamic_slice_in_dim(total, (group ^ turn) * share, share, 1)
        result = result + swap(part, "sta", turn)
    return result


def solution(mesh):
    in_specs = (
        P("sta", None, None, "gx", "gy", None),
        P("sta", None, None, "gx", "gy", None),
        P("gx", "gy", None),
        P(),
        P("sta", None, None),
        P("sta", None),
        P(),
        P(),
    )
    out_specs = P(None, ("gx", "sta"), "gy", None)
    return jax.shard_map(local, mesh=mesh, in_specs=in_specs, out_specs=out_specs, check_vma=False)
```

profile of v0, /device:TPU:0, one launch (start us, length us, event | category | flops | bytes accessed | tf_op | source)
XLA Modules:
  0.0 195.5 jit_solution(778057511686824577)
XLA Ops:
  0.0 2.9 %collective-permute-start.21 = (bf16[8,6,8,8,128]{4,3,2,1,0:T(8,128)(2,1)}, bf16[8,6,8,8,128]{4,3,2,1,0:T(8,128)(2,1)S(1)}, u32[]{:S(2)}, u32[]{:S(2)}) collective-permute-start(bf16[8,6,8,8,128]{4,3,2,1,0:T(8,128)(2,1)} %bitcast.33), channel_id=1, source_target_pairs={{0,16},{16,0},{1,17},{17,1},{2,18},{18,2},{3,19},{19,3},{4,20},{20... | collective-permute-start | bytes 2359304 | tf_op jit(solution)/shard_map/ppermute | solution.py:213
  4.3 16.4 %collective-permute-done.21 = bf16[8,6,8,8,128]{4,3,2,1,0:T(8,128)(2,1)S(1)} collective-permute-done((bf16[8,6,8,8,128]{4,3,2,1,0:T(8,128)(2,1)}, bf16[8,6,8,8,128]{4,3,2,1,0:T(8,128)(2,1)S(1)}, u32[]{:S(2)}, u32[]{:S(2)}) %collective-permute-start.21) | collective-permute-done | bytes 786464 | tf_op jit(solution)/shard_map/ppermute | solution.py:213
  20.7 1.5 multiply_add_fusion.refs_10_
  22.2 1.8 collective-permute-start.23
  26.8 1.8 collective-permute-start.1
  31.5 34.5 %collective-permute-done.2.refs_3_ = f32[10,8,8,128]{3,2,1,0:T(8,128)S(1)} collective-permute-done((f32[10,8,8,128]{3,2,1,0:T(8,128)}, f32[10,8,8,128]{3,2,1,0:T(8,128)S(1)}, u32[]{:S(2)}, u32[]{:S(2)}) %collective-permute-start.2) | collective-permute-done | bytes 327712 | tf_op jit(solution)/shard_map/ppermute | solution.py:213
  66.8 5.2 %collective-permute-done.1.refs_2_ = f32[10,8,8,128]{3,2,1,0:T(8,128)S(1)} collective-permute-done((f32[10,8,8,128]{3,2,1,0:T(8,128)}, f32[10,8,8,128]{3,2,1,0:T(8,128)S(1)}, u32[]{:S(2)}, u32[]{:S(2)}) %collective-permute-start.1) | collective-permute-done | bytes 327712 | tf_op jit(solution)/shard_map/ppermute | solution.py:213
  74.6 1.4 shard_map.82
  76.0 3.4 %collective-permute-start.3 = (f32[4,2,32,128]{3,2,1,0:T(8,128)}, f32[4,2,32,128]{3,2,1,0:T(8,128)S(1)}, u32[]{:S(2)}, u32[]{:S(2)}) collective-permute-start(f32[4,2,32,128]{3,2,1,0:T(8,128)} %get-tuple-element.68), channel_id=1, source_target_pairs={{0,4},{4,8},{8,12},{1,5},{5,9},{9,13},{2,6},{6,10},{10,14},{3,7},{... | collective-permute-start | bytes 393224 | tf_op jit(solution)/shard_map/ppermute | solution.py:220
  80.8 1.4 collective-permute-done.3.low
  82.2 4.3 %collective-permute-done.4.high = f32[4,2,32,128]{3,2,1,0:T(8,128)S(1)} collective-permute-done((f32[4,2,32,128]{3,2,1,0:T(8,128)}, f32[4,2,32,128]{3,2,1,0:T(8,128)S(1)}, u32[]{:S(2)}, u32[]{:S(2)}) %collective-permute-start.4) | collective-permute-done | bytes 131104 | tf_op jit(solution)/shard_map/ppermute | solution.py:220
  86.5 1.6 shard_map.83
  88.1 3.5 %collective-permute-start.5 = (f32[3,4,32,128]{3,2,1,0:T(8,128)S(1)}, f32[3,4,32,128]{3,2,1,0:T(8,128)S(1)}, u32[]{:S(2)}, u32[]{:S(2)}) collective-permute-start(f32[3,4,32,128]{3,2,1,0:T(8,128)S(1)} %get-tuple-element.71), channel_id=1, source_target_pairs={{0,4},{4,8},{8,12},{1,5},{5,9},{9,13},{2,6},{6,10},{10,14},{3,7},{... | collective-permute-start | bytes 589832 | tf_op jit(solution)/shard_map/ppermute | solution.py:220
  94.8 4.4 %collective-permute-done.6.refs_4_ = f32[3,4,32,128]{3,2,1,0:T(8,128)S(1)} collective-permute-done((f32[3,4,32,128]{3,2,1,0:T(8,128)S(1)}, f32[3,4,32,128]{3,2,1,0:T(8,128)S(1)}, u32[]{:S(2)}, u32[]{:S(2)}) %collective-permute-start.6) | collective-permute-done | bytes 196640 | tf_op jit(solution)/shard_map/ppermute | solution.py:220
  99.2 1.7 shard_map.84
  100.9 3.5 %collective-permute-start.7 = (f32[3,4,32,128]{3,2,1,0:T(8,128)S(1)}, f32[3,4,32,128]{3,2,1,0:T(8,128)S(1)}, u32[]{:S(2)}, u32[]{:S(2)}) collective-permute-start(f32[3,4,32,128]{3,2,1,0:T(8,128)S(1)} %get-tuple-element.78), channel_id=1, source_target_pairs={{0,4},{4,8},{8,12},{1,5},{5,9},{9,13},{2,6},{6,10},{10,14},{3,7},{... | collective-permute-start | bytes 589832 | tf_op jit(solution)/shard_map/ppermute | solution.py:220
  105.7 1.9 collective-permute-done.7.refs_3_
  107.6 4.4 %collective-permute-done.8.refs_4_ = f32[3,4,32,128]{3,2,1,0:T(8,128)S(1)} collective-permute-done((f32[3,4,32,128]{3,2,1,0:T(8,128)S(1)}, f32[3,4,32,128]{3,2,1,0:T(8,128)S(1)}, u32[]{:S(2)}, u32[]{:S(2)}) %collective-permute-start.8) | collective-permute-done | bytes 196640 | tf_op jit(solution)/shard_map/ppermute | solution.py:220
  112.0 1.7 shard_map.85
  113.7 1.9 collective-permute-start.9
  116.9 1.9 collective-permute-done.9.refs_3_
  118.7 4.4 %collective-permute-done.10.refs_4_ = f32[3,4,32,128]{3,2,1,0:T(8,128)S(1)} collective-permute-done((f32[3,4,32,128]{3,2,1,0:T(8,128)S(1)}, f32[3,4,32,128]{3,2,1,0:T(8,128)S(1)}, u32[]{:S(2)}, u32[]{:S(2)}) %collective-permute-start.10) | collective-permute-done | bytes 196640 | tf_op jit(solution)/shard_map/ppermute | solution.py:220
  123.1 1.7 shard_map.86
  124.8 1.9 collective-permute-start.11
  128.1 1.9 collective-permute-done.11.refs_3_
  129.9 4.4 %collective-permute-done.12.refs_4_ = f32[3,4,32,128]{3,2,1,0:T(8,128)S(1)} collective-permute-done((f32[3,4,32,128]{3,2,1,0:T(8,128)S(1)}, f32[3,4,32,128]{3,2,1,0:T(8,128)S(1)}, u32[]{:S(2)}, u32[]{:S(2)}) %collective-permute-start.12) | collective-permute-done | bytes 196640 | tf_op jit(solution)/shard_map/ppermute | solution.py:220
  134.3 1.7 shard_map.87
  136.0 1.9 collective-permute-start.13
  139.3 1.9 collective-permute-done.13.refs_3_
  141.1 4.4 %collective-permute-done.14.refs_4_ = f32[3,4,32,128]{3,2,1,0:T(8,128)S(1)} collective-permute-done((f32[3,4,32,128]{3,2,1,0:T(8,128)S(1)}, f32[3,4,32,128]{3,2,1,0:T(8,128)S(1)}, u32[]{:S(2)}, u32[]{:S(2)}) %collective-permute-start.14) | collective-permute-done | bytes 196640 | tf_op jit(solution)/shard_map/ppermute | solution.py:220
  145.5 1.7 shard_map.88
  147.2 1.9 collective-permute-start.15
  150.4 2.3 %collective-permute-done.15.refs_3_ = f32[3,4,32,128]{3,2,1,0:T(8,128)S(1)} collective-permute-done((f32[3,4,32,128]{3,2,1,0:T(8,128)S(1)}, f32[3,4,32,128]{3,2,1,0:T(8,128)S(1)}, u32[]{:S(2)}, u32[]{:S(2)}) %collective-permute-start.15) | collective-permute-done | bytes 196640 | tf_op jit(solution)/shard_map/ppermute | solution.py:220
  152.8 4.7 %collective-permute-done.16.refs_4_ = f32[3,4,32,128]{3,2,1,0:T(8,128)S(1)} collective-permute-done((f32[3,4,32,128]{3,2,1,0:T(8,128)S(1)}, f32[3,4,32,128]{3,2,1,0:T(8,128)S(1)}, u32[]{:S(2)}, u32[]{:S(2)}) %collective-permute-start.16) | collective-permute-done | bytes 196640 | tf_op jit(solution)/shard_map/ppermute | solution.py:220
  157.5 1.7 shard_map.89
  159.2 1.6 collective-permute-start.17
  160.8 1.5 collective-permute-start.18
  162.3 3.4 %collective-permute-done.17.refs_3_ = f32[3,4,32,128]{3,2,1,0:T(8,128)S(1)} collective-permute-done((f32[3,4,32,128]{3,2,1,0:T(8,128)S(1)}, f32[3,4,32,128]{3,2,1,0:T(8,128)S(1)}, u32[]{:S(2)}, u32[]{:S(2)}) %collective-permute-start.17) | collective-permute-done | bytes 196640 | tf_op jit(solution)/shard_map/ppermute | solution.py:220
  165.6 4.6 %collective-permute-done.18.refs_4_ = f32[3,4,32,128]{3,2,1,0:T(8,128)S(1)} collective-permute-done((f32[3,4,32,128]{3,2,1,0:T(8,128)S(1)}, f32[3,4,32,128]{3,2,1,0:T(8,128)S(1)}, u32[]{:S(2)}, u32[]{:S(2)}) %collective-permute-start.18) | collective-permute-done | bytes 196640 | tf_op jit(solution)/shard_map/ppermute | solution.py:220
  170.3 1.7 shard_map.90
  172.0 1.7 collective-permute-start.19
  175.0 1.9 collective-permute-done.19.refs_3_
  176.8 4.4 %collective-permute-done.20.refs_4_ = f32[3,4,32,128]{3,2,1,0:T(8,128)S(1)} collective-permute-done((f32[3,4,32,128]{3,2,1,0:T(8,128)S(1)}, f32[3,4,32,128]{3,2,1,0:T(8,128)S(1)}, u32[]{:S(2)}, u32[]{:S(2)}) %collective-permute-start.20) | collective-permute-done | bytes 196640 | tf_op jit(solution)/shard_map/ppermute | solution.py:220
  182.3 2.7 %shard_map.92 = f32[4,2,8,8,128]{4,3,2,1,0:T(8,128)S(1)} custom-call(s32[5]{0:T(128)S(1)} %stack.23.place.refs_0_, f32[4,8]{1,0:T(4,128)S(1)} %bitcast.32, f32[6,8,32,128]{3,2,1,0:T(8,128)S(1)} %get-tuple-element.76.refs_2_, f32[6,8,32,128]{3,2,1,0:T(8,128)S(1)} %get-tuple-element.83.refs_3_, f32[6,8,32,128]{3,2,1,0:T(8,128)S(1)} %get-tuple-element.90.refs_4_, ...), custom_call_target="tpu_custom_call" | custom-call | flops 2000000 | bytes 4000000 | tf_op jit(solution)/shard_map/pallas_call | solution.py:26
  186.5 1.6 collective-permute-start.26
  188.1 2.7 %collective-permute-done.26 = f32[1,2,8,8,128]{4,3,2,1,0:T(8,128)S(1)} collective-permute-done((f32[1,2,8,8,128]{4,3,2,1,0:T(8,128)S(1)}, f32[1,2,8,8,128]{4,3,2,1,0:T(8,128)S(1)}, u32[]{:S(2)}, u32[]{:S(2)}) %collective-permute-start.26) | collective-permute-done | bytes 65568 | tf_op jit(solution)/shard_map/ppermute | solution.py:213
  190.8 1.6 collective-permute-start.27
  192.4 2.4 %collective-permute-done.27 = f32[2,4,8,128]{3,2,1,0:T(8,128)S(1)} collective-permute-done((f32[2,4,8,128]{3,2,1,0:T(8,128)S(1)}, f32[2,4,8,128]{3,2,1,0:T(8,128)S(1)}, u32[]{:S(2)}, u32[]{:S(2)}) %collective-permute-start.27) | collective-permute-done | bytes 32800 | tf_op jit(solution)/shard_map/ppermute | solution.py:213
  (52 shorter events, 23.6 us)
Async XLA Ops:
  0.0 28.6 %copy-start = (s32[1,4]{1,0:T(1,128)S(1)}, s32[1,4]{1,0:T(1,128)}, u32[]{:S(2)}) copy-start(s32[1,4]{1,0:T(1,128)} %param.13) | copy-start | bytes 52
  0.0 20.7 %collective-permute-start.21 = (bf16[8,6,8,8,128]{4,3,2,1,0:T(8,128)(2,1)}, bf16[8,6,8,8,128]{4,3,2,1,0:T(8,128)(2,1)S(1)}, u32[]{:S(2)}, u32[]{:S(2)}) collective-permute-start(bf16[8,6,8,8,128]{4,3,2,1,0:T(8,128)(2,1)} %bitcast.33), channel_id=1, source_target_pairs={{0,16},{16,0},{1,17},{17,1},{2,18},{18,2},{3,19},{19,3},{4,20},{20... | collective-permute-start | bytes 2359304 | tf_op jit(solution)/shard_map/ppermute | solution.py:213
  22.2 3.2 %copy-start.6 = (s32[8,8,128]{2,1,0:T(8,128)S(1)}, s32[8,8,128]{2,1,0:T(8,128)}, u32[]{:S(2)}) copy-start(s32[8,8,128]{2,1,0:T(8,128)} %param.10) | copy-start | bytes 98308
  22.2 70.8 %collective-permute-start.23 = (f32[8,6,8,8,128]{4,3,2,1,0:T(8,128)S(1)}, f32[8,6,8,8,128]{4,3,2,1,0:T(8,128)}, u32[]{:S(2)}, u32[]{:S(2)}) collective-permute-start(f32[8,6,8,8,128]{4,3,2,1,0:T(8,128)S(1)} %multiply_add_fusion.refs_10_), channel_id=1, source_target_pairs={{0,2},{1,3},{2,0},{3,1},{4,6},{5,7},{6,4},{7,5},{8,10},{9,11},{10,... | collective-permute-start | bytes 4718600 | tf_op jit(solution)/shard_map/ppermute | solution.py:213
  25.4 55.3 %copy-start.7 = (f32[16,3]{0,1:T(4,128)S(1)}, f32[16,3]{0,1:T(4,128)}, u32[]{:S(2)}) copy-start(f32[16,3]{0,1:T(4,128)} %param.11) | copy-start | bytes 580
  25.4 61.1 %copy-start.5 = (f32[1,4,8]{2,1,0:T(4,128)S(1)}, f32[1,4,8]{2,1,0:T(4,128)}, u32[]{:S(2)}) copy-start(f32[1,4,8]{2,1,0:T(4,128)} %param.12) | copy-start | bytes 388
  26.4 39.6 %collective-permute-start.2 = (f32[10,8,8,128]{3,2,1,0:T(8,128)}, f32[10,8,8,128]{3,2,1,0:T(8,128)S(1)}, u32[]{:S(2)}, u32[]{:S(2)}) collective-permute-start(f32[10,8,8,128]{3,2,1,0:T(8,128)} %get-tuple-element.133), channel_id=1, source_target_pairs={{0,3},{1,2},{2,1},{3,0},{4,7},{5,6},{6,5},{7,4},{8,11},{9,10},{10,... | collective-permute-start | bytes 983048 | tf_op jit(solution)/shard_map/ppermute | solution.py:213
  26.4 39.6 %collective-permute-start = (f32[10,8,8,128]{3,2,1,0:T(8,128)}, f32[10,8,8,128]{3,2,1,0:T(8,128)S(1)}, u32[]{:S(2)}, u32[]{:S(2)}) collective-permute-start(f32[10,8,8,128]{3,2,1,0:T(8,128)} %get-tuple-element.134), channel_id=1, source_target_pairs={{0,1},{1,0},{2,3},{3,2},{4,5},{5,4},{6,7},{7,6},{8,9},{9,8},{10,11... | collective-permute-start | bytes 983048 | tf_op jit(solution)/shard_map/ppermute | solution.py:213
  26.8 45.1 %collective-permute-start.1 = (f32[10,8,8,128]{3,2,1,0:T(8,128)}, f32[10,8,8,128]{3,2,1,0:T(8,128)S(1)}, u32[]{:S(2)}, u32[]{:S(2)}) collective-permute-start(f32[10,8,8,128]{3,2,1,0:T(8,128)} %get-tuple-element.135), channel_id=1, source_target_pairs={{0,2},{1,3},{2,0},{3,1},{4,6},{5,7},{6,4},{7,5},{8,10},{9,11},{10,... | collective-permute-start | bytes 983048 | tf_op jit(solution)/shard_map/ppermute | solution.py:213
  66.0 0.7 copy-start.1
  71.9 0.7 copy-start.3
  72.6 1.0 copy-start.2
  73.6 1.0 copy-start.4
  76.0 6.2 %collective-permute-start.3 = (f32[4,2,32,128]{3,2,1,0:T(8,128)}, f32[4,2,32,128]{3,2,1,0:T(8,128)S(1)}, u32[]{:S(2)}, u32[]{:S(2)}) collective-permute-start(f32[4,2,32,128]{3,2,1,0:T(8,128)} %get-tuple-element.68), channel_id=1, source_target_pairs={{0,4},{4,8},{8,12},{1,5},{5,9},{9,13},{2,6},{6,10},{10,14},{3,7},{... | collective-permute-start | bytes 393224 | tf_op jit(solution)/shard_map/ppermute | solution.py:220
  79.4 7.1 %collective-permute-start.4 = (f32[4,2,32,128]{3,2,1,0:T(8,128)}, f32[4,2,32,128]{3,2,1,0:T(8,128)S(1)}, u32[]{:S(2)}, u32[]{:S(2)}) collective-permute-start(f32[4,2,32,128]{3,2,1,0:T(8,128)} %get-tuple-element.69), channel_id=1, source_target_pairs={{4,0},{8,4},{12,8},{5,1},{9,5},{13,9},{6,2},{10,6},{14,10},{7,3},{... | collective-permute-start | bytes 393224 | tf_op jit(solution)/shard_map/ppermute | solution.py:220
  88.1 6.7 %collective-permute-start.5 = (f32[3,4,32,128]{3,2,1,0:T(8,128)S(1)}, f32[3,4,32,128]{3,2,1,0:T(8,128)S(1)}, u32[]{:S(2)}, u32[]{:S(2)}) collective-permute-start(f32[3,4,32,128]{3,2,1,0:T(8,128)S(1)} %get-tuple-element.71), channel_id=1, source_target_pairs={{0,4},{4,8},{8,12},{1,5},{5,9},{9,13},{2,6},{6,10},{10,14},{3,7},{... | collective-permute-start | bytes 589832 | tf_op jit(solution)/shard_map/ppermute | solution.py:220
  91.6 7.6 %collective-permute-start.6 = (f32[3,4,32,128]{3,2,1,0:T(8,128)S(1)}, f32[3,4,32,128]{3,2,1,0:T(8,128)S(1)}, u32[]{:S(2)}, u32[]{:S(2)}) collective-permute-start(f32[3,4,32,128]{3,2,1,0:T(8,128)S(1)} %get-tuple-element.72), channel_id=1, source_target_pairs={{4,0},{8,4},{12,8},{5,1},{9,5},{13,9},{6,2},{10,6},{14,10},{7,3},{... | collective-permute-start | bytes 589832 | tf_op jit(solution)/shard_map/ppermute | solution.py:220
  92.9 89.4 %collective-permute-start.22 = (f32[8,6,8,8,128]{4,3,2,1,0:T(8,128)S(1)}, f32[8,6,8,8,128]{4,3,2,1,0:T(8,128)S(1)}, u32[]{:S(2)}, u32[]{:S(2)}) collective-permute-start(f32[8,6,8,8,128]{4,3,2,1,0:T(8,128)S(1)} %multiply_add_fusion.refs_10_), channel_id=1, source_target_pairs={{0,1},{1,0},{2,3},{3,2},{4,5},{5,4},{6,7},{7,6},{8,9},{9,8},{10,11... | collective-permute-start | bytes 4718600 | tf_op jit(solution)/shard_map/ppermute | solution.py:213
  93.0 89.3 %collective-permute-start.24 = (f32[8,6,8,8,128]{4,3,2,1,0:T(8,128)}, f32[8,6,8,8,128]{4,3,2,1,0:T(8,128)S(1)}, u32[]{:S(2)}, u32[]{:S(2)}) collective-permute-start(f32[8,6,8,8,128]{4,3,2,1,0:T(8,128)} %collective-permute-done.23.refs_12_), channel_id=1, source_target_pairs={{0,1},{1,0},{2,3},{3,2},{4,5},{5,4},{6,7},{7,6},{8,9},{9,8},{10,11... | collective-permute-start | bytes 4718600 | tf_op jit(solution)/shard_map/ppermute | solution.py:213
  100.9 6.7 %collective-permute-start.7 = (f32[3,4,32,128]{3,2,1,0:T(8,128)S(1)}, f32[3,4,32,128]{3,2,1,0:T(8,128)S(1)}, u32[]{:S(2)}, u32[]{:S(2)}) collective-permute-start(f32[3,4,32,128]{3,2,1,0:T(8,128)S(1)} %get-tuple-element.78), channel_id=1, source_target_pairs={{0,4},{4,8},{8,12},{1,5},{5,9},{9,13},{2,6},{6,10},{10,14},{3,7},{... | collective-permute-start | bytes 589832 | tf_op jit(solution)/shard_map/ppermute | solution.py:220
  104.4 7.6 %collective-permute-start.8 = (f32[3,4,32,128]{3,2,1,0:T(8,128)S(1)}, f32[3,4,32,128]{3,2,1,0:T(8,128)S(1)}, u32[]{:S(2)}, u32[]{:S(2)}) collective-permute-start(f32[3,4,32,128]{3,2,1,0:T(8,128)S(1)} %get-tuple-element.79), channel_id=1, source_target_pairs={{4,0},{8,4},{12,8},{5,1},{9,5},{13,9},{6,2},{10,6},{14,10},{7,3},{... | collective-permute-start | bytes 589832 | tf_op jit(solution)/shard_map/ppermute | solution.py:220
  113.7 5.1 %collective-permute-start.9 = (f32[3,4,32,128]{3,2,1,0:T(8,128)S(1)}, f32[3,4,32,128]{3,2,1,0:T(8,128)S(1)}, u32[]{:S(2)}, u32[]{:S(2)}) collective-permute-start(f32[3,4,32,128]{3,2,1,0:T(8,128)S(1)} %get-tuple-element.85), channel_id=1, source_target_pairs={{0,4},{4,8},{8,12},{1,5},{5,9},{9,13},{2,6},{6,10},{10,14},{3,7},{... | collective-permute-start | bytes 589832 | tf_op jit(solution)/shard_map/ppermute | solution.py:220
  115.6 7.6 %collective-permute-start.10 = (f32[3,4,32,128]{3,2,1,0:T(8,128)S(1)}, f32[3,4,32,128]{3,2,1,0:T(8,128)S(1)}, u32[]{:S(2)}, u32[]{:S(2)}) collective-permute-start(f32[3,4,32,128]{3,2,1,0:T(8,128)S(1)} %get-tuple-element.86), channel_id=1, source_target_pairs={{4,0},{8,4},{12,8},{5,1},{9,5},{13,9},{6,2},{10,6},{14,10},{7,3},{... | collective-permute-start | bytes 589832 | tf_op jit(solution)/shard_map/ppermute | solution.py:220
  124.8 5.1 %collective-permute-start.11 = (f32[3,4,32,128]{3,2,1,0:T(8,128)S(1)}, f32[3,4,32,128]{3,2,1,0:T(8,128)S(1)}, u32[]{:S(2)}, u32[]{:S(2)}) collective-permute-start(f32[3,4,32,128]{3,2,1,0:T(8,128)S(1)} %get-tuple-element.92), channel_id=1, source_target_pairs={{0,4},{4,8},{8,12},{1,5},{5,9},{9,13},{2,6},{6,10},{10,14},{3,7},{... | collective-permute-start | bytes 589832 | tf_op jit(solution)/shard_map/ppermute | solution.py:220
  126.8 7.6 %collective-permute-start.12 = (f32[3,4,32,128]{3,2,1,0:T(8,128)S(1)}, f32[3,4,32,128]{3,2,1,0:T(8,128)S(1)}, u32[]{:S(2)}, u32[]{:S(2)}) collective-permute-start(f32[3,4,32,128]{3,2,1,0:T(8,128)S(1)} %get-tuple-element.93), channel_id=1, source_target_pairs={{4,0},{8,4},{12,8},{5,1},{9,5},{13,9},{6,2},{10,6},{14,10},{7,3},{... | collective-permute-start | bytes 589832 | tf_op jit(solution)/shard_map/ppermute | solution.py:220
  136.0 5.1 %collective-permute-start.13 = (f32[3,4,32,128]{3,2,1,0:T(8,128)S(1)}, f32[3,4,32,128]{3,2,1,0:T(8,128)S(1)}, u32[]{:S(2)}, u32[]{:S(2)}) collective-permute-start(f32[3,4,32,128]{3,2,1,0:T(8,128)S(1)} %get-tuple-element.99), channel_id=1, source_target_pairs={{0,4},{4,8},{8,12},{1,5},{5,9},{9,13},{2,6},{6,10},{10,14},{3,7},{... | collective-permute-start | bytes 589832 | tf_op jit(solution)/shard_map/ppermute | solution.py:220
  138.0 7.6 %collective-permute-start.14 = (f32[3,4,32,128]{3,2,1,0:T(8,128)S(1)}, f32[3,4,32,128]{3,2,1,0:T(8,128)S(1)}, u32[]{:S(2)}, u32[]{:S(2)}) collective-permute-start(f32[3,4,32,128]{3,2,1,0:T(8,128)S(1)} %get-tuple-element.100), channel_id=1, source_target_pairs={{4,0},{8,4},{12,8},{5,1},{9,5},{13,9},{6,2},{10,6},{14,10},{7,3},{... | collective-permute-start | bytes 589832 | tf_op jit(solution)/shard_map/ppermute | solution.py:220
  147.2 5.6 %collective-permute-start.15 = (f32[3,4,32,128]{3,2,1,0:T(8,128)S(1)}, f32[3,4,32,128]{3,2,1,0:T(8,128)S(1)}, u32[]{:S(2)}, u32[]{:S(2)}) collective-permute-start(f32[3,4,32,128]{3,2,1,0:T(8,128)S(1)} %get-tuple-element.106), channel_id=1, source_target_pairs={{0,4},{4,8},{8,12},{1,5},{5,9},{9,13},{2,6},{6,10},{10,14},{3,7},{... | collective-permute-start | bytes 589832 | tf_op jit(solution)/shard_map/ppermute | solution.py:220
  149.1 8.3 %collective-permute-start.16 = (f32[3,4,32,128]{3,2,1,0:T(8,128)S(1)}, f32[3,4,32,128]{3,2,1,0:T(8,128)S(1)}, u32[]{:S(2)}, u32[]{:S(2)}) collective-permute-start(f32[3,4,32,128]{3,2,1,0:T(8,128)S(1)} %get-tuple-element.107), channel_id=1, source_target_pairs={{4,0},{8,4},{12,8},{5,1},{9,5},{13,9},{6,2},{10,6},{14,10},{7,3},{... | collective-permute-start | bytes 589832 | tf_op jit(solution)/shard_map/ppermute | solution.py:220
  159.2 6.5 %collective-permute-start.17 = (f32[3,4,32,128]{3,2,1,0:T(8,128)S(1)}, f32[3,4,32,128]{3,2,1,0:T(8,128)S(1)}, u32[]{:S(2)}, u32[]{:S(2)}) collective-permute-start(f32[3,4,32,128]{3,2,1,0:T(8,128)S(1)} %get-tuple-element.113), channel_id=1, source_target_pairs={{0,4},{4,8},{8,12},{1,5},{5,9},{9,13},{2,6},{6,10},{10,14},{3,7},{... | collective-permute-start | bytes 589832 | tf_op jit(solution)/shard_map/ppermute | solution.py:220
  160.8 9.5 %collective-permute-start.18 = (f32[3,4,32,128]{3,2,1,0:T(8,128)S(1)}, f32[3,4,32,128]{3,2,1,0:T(8,128)S(1)}, u32[]{:S(2)}, u32[]{:S(2)}) collective-permute-start(f32[3,4,32,128]{3,2,1,0:T(8,128)S(1)} %get-tuple-element.114), channel_id=1, source_target_pairs={{4,0},{8,4},{12,8},{5,1},{9,5},{13,9},{6,2},{10,6},{14,10},{7,3},{... | collective-permute-start | bytes 589832 | tf_op jit(solution)/shard_map/ppermute | solution.py:220
  172.0 4.9 %collective-permute-start.19 = (f32[3,4,32,128]{3,2,1,0:T(8,128)S(1)}, f32[3,4,32,128]{3,2,1,0:T(8,128)S(1)}, u32[]{:S(2)}, u32[]{:S(2)}) collective-permute-start(f32[3,4,32,128]{3,2,1,0:T(8,128)S(1)} %get-tuple-element.120), channel_id=1, source_target_pairs={{0,4},{4,8},{8,12},{1,5},{5,9},{9,13},{2,6},{6,10},{10,14},{3,7},{... | collective-permute-start | bytes 589832 | tf_op jit(solution)/shard_map/ppermute | solution.py:220
  173.7 7.6 %collective-permute-start.20 = (f32[3,4,32,128]{3,2,1,0:T(8,128)S(1)}, f32[3,4,32,128]{3,2,1,0:T(8,128)S(1)}, u32[]{:S(2)}, u32[]{:S(2)}) collective-permute-start(f32[3,4,32,128]{3,2,1,0:T(8,128)S(1)} %get-tuple-element.121), channel_id=1, source_target_pairs={{4,0},{8,4},{12,8},{5,1},{9,5},{13,9},{6,2},{10,6},{14,10},{7,3},{... | collective-permute-start | bytes 589832 | tf_op jit(solution)/shard_map/ppermute | solution.py:220
  185.1 1.4 collective-permute-start.25
  186.5 4.3 %collective-permute-start.26 = (f32[1,2,8,8,128]{4,3,2,1,0:T(8,128)S(1)}, f32[1,2,8,8,128]{4,3,2,1,0:T(8,128)S(1)}, u32[]{:S(2)}, u32[]{:S(2)}) collective-permute-start(f32[1,2,8,8,128]{4,3,2,1,0:T(8,128)S(1)} %slice_add_fusion), channel_id=1, source_target_pairs={{0,2},{1,3},{2,0},{3,1},{4,6},{5,7},{6,4},{7,5},{8,10},{9,11},{10,... | collective-permute-start | bytes 196616 | tf_op jit(solution)/shard_map/ppermute | solution.py:213
  190.8 4.0 %collective-permute-start.27 = (f32[2,4,8,128]{3,2,1,0:T(8,128)S(1)}, f32[2,4,8,128]{3,2,1,0:T(8,128)S(1)}, u32[]{:S(2)}, u32[]{:S(2)}) collective-permute-start(f32[2,4,8,128]{3,2,1,0:T(8,128)S(1)} %dynamic-slice_bitcast_fusion.4), channel_id=1, source_target_pairs={{0,16},{16,0},{1,17},{17,1},{2,18},{18,2},{3,19},{19,3},{4,20},{20... | collective-permute-start | bytes 98312 | tf_op jit(solution)/shard_map/ppermute | solution.py:213
where the time goes:
time: 196 us; the launch traced here: 195 us
  waiting for transfers between devices  120 us (61%)
  starting transfers between devices  43.9 us (22%)
  Pallas kernels  18.7 us (10%)
  local copies, waits for them, and re-layouts  5.51 us (3%)
  other arithmetic  4.58 us (2%)
  between operations  2.62 us (1%)
    ppermute x10, waiting for transfers between devices, swap(): return lax.ppermute(array, axis, [(i, i ^ turn) for i in range(count)])  62.5 us
    ppermute x18, waiting for transfers between devices, to_neighbours(): return (lax.ppermute(high, axis, up), lax.ppermute(low, axis, down))  57.7 us
    ppermute x18, starting transfers between devices, to_neighbours(): return (lax.ppermute(high, axis, up), lax.ppermute(low, axis, down))  33.2 us
    pallas_call x11, Pallas kernels, call(): pl.pallas_call(body, out_shape=[jax.ShapeDtypeStruct(shape, F32) for shap...  18.7 us
    ppermute x10, starting transfers between devices, swap(): return lax.ppermute(array, axis, [(i, i ^ turn) for i in range(count)])  10.7 us
  transfers between devices with their start and end apart: 28, of which 24 were waited for; matrix products, arithmetic and copies ran while one was open for 2% of the time, Pallas kernels for 8%

commit v1 on v0

--- a/solution.py
+++ b/solution.py
@@ -16,6 +16,7 @@
 REACH = 2
 DEEP = 2 * REACH
 ALONG_X = (0, 3, 4)
+ME, FLIP, HAS_LOW, HAS_HIGH, SPOT_X, SPOT_Y = range(6)
 
 VMEM = pl.BlockSpec(memory_space=pltpu.VMEM)
 SMEM = pl.BlockSpec(memory_space=pltpu.SMEM)
@@ -52,8 +53,17 @@
     return near - far
 
 
-def across(rows, x):
-    return C_NEAR * (rows(x + 1) - rows(x - 1)) - C_FAR * (rows(x + 2) - rows(x - 2))
+def across(rows, x, sign):
+    near, far = sign * C_NEAR, sign * C_FAR
+    return near * (rows(x + 1) - rows(x - 1)) - far * (rows(x + 2) - rows(x - 2))
+
+
+def sign_of(place):
+    return 1.0 - 2.0 * place[FLIP].astype(F32)
+
+
+def mirrored(place, x, tile_x):
+    return x + place[FLIP] * (tile_x - 1 - 2 * x)
 
 
 def assemble(place, *refs):
@@ -61,22 +71,27 @@
     tiles, (vel, stress, cells, low, high) = refs[:count], refs[count:]
     tile_x, tile_y = tiles[0].shape[1:3]
     for turn, tile in enumerate(tiles):
-        spot = pl.ds(pl.multiple_of((place[0] ^ turn) * tile_y, tile_y), tile_y)
-        vel[:, :, spot, :] = tile[0:3]
-        stress[:, :, spot, :] = tile[3:9]
-        cells[:, spot, :] = tile[9]
-        for at, comp in enumerate(ALONG_X):
-            low[at, :, spot, :] = tile[3 + comp, :REACH]
-            high[at, :, spot, :] = tile[3 + comp, tile_x - REACH :]
-        low[len(ALONG_X), :, spot, :] = tile[9, :REACH]
-        high[len(ALONG_X), :, spot, :] = tile[9, tile_x - REACH :]
+        spot = pl.ds(pl.multiple_of((place[ME] ^ turn) * tile_y, tile_y), tile_y)
+        for x in range(tile_x):
+            row = mirrored(place, x, tile_x)
+            for comp in range(3):
+                vel[comp, x, spot, :] = tile[comp, row]
+            for comp in range(6):
+                stress[comp, x, spot, :] = tile[3 + comp, row]
+            cells[x, spot, :] = tile[9, row]
+            for at, comp in enumerate(ALONG_X + (6,)):
+                if x < REACH:
+                    low[at, x, spot, :] = tile[3 + comp, row]
+                if x >= tile_x - REACH:
+                    high[at, x - (tile_x - REACH), spot, :] = tile[3 + comp, row]
 
 
 def push(place, amount, stress, vel, low_stress, high_stress, buoyancy, vel_out, low_out, high_out):
     _, tile_x, size_y, depth = vel.shape
     shape = (size_y, depth)
     coef_y, coef_z = edge_coefs(shape, 0), edge_coefs(shape, 1)
-    spot = (lax.broadcasted_iota(jnp.int32, shape, 0) == place[4]) & (
+    sign = sign_of(place)
+    spot = (lax.broadcasted_iota(jnp.int32, shape, 0) == place[SPOT_Y]) & (
         lax.broadcasted_iota(jnp.int32, shape, 1) == 0
     )
     spot = jnp.where(spot, amount, 0.0)
@@ -84,19 +99,19 @@
     def rows(at):
         def row(x):
             if x < 0:
-                return low_stress[at, x + REACH]
+                return low_stress[at, -1 - x]
             if x >= tile_x:
-                return high_stress[at, x - tile_x]
+                return high_stress[at, REACH - 1 - (x - tile_x)]
             return stress[ALONG_X[at], x]
 
         return row
 
     for x in range(tile_x):
         xy, xz, yz = stress[3, x], stress[4, x], stress[5, x]
-        force_x = across(rows(0), x) + in_row(xy, coef_y, 0) + in_row(xz, coef_z, 1)
-        force_y = across(rows(1), x) + in_row(stress[1, x], coef_y, 0) + in_row(yz, coef_z, 1)
-        force_z = across(rows(2), x) + in_row(yz, coef_y, 0) + in_row(stress[2, x], coef_z, 1)
-        force_z = force_z + jnp.where(place[3] == x, 1.0, 0.0) * spot
+        force_x = across(rows(0), x, sign) + in_row(xy, coef_y, 0) + in_row(xz, coef_z, 1)
+        force_y = across(rows(1), x, sign) + in_row(stress[1, x], coef_y, 0) + in_row(yz, coef_z, 1)
+        force_z = across(rows(2), x, sign) + in_row(yz, coef_y, 0) + in_row(stress[2, x], coef_z, 1)
+        force_z = force_z + jnp.where(place[SPOT_X] == x, 1.0, 0.0) * spot
         light = buoyancy[x]
         for comp, force in enumerate((force_x, force_y, force_z)):
             fresh = vel[comp, x] + light * force
@@ -112,9 +127,9 @@
     count = table.shape[0]
     for x in range(-REACH, tile_x + REACH):
         if x < 0:
-            number, inside = low[len(ALONG_X), x + REACH], place[1] > 0
+            number, inside = low[len(ALONG_X), -1 - x], place[HAS_LOW] > 0
         elif x >= tile_x:
-            number, inside = high[len(ALONG_X), x - tile_x], place[1] < place[2] - 1
+            number, inside = high[len(ALONG_X), REACH - 1 - (x - tile_x)], place[HAS_HIGH] > 0
         else:
             number, inside = cells[x], None
         parts = [jnp.full(number.shape, table[0, c], F32) for c in range(3)]
@@ -126,7 +141,7 @@
         shear[x + REACH] = (2.0 * TIME_STEP * STIFFNESS * half_step) * parts[2]
         if inside is None:
             light[x] = TIME_STEP / parts[0]
-    amount = AMPLITUDE * residual[place[0], 0]
+    amount = AMPLITUDE * residual[place[ME], 0]
     push(place, amount, stress, vel, low, high, light, vel_out, low_out, high_out)
 
 
@@ -143,22 +158,23 @@
     def rows(comp):
         def row(x):
             if x < 0:
-                return low[comp, x + DEEP]
+                return low[comp, -1 - x]
             if x >= tile_x:
-                return high[comp, x - tile_x]
+                return high[comp, DEEP - 1 - (x - tile_x)]
             return vel[comp, x]
 
         return row
 
     vx, vy, vz = rows(0), rows(1), rows(2)
+    sign = sign_of(place)
     reach = 0 if last else REACH
     for x in range(-reach, tile_x + reach):
         own = 0 <= x < tile_x
-        xx = across(vx, x)
+        xx = across(vx, x, sign)
         yy = in_row(vy(x), coef_y, 0)
         zz = in_row(vz(x), coef_z, 1)
-        xy = 0.5 * (in_row(vx(x), coef_y, 0) + across(vy, x))
-        xz = 0.5 * (in_row(vx(x), coef_z, 1) + across(vz, x))
+        xy = 0.5 * (in_row(vx(x), coef_y, 0) + across(vy, x, sign))
+        xz = 0.5 * (in_row(vx(x), coef_z, 1) + across(vz, x, sign))
         if own:
             yz = 0.5 * (in_row(vy(x), coef_z, 1) + in_row(vz(x), coef_y, 0))
             for comp, rate in enumerate((xx, yy, zz, xy, xz, yz)):
@@ -174,13 +190,15 @@
                 stress_out[3 + comp, x] = stress[3 + comp, x] + stiff * rate
         else:
             source, target, row = (
-                (low_stress, low_stress_out, x + REACH) if x < 0 else (high_stress, high_stress_out, x - tile_x)
+                (low_stress, low_stress_out, -1 - x)
+                if x < 0
+                else (high_stress, high_stress_out, REACH - 1 - (x - tile_x))
             )
             target[0, row] = source[0, row] + (bulk + stiff * xx)
             target[1, row] = source[1, row] + stiff * xy
             target[2, row] = source[2, row] + stiff * xz
     if not last:
-        amount = AMPLITUDE * residual[place[0], moment + 1]
+        amount = AMPLITUDE * residual[place[ME], moment + 1]
         push(place, amount, stress_out, vel, low_stress_out, high_stress_out, light, vel_out, low_out, high_out)
 
 
@@ -191,21 +209,22 @@
     (terms,) = refs[2 + moments + pieces :]
     tile_x, tile_y = sources[0].shape[2:4]
     for turn in range(pieces):
-        spot = pl.ds(pl.multiple_of((place[0] ^ turn) * tile_y, tile_y), tile_y)
+        spot = pl.ds(pl.multiple_of((place[ME] ^ turn) * tile_y, tile_y), tile_y)
         for x in range(tile_x):
+            row = mirrored(place, x, tile_x)
             lam = mu = None
             for moment in range(moments):
-                weight = KERNEL_SCALE * residual[place[0], moment]
+                weight = KERNEL_SCALE * residual[place[ME], moment]
                 rate = [rates[moment][c, x, spot, :] for c in range(6)]
-                source = [sources[turn][moment, c, x] for c in range(6)]
+                source = [sources[turn][moment, c, row] for c in range(6)]
                 bulk = (source[0] + source[1] + source[2]) * (rate[0] + rate[1] + rate[2])
                 diag = source[0] * rate[0] + source[1] * rate[1] + source[2] * rate[2]
                 off = source[3] * rate[3] + source[4] * rate[4] + source[5] * rate[5]
                 bulk, both = weight * bulk, (2.0 * weight) * (diag + 2.0 * off)
                 lam = bulk if lam is None else lam + bulk
                 mu = both if mu is None else mu + both
-            terms[turn, 0, x] = lam
-            terms[turn, 1, x] = mu
+            terms[turn, 0, row] = lam
+            terms[turn, 1, row] = mu
 
 
 def swap(array, axis, turn):
@@ -213,11 +232,23 @@
     return lax.ppermute(array, axis, [(i, i ^ turn) for i in range(count)])
 
 
-def to_neighbours(low, high, axis):
-    count = lax.axis_size(axis)
-    up = [(i, i + 1) for i in range(count - 1)]
-    down = [(i + 1, i) for i in range(count - 1)]
-    return lax.ppermute(high, axis, up), lax.ppermute(low, axis, down)
+def partner(slab, piece, slabs, turn):
+    other = slab + 1 - 2 * ((slab + piece + turn) % 2)
+    return other, (other >= 0) & (other < slabs)
+
+
+def to_neighbours(low, high):
+    slabs, pieces = lax.axis_size("gx"), lax.axis_size("gy")
+    got = []
+    for turn, face in enumerate((high, low)):
+        pairs = []
+        for slab in range(slabs):
+            for piece in range(pieces):
+                other, inside = partner(slab, piece, slabs, turn)
+                if inside:
+                    pairs.append((slab * pieces + piece, other * pieces + piece))
+        got.append(lax.ppermute(face, ("gx", "gy"), pairs))
+    return got[1], got[0]
 
 
 def local(rec_state, source_strain, material, material_table, residual, rec_cell, listed, src_pick):
@@ -237,17 +268,15 @@
         mine = jnp.concatenate([mine, numbers], 0)
         chunks.append(swap(mine, "gy", turn) if turn else mine)
 
-    weights = lax.dynamic_slice_in_dim(listed, group, 1, 2)[:, :, 0].astype(F32)
-    combined = 0.0
-    for turn in range(groups):
-        piece = swap(source_strain[0], "sta", turn) if turn else source_strain[0]
-        factor = jnp.sum(weights * (src_pick == (group ^ turn)).astype(F32), 0)
-        combined = combined + factor[:, None, None, None, None] * piece.astype(F32)
+    strains = [swap(source_strain[0], "sta", turn) if turn else source_strain[0] for turn in range(groups)]
 
     cell = lax.dynamic_index_in_dim(rec_cell[0], me, 0, keepdims=False)
-    place = jnp.stack(
-        [me, slab, jnp.full((), lax.axis_size("gx")), cell // size_y - slab * tile_x, cell % size_y]
-    ).astype(jnp.int32)
+    flip = (slab + me) % 2
+    has_high = partner(slab, me, lax.axis_size("gx"), 0)[1]
+    has_low = partner(slab, me, lax.axis_size("gx"), 1)[1]
+    spot_x = cell // size_y - slab * tile_x
+    spot_x = spot_x + flip * (tile_x - 1 - 2 * spot_x)
+    place = jnp.stack([me, flip, has_low, has_high, spot_x, cell % size_y]).astype(jnp.int32)
     rows = residual[0]
     whole, halo, face = (size_y, depth), (3, REACH, size_y, depth), (3, DEEP, size_y, depth)
     vel_shape, stress_shape = (3, tile_x) + whole, (6, tile_x) + whole
@@ -258,7 +287,7 @@
         [vel_shape, stress_shape, (tile_x,) + whole, ends, ends],
         [(place, True)] + [(chunk, False) for chunk in chunks],
     )
-    low_stress, high_stress = to_neighbours(low, high, "gx")
+    low_stress, high_stress = to_neighbours(low, high)
     vel, low, high, light, lame, shear = call(
         first,
         [vel_shape, face, face, (tile_x,) + whole, (tile_x + 2 * REACH,) + whole, (tile_x + 2 * REACH,) + whole],
@@ -267,10 +296,29 @@
     )
     low_stress, high_stress = low_stress[:3], high_stress[:3]
 
+    strains, low, high = lax.optimization_barrier((strains, low, high))
+    weights = lax.dynamic_slice_in_dim(listed, group, 1, 2)[:, :, 0].astype(F32)
+    combined = 0.0
+    for turn in range(groups):
+        factor = jnp.sum(weights * (src_pick == (group ^ turn)).astype(F32), 0)
+        combined = combined + factor[:, None, None, None, None] * strains[turn].astype(F32)
+
+    width = pieces // 2
+    found = {0: combined}
+    if width:
+        found[width] = swap(combined, "gy", width)
+        width //= 2
+
     rates = []
     for moment in range(moments):
+        if moment == 5 * moments // 8:
+            found, low, high = lax.optimization_barrier((found, low, high))
+            while width:
+                for turn in list(found):
+                    found[turn ^ width] = swap(found[turn], "gy", width)
+                width //= 2
         last = moment == moments - 1
-        low, high = to_neighbours(low, high, "gx")
+        low, high = to_neighbours(low, high)
         outs = [stress_shape]
         if not last:
             outs += [stress_shape, halo, halo, vel_shape, face, face]
@@ -287,13 +335,6 @@
         if not last:
             stress, low_stress, high_stress, vel, low, high = results[1:]
 
-    sources = [combined]
-    width = pieces // 2
-    found = {0: combined}
-    while width:
-        for turn in list(found):
-            found[turn ^ width] = swap(found[turn], "gy", width)
-        width //= 2
     sources = [found[turn] for turn in range(pieces)]
 
     (terms,) = call(

time: 196 us -> 148 us (0.76)
  waiting for transfers between devices: 120 us -> 51.2 us
  starting transfers between devices: 43.9 us -> 70.4 us
  local copies, waits for them, and re-layouts: 5.51 us -> 2.14 us
    ppermute x10, waiting for transfers between devices: 62.5 us -> 19.6 us  [swap(): return lax.ppermute(array, axis, [(i, i ^ turn) for i in range(count)])]
    ppermute x18, starting transfers between devices: 33.2 us -> 61.9 us  [to_neighbours(): got.append(lax.ppermute(face, ('gx', 'gy'), pairs))]
    ppermute x18, waiting for transfers between devices: 57.7 us -> 31.6 us  [to_neighbours(): got.append(lax.ppermute(face, ('gx', 'gy'), pairs))]
    unnamed x17 -> x11, local copies, waits for them, and re-layouts: 3.49 us -> 0.11 us
    ppermute x10, starting transfers between devices: 10.7 us -> 8.57 us  [swap(): return lax.ppermute(array, axis, [(i, i ^ turn) for i in range(count)])]
  transfers between devices with their start and end apart: 28 -> 28, of which waited for: 24 -> 14; matrix products, arithmetic and copies ran while one was open for 2% -> 2% of each run, Pallas kernels for 8% -> 10%
where the time goes in v1:
time: 148 us; the launch traced here: 147 us
  starting transfers between devices  70.4 us (48%)
  waiting for transfers between devices  51.2 us (35%)
  Pallas kernels  17.3 us (12%)
  other arithmetic  3.29 us (2%)
  between operations  2.97 us (2%)
  local copies, waits for them, and re-layouts  2.14 us (1%)
    ppermute x18, starting transfers between devices, to_neighbours(): got.append(lax.ppermute(face, ('gx', 'gy'), pairs))  61.9 us
    ppermute x18, waiting for transfers between devices, to_neighbours(): got.append(lax.ppermute(face, ('gx', 'gy'), pairs))  31.6 us
    ppermute x10, waiting for transfers between devices, swap(): return lax.ppermute(array, axis, [(i, i ^ turn) for i in range(count)])  19.6 us
    pallas_call x11, Pallas kernels, call(): pl.pallas_call(body, out_shape=[jax.ShapeDtypeStruct(shape, F32) for shap...  17.3 us
    ppermute x10, starting transfers between devices, swap(): return lax.ppermute(array, axis, [(i, i ^ turn) for i in range(count)])  8.57 us
  transfers between devices with their start and end apart: 28, of which 14 were waited for; matrix products, arithmetic and copies ran while one was open for 2% of the time, Pallas kernels for 10%

profile of v1, /device:TPU:0, one launch (start us, length us, event | category | flops | bytes accessed | tf_op | source)
XLA Modules:
  0.0 147.3 jit_solution(5572952440969751747)
XLA Ops:
  0.0 2.9 %collective-permute-start.5 = (bf16[8,6,8,8,128]{4,3,2,1,0:T(8,128)(2,1)}, bf16[8,6,8,8,128]{4,3,2,1,0:T(8,128)(2,1)}, u32[]{:S(2)}, u32[]{:S(2)}) collective-permute-start(bf16[8,6,8,8,128]{4,3,2,1,0:T(8,128)(2,1)} %bitcast.34), channel_id=1, source_target_pairs={{0,16},{16,0},{1,17},{17,1},{2,18},{18,2},{3,19},{19,3},{4,20},{20... | collective-permute-start | bytes 2359304 | tf_op jit(solution)/shard_map/ppermute | solution.py:232
  2.9 0.8 convert_bitcast_fusion
  3.7 1.3 dynamic-slice_bitcast_fusion
  5.2 0.7 collective-permute-start.2
  5.9 1.0 collective-permute-start
  10.6 4.6 %collective-permute-done.2.refs_3_ = f32[10,8,8,128]{3,2,1,0:T(8,128)S(1)} collective-permute-done((f32[10,8,8,128]{3,2,1,0:T(8,128)S(1)}, f32[10,8,8,128]{3,2,1,0:T(8,128)S(1)}, u32[]{:S(2)}, u32[]{:S(2)}) %collective-permute-start.2) | collective-permute-done | bytes 327712 | tf_op jit(solution)/shard_map/ppermute | solution.py:232
  15.2 7.1 %collective-permute-done.1.refs_2_ = f32[10,8,8,128]{3,2,1,0:T(8,128)S(1)} collective-permute-done((f32[10,8,8,128]{3,2,1,0:T(8,128)S(1)}, f32[10,8,8,128]{3,2,1,0:T(8,128)S(1)}, u32[]{:S(2)}, u32[]{:S(2)}) %collective-permute-start.1) | collective-permute-done | bytes 327712 | tf_op jit(solution)/shard_map/ppermute | solution.py:232
  22.3 0.8 shard_map.82
  23.7 6.3 %collective-permute-start.4 = (f32[4,2,32,128]{3,2,1,0:T(8,128)S(1)}, f32[4,2,32,128]{3,2,1,0:T(8,128)S(1)}, u32[]{:S(2)}, u32[]{:S(2)}) collective-permute-start(f32[4,2,32,128]{3,2,1,0:T(8,128)S(1)} %get-tuple-element.77), channel_id=1, source_target_pairs={{0,4},{2,6},{4,0},{5,9},{6,2},{7,11},{8,12},{9,5},{10,14},{11,7},{... | collective-permute-start | bytes 393224 | tf_op jit(solution)/shard_map/ppermute | solution.py:250
  30.2 2.8 %collective-permute-done.4.high = f32[4,2,32,128]{3,2,1,0:T(8,128)S(1)} collective-permute-done((f32[4,2,32,128]{3,2,1,0:T(8,128)S(1)}, f32[4,2,32,128]{3,2,1,0:T(8,128)S(1)}, u32[]{:S(2)}, u32[]{:S(2)}) %collective-permute-start.4) | collective-permute-done | bytes 131104 | tf_op jit(solution)/shard_map/ppermute | solution.py:250
  33.0 1.6 %shard_map.83 = (f32[3,8,32,128]{3,2,1,0:T(8,128)S(1)}, f32[3,4,32,128]{3,2,1,0:T(8,128)S(1)}, f32[3,4,32,128]{3,2,1,0:T(8,128)S(1)}, f32[8,32,128]{2,1,0:T(8,12...) custom-call(s32[6]{0:T(128)S(1)} %stack.39.place.refs_0_, f32[16,3]{1,0:T(8,128)S(1)} %copy.9.table, ...), custom_call_target="tpu_custom_call" | custom-call | flops 2000000 | bytes 4000000 | tf_op jit(solution)/shard_map/pallas_call | solution.py:27
  34.6 1.7 %multiply_add_fusion.refs_10_ = f32[8,6,8,8,128]{4,3,2,1,0:T(8,128)S(1)} fusion(bf16[8,6,8,8,128]{4,3,2,1,0:T(8,128)(2,1)} %collective-permute-done.5, bf16[8,6,8,8,128]{4,3,2,1,0:T(8,128)(2,1)} %bitcast.35, f32[8]{0:T(128)S(1)} %get-tuple-element.142, f32[8]{0:T(128)S(1)} %get-tuple-element.141), kind=kLoop, calls=%fused_computation | loop fusion | flops 1966080 | bytes 3145792 | tf_op jit(solution)/shard_map/add | solution.py:304
  36.3 1.0 collective-permute-start.16
  38.1 5.6 %collective-permute-start.7 = (f32[3,4,32,128]{3,2,1,0:T(8,128)S(1)}, f32[3,4,32,128]{3,2,1,0:T(8,128)S(1)}, u32[]{:S(2)}, u32[]{:S(2)}) collective-permute-start(f32[3,4,32,128]{3,2,1,0:T(8,128)S(1)} %get-tuple-element.82), channel_id=1, source_target_pairs={{0,4},{2,6},{4,0},{5,9},{6,2},{7,11},{8,12},{9,5},{10,14},{11,7},{... | collective-permute-start | bytes 589832 | tf_op jit(solution)/shard_map/ppermute | solution.py:250
  43.7 3.6 %collective-permute-done.7.refs_4_ = f32[3,4,32,128]{3,2,1,0:T(8,128)S(1)} collective-permute-done((f32[3,4,32,128]{3,2,1,0:T(8,128)S(1)}, f32[3,4,32,128]{3,2,1,0:T(8,128)S(1)}, u32[]{:S(2)}, u32[]{:S(2)}) %collective-permute-start.7) | collective-permute-done | bytes 196640 | tf_op jit(solution)/shard_map/ppermute | solution.py:250
  47.3 1.7 %shard_map.84 = (f32[6,8,32,128]{3,2,1,0:T(8,128)S(1)}, f32[6,8,32,128]{3,2,1,0:T(8,128)S(1)}, f32[3,2,32,128]{3,2,1,0:T(8,128)S(1)}, f32[3,2,32,128]{3,2,1,0:T(...) custom-call(s32[6]{0:T(128)S(1)} %stack.39.place.refs_0_, ...), custom_call_target="tpu_custom_call" | custom-call | flops 2000000 | bytes 4000000 | tf_op jit(solution)/shard_map/pallas_call | solution.py:27
  49.0 0.7 collective-permute-start.8
  49.7 6.7 %collective-permute-start.9 = (f32[3,4,32,128]{3,2,1,0:T(8,128)S(1)}, f32[3,4,32,128]{3,2,1,0:T(8,128)S(1)}, u32[]{:S(2)}, u32[]{:S(2)}) collective-permute-start(f32[3,4,32,128]{3,2,1,0:T(8,128)S(1)} %get-tuple-element.89), channel_id=1, source_target_pairs={{0,4},{2,6},{4,0},{5,9},{6,2},{7,11},{8,12},{9,5},{10,14},{11,7},{... | collective-permute-start | bytes 589832 | tf_op jit(solution)/shard_map/ppermute | solution.py:250
  56.5 3.6 %collective-permute-done.9.refs_4_ = f32[3,4,32,128]{3,2,1,0:T(8,128)S(1)} collective-permute-done((f32[3,4,32,128]{3,2,1,0:T(8,128)S(1)}, f32[3,4,32,128]{3,2,1,0:T(8,128)S(1)}, u32[]{:S(2)}, u32[]{:S(2)}) %collective-permute-start.9) | collective-permute-done | bytes 196640 | tf_op jit(solution)/shard_map/ppermute | solution.py:250
  60.1 1.7 %shard_map.85 = (f32[6,8,32,128]{3,2,1,0:T(8,128)S(1)}, f32[6,8,32,128]{3,2,1,0:T(8,128)S(1)}, f32[3,2,32,128]{3,2,1,0:T(8,128)S(1)}, f32[3,2,32,128]{3,2,1,0:T(...) custom-call(s32[6]{0:T(128)S(1)} %stack.39.place.refs_0_, ...), custom_call_target="tpu_custom_call" | custom-call | flops 2000000 | bytes 4000000 | tf_op jit(solution)/shard_map/pallas_call | solution.py:27
  61.8 0.7 collective-permute-start.10
  62.5 5.6 %collective-permute-start.11 = (f32[3,4,32,128]{3,2,1,0:T(8,128)S(1)}, f32[3,4,32,128]{3,2,1,0:T(8,128)S(1)}, u32[]{:S(2)}, u32[]{:S(2)}) collective-permute-start(f32[3,4,32,128]{3,2,1,0:T(8,128)S(1)} %get-tuple-element.96), channel_id=1, source_target_pairs={{0,4},{2,6},{4,0},{5,9},{6,2},{7,11},{8,12},{9,5},{10,14},{11,7},{... | collective-permute-start | bytes 589832 | tf_op jit(solution)/shard_map/ppermute | solution.py:250
  68.1 3.6 %collective-permute-done.11.refs_4_ = f32[3,4,32,128]{3,2,1,0:T(8,128)S(1)} collective-permute-done((f32[3,4,32,128]{3,2,1,0:T(8,128)S(1)}, f32[3,4,32,128]{3,2,1,0:T(8,128)S(1)}, u32[]{:S(2)}, u32[]{:S(2)}) %collective-permute-start.11) | collective-permute-done | bytes 196640 | tf_op jit(solution)/shard_map/ppermute | solution.py:250
  71.7 1.7 %shard_map.86 = (f32[6,8,32,128]{3,2,1,0:T(8,128)S(1)}, f32[6,8,32,128]{3,2,1,0:T(8,128)S(1)}, f32[3,2,32,128]{3,2,1,0:T(8,128)S(1)}, f32[3,2,32,128]{3,2,1,0:T(...) custom-call(s32[6]{0:T(128)S(1)} %stack.39.place.refs_0_, ...), custom_call_target="tpu_custom_call" | custom-call | flops 2000000 | bytes 4000000 | tf_op jit(solution)/shard_map/pallas_call | solution.py:27
  73.5 0.7 collective-permute-start.12
  74.2 6.7 %collective-permute-start.13 = (f32[3,4,32,128]{3,2,1,0:T(8,128)S(1)}, f32[3,4,32,128]{3,2,1,0:T(8,128)S(1)}, u32[]{:S(2)}, u32[]{:S(2)}) collective-permute-start(f32[3,4,32,128]{3,2,1,0:T(8,128)S(1)} %get-tuple-element.103), channel_id=1, source_target_pairs={{0,4},{2,6},{4,0},{5,9},{6,2},{7,11},{8,12},{9,5},{10,14},{11,7},{... | collective-permute-start | bytes 589832 | tf_op jit(solution)/shard_map/ppermute | solution.py:250
  80.9 3.6 %collective-permute-done.13.refs_4_ = f32[3,4,32,128]{3,2,1,0:T(8,128)S(1)} collective-permute-done((f32[3,4,32,128]{3,2,1,0:T(8,128)S(1)}, f32[3,4,32,128]{3,2,1,0:T(8,128)S(1)}, u32[]{:S(2)}, u32[]{:S(2)}) %collective-permute-start.13) | collective-permute-done | bytes 196640 | tf_op jit(solution)/shard_map/ppermute | solution.py:250
  84.5 1.7 %shard_map.87 = (f32[6,8,32,128]{3,2,1,0:T(8,128)S(1)}, f32[6,8,32,128]{3,2,1,0:T(8,128)S(1)}, f32[3,2,32,128]{3,2,1,0:T(8,128)S(1)}, f32[3,2,32,128]{3,2,1,0:T(...) custom-call(s32[6]{0:T(128)S(1)} %stack.39.place.refs_0_, ...), custom_call_target="tpu_custom_call" | custom-call | flops 2000000 | bytes 4000000 | tf_op jit(solution)/shard_map/pallas_call | solution.py:27
  86.3 0.7 collective-permute-start.14
  86.9 5.6 %collective-permute-start.15 = (f32[3,4,32,128]{3,2,1,0:T(8,128)S(1)}, f32[3,4,32,128]{3,2,1,0:T(8,128)S(1)}, u32[]{:S(2)}, u32[]{:S(2)}) collective-permute-start(f32[3,4,32,128]{3,2,1,0:T(8,128)S(1)} %get-tuple-element.110), channel_id=1, source_target_pairs={{0,4},{2,6},{4,0},{5,9},{6,2},{7,11},{8,12},{9,5},{10,14},{11,7},{... | collective-permute-start | bytes 589832 | tf_op jit(solution)/shard_map/ppermute | solution.py:250
  92.6 3.6 %collective-permute-done.15.refs_4_ = f32[3,4,32,128]{3,2,1,0:T(8,128)S(1)} collective-permute-done((f32[3,4,32,128]{3,2,1,0:T(8,128)S(1)}, f32[3,4,32,128]{3,2,1,0:T(8,128)S(1)}, u32[]{:S(2)}, u32[]{:S(2)}) %collective-permute-start.15) | collective-permute-done | bytes 196640 | tf_op jit(solution)/shard_map/ppermute | solution.py:250
  96.2 1.7 %shard_map.88 = (f32[6,8,32,128]{3,2,1,0:T(8,128)S(1)}, f32[6,8,32,128]{3,2,1,0:T(8,128)S(1)}, f32[3,2,32,128]{3,2,1,0:T(8,128)S(1)}, f32[3,2,32,128]{3,2,1,0:T(...) custom-call(s32[6]{0:T(128)S(1)} %stack.39.place.refs_0_, ...), custom_call_target="tpu_custom_call" | custom-call | flops 2000000 | bytes 4000000 | tf_op jit(solution)/shard_map/pallas_call | solution.py:27
  99.2 6.7 %collective-permute-start.18 = (f32[3,4,32,128]{3,2,1,0:T(8,128)S(1)}, f32[3,4,32,128]{3,2,1,0:T(8,128)S(1)}, u32[]{:S(2)}, u32[]{:S(2)}) collective-permute-start(f32[3,4,32,128]{3,2,1,0:T(8,128)S(1)} %get-tuple-element.121), channel_id=1, source_target_pairs={{0,4},{2,6},{4,0},{5,9},{6,2},{7,11},{8,12},{9,5},{10,14},{11,7},{... | collective-permute-start | bytes 589832 | tf_op jit(solution)/shard_map/ppermute | solution.py:250
  105.9 3.6 %collective-permute-done.18.refs_4_ = f32[3,4,32,128]{3,2,1,0:T(8,128)S(1)} collective-permute-done((f32[3,4,32,128]{3,2,1,0:T(8,128)S(1)}, f32[3,4,32,128]{3,2,1,0:T(8,128)S(1)}, u32[]{:S(2)}, u32[]{:S(2)}) %collective-permute-start.18) | collective-permute-done | bytes 196640 | tf_op jit(solution)/shard_map/ppermute | solution.py:250
  109.5 1.7 %shard_map.89 = (f32[6,8,32,128]{3,2,1,0:T(8,128)S(1)}, f32[6,8,32,128]{3,2,1,0:T(8,128)S(1)}, f32[3,2,32,128]{3,2,1,0:T(8,128)S(1)}, f32[3,2,32,128]{3,2,1,0:T(...) custom-call(s32[6]{0:T(128)S(1)} %stack.39.place.refs_0_, ...), custom_call_target="tpu_custom_call" | custom-call | flops 2000000 | bytes 4000000 | tf_op jit(solution)/shard_map/pallas_call | solution.py:27
  111.3 0.7 collective-permute-start.19
  111.9 5.8 %collective-permute-start.20 = (f32[3,4,32,128]{3,2,1,0:T(8,128)S(1)}, f32[3,4,32,128]{3,2,1,0:T(8,128)S(1)}, u32[]{:S(2)}, u32[]{:S(2)}) collective-permute-start(f32[3,4,32,128]{3,2,1,0:T(8,128)S(1)} %get-tuple-element.128), channel_id=1, source_target_pairs={{0,4},{2,6},{4,0},{5,9},{6,2},{7,11},{8,12},{9,5},{10,14},{11,7},{... | collective-permute-start | bytes 589832 | tf_op jit(solution)/shard_map/ppermute | solution.py:250
  117.7 3.4 %collective-permute-done.20.refs_4_ = f32[3,4,32,128]{3,2,1,0:T(8,128)S(1)} collective-permute-done((f32[3,4,32,128]{3,2,1,0:T(8,128)S(1)}, f32[3,4,32,128]{3,2,1,0:T(8,128)S(1)}, u32[]{:S(2)}, u32[]{:S(2)}) %collective-permute-start.20) | collective-permute-done | bytes 196640 | tf_op jit(solution)/shard_map/ppermute | solution.py:250
  121.2 1.7 %shard_map.90 = (f32[6,8,32,128]{3,2,1,0:T(8,128)S(1)}, f32[6,8,32,128]{3,2,1,0:T(8,128)S(1)}, f32[3,2,32,128]{3,2,1,0:T(8,128)S(1)}, f32[3,2,32,128]{3,2,1,0:T(...) custom-call(s32[6]{0:T(128)S(1)} %stack.39.place.refs_0_, ...), custom_call_target="tpu_custom_call" | custom-call | flops 2000000 | bytes 4000000 | tf_op jit(solution)/shard_map/pallas_call | solution.py:27
  122.9 0.7 collective-permute-start.21
  123.6 6.7 %collective-permute-start.22 = (f32[3,4,32,128]{3,2,1,0:T(8,128)S(1)}, f32[3,4,32,128]{3,2,1,0:T(8,128)S(1)}, u32[]{:S(2)}, u32[]{:S(2)}) collective-permute-start(f32[3,4,32,128]{3,2,1,0:T(8,128)S(1)} %get-tuple-element.135), channel_id=1, source_target_pairs={{0,4},{2,6},{4,0},{5,9},{6,2},{7,11},{8,12},{9,5},{10,14},{11,7},{... | collective-permute-start | bytes 589832 | tf_op jit(solution)/shard_map/ppermute | solution.py:250
  130.3 3.6 %collective-permute-done.22.refs_4_ = f32[3,4,32,128]{3,2,1,0:T(8,128)S(1)} collective-permute-done((f32[3,4,32,128]{3,2,1,0:T(8,128)S(1)}, f32[3,4,32,128]{3,2,1,0:T(8,128)S(1)}, u32[]{:S(2)}, u32[]{:S(2)}) %collective-permute-start.22) | collective-permute-done | bytes 196640 | tf_op jit(solution)/shard_map/ppermute | solution.py:250
  134.0 1.0 shard_map.91.refs_9_
  135.0 1.9 %shard_map.92 = f32[4,2,8,8,128]{4,3,2,1,0:T(8,128)S(1)} custom-call(s32[6]{0:T(128)S(1)} %stack.39.place.refs_0_, f32[4,8]{1,0:T(4,128)S(1)} %bitcast.33, f32[6,8,32,128]{3,2,1,0:T(8,128)S(1)} %get-tuple-element.86.refs_2_, f32[6,8,32,128]{3,2,1,0:T(8,128)S(1)} %get-tuple-element.93.refs_3_, f32[6,8,32,128]{3,2,1,0:T(8,128)S(1)} %get-tuple-element.100.refs_4_, ...), custom_call_target="tpu_custom_call" | custom-call | flops 2000000 | bytes 4000000 | tf_op jit(solution)/shard_map/pallas_call | solution.py:27
  137.0 1.3 collective-permute-done.25
  138.4 1.1 collective-permute-start.26
  139.5 3.2 %collective-permute-done.26 = f32[1,2,8,8,128]{4,3,2,1,0:T(8,128)S(1)} collective-permute-done((f32[1,2,8,8,128]{4,3,2,1,0:T(8,128)S(1)}, f32[1,2,8,8,128]{4,3,2,1,0:T(8,128)S(1)}, u32[]{:S(2)}, u32[]{:S(2)}) %collective-permute-start.26) | collective-permute-done | bytes 65568 | tf_op jit(solution)/shard_map/ppermute | solution.py:232
  143.3 3.4 %collective-permute-done.27 = f32[2,4,8,128]{3,2,1,0:T(8,128)S(1)} collective-permute-done((f32[2,4,8,128]{3,2,1,0:T(8,128)S(1)}, f32[2,4,8,128]{3,2,1,0:T(8,128)S(1)}, u32[]{:S(2)}, u32[]{:S(2)}) %collective-permute-start.27) | collective-permute-done | bytes 32800 | tf_op jit(solution)/shard_map/ppermute | solution.py:232
  (46 shorter events, 5.4 us)
Async XLA Ops:
  0.0 7.4 %copy-start = (s32[1,4]{1,0:T(1,128)S(1)}, s32[1,4]{1,0:T(1,128)}, u32[]{:S(2)}) copy-start(s32[1,4]{1,0:T(1,128)} %param.13) | copy-start | bytes 52
  0.0 34.6 %collective-permute-start.5 = (bf16[8,6,8,8,128]{4,3,2,1,0:T(8,128)(2,1)}, bf16[8,6,8,8,128]{4,3,2,1,0:T(8,128)(2,1)}, u32[]{:S(2)}, u32[]{:S(2)}) collective-permute-start(bf16[8,6,8,8,128]{4,3,2,1,0:T(8,128)(2,1)} %bitcast.34), channel_id=1, source_target_pairs={{0,16},{16,0},{1,17},{17,1},{2,18},{18,2},{3,19},{19,3},{4,20},{20... | collective-permute-start | bytes 2359304 | tf_op jit(solution)/shard_map/ppermute | solution.py:232
  5.0 25.0 %copy-start.4 = (s32[2,8,2]{1,2,0:T(2,128)S(1)}, s32[2,8,2]{1,2,0:T(2,128)}, u32[]{:S(2)}) copy-start(s32[2,8,2]{1,2,0:T(2,128)} %param.14) | copy-start | bytes 388
  5.0 25.0 %copy-start.2 = (f32[16,3]{0,1:T(4,128)S(1)}, f32[16,3]{0,1:T(4,128)}, u32[]{:S(2)}) copy-start(f32[16,3]{0,1:T(4,128)} %param.11) | copy-start | bytes 580
  5.0 25.1 %copy-start.3 = (s32[2,8]{1,0:T(2,128)S(1)}, s32[2,8]{1,0:T(2,128)}, u32[]{:S(2)}) copy-start(s32[2,8]{1,0:T(2,128)} %param.15) | copy-start | bytes 196
  5.0 27.9 %copy-start.1 = (f32[1,4,8]{2,1,0:T(4,128)S(1)}, f32[1,4,8]{2,1,0:T(4,128)}, u32[]{:S(2)}) copy-start(f32[1,4,8]{2,1,0:T(4,128)} %param.12) | copy-start | bytes 388
  5.2 10.0 %collective-permute-start.2 = (f32[10,8,8,128]{3,2,1,0:T(8,128)S(1)}, f32[10,8,8,128]{3,2,1,0:T(8,128)S(1)}, u32[]{:S(2)}, u32[]{:S(2)}) collective-permute-start(f32[10,8,8,128]{3,2,1,0:T(8,128)S(1)} %get-tuple-element.149), channel_id=1, source_target_pairs={{0,3},{1,2},{2,1},{3,0},{4,7},{5,6},{6,5},{7,4},{8,11},{9,10},{10,... | collective-permute-start | bytes 983048 | tf_op jit(solution)/shard_map/ppermute | solution.py:232
  5.9 9.3 %collective-permute-start = (f32[10,8,8,128]{3,2,1,0:T(8,128)S(1)}, f32[10,8,8,128]{3,2,1,0:T(8,128)S(1)}, u32[]{:S(2)}, u32[]{:S(2)}) collective-permute-start(f32[10,8,8,128]{3,2,1,0:T(8,128)S(1)} %get-tuple-element.150), channel_id=1, source_target_pairs={{0,1},{1,0},{2,3},{3,2},{4,5},{5,4},{6,7},{7,6},{8,9},{9,8},{10,11... | collective-permute-start | bytes 983048 | tf_op jit(solution)/shard_map/ppermute | solution.py:232
  6.9 15.4 %collective-permute-start.1 = (f32[10,8,8,128]{3,2,1,0:T(8,128)S(1)}, f32[10,8,8,128]{3,2,1,0:T(8,128)S(1)}, u32[]{:S(2)}, u32[]{:S(2)}) collective-permute-start(f32[10,8,8,128]{3,2,1,0:T(8,128)S(1)} %get-tuple-element.151), channel_id=1, source_target_pairs={{0,2},{1,3},{2,0},{3,1},{4,6},{5,7},{6,4},{7,5},{8,10},{9,11},{10,... | collective-permute-start | bytes 983048 | tf_op jit(solution)/shard_map/ppermute | solution.py:232
  23.0 7.1 %collective-permute-start.3 = (f32[4,2,32,128]{3,2,1,0:T(8,128)S(1)}, f32[4,2,32,128]{3,2,1,0:T(8,128)S(1)}, u32[]{:S(2)}, u32[]{:S(2)}) collective-permute-start(f32[4,2,32,128]{3,2,1,0:T(8,128)S(1)} %get-tuple-element.76), channel_id=1, source_target_pairs={{1,5},{3,7},{4,8},{5,1},{6,10},{7,3},{8,4},{9,13},{10,6},{11,15},{... | collective-permute-start | bytes 393224 | tf_op jit(solution)/shard_map/ppermute | solution.py:250
  23.7 9.2 %collective-permute-start.4 = (f32[4,2,32,128]{3,2,1,0:T(8,128)S(1)}, f32[4,2,32,128]{3,2,1,0:T(8,128)S(1)}, u32[]{:S(2)}, u32[]{:S(2)}) collective-permute-start(f32[4,2,32,128]{3,2,1,0:T(8,128)S(1)} %get-tuple-element.77), channel_id=1, source_target_pairs={{0,4},{2,6},{4,0},{5,9},{6,2},{7,11},{8,12},{9,5},{10,14},{11,7},{... | collective-permute-start | bytes 393224 | tf_op jit(solution)/shard_map/ppermute | solution.py:250
  36.3 61.6 %collective-permute-start.16 = (f32[8,6,8,8,128]{4,3,2,1,0:T(8,128)S(1)}, f32[8,6,8,8,128]{4,3,2,1,0:T(8,128)S(1)}, u32[]{:S(2)}, u32[]{:S(2)}) collective-permute-start(f32[8,6,8,8,128]{4,3,2,1,0:T(8,128)S(1)} %multiply_add_fusion.refs_10_), channel_id=1, source_target_pairs={{0,2},{1,3},{2,0},{3,1},{4,6},{5,7},{6,4},{7,5},{8,10},{9,11},{10,... | collective-permute-start | bytes 4718600 | tf_op jit(solution)/shard_map/ppermute | solution.py:232
  37.4 6.3 %collective-permute-start.6 = (f32[3,4,32,128]{3,2,1,0:T(8,128)S(1)}, f32[3,4,32,128]{3,2,1,0:T(8,128)S(1)}, u32[]{:S(2)}, u32[]{:S(2)}) collective-permute-start(f32[3,4,32,128]{3,2,1,0:T(8,128)S(1)} %get-tuple-element.81), channel_id=1, source_target_pairs={{1,5},{3,7},{4,8},{5,1},{6,10},{7,3},{8,4},{9,13},{10,6},{11,15},{... | collective-permute-start | bytes 589832 | tf_op jit(solution)/shard_map/ppermute | solution.py:250
  38.1 9.2 %collective-permute-start.7 = (f32[3,4,32,128]{3,2,1,0:T(8,128)S(1)}, f32[3,4,32,128]{3,2,1,0:T(8,128)S(1)}, u32[]{:S(2)}, u32[]{:S(2)}) collective-permute-start(f32[3,4,32,128]{3,2,1,0:T(8,128)S(1)} %get-tuple-element.82), channel_id=1, source_target_pairs={{0,4},{2,6},{4,0},{5,9},{6,2},{7,11},{8,12},{9,5},{10,14},{11,7},{... | collective-permute-start | bytes 589832 | tf_op jit(solution)/shard_map/ppermute | solution.py:250
  49.0 7.4 %collective-permute-start.8 = (f32[3,4,32,128]{3,2,1,0:T(8,128)S(1)}, f32[3,4,32,128]{3,2,1,0:T(8,128)S(1)}, u32[]{:S(2)}, u32[]{:S(2)}) collective-permute-start(f32[3,4,32,128]{3,2,1,0:T(8,128)S(1)} %get-tuple-element.88), channel_id=1, source_target_pairs={{1,5},{3,7},{4,8},{5,1},{6,10},{7,3},{8,4},{9,13},{10,6},{11,15},{... | collective-permute-start | bytes 589832 | tf_op jit(solution)/shard_map/ppermute | solution.py:250
  49.7 10.4 %collective-permute-start.9 = (f32[3,4,32,128]{3,2,1,0:T(8,128)S(1)}, f32[3,4,32,128]{3,2,1,0:T(8,128)S(1)}, u32[]{:S(2)}, u32[]{:S(2)}) collective-permute-start(f32[3,4,32,128]{3,2,1,0:T(8,128)S(1)} %get-tuple-element.89), channel_id=1, source_target_pairs={{0,4},{2,6},{4,0},{5,9},{6,2},{7,11},{8,12},{9,5},{10,14},{11,7},{... | collective-permute-start | bytes 589832 | tf_op jit(solution)/shard_map/ppermute | solution.py:250
  61.8 6.3 %collective-permute-start.10 = (f32[3,4,32,128]{3,2,1,0:T(8,128)S(1)}, f32[3,4,32,128]{3,2,1,0:T(8,128)S(1)}, u32[]{:S(2)}, u32[]{:S(2)}) collective-permute-start(f32[3,4,32,128]{3,2,1,0:T(8,128)S(1)} %get-tuple-element.95), channel_id=1, source_target_pairs={{1,5},{3,7},{4,8},{5,1},{6,10},{7,3},{8,4},{9,13},{10,6},{11,15},{... | collective-permute-start | bytes 589832 | tf_op jit(solution)/shard_map/ppermute | solution.py:250
  62.5 9.2 %collective-permute-start.11 = (f32[3,4,32,128]{3,2,1,0:T(8,128)S(1)}, f32[3,4,32,128]{3,2,1,0:T(8,128)S(1)}, u32[]{:S(2)}, u32[]{:S(2)}) collective-permute-start(f32[3,4,32,128]{3,2,1,0:T(8,128)S(1)} %get-tuple-element.96), channel_id=1, source_target_pairs={{0,4},{2,6},{4,0},{5,9},{6,2},{7,11},{8,12},{9,5},{10,14},{11,7},{... | collective-permute-start | bytes 589832 | tf_op jit(solution)/shard_map/ppermute | solution.py:250
  73.5 7.4 %collective-permute-start.12 = (f32[3,4,32,128]{3,2,1,0:T(8,128)S(1)}, f32[3,4,32,128]{3,2,1,0:T(8,128)S(1)}, u32[]{:S(2)}, u32[]{:S(2)}) collective-permute-start(f32[3,4,32,128]{3,2,1,0:T(8,128)S(1)} %get-tuple-element.102), channel_id=1, source_target_pairs={{1,5},{3,7},{4,8},{5,1},{6,10},{7,3},{8,4},{9,13},{10,6},{11,15},{... | collective-permute-start | bytes 589832 | tf_op jit(solution)/shard_map/ppermute | solution.py:250
  74.2 10.4 %collective-permute-start.13 = (f32[3,4,32,128]{3,2,1,0:T(8,128)S(1)}, f32[3,4,32,128]{3,2,1,0:T(8,128)S(1)}, u32[]{:S(2)}, u32[]{:S(2)}) collective-permute-start(f32[3,4,32,128]{3,2,1,0:T(8,128)S(1)} %get-tuple-element.103), channel_id=1, source_target_pairs={{0,4},{2,6},{4,0},{5,9},{6,2},{7,11},{8,12},{9,5},{10,14},{11,7},{... | collective-permute-start | bytes 589832 | tf_op jit(solution)/shard_map/ppermute | solution.py:250
  86.3 6.3 %collective-permute-start.14 = (f32[3,4,32,128]{3,2,1,0:T(8,128)S(1)}, f32[3,4,32,128]{3,2,1,0:T(8,128)S(1)}, u32[]{:S(2)}, u32[]{:S(2)}) collective-permute-start(f32[3,4,32,128]{3,2,1,0:T(8,128)S(1)} %get-tuple-element.109), channel_id=1, source_target_pairs={{1,5},{3,7},{4,8},{5,1},{6,10},{7,3},{8,4},{9,13},{10,6},{11,15},{... | collective-permute-start | bytes 589832 | tf_op jit(solution)/shard_map/ppermute | solution.py:250
  86.9 9.2 %collective-permute-start.15 = (f32[3,4,32,128]{3,2,1,0:T(8,128)S(1)}, f32[3,4,32,128]{3,2,1,0:T(8,128)S(1)}, u32[]{:S(2)}, u32[]{:S(2)}) collective-permute-start(f32[3,4,32,128]{3,2,1,0:T(8,128)S(1)} %get-tuple-element.110), channel_id=1, source_target_pairs={{0,4},{2,6},{4,0},{5,9},{6,2},{7,11},{8,12},{9,5},{10,14},{11,7},{... | collective-permute-start | bytes 589832 | tf_op jit(solution)/shard_map/ppermute | solution.py:250
  97.9 37.1 %collective-permute-start.23 = (f32[8,6,8,8,128]{4,3,2,1,0:T(8,128)S(1)}, f32[8,6,8,8,128]{4,3,2,1,0:T(8,128)S(1)}, u32[]{:S(2)}, u32[]{:S(2)}) collective-permute-start(f32[8,6,8,8,128]{4,3,2,1,0:T(8,128)S(1)} %multiply_add_fusion.refs_10_), channel_id=1, source_target_pairs={{0,1},{1,0},{2,3},{3,2},{4,5},{5,4},{6,7},{7,6},{8,9},{9,8},{10,11... | collective-permute-start | bytes 4718600 | tf_op jit(solution)/shard_map/ppermute | solution.py:232
  98.0 37.0 %collective-permute-start.24 = (f32[8,6,8,8,128]{4,3,2,1,0:T(8,128)S(1)}, f32[8,6,8,8,128]{4,3,2,1,0:T(8,128)S(1)}, u32[]{:S(2)}, u32[]{:S(2)}) collective-permute-start(f32[8,6,8,8,128]{4,3,2,1,0:T(8,128)S(1)} %collective-permute-done.16.refs_12_), channel_id=1, source_target_pairs={{0,1},{1,0},{2,3},{3,2},{4,5},{5,4},{6,7},{7,6},{8,9},{9,8},{10,11... | collective-permute-start | bytes 4718600 | tf_op jit(solution)/shard_map/ppermute | solution.py:232
  98.5 7.4 %collective-permute-start.17 = (f32[3,4,32,128]{3,2,1,0:T(8,128)S(1)}, f32[3,4,32,128]{3,2,1,0:T(8,128)S(1)}, u32[]{:S(2)}, u32[]{:S(2)}) collective-permute-start(f32[3,4,32,128]{3,2,1,0:T(8,128)S(1)} %get-tuple-element.120), channel_id=1, source_target_pairs={{1,5},{3,7},{4,8},{5,1},{6,10},{7,3},{8,4},{9,13},{10,6},{11,15},{... | collective-permute-start | bytes 589832 | tf_op jit(solution)/shard_map/ppermute | solution.py:250
  99.2 10.4 %collective-permute-start.18 = (f32[3,4,32,128]{3,2,1,0:T(8,128)S(1)}, f32[3,4,32,128]{3,2,1,0:T(8,128)S(1)}, u32[]{:S(2)}, u32[]{:S(2)}) collective-permute-start(f32[3,4,32,128]{3,2,1,0:T(8,128)S(1)} %get-tuple-element.121), channel_id=1, source_target_pairs={{0,4},{2,6},{4,0},{5,9},{6,2},{7,11},{8,12},{9,5},{10,14},{11,7},{... | collective-permute-start | bytes 589832 | tf_op jit(solution)/shard_map/ppermute | solution.py:250
  111.3 6.5 %collective-permute-start.19 = (f32[3,4,32,128]{3,2,1,0:T(8,128)S(1)}, f32[3,4,32,128]{3,2,1,0:T(8,128)S(1)}, u32[]{:S(2)}, u32[]{:S(2)}) collective-permute-start(f32[3,4,32,128]{3,2,1,0:T(8,128)S(1)} %get-tuple-element.127), channel_id=1, source_target_pairs={{1,5},{3,7},{4,8},{5,1},{6,10},{7,3},{8,4},{9,13},{10,6},{11,15},{... | collective-permute-start | bytes 589832 | tf_op jit(solution)/shard_map/ppermute | solution.py:250
  111.9 9.2 %collective-permute-start.20 = (f32[3,4,32,128]{3,2,1,0:T(8,128)S(1)}, f32[3,4,32,128]{3,2,1,0:T(8,128)S(1)}, u32[]{:S(2)}, u32[]{:S(2)}) collective-permute-start(f32[3,4,32,128]{3,2,1,0:T(8,128)S(1)} %get-tuple-element.128), channel_id=1, source_target_pairs={{0,4},{2,6},{4,0},{5,9},{6,2},{7,11},{8,12},{9,5},{10,14},{11,7},{... | collective-permute-start | bytes 589832 | tf_op jit(solution)/shard_map/ppermute | solution.py:250
  122.9 7.4 %collective-permute-start.21 = (f32[3,4,32,128]{3,2,1,0:T(8,128)S(1)}, f32[3,4,32,128]{3,2,1,0:T(8,128)S(1)}, u32[]{:S(2)}, u32[]{:S(2)}) collective-permute-start(f32[3,4,32,128]{3,2,1,0:T(8,128)S(1)} %get-tuple-element.134), channel_id=1, source_target_pairs={{1,5},{3,7},{4,8},{5,1},{6,10},{7,3},{8,4},{9,13},{10,6},{11,15},{... | collective-permute-start | bytes 589832 | tf_op jit(solution)/shard_map/ppermute | solution.py:250
  123.6 10.4 %collective-permute-start.22 = (f32[3,4,32,128]{3,2,1,0:T(8,128)S(1)}, f32[3,4,32,128]{3,2,1,0:T(8,128)S(1)}, u32[]{:S(2)}, u32[]{:S(2)}) collective-permute-start(f32[3,4,32,128]{3,2,1,0:T(8,128)S(1)} %get-tuple-element.135), channel_id=1, source_target_pairs={{0,4},{2,6},{4,0},{5,9},{6,2},{7,11},{8,12},{9,5},{10,14},{11,7},{... | collective-permute-start | bytes 589832 | tf_op jit(solution)/shard_map/ppermute | solution.py:250
  136.9 1.4 collective-permute-start.25
  138.4 4.3 %collective-permute-start.26 = (f32[1,2,8,8,128]{4,3,2,1,0:T(8,128)S(1)}, f32[1,2,8,8,128]{4,3,2,1,0:T(8,128)S(1)}, u32[]{:S(2)}, u32[]{:S(2)}) collective-permute-start(f32[1,2,8,8,128]{4,3,2,1,0:T(8,128)S(1)} %slice_add_fusion), channel_id=1, source_target_pairs={{0,2},{1,3},{2,0},{3,1},{4,6},{5,7},{6,4},{7,5},{8,10},{9,11},{10,... | collective-permute-start | bytes 196616 | tf_op jit(solution)/shard_map/ppermute | solution.py:232
  142.7 4.0 %collective-permute-start.27 = (f32[2,4,8,128]{3,2,1,0:T(8,128)S(1)}, f32[2,4,8,128]{3,2,1,0:T(8,128)S(1)}, u32[]{:S(2)}, u32[]{:S(2)}) collective-permute-start(f32[2,4,8,128]{3,2,1,0:T(8,128)S(1)} %dynamic-slice_bitcast_fusion.4), channel_id=1, source_target_pairs={{0,16},{16,0},{1,17},{17,1},{2,18},{18,2},{3,19},{19,3},{4,20},{20... | collective-permute-start | bytes 98312 | tf_op jit(solution)/shard_map/ppermute | solution.py:232

commit v2 on v1

v2 whole, which is shorter than its diff:
```python
import functools

import jax
import jax.numpy as jnp
from jax import lax
from jax.experimental import pallas as pl
from jax.experimental.pallas import tpu as pltpu
from jax.sharding import PartitionSpec as P

C_NEAR = 8.0 / 12.0
C_FAR = 1.0 / 12.0
TIME_STEP = 0.25
AMPLITUDE = 4.0
KERNEL_SCALE = 0.0625
STIFFNESS = 0.3
REACH = 2
DEEP = 2 * REACH
ALONG_X = (0, 3, 4)
ME, FLIP, HAS_HIGH, HAS_LOW, SPOT_X, SPOT_Y = range(6)
NEAR_ROWS = 2
PACKED = DEEP + NEAR_ROWS

VMEM = pl.BlockSpec(memory_space=pltpu.VMEM)
SMEM = pl.BlockSpec(memory_space=pltpu.SMEM)
F32, BF16 = jnp.float32, jnp.bfloat16


def call(body, outs, ins, flops=1_000_000):
    scalars, arrays = ins
    return list(pl.pallas_call(
        body,
        out_shape=[jax.ShapeDtypeStruct(shape, kind) for shape, kind in outs],
        in_specs=[SMEM] * len(scalars) + [VMEM] * len(arrays),
        out_specs=[VMEM] * len(outs),
        compiler_params=pltpu.CompilerParams(vmem_limit_bytes=32 * 1024 * 1024),
        cost_estimate=pl.CostEstimate(flops=flops, bytes_accessed=2_000_000, transcendentals=0),
    )(*scalars, *arrays))


def edge_coefs(shape, axis):
    at = lax.broadcasted_iota(jnp.int32, shape, axis)
    size = shape[axis]
    return (
        jnp.where(at < size - 1, C_NEAR, 0.0).astype(F32),
        jnp.where(at >= 1, C_NEAR, 0.0).astype(F32),
        jnp.where(at < size - 2, C_FAR, 0.0).astype(F32),
        jnp.where(at >= 2, C_FAR, 0.0).astype(F32),
    )


def in_row(row, coefs, axis):
    size = row.shape[axis]
    near = coefs[0] * pltpu.roll(row, size - 1, axis) - coefs[1] * pltpu.roll(row, 1, axis)
    far = coefs[2] * pltpu.roll(row, size - 2, axis) - coefs[3] * pltpu.roll(row, 2, axis)
    return near - far


def across(rows, out, sign):
    near, far = sign * C_NEAR, sign * C_FAR
    return near * (rows(out + 1) - rows(out - 1)) - far * (rows(out + 2) - rows(out - 2))


def sign_of(place, side):
    return (1.0 - 2.0 * place[FLIP].astype(F32)) * (1.0 - 2.0 * side)


def row_of(place, side, out, tile_x):
    x = tile_x // 2 - 1 - out if side else tile_x // 2 + out
    return x + place[FLIP] * (tile_x - 1 - 2 * x)


def assemble(place, *refs):
    count = len(refs) - 10
    tiles, sides = refs[:count], (refs[count : count + 5], refs[count + 5 :])
    tile_x, tile_y = tiles[0].shape[1:3]
    for side, (vel, middle, edge, cells, face) in enumerate(sides):
        for turn, tile in enumerate(tiles):
            spot = pl.ds(pl.multiple_of((place[ME] ^ turn) * tile_y, tile_y), tile_y)
            for out in range(DEEP):
                row = row_of(place, side, out, tile_x)
                for comp in range(3):
                    vel[comp, out, spot, :] = tile[comp, row]
                part, at = (middle, out) if out < REACH else (edge, out - REACH)
                for comp in range(6):
                    part[comp, at, spot, :] = tile[3 + comp, row]
                cells[out, spot, :] = tile[9, row]
                if out >= REACH:
                    for at, comp in enumerate(ALONG_X + (6,)):
                        face[at, out - REACH, spot, :] = tile[3 + comp, row]


def push(place, side, amount, stress_row, vel, light, vel_out, sent):
    shape = vel.shape[2:]
    coef_y, coef_z = edge_coefs(shape, 0), edge_coefs(shape, 1)
    sign = sign_of(place, side)
    spot = (lax.broadcasted_iota(jnp.int32, shape, 0) == place[SPOT_Y]) & (
        lax.broadcasted_iota(jnp.int32, shape, 1) == 0
    )
    spot = jnp.where(spot, amount, 0.0)
    rows = [functools.partial(stress_row, comp) for comp in range(6)]
    for out in reversed(range(DEEP)):
        xy, xz, yz = rows[3](out), rows[4](out), rows[5](out)
        force_x = across(rows[0], out, sign) + in_row(xy, coef_y, 0) + in_row(xz, coef_z, 1)
        force_y = across(rows[3], out, sign) + in_row(rows[1](out), coef_y, 0) + in_row(yz, coef_z, 1)
        force_z = across(rows[4], out, sign) + in_row(yz, coef_y, 0) + in_row(rows[2](out), coef_z, 1)
        here = place[SPOT_X] == (-1 - out if side else out)
        force_z = force_z + jnp.where(here, 1.0, 0.0) * spot
        near = DEEP - 1 - out
        for comp, force in enumerate((force_x, force_y, force_z)):
            fresh = vel[comp, out] + light[out] * force
            vel_out[comp, out] = fresh
            high = fresh.astype(BF16)
            if near < NEAR_ROWS:
                sent[comp * PACKED + 2 * near] = high
                sent[comp * PACKED + 2 * near + 1] = (fresh - high.astype(F32)).astype(BF16)
            else:
                sent[comp * PACKED + NEAR_ROWS + near] = high


def from_halo(halo, comp, near):
    if near < NEAR_ROWS:
        at = comp * PACKED + 2 * near
        return halo[at].astype(F32) + halo[at + 1].astype(F32)
    return halo[comp * PACKED + NEAR_ROWS + near].astype(F32)


def first(side, place, table, residual, vel, middle, other, edge, cells, halo, *outs):
    vel_out, sent, light, lame, shear, halo_out = outs
    count = table.shape[0]
    for out in range(DEEP + REACH):
        if out < DEEP:
            number, share = cells[out], 1.0
        else:
            number = halo[len(ALONG_X), REACH - 1 - (out - DEEP)]
            share = jnp.where(place[HAS_LOW if side else HAS_HIGH] > 0, 1.0, 0.0)
        parts = [jnp.full(number.shape, table[0, c], F32) for c in range(3)]
        for m in range(1, count):
            hit = number == float(m)
            parts = [jnp.where(hit, table[m, c], parts[c]) for c in range(3)]
        lame[out] = (TIME_STEP * STIFFNESS * share) * parts[1]
        shear[out] = (2.0 * TIME_STEP * STIFFNESS * share) * parts[2]
        if out < DEEP:
            light[out] = TIME_STEP / parts[0]
    for at in range(len(ALONG_X)):
        for near in range(REACH):
            halo_out[at, near] = halo[at, REACH - 1 - near]
    amount = AMPLITUDE * residual[place[ME], 0]
    push(place, side, amount, stress_rows(middle, other, edge, halo_out), vel, light, vel_out, sent)


def stress_rows(middle, other, edge, halo):
    def row(comp, out):
        if out < 0:
            return other[comp, -1 - out]
        if out < REACH:
            return middle[comp, out]
        if out < DEEP:
            return edge[comp, out - REACH]
        return halo[ALONG_X.index(comp), out - DEEP]

    return row


def strain_rate(vx, vy, vz, out, sign, coef_y, coef_z, full):
    x, y, z = vx(out), vy(out), vz(out)
    rates = [
        across(vx, out, sign),
        in_row(y, coef_y, 0),
        in_row(z, coef_z, 1),
        0.5 * (in_row(x, coef_y, 0) + across(vy, out, sign)),
        0.5 * (in_row(x, coef_z, 1) + across(vz, out, sign)),
    ]
    if full:
        rates.append(0.5 * (in_row(y, coef_z, 1) + in_row(z, coef_y, 0)))
    return rates


def renew(rates, lame, shear, before):
    bulk = lame * (rates[0] + rates[1] + rates[2])
    return {
        comp: old + (bulk + shear * rates[comp] if comp < 3 else shear * rates[comp])
        for comp, old in before.items()
    }


def outer(side, moment, last, place, residual, vel, halo, edge, *refs):
    if last:
        (rates_out,) = refs
    else:
        old_halo, middle, other, light, lame, shear, rates_out, edge_out, halo_out, vel_out, sent = refs
    shape = vel.shape[2:]
    coef_y, coef_z = edge_coefs(shape, 0), edge_coefs(shape, 1)
    sign = sign_of(place, side)

    def rows(comp):
        return lambda out: vel[comp, out] if out < DEEP else from_halo(halo, comp, out - DEEP)

    vx, vy, vz = rows(0), rows(1), rows(2)
    for out in range(REACH, DEEP if last else DEEP + REACH):
        own = out < DEEP
        rates = strain_rate(vx, vy, vz, out, sign, coef_y, coef_z, own)
        if own:
            for comp in range(6):
                rates_out[comp, out - REACH] = rates[comp]
        if last:
            continue
        if own:
            fresh = renew(rates, lame[out], shear[out], {comp: edge[comp, out - REACH] for comp in range(6)})
            for comp, value in fresh.items():
                edge_out[comp, out - REACH] = value
        else:
            before = {comp: old_halo[at, out - DEEP] for at, comp in enumerate(ALONG_X)}
            fresh = renew(rates, lame[out], shear[out], before)
            for at, comp in enumerate(ALONG_X):
                halo_out[at, out - DEEP] = fresh[comp]
    if not last:
        amount = AMPLITUDE * residual[place[ME], moment + 1]
        push(place, side, amount, stress_rows(middle, other, edge_out, halo_out), vel, light, vel_out, sent)


def inner(last, place, *refs):
    vels = refs[:2]
    shape = vels[0].shape[2:]
    coef_y, coef_z = edge_coefs(shape, 0), edge_coefs(shape, 1)
    if last:
        rates_out = refs[2:]
    else:
        middles, lames, shears = refs[2:4], refs[4:6], refs[6:8]
        rates_out, middles_out = refs[8:10], refs[10:12]
    for side in range(2):
        sign = sign_of(place, side)

        def rows(comp):
            return lambda out: vels[side][comp, out] if out >= 0 else vels[1 - side][comp, -1 - out]

        for out in range(REACH):
            rates = strain_rate(rows(0), rows(1), rows(2), out, sign, coef_y, coef_z, True)
            for comp in range(6):
                rates_out[side][comp, out] = rates[comp]
            if not last:
                before = {comp: middles[side][comp, out] for comp in range(6)}
                fresh = renew(rates, lames[side][out], shears[side][out], before)
                for comp, value in fresh.items():
                    middles_out[side][comp, out] = value


def correlate(moments, pieces, place, residual, *refs):
    rates, sources, terms = refs[: 4 * moments], refs[4 * moments : 4 * moments + pieces], refs[-1]
    tile_x, tile_y = sources[0].shape[2:4]
    for turn in range(pieces):
        spot = pl.ds(pl.multiple_of((place[ME] ^ turn) * tile_y, tile_y), tile_y)
        for side in range(2):
            for out in range(DEEP):
                row = row_of(place, side, out, tile_x)
                lam = mu = None
                for moment in range(moments):
                    weight = KERNEL_SCALE * residual[place[ME], moment]
                    held = rates[4 * moment + 2 * (out // REACH) + side]
                    rate = [held[c, out % REACH, spot, :] for c in range(6)]
                    source = [sources[turn][moment, c, row] for c in range(6)]
                    bulk = (source[0] + source[1] + source[2]) * (rate[0] + rate[1] + rate[2])
                    diag = source[0] * rate[0] + source[1] * rate[1] + source[2] * rate[2]
                    off = source[3] * rate[3] + source[4] * rate[4] + source[5] * rate[5]
                    bulk, both = weight * bulk, (2.0 * weight) * (diag + 2.0 * off)
                    lam = bulk if lam is None else lam + bulk
                    mu = both if mu is None else mu + both
                terms[turn, 0, row] = lam
                terms[turn, 1, row] = mu


def swap(array, axis, turn):
    count = lax.axis_size(axis)
    return lax.ppermute(array, axis, [(i, i ^ turn) for i in range(count)])


def partner(slab, piece, slabs, side):
    other = slab + 1 - 2 * ((slab + piece + side) % 2)
    return other, (other >= 0) & (other < slabs)


def to_neighbour(face, side):
    slabs, pieces = lax.axis_size("gx"), lax.axis_size("gy")
    pairs = []
    for slab in range(slabs):
        for piece in range(pieces):
            other, inside = partner(slab, piece, slabs, side)
            if inside:
                pairs.append((slab * pieces + piece, other * pieces + piece))
    return lax.ppermute(face, ("gx", "gy"), pairs)


def local(rec_state, source_strain, material, material_table, residual, rec_cell, listed, src_pick):
    state = rec_state[0]
    receivers, _, tile_x, tile_y, depth = state.shape
    pieces, slabs, groups = lax.axis_size("gy"), lax.axis_size("gx"), lax.axis_size("sta")
    assert receivers == pieces and tile_x == 2 * DEEP
    assert pieces & (pieces - 1) == 0 and groups & (groups - 1) == 0
    size_y = pieces * tile_y
    group, slab, me = lax.axis_index("sta"), lax.axis_index("gx"), lax.axis_index("gy")
    moments = residual.shape[2]

    numbers = material.astype(F32)[None]
    chunks = []
    for turn in range(pieces):
        mine = lax.dynamic_index_in_dim(state, me ^ turn, 0, keepdims=False)
        mine = jnp.concatenate([mine, numbers], 0)
        chunks.append(swap(mine, "gy", turn) if turn else mine)

    strains = [swap(source_strain[0], "sta", turn) if turn else source_strain[0] for turn in range(groups)]

    cell = lax.dynamic_index_in_dim(rec_cell[0], me, 0, keepdims=False)
    flip = (slab + me) % 2
    spot_x = cell // size_y - slab * tile_x
    spot_x = spot_x + flip * (tile_x - 1 - 2 * spot_x) - tile_x // 2
    inside = [partner(slab, me, slabs, side)[1] for side in range(2)]
    place = jnp.stack([me, flip, *inside, spot_x, cell % size_y]).astype(jnp.int32)
    rows = residual[0]

    def shape(*lead, kind=F32):
        return lead + (size_y, depth), kind

    vel_shape, pair_shape = shape(3, DEEP), shape(6, REACH)
    halo_shape, sent_shape = shape(3, REACH), shape(3 * PACKED, kind=BF16)

    results = call(
        assemble,
        [vel_shape, pair_shape, pair_shape, shape(DEEP), shape(4, REACH)] * 2,
        ([place], chunks),
    )
    vels, middles, edges, cells, faces = ([results[at], results[5 + at]] for at in range(5))
    halos = [to_neighbour(faces[side], side) for side in range(2)]

    strains, vels = lax.optimization_barrier((strains, vels))
    weights = lax.dynamic_slice_in_dim(listed, group, 1, 2)[:, :, 0].astype(F32)
    combined = 0.0
    for turn in range(groups):
        factor = jnp.sum(weights * (src_pick == (group ^ turn)).astype(F32), 0)
        combined = combined + factor[:, None, None, None, None] * strains[turn].astype(F32)
    width = pieces // 2
    found = {0: combined}
    if width:
        found[width] = swap(combined, "gy", width)
        width //= 2

    sent, lights, lames, shears, old_halos = ([None, None] for _ in range(5))
    fresh = [None, None]
    for side in range(2):
        fresh[side], sent[side], lights[side], lames[side], shears[side], old_halos[side] = call(
            functools.partial(first, side),
            [vel_shape, sent_shape, shape(DEEP), shape(DEEP + REACH), shape(DEEP + REACH), halo_shape],
            (
                [place, material_table, rows],
                [vels[side], middles[side], middles[1 - side], edges[side], cells[side], halos[side]],
            ),
        )
        sent[side] = to_neighbour(sent[side], side)
    vels = fresh

    rates = []
    for moment in range(moments):
        last = moment == moments - 1
        if moment == 3 * moments // 4:
            found, vels = lax.optimization_barrier((found, vels))
            while width:
                for turn in list(found):
                    found[turn ^ width] = swap(found[turn], "gy", width)
                width //= 2
        results = call(
            functools.partial(inner, last),
            [pair_shape] * (2 if last else 4),
            ([place], vels if last else vels + middles + lames + shears),
        )
        rates += results[:2]
        if not last:
            middles = results[2:]
        fresh = [None, None]
        for side in range(2):
            arrays = [vels[side], sent[side], edges[side]]
            outs = [pair_shape]
            if not last:
                arrays += [old_halos[side], middles[side], middles[1 - side]]
                arrays += [lights[side], lames[side], shears[side]]
                outs += [pair_shape, halo_shape, vel_shape, sent_shape]
            results = call(functools.partial(outer, side, moment, last), outs, ([place, rows], arrays))
            rates.append(results[0])
            if not last:
                edges[side], old_halos[side], fresh[side] = results[1:4]
                sent[side] = to_neighbour(results[4], side)
        vels = fresh

    (terms,) = call(
        functools.partial(correlate, moments, pieces),
        [((pieces, 2, tile_x, tile_y, depth), F32)],
        ([place, rows], rates + [found[turn] for turn in range(pieces)]),
    )
    held = {turn: terms[turn] for turn in range(pieces)}
    width = 1
    while width < pieces:
        keep = [turn for turn in held if not turn & width]
        got = swap(jnp.stack([held[turn ^ width] for turn in keep]), "gy", width)
        held = {turn: held[turn] + got[at] for at, turn in enumerate(keep)}
        width *= 2
    total = held[0]
    share = tile_x // groups
    result = lax.dynamic_slice_in_dim(total, group * share, share, 1)
    for turn in range(1, groups):
        part = lax.dynamic_slice_in_dim(total, (group ^ turn) * share, share, 1)
        result = result + swap(part, "sta", turn)
    return result


def solution(mesh):
    in_specs = (
        P("sta", None, None, "gx", "gy", None),
        P("sta", None, None, "gx", "gy", None),
        P("gx", "gy", None),
        P(),
        P("sta", None, None),
        P("sta", None),
        P(),
        P(),
    )
    out_specs = P(None, ("gx", "sta"), "gy", None)
    return jax.shard_map(local, mesh=mesh, in_specs=in_specs, out_specs=out_specs, check_vma=False)
```

time: 148 us -> 133 us (0.90)
  waiting for transfers between devices: 51.2 us -> 26.1 us
  Pallas kernels: 17.3 us -> 30.5 us
  starting transfers between devices: 70.4 us -> 59.7 us
  local copies, waits for them, and re-layouts: 2.14 us -> 10.5 us
    ppermute x18, waiting for transfers between devices: 31.6 us -> 6.86 us  [to_neighbour(): return lax.ppermute(face, ('gx', 'gy'), pairs)]
    pallas_call x11 -> x28, Pallas kernels: 17.3 us -> 30.5 us  [call(): pl.pallas_call(body, out_shape=[jax.ShapeDtypeStruct(shape, kind) for sha...]
    ppermute x18, starting transfers between devices: 61.9 us -> 51.1 us  [to_neighbour(): return lax.ppermute(face, ('gx', 'gy'), pairs)]
    unnamed x11 -> x43, local copies, waits for them, and re-layouts: 0.11 us -> 8.55 us
  transfers between devices with their start and end apart: 28 -> 28, of which waited for: 14 -> 12; matrix products, arithmetic and copies ran while one was open for 2% -> 3% of each run, Pallas kernels for 10% -> 22%
where the time goes in v2:
time: 133 us; the launch traced here: 132 us
  starting transfers between devices  59.7 us (45%)
  Pallas kernels  30.5 us (23%)
  waiting for transfers between devices  26.1 us (20%)
  local copies, waits for them, and re-layouts  10.5 us (8%)
  between operations  2.8 us (2%)
  other arithmetic  2.64 us (2%)
    ppermute x18, starting transfers between devices, to_neighbour(): return lax.ppermute(face, ('gx', 'gy'), pairs)  51.1 us
    pallas_call x28, Pallas kernels, call(): pl.pallas_call(body, out_shape=[jax.ShapeDtypeStruct(shape, kind) for sha...  30.5 us
    ppermute x10, waiting for transfers between devices, swap(): return lax.ppermute(array, axis, [(i, i ^ turn) for i in range(count)])  19.2 us
    ppermute x10, starting transfers between devices, swap(): return lax.ppermute(array, axis, [(i, i ^ turn) for i in range(count)])  8.58 us
    unnamed x43, local copies, waits for them, and re-layouts  8.55 us
    ppermute x18, waiting for transfers between devices, to_neighbour(): return lax.ppermute(face, ('gx', 'gy'), pairs)  6.86 us
  transfers between devices with their start and end apart: 28, of which 12 were waited for; matrix products, arithmetic and copies ran while one was open for 3% of the time, Pallas kernels for 22%

profile of v2, /device:TPU:0, one launch (start us, length us, event | category | flops | bytes accessed | tf_op | source)
XLA Modules:
  0.0 132.2 jit_solution(4170529284745466261)
XLA Ops:
  0.0 2.9 %collective-permute-start = (bf16[8,6,8,8,128]{4,3,2,1,0:T(8,128)(2,1)}, bf16[8,6,8,8,128]{4,3,2,1,0:T(8,128)(2,1)S(1)}, u32[]{:S(2)}, u32[]{:S(2)}) collective-permute-start(bf16[8,6,8,8,128]{4,3,2,1,0:T(8,128)(2,1)} %bitcast.43), channel_id=1, source_target_pairs={{0,16},{16,0},{1,17},{17,1},{2,18},{18,2},{3,19},{19,3},{4,20},{20... | collective-permute-start | bytes 2359304 | tf_op jit(solution)/shard_map/ppermute | solution.py:273
  2.9 1.3 dynamic-slice_bitcast_fusion
  4.3 0.9 pad_maximum_fusion
  5.9 1.0 collective-permute-start.1
  11.0 4.3 %collective-permute-done.3.refs_3_ = f32[10,8,8,128]{3,2,1,0:T(8,128)S(1)} collective-permute-done((f32[10,8,8,128]{3,2,1,0:T(8,128)}, f32[10,8,8,128]{3,2,1,0:T(8,128)S(1)}, u32[]{:S(2)}, u32[]{:S(2)}) %collective-permute-start.3) | collective-permute-done | bytes 327712 | tf_op jit(solution)/shard_map/ppermute | solution.py:273
  15.4 7.1 %collective-permute-done.2.refs_2_ = f32[10,8,8,128]{3,2,1,0:T(8,128)S(1)} collective-permute-done((f32[10,8,8,128]{3,2,1,0:T(8,128)S(1)}, f32[10,8,8,128]{3,2,1,0:T(8,128)S(1)}, u32[]{:S(2)}, u32[]{:S(2)}) %collective-permute-start.2) | collective-permute-done | bytes 327712 | tf_op jit(solution)/shard_map/ppermute | solution.py:273
  22.4 1.4 %shard_map.82 = (f32[3,4,32,128]{3,2,1,0:T(8,128)S(1)}, f32[6,2,32,128]{3,2,1,0:T(8,128)S(1)}, f32[6,2,32,128]{3,2,1,0:T(8,128)S(1)}, f32[4,32,128]{2,1,0:T(8,12...) custom-call(s32[6]{0:T(128)S(1)} %stack.39.place, ...), custom_call_target="tpu_custom_call" | custom-call | flops 1000000 | bytes 2000000 | tf_op jit(solution)/shard_map/pallas_call | solution.py:30
  26.1 1.0 collective-permute-start.18
  27.1 1.3 collective-permute-start.5
  28.4 5.7 %collective-permute-start.4 = (f32[4,2,32,128]{3,2,1,0:T(8,128)}, f32[4,2,32,128]{3,2,1,0:T(8,128)}, u32[]{:S(2)}, u32[]{:S(2)}) collective-permute-start(f32[4,2,32,128]{3,2,1,0:T(8,128)} %get-tuple-element.140), channel_id=1, source_target_pairs={{0,4},{2,6},{4,0},{5,9},{6,2},{7,11},{8,12},{9,5},{10,14},{11,7},{... | collective-permute-start | bytes 393224 | tf_op jit(solution)/shard_map/ppermute | solution.py:289
  34.7 0.9 copy-done.5
  35.7 0.9 copy-done.11
  38.1 1.4 %shard_map.84 = (f32[3,4,32,128]{3,2,1,0:T(8,128)S(1)}, bf16[18,32,128]{2,1,0:T(8,128)(2,1)S(1)}, f32[4,32,128]{2,1,0:T(8,128)S(1)}, f32[6,32,128]{2,1,0:T(8,128...) custom-call(s32[6]{0:T(128)S(1)} %stack.39.place, f32[16,3]{1,0:T(8,128)S(1)} %copy-done.12, ...), custom_call_target="tpu_custom_call" | custom-call | flops 1000000 | bytes 2000000 | tf_op jit(solution)/shard_map/pallas_call | solution.py:30
  40.3 0.9 copy-done.2
  41.2 0.9 copy-done.9
  42.9 1.4 %shard_map.83 = (f32[3,4,32,128]{3,2,1,0:T(8,128)S(1)}, bf16[18,32,128]{2,1,0:T(8,128)(2,1)S(1)}, f32[4,32,128]{2,1,0:T(8,128)S(1)}, f32[6,32,128]{2,1,0:T(8,128...) custom-call(s32[6]{0:T(128)S(1)} %stack.39.place, f32[16,3]{1,0:T(8,128)S(1)} %copy-done.12, ...), custom_call_target="tpu_custom_call" | custom-call | flops 1000000 | bytes 2000000 | tf_op jit(solution)/shard_map/pallas_call | solution.py:30
  44.4 5.8 %collective-permute-start.6 = (bf16[18,32,128]{2,1,0:T(8,128)(2,1)S(1)}, bf16[18,32,128]{2,1,0:T(8,128)(2,1)S(1)}, u32[]{:S(2)}, u32[]{:S(2)}) collective-permute-start(bf16[18,32,128]{2,1,0:T(8,128)(2,1)S(1)} %get-tuple-element.153), channel_id=1, source_target_pairs={{0,4},{2,6},{4,0},{5,9},{6,2},{7,11},{8,12},{9,5},{10,14},{11,7},{... | collective-permute-start | bytes 442376 | tf_op jit(solution)/shard_map/ppermute | solution.py:289
  51.1 1.1 shard_map.87
  53.3 1.1 shard_map.86
  54.3 3.9 %collective-permute-start.8 = (bf16[18,32,128]{2,1,0:T(8,128)(2,1)S(1)}, bf16[18,32,128]{2,1,0:T(8,128)(2,1)S(1)}, u32[]{:S(2)}, u32[]{:S(2)}) collective-permute-start(bf16[18,32,128]{2,1,0:T(8,128)(2,1)S(1)} %get-tuple-element.167), channel_id=1, source_target_pairs={{0,4},{2,6},{4,0},{5,9},{6,2},{7,11},{8,12},{9,5},{10,14},{11,7},{... | collective-permute-start | bytes 442376 | tf_op jit(solution)/shard_map/ppermute | solution.py:289
  59.1 1.1 shard_map.90
  61.4 1.1 shard_map.89
  62.5 3.9 %collective-permute-start.10 = (bf16[18,32,128]{2,1,0:T(8,128)(2,1)S(1)}, bf16[18,32,128]{2,1,0:T(8,128)(2,1)S(1)}, u32[]{:S(2)}, u32[]{:S(2)}) collective-permute-start(bf16[18,32,128]{2,1,0:T(8,128)(2,1)S(1)} %get-tuple-element.181), channel_id=1, source_target_pairs={{0,4},{2,6},{4,0},{5,9},{6,2},{7,11},{8,12},{9,5},{10,14},{11,7},{... | collective-permute-start | bytes 442376 | tf_op jit(solution)/shard_map/ppermute | solution.py:289
  66.4 0.9 shard_map.91
  67.2 1.1 shard_map.93
  69.5 1.1 shard_map.92
  70.6 3.9 %collective-permute-start.12 = (bf16[18,32,128]{2,1,0:T(8,128)(2,1)S(1)}, bf16[18,32,128]{2,1,0:T(8,128)(2,1)S(1)}, u32[]{:S(2)}, u32[]{:S(2)}) collective-permute-start(bf16[18,32,128]{2,1,0:T(8,128)(2,1)S(1)} %get-tuple-element.195), channel_id=1, source_target_pairs={{0,4},{2,6},{4,0},{5,9},{6,2},{7,11},{8,12},{9,5},{10,14},{11,7},{... | collective-permute-start | bytes 442376 | tf_op jit(solution)/shard_map/ppermute | solution.py:289
  75.4 1.1 shard_map.96
  77.1 0.9 collective-permute-done.12.halo
  78.0 1.1 shard_map.95
  79.0 4.2 %collective-permute-start.14 = (bf16[18,32,128]{2,1,0:T(8,128)(2,1)S(1)}, bf16[18,32,128]{2,1,0:T(8,128)(2,1)S(1)}, u32[]{:S(2)}, u32[]{:S(2)}) collective-permute-start(bf16[18,32,128]{2,1,0:T(8,128)(2,1)S(1)} %get-tuple-element.209), channel_id=1, source_target_pairs={{0,4},{2,6},{4,0},{5,9},{6,2},{7,11},{8,12},{9,5},{10,14},{11,7},{... | collective-permute-start | bytes 442376 | tf_op jit(solution)/shard_map/ppermute | solution.py:289
  84.1 1.1 shard_map.99
  85.9 1.8 %collective-permute-done.14.halo = bf16[18,32,128]{2,1,0:T(8,128)(2,1)S(1)} collective-permute-done((bf16[18,32,128]{2,1,0:T(8,128)(2,1)S(1)}, bf16[18,32,128]{2,1,0:T(8,128)(2,1)S(1)}, u32[]{:S(2)}, u32[]{:S(2)}) %collective-permute-start.14) | collective-permute-done | bytes 147488 | tf_op jit(solution)/shard_map/ppermute | solution.py:289
  87.7 1.1 shard_map.98
  88.7 4.2 %collective-permute-start.16 = (bf16[18,32,128]{2,1,0:T(8,128)(2,1)S(1)}, bf16[18,32,128]{2,1,0:T(8,128)(2,1)S(1)}, u32[]{:S(2)}, u32[]{:S(2)}) collective-permute-start(bf16[18,32,128]{2,1,0:T(8,128)(2,1)S(1)} %get-tuple-element.223), channel_id=1, source_target_pairs={{0,4},{2,6},{4,0},{5,9},{6,2},{7,11},{8,12},{9,5},{10,14},{11,7},{... | collective-permute-start | bytes 442376 | tf_op jit(solution)/shard_map/ppermute | solution.py:289
  93.8 1.1 shard_map.102
  94.8 1.2 collective-permute-done.16.halo
  96.0 1.1 shard_map.101
  98.3 7.0 %collective-permute-start.19 = (bf16[18,32,128]{2,1,0:T(8,128)(2,1)S(1)}, bf16[18,32,128]{2,1,0:T(8,128)(2,1)S(1)}, u32[]{:S(2)}, u32[]{:S(2)}) collective-permute-start(bf16[18,32,128]{2,1,0:T(8,128)(2,1)S(1)} %get-tuple-element.241), channel_id=1, source_target_pairs={{0,4},{2,6},{4,0},{5,9},{6,2},{7,11},{8,12},{9,5},{10,14},{11,7},{... | collective-permute-start | bytes 442376 | tf_op jit(solution)/shard_map/ppermute | solution.py:289
  106.2 1.6 %shard_map.105 = (f32[6,2,32,128]{3,2,1,0:T(8,128)S(1)}, f32[6,2,32,128]{3,2,1,0:T(8,128)S(1)}, f32[3,2,32,128]{3,2,1,0:T(8,128)}, f32[3,4,32,128]{3,2,1,0:T(8,128)S(1)}, bf16[18,32,128]{2,1,0:T(8,128)(2,1)S(1)}) custom-call(s32[6]{0:T(128)S(1)} %stack.39.place, f32[4,8]{1,0:T(4,128)S(1)} %bitcast.38, f32[3,4,32,128]{3,2,1,0:T(8,128)S(1)} %get-tuple-element.238.refs_1_.vel, ...), custom_call_target="tpu_custom_call" | custom-call | flops 1000000 | bytes 2000000 | tf_op jit(solution)/shard_map/pallas_call | solution.py:30
  108.5 1.6 %shard_map.104 = (f32[6,2,32,128]{3,2,1,0:T(8,128)S(1)}, f32[6,2,32,128]{3,2,1,0:T(8,128)S(1)}, f32[3,2,32,128]{3,2,1,0:T(8,128)}, f32[3,4,32,128]{3,2,1,0:T(8,128)S(1)}, bf16[18,32,128]{2,1,0:T(8,128)(2,1)S(1)}) custom-call(s32[6]{0:T(128)S(1)} %stack.39.place, f32[4,8]{1,0:T(4,128)S(1)} %bitcast.39, f32[3,4,32,128]{3,2,1,0:T(8,128)S(1)} %get-tuple-element.237.refs_0_.vel, ...), custom_call_target="tpu_custom_call" | custom-call | flops 1000000 | bytes 2000000 | tf_op jit(solution)/shard_map/pallas_call | solution.py:30
  110.1 5.8 %collective-permute-start.21 = (bf16[18,32,128]{2,1,0:T(8,128)(2,1)S(1)}, bf16[18,32,128]{2,1,0:T(8,128)(2,1)S(1)}, u32[]{:S(2)}, u32[]{:S(2)}) collective-permute-start(bf16[18,32,128]{2,1,0:T(8,128)(2,1)S(1)} %get-tuple-element.255), channel_id=1, source_target_pairs={{0,4},{2,6},{4,0},{5,9},{6,2},{7,11},{8,12},{9,5},{10,14},{11,7},{... | collective-permute-start | bytes 442376 | tf_op jit(solution)/shard_map/ppermute | solution.py:289
  117.5 1.5 %collective-permute-done.21.halo = bf16[18,32,128]{2,1,0:T(8,128)(2,1)S(1)} collective-permute-done((bf16[18,32,128]{2,1,0:T(8,128)(2,1)S(1)}, bf16[18,32,128]{2,1,0:T(8,128)(2,1)S(1)}, u32[]{:S(2)}, u32[]{:S(2)}) %collective-permute-start.21) | collective-permute-done | bytes 147488 | tf_op jit(solution)/shard_map/ppermute | solution.py:289
  119.8 2.0 %shard_map.109 = f32[4,2,8,8,128]{4,3,2,1,0:T(8,128)S(1)} custom-call(s32[6]{0:T(128)S(1)} %stack.39.place, f32[4,8]{1,0:T(4,128)S(1)} %bitcast.42, f32[6,2,32,128]{3,2,1,0:T(8,128)S(1)} %get-tuple-element.151.refs_0_, f32[6,2,32,128]{3,2,1,0:T(8,128)S(1)} %get-tuple-element.152.refs_1_, f32[6,2,32,128]{3,2,1,0:T(8,128)S(1)} %get-tuple-element.158.refs_2_, ...), custom_call_target="tpu_custom_call" | custom-call | flops 1000000 | bytes 2000000 | tf_op jit(solution)/shard_map/pallas_call | solution.py:30
  121.9 1.3 %collective-permute-done.25 = f32[2,2,8,8,128]{4,3,2,1,0:T(8,128)S(1)} collective-permute-done((f32[2,2,8,8,128]{4,3,2,1,0:T(8,128)S(1)}, f32[2,2,8,8,128]{4,3,2,1,0:T(8,128)S(1)}, u32[]{:S(2)}, u32[]{:S(2)}) %collective-permute-start.25) | collective-permute-done | bytes 131104 | tf_op jit(solution)/shard_map/ppermute | solution.py:273
  123.3 1.3 collective-permute-start.26
  124.5 3.0 %collective-permute-done.26 = f32[1,2,8,8,128]{4,3,2,1,0:T(8,128)S(1)} collective-permute-done((f32[1,2,8,8,128]{4,3,2,1,0:T(8,128)S(1)}, f32[1,2,8,8,128]{4,3,2,1,0:T(8,128)S(1)}, u32[]{:S(2)}, u32[]{:S(2)}) %collective-permute-start.26) | collective-permute-done | bytes 65568 | tf_op jit(solution)/shard_map/ppermute | solution.py:273
  128.2 3.4 %collective-permute-done.27 = f32[2,4,8,128]{3,2,1,0:T(8,128)S(1)} collective-permute-done((f32[2,4,8,128]{3,2,1,0:T(8,128)S(1)}, f32[2,4,8,128]{3,2,1,0:T(8,128)S(1)}, u32[]{:S(2)}, u32[]{:S(2)}) %collective-permute-start.27) | collective-permute-done | bytes 32800 | tf_op jit(solution)/shard_map/ppermute | solution.py:273
  (93 shorter events, 23.9 us)
Async XLA Ops:
  0.0 7.3 %copy-start = (s32[1,4]{1,0:T(1,128)S(1)}, s32[1,4]{1,0:T(1,128)}, u32[]{:S(2)}) copy-start(s32[1,4]{1,0:T(1,128)} %param.13) | copy-start | bytes 52
  0.0 4.3 %copy-start.18 = (s32[8,8,128]{2,1,0:T(8,128)S(1)}, s32[8,8,128]{2,1,0:T(8,128)}, u32[]{:S(2)}) copy-start(s32[8,8,128]{2,1,0:T(8,128)} %param.10) | copy-start | bytes 98308
  0.0 25.2 %collective-permute-start = (bf16[8,6,8,8,128]{4,3,2,1,0:T(8,128)(2,1)}, bf16[8,6,8,8,128]{4,3,2,1,0:T(8,128)(2,1)S(1)}, u32[]{:S(2)}, u32[]{:S(2)}) collective-permute-start(bf16[8,6,8,8,128]{4,3,2,1,0:T(8,128)(2,1)} %bitcast.43), channel_id=1, source_target_pairs={{0,16},{16,0},{1,17},{17,1},{2,18},{18,2},{3,19},{19,3},{4,20},{20... | collective-permute-start | bytes 2359304 | tf_op jit(solution)/shard_map/ppermute | solution.py:273
  4.3 6.7 %copy-start.20 = (s32[2,8]{1,0:T(2,128)S(1)}, s32[2,8]{1,0:T(2,128)}, u32[]{:S(2)}) copy-start(s32[2,8]{1,0:T(2,128)} %param.15) | copy-start | bytes 196
  4.3 21.0 %copy-start.17 = (bf16[1,8,6,8,8,128]{5,4,3,2,1,0:T(8,128)(2,1)S(1)}, bf16[1,8,6,8,8,128]{5,4,3,2,1,0:T(8,128)(2,1)}, u32[]{:S(2)}) copy-start(bf16[1,8,6,8,8,128]{5,4,3,2,1,0:T(8,128)(2,1)} %param.9) | copy-start | bytes 2359300
  5.2 10.2 %collective-permute-start.3 = (f32[10,8,8,128]{3,2,1,0:T(8,128)}, f32[10,8,8,128]{3,2,1,0:T(8,128)S(1)}, u32[]{:S(2)}, u32[]{:S(2)}) collective-permute-start(f32[10,8,8,128]{3,2,1,0:T(8,128)} %get-tuple-element.269), channel_id=1, source_target_pairs={{0,3},{1,2},{2,1},{3,0},{4,7},{5,6},{6,5},{7,4},{8,11},{9,10},{10,... | collective-permute-start | bytes 983048 | tf_op jit(solution)/shard_map/ppermute | solution.py:273
  5.9 9.5 %collective-permute-start.1 = (f32[10,8,8,128]{3,2,1,0:T(8,128)S(1)}, f32[10,8,8,128]{3,2,1,0:T(8,128)S(1)}, u32[]{:S(2)}, u32[]{:S(2)}) collective-permute-start(f32[10,8,8,128]{3,2,1,0:T(8,128)S(1)} %get-tuple-element.270), channel_id=1, source_target_pairs={{0,1},{1,0},{2,3},{3,2},{4,5},{5,4},{6,7},{7,6},{8,9},{9,8},{10,11... | collective-permute-start | bytes 983048 | tf_op jit(solution)/shard_map/ppermute | solution.py:273
  6.8 15.6 %collective-permute-start.2 = (f32[10,8,8,128]{3,2,1,0:T(8,128)S(1)}, f32[10,8,8,128]{3,2,1,0:T(8,128)S(1)}, u32[]{:S(2)}, u32[]{:S(2)}) collective-permute-start(f32[10,8,8,128]{3,2,1,0:T(8,128)S(1)} %get-tuple-element.271), channel_id=1, source_target_pairs={{0,2},{1,3},{2,0},{3,1},{4,6},{5,7},{6,4},{7,5},{8,10},{9,11},{10,... | collective-permute-start | bytes 983048 | tf_op jit(solution)/shard_map/ppermute | solution.py:273
  23.9 0.7 copy-start.8
  25.2 0.7 copy-start.1
  25.2 0.8 copy-start.4
  25.2 0.8 copy-start.10
  25.2 0.8 copy-start.15
  25.3 8.8 %copy-start.19 = (f32[16,3]{0,1:T(4,128)S(1)}, f32[16,3]{0,1:T(4,128)}, u32[]{:S(2)}) copy-start(f32[16,3]{0,1:T(4,128)} %param.11) | copy-start | bytes 580
  25.3 9.5 %copy-start.7 = (f32[1,4,8]{2,1,0:T(4,128)S(1)}, f32[1,4,8]{2,1,0:T(4,128)}, u32[]{:S(2)}) copy-start(f32[1,4,8]{2,1,0:T(4,128)} %param.12) | copy-start | bytes 388
  26.1 71.0 %collective-permute-start.18 = (f32[8,6,8,8,128]{4,3,2,1,0:T(8,128)S(1)}, f32[8,6,8,8,128]{4,3,2,1,0:T(8,128)S(1)}, u32[]{:S(2)}, u32[]{:S(2)}) collective-permute-start(f32[8,6,8,8,128]{4,3,2,1,0:T(8,128)S(1)} %multiply_add_fusion.refs_32_), channel_id=1, source_target_pairs={{0,2},{1,3},{2,0},{3,1},{4,6},{5,7},{6,4},{7,5},{8,10},{9,11},{10,... | collective-permute-start | bytes 4718600 | tf_op jit(solution)/shard_map/ppermute | solution.py:273
  27.1 7.7 %collective-permute-start.5 = (f32[4,2,32,128]{3,2,1,0:T(8,128)}, f32[4,2,32,128]{3,2,1,0:T(8,128)}, u32[]{:S(2)}, u32[]{:S(2)}) collective-permute-start(f32[4,2,32,128]{3,2,1,0:T(8,128)} %get-tuple-element.145), channel_id=1, source_target_pairs={{1,5},{3,7},{4,8},{5,1},{6,10},{7,3},{8,4},{9,13},{10,6},{11,15},{... | collective-permute-start | bytes 393224 | tf_op jit(solution)/shard_map/ppermute | solution.py:289
  28.4 11.9 %collective-permute-start.4 = (f32[4,2,32,128]{3,2,1,0:T(8,128)}, f32[4,2,32,128]{3,2,1,0:T(8,128)}, u32[]{:S(2)}, u32[]{:S(2)}) collective-permute-start(f32[4,2,32,128]{3,2,1,0:T(8,128)} %get-tuple-element.140), channel_id=1, source_target_pairs={{0,4},{2,6},{4,0},{5,9},{6,2},{7,11},{8,12},{9,5},{10,14},{11,7},{... | collective-permute-start | bytes 393224 | tf_op jit(solution)/shard_map/ppermute | solution.py:289
  34.7 0.9 copy-start.5
  35.7 0.9 copy-start.11
  36.6 0.7 copy-start.12
  37.3 0.8 copy-start.16
  38.1 12.9 %copy-start.6 = (f32[6,2,32,128]{3,2,1,0:T(8,128)S(1)}, f32[6,2,32,128]{3,2,1,0:T(8,128)}, u32[]{:S(2)}) copy-start(f32[6,2,32,128]{3,2,1,0:T(8,128)} %copy-done.4) | copy-start | bytes 589828
  39.6 11.5 %collective-permute-start.7 = (bf16[18,32,128]{2,1,0:T(8,128)(2,1)S(1)}, bf16[18,32,128]{2,1,0:T(8,128)(2,1)S(1)}, u32[]{:S(2)}, u32[]{:S(2)}) collective-permute-start(bf16[18,32,128]{2,1,0:T(8,128)(2,1)S(1)} %get-tuple-element.159), channel_id=1, source_target_pairs={{1,5},{3,7},{4,8},{5,1},{6,10},{7,3},{8,4},{9,13},{10,6},{11,15},{... | collective-permute-start | bytes 442376 | tf_op jit(solution)/shard_map/ppermute | solution.py:289
  40.2 0.9 copy-start.2
  41.2 0.9 copy-start.9
  42.1 0.8 copy-start.14
  42.9 10.4 %copy-start.3 = (f32[6,2,32,128]{3,2,1,0:T(8,128)S(1)}, f32[6,2,32,128]{3,2,1,0:T(8,128)}, u32[]{:S(2)}) copy-start(f32[6,2,32,128]{3,2,1,0:T(8,128)} %copy-done.1) | copy-start | bytes 589828
  44.4 8.9 %collective-permute-start.6 = (bf16[18,32,128]{2,1,0:T(8,128)(2,1)S(1)}, bf16[18,32,128]{2,1,0:T(8,128)(2,1)S(1)}, u32[]{:S(2)}, u32[]{:S(2)}) collective-permute-start(bf16[18,32,128]{2,1,0:T(8,128)(2,1)S(1)} %get-tuple-element.153), channel_id=1, source_target_pairs={{0,4},{2,6},{4,0},{5,9},{6,2},{7,11},{8,12},{9,5},{10,14},{11,7},{... | collective-permute-start | bytes 442376 | tf_op jit(solution)/shard_map/ppermute | solution.py:289
  52.1 7.0 %collective-permute-start.9 = (bf16[18,32,128]{2,1,0:T(8,128)(2,1)S(1)}, bf16[18,32,128]{2,1,0:T(8,128)(2,1)S(1)}, u32[]{:S(2)}, u32[]{:S(2)}) collective-permute-start(bf16[18,32,128]{2,1,0:T(8,128)(2,1)S(1)} %get-tuple-element.173), channel_id=1, source_target_pairs={{1,5},{3,7},{4,8},{5,1},{6,10},{7,3},{8,4},{9,13},{10,6},{11,15},{... | collective-permute-start | bytes 442376 | tf_op jit(solution)/shard_map/ppermute | solution.py:289
  54.3 7.0 %collective-permute-start.8 = (bf16[18,32,128]{2,1,0:T(8,128)(2,1)S(1)}, bf16[18,32,128]{2,1,0:T(8,128)(2,1)S(1)}, u32[]{:S(2)}, u32[]{:S(2)}) collective-permute-start(bf16[18,32,128]{2,1,0:T(8,128)(2,1)S(1)} %get-tuple-element.167), channel_id=1, source_target_pairs={{0,4},{2,6},{4,0},{5,9},{6,2},{7,11},{8,12},{9,5},{10,14},{11,7},{... | collective-permute-start | bytes 442376 | tf_op jit(solution)/shard_map/ppermute | solution.py:289
  60.2 7.0 %collective-permute-start.11 = (bf16[18,32,128]{2,1,0:T(8,128)(2,1)S(1)}, bf16[18,32,128]{2,1,0:T(8,128)(2,1)S(1)}, u32[]{:S(2)}, u32[]{:S(2)}) collective-permute-start(bf16[18,32,128]{2,1,0:T(8,128)(2,1)S(1)} %get-tuple-element.187), channel_id=1, source_target_pairs={{1,5},{3,7},{4,8},{5,1},{6,10},{7,3},{8,4},{9,13},{10,6},{11,15},{... | collective-permute-start | bytes 442376 | tf_op jit(solution)/shard_map/ppermute | solution.py:289
  62.5 7.0 %collective-permute-start.10 = (bf16[18,32,128]{2,1,0:T(8,128)(2,1)S(1)}, bf16[18,32,128]{2,1,0:T(8,128)(2,1)S(1)}, u32[]{:S(2)}, u32[]{:S(2)}) collective-permute-start(bf16[18,32,128]{2,1,0:T(8,128)(2,1)S(1)} %get-tuple-element.181), channel_id=1, source_target_pairs={{0,4},{2,6},{4,0},{5,9},{6,2},{7,11},{8,12},{9,5},{10,14},{11,7},{... | collective-permute-start | bytes 442376 | tf_op jit(solution)/shard_map/ppermute | solution.py:289
  68.3 7.0 %collective-permute-start.13 = (bf16[18,32,128]{2,1,0:T(8,128)(2,1)S(1)}, bf16[18,32,128]{2,1,0:T(8,128)(2,1)S(1)}, u32[]{:S(2)}, u32[]{:S(2)}) collective-permute-start(bf16[18,32,128]{2,1,0:T(8,128)(2,1)S(1)} %get-tuple-element.201), channel_id=1, source_target_pairs={{1,5},{3,7},{4,8},{5,1},{6,10},{7,3},{8,4},{9,13},{10,6},{11,15},{... | collective-permute-start | bytes 442376 | tf_op jit(solution)/shard_map/ppermute | solution.py:289
  70.6 7.4 %collective-permute-start.12 = (bf16[18,32,128]{2,1,0:T(8,128)(2,1)S(1)}, bf16[18,32,128]{2,1,0:T(8,128)(2,1)S(1)}, u32[]{:S(2)}, u32[]{:S(2)}) collective-permute-start(bf16[18,32,128]{2,1,0:T(8,128)(2,1)S(1)} %get-tuple-element.195), channel_id=1, source_target_pairs={{0,4},{2,6},{4,0},{5,9},{6,2},{7,11},{8,12},{9,5},{10,14},{11,7},{... | collective-permute-start | bytes 442376 | tf_op jit(solution)/shard_map/ppermute | solution.py:289
  76.4 7.7 %collective-permute-start.15 = (bf16[18,32,128]{2,1,0:T(8,128)(2,1)S(1)}, bf16[18,32,128]{2,1,0:T(8,128)(2,1)S(1)}, u32[]{:S(2)}, u32[]{:S(2)}) collective-permute-start(bf16[18,32,128]{2,1,0:T(8,128)(2,1)S(1)} %get-tuple-element.215), channel_id=1, source_target_pairs={{1,5},{3,7},{4,8},{5,1},{6,10},{7,3},{8,4},{9,13},{10,6},{11,15},{... | collective-permute-start | bytes 442376 | tf_op jit(solution)/shard_map/ppermute | solution.py:289
  79.0 8.6 %collective-permute-start.14 = (bf16[18,32,128]{2,1,0:T(8,128)(2,1)S(1)}, bf16[18,32,128]{2,1,0:T(8,128)(2,1)S(1)}, u32[]{:S(2)}, u32[]{:S(2)}) collective-permute-start(bf16[18,32,128]{2,1,0:T(8,128)(2,1)S(1)} %get-tuple-element.209), channel_id=1, source_target_pairs={{0,4},{2,6},{4,0},{5,9},{6,2},{7,11},{8,12},{9,5},{10,14},{11,7},{... | collective-permute-start | bytes 442376 | tf_op jit(solution)/shard_map/ppermute | solution.py:289
  85.2 8.6 %collective-permute-start.17 = (bf16[18,32,128]{2,1,0:T(8,128)(2,1)S(1)}, bf16[18,32,128]{2,1,0:T(8,128)(2,1)S(1)}, u32[]{:S(2)}, u32[]{:S(2)}) collective-permute-start(bf16[18,32,128]{2,1,0:T(8,128)(2,1)S(1)} %get-tuple-element.229), channel_id=1, source_target_pairs={{1,5},{3,7},{4,8},{5,1},{6,10},{7,3},{8,4},{9,13},{10,6},{11,15},{... | collective-permute-start | bytes 442376 | tf_op jit(solution)/shard_map/ppermute | solution.py:289
  88.7 7.3 %collective-permute-start.16 = (bf16[18,32,128]{2,1,0:T(8,128)(2,1)S(1)}, bf16[18,32,128]{2,1,0:T(8,128)(2,1)S(1)}, u32[]{:S(2)}, u32[]{:S(2)}) collective-permute-start(bf16[18,32,128]{2,1,0:T(8,128)(2,1)S(1)} %get-tuple-element.223), channel_id=1, source_target_pairs={{0,4},{2,6},{4,0},{5,9},{6,2},{7,11},{8,12},{9,5},{10,14},{11,7},{... | collective-permute-start | bytes 442376 | tf_op jit(solution)/shard_map/ppermute | solution.py:289
  97.1 22.7 %collective-permute-start.23 = (f32[8,6,8,8,128]{4,3,2,1,0:T(8,128)S(1)}, f32[8,6,8,8,128]{4,3,2,1,0:T(8,128)S(1)}, u32[]{:S(2)}, u32[]{:S(2)}) collective-permute-start(f32[8,6,8,8,128]{4,3,2,1,0:T(8,128)S(1)} %multiply_add_fusion.refs_32_), channel_id=1, source_target_pairs={{0,1},{1,0},{2,3},{3,2},{4,5},{5,4},{6,7},{7,6},{8,9},{9,8},{10,11... | collective-permute-start | bytes 4718600 | tf_op jit(solution)/shard_map/ppermute | solution.py:273
  97.2 22.6 %collective-permute-start.24 = (f32[8,6,8,8,128]{4,3,2,1,0:T(8,128)S(1)}, f32[8,6,8,8,128]{4,3,2,1,0:T(8,128)S(1)}, u32[]{:S(2)}, u32[]{:S(2)}) collective-permute-start(f32[8,6,8,8,128]{4,3,2,1,0:T(8,128)S(1)} %collective-permute-done.18.refs_34_), channel_id=1, source_target_pairs={{0,1},{1,0},{2,3},{3,2},{4,5},{5,4},{6,7},{7,6},{8,9},{9,8},{10,11... | collective-permute-start | bytes 4718600 | tf_op jit(solution)/shard_map/ppermute | solution.py:273
  97.7 8.5 %collective-permute-start.20 = (bf16[18,32,128]{2,1,0:T(8,128)(2,1)S(1)}, bf16[18,32,128]{2,1,0:T(8,128)(2,1)S(1)}, u32[]{:S(2)}, u32[]{:S(2)}) collective-permute-start(bf16[18,32,128]{2,1,0:T(8,128)(2,1)S(1)} %get-tuple-element.247), channel_id=1, source_target_pairs={{1,5},{3,7},{4,8},{5,1},{6,10},{7,3},{8,4},{9,13},{10,6},{11,15},{... | collective-permute-start | bytes 442376 | tf_op jit(solution)/shard_map/ppermute | solution.py:289
  98.3 10.1 %collective-permute-start.19 = (bf16[18,32,128]{2,1,0:T(8,128)(2,1)S(1)}, bf16[18,32,128]{2,1,0:T(8,128)(2,1)S(1)}, u32[]{:S(2)}, u32[]{:S(2)}) collective-permute-start(bf16[18,32,128]{2,1,0:T(8,128)(2,1)S(1)} %get-tuple-element.241), channel_id=1, source_target_pairs={{0,4},{2,6},{4,0},{5,9},{6,2},{7,11},{8,12},{9,5},{10,14},{11,7},{... | collective-permute-start | bytes 442376 | tf_op jit(solution)/shard_map/ppermute | solution.py:289
  107.8 9.0 %collective-permute-start.22 = (bf16[18,32,128]{2,1,0:T(8,128)(2,1)S(1)}, bf16[18,32,128]{2,1,0:T(8,128)(2,1)S(1)}, u32[]{:S(2)}, u32[]{:S(2)}) collective-permute-start(bf16[18,32,128]{2,1,0:T(8,128)(2,1)S(1)} %get-tuple-element.257), channel_id=1, source_target_pairs={{1,5},{3,7},{4,8},{5,1},{6,10},{7,3},{8,4},{9,13},{10,6},{11,15},{... | collective-permute-start | bytes 442376 | tf_op jit(solution)/shard_map/ppermute | solution.py:289
  110.1 8.9 %collective-permute-start.21 = (bf16[18,32,128]{2,1,0:T(8,128)(2,1)S(1)}, bf16[18,32,128]{2,1,0:T(8,128)(2,1)S(1)}, u32[]{:S(2)}, u32[]{:S(2)}) collective-permute-start(bf16[18,32,128]{2,1,0:T(8,128)(2,1)S(1)} %get-tuple-element.255), channel_id=1, source_target_pairs={{0,4},{2,6},{4,0},{5,9},{6,2},{7,11},{8,12},{9,5},{10,14},{11,7},{... | collective-permute-start | bytes 442376 | tf_op jit(solution)/shard_map/ppermute | solution.py:289
  121.8 1.4 %collective-permute-start.25 = (f32[2,2,8,8,128]{4,3,2,1,0:T(8,128)S(1)}, f32[2,2,8,8,128]{4,3,2,1,0:T(8,128)S(1)}, u32[]{:S(2)}, u32[]{:S(2)}) collective-permute-start(f32[2,2,8,8,128]{4,3,2,1,0:T(8,128)S(1)} %pad_maximum_fusion.4), channel_id=1, source_target_pairs={{0,1},{1,0},{2,3},{3,2},{4,5},{5,4},{6,7},{7,6},{8,9},{9,8},{10,11... | collective-permute-start | bytes 393224 | tf_op jit(solution)/shard_map/ppermute | solution.py:273
  123.3 4.3 %collective-permute-start.26 = (f32[1,2,8,8,128]{4,3,2,1,0:T(8,128)S(1)}, f32[1,2,8,8,128]{4,3,2,1,0:T(8,128)S(1)}, u32[]{:S(2)}, u32[]{:S(2)}) collective-permute-start(f32[1,2,8,8,128]{4,3,2,1,0:T(8,128)S(1)} %slice_add_fusion), channel_id=1, source_target_pairs={{0,2},{1,3},{2,0},{3,1},{4,6},{5,7},{6,4},{7,5},{8,10},{9,11},{10,... | collective-permute-start | bytes 196616 | tf_op jit(solution)/shard_map/ppermute | solution.py:273
  127.6 4.0 %collective-permute-start.27 = (f32[2,4,8,128]{3,2,1,0:T(8,128)S(1)}, f32[2,4,8,128]{3,2,1,0:T(8,128)S(1)}, u32[]{:S(2)}, u32[]{:S(2)}) collective-permute-start(f32[2,4,8,128]{3,2,1,0:T(8,128)S(1)} %dynamic-slice_bitcast_fusion.4), channel_id=1, source_target_pairs={{0,16},{16,0},{1,17},{17,1},{2,18},{18,2},{3,19},{19,3},{4,20},{20... | collective-permute-start | bytes 98312 | tf_op jit(solution)/shard_map/ppermute | solution.py:273
  (1 other events, 0.6 us)

commit v3 on v2

v3 whole, which is shorter than its diff:
```python
import functools

import jax
import jax.numpy as jnp
from jax import lax
from jax.experimental import pallas as pl
from jax.experimental.pallas import tpu as pltpu
from jax.sharding import PartitionSpec as P

NEAR = 8.0
UNIT = 12.0
SUBLANES = 8
TIME_STEP = 0.25
AMPLITUDE = 4.0
KERNEL_SCALE = 0.0625
STIFFNESS = 0.3
REACH = 2
DEEP = 2 * REACH
ALONG_X = (0, 3, 4)
ME, FLIP, HAS_HIGH, HAS_LOW, SPOT_X, SPOT_Y = range(6)
NEAR_ROWS = 2
PACKED = DEEP + NEAR_ROWS

VMEM = pl.BlockSpec(memory_space=pltpu.VMEM)
SMEM = pl.BlockSpec(memory_space=pltpu.SMEM)
F32, BF16 = jnp.float32, jnp.bfloat16


def call(body, outs, ins, scratch=(), flops=1_000_000):
    scalars, arrays = ins
    return list(pl.pallas_call(
        body,
        out_shape=[jax.ShapeDtypeStruct(shape, kind) for shape, kind in outs],
        in_specs=[SMEM] * len(scalars) + [VMEM] * len(arrays),
        out_specs=[VMEM] * len(outs),
        scratch_shapes=list(scratch),
        compiler_params=pltpu.CompilerParams(vmem_limit_bytes=6 * 1024 * 1024),
        cost_estimate=pl.CostEstimate(flops=flops, bytes_accessed=2_000_000, transcendentals=0),
    )(*scalars, *arrays))


def band(depth):
    row = lax.broadcasted_iota(jnp.int32, (depth, depth), 0)
    step = row - lax.broadcasted_iota(jnp.int32, (depth, depth), 1)
    parts = jnp.where(step == 1, NEAR, 0.0) - jnp.where(step == -1, NEAR, 0.0)
    parts = parts - jnp.where(step == 2, 1.0, 0.0) + jnp.where(step == -2, 1.0, 0.0)
    parts = parts.astype(BF16)
    return jnp.concatenate([parts, parts], 0)


def along_depth(rows):
    stacked = jnp.concatenate(rows, 0)
    high = stacked.astype(BF16)
    low = (stacked - high.astype(F32)).astype(BF16)
    split = jnp.concatenate([high, low], 1)
    result = jnp.dot(split, band(stacked.shape[1]), preferred_element_type=F32)
    size = rows[0].shape[0]
    return [result[at * size : (at + 1) * size] for at in range(len(rows))]


def along_y(row):
    count = row.shape[0] // SUBLANES
    at = lax.broadcasted_iota(jnp.int32, (SUBLANES, row.shape[1]), 0)
    planes = [row[SUBLANES * p : SUBLANES * (p + 1)] for p in range(count)]
    before = [jnp.where(at > 0, pltpu.roll(plane, 1, 0), 0.0) for plane in planes[-2:]]
    after = [jnp.where(at < SUBLANES - 1, pltpu.roll(plane, SUBLANES - 1, 0), 0.0) for plane in planes[:2]]
    spread = before + planes + after

    def shifted(by):
        return jnp.concatenate(spread[2 + by : 2 + by + count], 0)

    return shifted(1) - shifted(-1), shifted(2) - shifted(-2)


def across(rows, out, side):
    near, far = rows(out + 1) - rows(out - 1), rows(out + 2) - rows(out - 2)
    return (-near, -far) if side else (near, far)


def across_and_along(rows, out, side, row):
    near_y, far_y = along_y(row)
    near, far = rows(out + 1) - rows(out - 1), rows(out + 2) - rows(out - 2)
    if side:
        return NEAR * (near_y - near) - (far_y - far)
    return NEAR * (near_y + near) - (far_y + far)


def derivative(pair):
    return NEAR * pair[0] - pair[1]


MIRRORED_VEL = (0,)
MIRRORED_STRESS = (3, 4)


def sign_of(place):
    return 1.0 - 2.0 * place[FLIP].astype(F32)


def row_of(place, side, out, tile_x):
    x = tile_x // 2 - 1 - out if side else tile_x // 2 + out
    return x + place[FLIP] * (tile_x - 1 - 2 * x)


def interleave(place, tiles, comp, row, held):
    tile_y = tiles[0].shape[2]
    for turn, tile in enumerate(tiles):
        held[pl.ds(pl.multiple_of((place[ME] ^ turn) * tile_y, tile_y), tile_y), :] = tile[comp, row]
    count = held.shape[0] // SUBLANES
    return jnp.concatenate([held[pl.ds(p, SUBLANES, stride=count), :] for p in range(count)], 0)


def assemble_stress(place, *refs):
    count = len(refs) - 9
    tiles, sides, held = refs[:count], (refs[count : count + 4], refs[count + 4 : -1]), refs[-1]
    tile_x = tiles[0].shape[1]
    sign = sign_of(place)
    for side, (middle, edge, cells, face) in enumerate(sides):
        for out in range(DEEP):
            row = row_of(place, side, out, tile_x)
            part, at = (middle, out) if out < REACH else (edge, out - REACH)
            for comp in range(7):
                value = interleave(place, tiles, comp, row, held.at[(out * 7 + comp) % held.shape[0]])
                if comp in MIRRORED_STRESS:
                    value = sign * value
                if comp < 6:
                    part[comp, at] = value
                else:
                    cells[out] = value
                if out >= REACH and comp in ALONG_X + (6,):
                    face[(ALONG_X + (6,)).index(comp), out - REACH] = value


def assemble_vel(place, *refs):
    count = len(refs) - 3
    tiles, vels, held = refs[:count], refs[count:-1], refs[-1]
    tile_x = tiles[0].shape[1]
    sign = sign_of(place)
    for side, vel in enumerate(vels):
        for out in range(DEEP):
            row = row_of(place, side, out, tile_x)
            for comp in range(3):
                value = interleave(place, tiles, comp, row, held.at[(out * 3 + comp) % held.shape[0]])
                vel[comp, out] = sign * value if comp in MIRRORED_VEL else value


def push(place, side, amount, stress_row, vel, light, vel_out, sent):
    shape = vel.shape[2:]
    spot = (lax.broadcasted_iota(jnp.int32, shape, 0) == place[SPOT_Y]) & (
        lax.broadcasted_iota(jnp.int32, shape, 1) == 0
    )
    spot = jnp.where(spot, UNIT * amount, 0.0)
    rows = [functools.partial(stress_row, comp) for comp in range(6)]
    deep = along_depth([rows[comp](out) for out in range(DEEP) for comp in (4, 5, 2)])
    for out in range(DEEP):
        force_x = across_and_along(rows[0], out, side, rows[3](out)) + deep[3 * out]
        force_y = across_and_along(rows[3], out, side, rows[1](out)) + deep[3 * out + 1]
        force_z = across_and_along(rows[4], out, side, rows[5](out)) + deep[3 * out + 2]
        here = place[SPOT_X] == (-1 - out if side else out)
        force_z = force_z + jnp.where(here, 1.0, 0.0) * spot
        near = DEEP - 1 - out
        for comp, force in enumerate((force_x, force_y, force_z)):
            fresh = vel[comp, out] + light[out] * force
            vel_out[comp, out] = fresh
            if comp in MIRRORED_VEL:
                fresh = -fresh
            high = fresh.astype(BF16)
            if near < NEAR_ROWS:
                sent[comp * PACKED + 2 * near] = high
                sent[comp * PACKED + 2 * near + 1] = (fresh - high.astype(F32)).astype(BF16)
            else:
                sent[comp * PACKED + NEAR_ROWS + near] = high


def from_halo(halo, comp, near):
    if near < NEAR_ROWS:
        at = comp * PACKED + 2 * near
        return halo[at].astype(F32) + halo[at + 1].astype(F32)
    return halo[comp * PACKED + NEAR_ROWS + near].astype(F32)


def first(side, place, table, residual, vel, middle, other, edge, cells, halo, *outs):
    vel_out, sent, light, lame, shear, halo_out = outs
    count = table.shape[0]
    for out in range(DEEP + REACH):
        if out < DEEP:
            number, share = cells[out], 1.0
        else:
            number = halo[len(ALONG_X), REACH - 1 - (out - DEEP)]
            share = jnp.where(place[HAS_LOW if side else HAS_HIGH] > 0, 1.0, 0.0)
        parts = [jnp.full(number.shape, table[0, c], F32) for c in range(3)]
        for m in range(1, count):
            hit = number == float(m)
            parts = [jnp.where(hit, table[m, c], parts[c]) for c in range(3)]
        lame[out] = (TIME_STEP * STIFFNESS / UNIT * share) * parts[1]
        shear[out] = (TIME_STEP * STIFFNESS / UNIT * share) * parts[2]
        if out < DEEP:
            light[out] = (TIME_STEP / UNIT) / parts[0]
    for at in range(len(ALONG_X)):
        for near in range(REACH):
            value = halo[at, REACH - 1 - near]
            halo_out[at, near] = -value if ALONG_X[at] in MIRRORED_STRESS else value
    amount = AMPLITUDE * residual[place[ME], 0]
    push(place, side, amount, stress_rows(middle, other, edge, halo_out), vel, light, vel_out, sent)


def stress_rows(middle, other, edge, halo):
    def row(comp, out):
        if out < 0:
            return other[comp, -1 - out]
        if out < REACH:
            return middle[comp, out]
        if out < DEEP:
            return edge[comp, out - REACH]
        return halo[ALONG_X.index(comp), out - DEEP]

    return row


def strain_rates(vx, vy, vz, side, first_out, last_out, full_out):
    outs = range(first_out, last_out)
    wanted = [(vel, out) for out in outs for vel in (vx, vz)] + [(vy, out) for out in outs if out < full_out]
    deep = along_depth([vel(out) for vel, out in wanted])
    deep = {key: value for key, value in zip(wanted, deep)}
    for out in outs:
        rates = [
            derivative(across(vx, out, side)),
            derivative(along_y(vy(out))),
            deep[vz, out],
            across_and_along(vy, out, side, vx(out)),
            deep[vx, out] + derivative(across(vz, out, side)),
        ]
        if out < full_out:
            rates.append(deep[vy, out] + derivative(along_y(vz(out))))
        yield out, rates


def store(target, at, rates):
    count = rates[0].shape[0] // SUBLANES
    for comp, rate in enumerate(rates):
        for p in range(count):
            spot = pl.ds(p, SUBLANES, stride=count)
            target[comp, at, spot, :] = rate[SUBLANES * p : SUBLANES * (p + 1)]


def renew(rates, lame, shear, before):
    bulk = lame * (rates[0] + rates[1] + rates[2])
    twice = shear + shear
    return {
        comp: old + (bulk + twice * rates[comp] if comp < 3 else shear * rates[comp])
        for comp, old in before.items()
    }


def outer(side, moment, last, place, residual, vel, halo, edge, *refs):
    if last:
        (rates_out,) = refs
    else:
        old_halo, middle, other, light, lame, shear, rates_out, edge_out, halo_out, vel_out, sent = refs

    def rows(comp):
        return lambda out: vel[comp, out] if out < DEEP else from_halo(halo, comp, out - DEEP)

    until = DEEP if last else DEEP + REACH
    for out, rates in strain_rates(rows(0), rows(1), rows(2), side, REACH, until, DEEP):
        own = out < DEEP
        if own:
            store(rates_out, out - REACH, rates)
        if last:
            continue
        if own:
            fresh = renew(rates, lame[out], shear[out], {comp: edge[comp, out - REACH] for comp in range(6)})
            for comp, value in fresh.items():
                edge_out[comp, out - REACH] = value
        else:
            before = {comp: old_halo[at, out - DEEP] for at, comp in enumerate(ALONG_X)}
            fresh = renew(rates, lame[out], shear[out], before)
            for at, comp in enumerate(ALONG_X):
                halo_out[at, out - DEEP] = fresh[comp]
    if not last:
        amount = AMPLITUDE * residual[place[ME], moment + 1]
        push(place, side, amount, stress_rows(middle, other, edge_out, halo_out), vel, light, vel_out, sent)


def inner(last, place, *refs):
    vels = refs[:2]
    if last:
        rates_out = refs[2:]
    else:
        middles, lames, shears = refs[2:4], refs[4:6], refs[6:8]
        rates_out, middles_out = refs[8:10], refs[10:12]
    for side in range(2):

        def rows(comp):
            return lambda out: vels[side][comp, out] if out >= 0 else vels[1 - side][comp, -1 - out]

        for out, rates in strain_rates(rows(0), rows(1), rows(2), side, 0, REACH, REACH):
            store(rates_out[side], out, rates)
            if not last:
                before = {comp: middles[side][comp, out] for comp in range(6)}
                fresh = renew(rates, lames[side][out], shears[side][out], before)
                for comp, value in fresh.items():
                    middles_out[side][comp, out] = value


def correlate(moments, pieces, place, residual, *refs):
    rates, sources, terms = refs[: 4 * moments], refs[4 * moments : 4 * moments + pieces], refs[-1]
    tile_x, tile_y = sources[0].shape[2:4]
    sign = sign_of(place)
    for turn in range(pieces):
        spot = pl.ds(pl.multiple_of((place[ME] ^ turn) * tile_y, tile_y), tile_y)
        for side in range(2):
            for out in range(DEEP):
                row = row_of(place, side, out, tile_x)
                lam = mu = None
                for moment in range(moments):
                    weight = (KERNEL_SCALE / UNIT) * residual[place[ME], moment]
                    held = rates[4 * moment + 2 * (out // REACH) + side]
                    rate = [held[c, out % REACH, spot, :] for c in range(6)]
                    source = [sources[turn][moment, c, row] for c in range(6)]
                    bulk = (source[0] + source[1] + source[2]) * (rate[0] + rate[1] + rate[2])
                    diag = source[0] * rate[0] + source[1] * rate[1] + source[2] * rate[2]
                    off = sign * (source[3] * rate[3] + source[4] * rate[4]) + source[5] * rate[5]
                    bulk, both = weight * bulk, (2.0 * weight) * (diag + off)
                    lam = bulk if lam is None else lam + bulk
                    mu = both if mu is None else mu + both
                terms[turn, 0, row] = lam
                terms[turn, 1, row] = mu


def swap(array, axis, turn):
    count = lax.axis_size(axis)
    return lax.ppermute(array, axis, [(i, i ^ turn) for i in range(count)])


def partner(slab, piece, slabs, side):
    other = slab + 1 - 2 * ((slab + piece + side) % 2)
    return other, (other >= 0) & (other < slabs)


def to_neighbour(face, side):
    slabs, pieces = lax.axis_size("gx"), lax.axis_size("gy")
    pairs = []
    for slab in range(slabs):
        for piece in range(pieces):
            other, inside = partner(slab, piece, slabs, side)
            if inside:
                pairs.append((slab * pieces + piece, other * pieces + piece))
    return lax.ppermute(face, ("gx", "gy"), pairs)


def local(rec_state, source_strain, material, material_table, residual, rec_cell, listed, src_pick):
    state = rec_state[0]
    receivers, _, tile_x, tile_y, depth = state.shape
    pieces, slabs, groups = lax.axis_size("gy"), lax.axis_size("gx"), lax.axis_size("sta")
    assert receivers == pieces and tile_x == 2 * DEEP
    assert pieces & (pieces - 1) == 0 and groups & (groups - 1) == 0
    size_y = pieces * tile_y
    group, slab, me = lax.axis_index("sta"), lax.axis_index("gx"), lax.axis_index("gy")
    moments = residual.shape[2]

    numbers = material.astype(F32)[None]
    picked = [lax.dynamic_index_in_dim(state, me ^ turn, 0, keepdims=False) for turn in range(pieces)]
    order = sorted(range(pieces), reverse=True)
    stresses = {turn: jnp.concatenate([picked[turn][3:], numbers], 0) for turn in order}
    stresses = {turn: swap(stresses[turn], "gy", turn) if turn else stresses[turn] for turn in order}
    speeds = {turn: swap(picked[turn][:3], "gy", turn) if turn else picked[turn][:3] for turn in order}
    strains = [swap(source_strain[0], "sta", turn) if turn else source_strain[0] for turn in range(groups)]

    cell = lax.dynamic_index_in_dim(rec_cell[0], me, 0, keepdims=False)
    flip = (slab + me) % 2
    spot_x = cell // size_y - slab * tile_x
    spot_x = spot_x + flip * (tile_x - 1 - 2 * spot_x) - tile_x // 2
    inside = [partner(slab, me, slabs, side)[1] for side in range(2)]
    planes = size_y // SUBLANES
    spot_y = cell % size_y
    spot_y = (spot_y % planes) * SUBLANES + spot_y // planes
    place = jnp.stack([me, flip, *inside, spot_x, spot_y]).astype(jnp.int32)
    rows = residual[0]

    def shape(*lead, kind=F32):
        return lead + (size_y, depth), kind

    vel_shape, pair_shape = shape(3, DEEP), shape(6, REACH)
    halo_shape, sent_shape = shape(3, REACH), shape(3 * PACKED, kind=BF16)

    held = [pltpu.VMEM((8, size_y, depth), F32)]
    results = call(
        assemble_stress,
        [pair_shape, pair_shape, shape(DEEP), shape(4, REACH)] * 2,
        ([place], [stresses[turn] for turn in range(pieces)]),
        held,
    )
    middles, edges, cells, faces = ([results[at], results[4 + at]] for at in range(4))
    halos = [to_neighbour(faces[side], side) for side in range(2)]
    vels = call(
        assemble_vel, [vel_shape] * 2, ([place], [speeds[turn] for turn in range(pieces)]), held
    )

    sent, lights, lames, shears, old_halos = ([None, None] for _ in range(5))
    fresh = [None, None]
    for side in range(2):
        fresh[side], sent[side], lights[side], lames[side], shears[side], old_halos[side] = call(
            functools.partial(first, side),
            [vel_shape, sent_shape, shape(DEEP), shape(DEEP + REACH), shape(DEEP + REACH), halo_shape],
            (
                [place, material_table, rows],
                [vels[side], middles[side], middles[1 - side], edges[side], cells[side], halos[side]],
            ),
        )
        sent[side] = to_neighbour(sent[side], side)
    vels = fresh

    strains, vels = lax.optimization_barrier((strains, vels))
    weights = lax.dynamic_slice_in_dim(listed, group, 1, 2)[:, :, 0].astype(F32)
    combined = 0.0
    for turn in range(groups):
        factor = jnp.sum(weights * (src_pick == (group ^ turn)).astype(F32), 0)
        combined = combined + factor[:, None, None, None, None] * strains[turn].astype(F32)
    width = pieces // 2
    found = {0: combined}
    if width:
        found[width] = swap(combined, "gy", width)
        width //= 2

    rates = []
    for moment in range(moments):
        last = moment == moments - 1
        results = call(
            functools.partial(inner, last),
            [pair_shape] * (2 if last else 4),
            ([place], vels if last else vels + middles + lames + shears),
        )
        rates += results[:2]
        if not last:
            middles = results[2:]
        if moment == 3 * moments // 4:
            found, middles = lax.optimization_barrier((found, middles))
            while width:
                for turn in list(found):
                    found[turn ^ width] = swap(found[turn], "gy", width)
                width //= 2
        fresh = [None, None]
        for side in range(2):
            arrays = [vels[side], sent[side], edges[side]]
            outs = [pair_shape]
            if not last:
                arrays += [old_halos[side], middles[side], middles[1 - side]]
                arrays += [lights[side], lames[side], shears[side]]
                outs += [pair_shape, halo_shape, vel_shape, sent_shape]
            results = call(functools.partial(outer, side, moment, last), outs, ([place, rows], arrays))
            rates.append(results[0])
            if not last:
                edges[side], old_halos[side], fresh[side] = results[1:4]
                sent[side] = to_neighbour(results[4], side)
        vels = fresh

    (terms,) = call(
        functools.partial(correlate, moments, pieces),
        [((pieces, 2, tile_x, tile_y, depth), F32)],
        ([place, rows], rates + [found[turn] for turn in range(pieces)]),
    )
    held = {turn: terms[turn] for turn in range(pieces)}
    if pieces > 1:
        keep = [turn for turn in held if not turn & 1]
        got = swap(jnp.stack([held[turn ^ 1] for turn in keep]), "gy", 1)
        held = {turn: held[turn] + got[at] for at, turn in enumerate(keep)}
    share = tile_x // groups
    result = 0.0
    for across_sta in reversed(range(groups)):
        for turn in reversed(list(held)):
            part = lax.dynamic_slice_in_dim(held[turn], (group ^ across_sta) * share, share, 1)
            if across_sta or turn:
                pairs = [
                    (a * pieces + b, (a ^ across_sta) * pieces + (b ^ turn))
                    for a in range(groups)
                    for b in range(pieces)
                ]
                part = lax.ppermute(part, ("sta", "gy"), pairs)
            result = result + part
    return result


def solution(mesh):
    in_specs = (
        P("sta", None, None, "gx", "gy", None),
        P("sta", None, None, "gx", "gy", None),
        P("gx", "gy", None),
        P(),
        P("sta", None, None),
        P("sta", None),
        P(),
        P(),
    )
    out_specs = P(None, ("gx", "sta"), "gy", None)
    return jax.shard_map(local, mesh=mesh, in_specs=in_specs, out_specs=out_specs, check_vma=False)
```

time: 133 us -> 123 us (0.925)
  local copies, waits for them, and re-layouts: 10.5 us -> 3.22 us
  waiting for transfers between devices: 26.1 us -> 19 us
  starting transfers between devices: 59.7 us -> 65.1 us
    ppermute x10 -> x11, waiting for transfers between devices: 19.2 us -> 5.9 us  [swap(): return lax.ppermute(array, axis, [(i, i ^ turn) for i in range(count)])]
    unnamed x43 -> x15, local copies, waits for them, and re-layouts: 8.55 us -> 0.12 us
    ppermute x10 -> x11, starting transfers between devices: 8.58 us -> 12.3 us  [swap(): return lax.ppermute(array, axis, [(i, i ^ turn) for i in range(count)])]
    ppermute x0 -> x3, starting transfers between devices: none -> 3.55 us  [local(): part = lax.ppermute(part, ('sta', 'gy'), pairs)]
    ppermute x0 -> x3, waiting for transfers between devices: none -> 3.54 us  [local(): part = lax.ppermute(part, ('sta', 'gy'), pairs)]
    ppermute x18, waiting for transfers between devices: 6.86 us -> 9.59 us  [to_neighbour(): return lax.ppermute(face, ('gx', 'gy'), pairs)]
    slice x0 -> x2, local copies, waits for them, and re-layouts: none -> 2.33 us  [the longest x1 1.27 us: local(): picked[turn][3:]]
    ppermute x18, starting transfers between devices: 51.1 us -> 49.2 us  [to_neighbour(): return lax.ppermute(face, ('gx', 'gy'), pairs)]
  transfers between devices with their start and end apart: 28 -> 32, of which waited for: 12 -> 15; matrix products, arithmetic and copies ran while one was open for 3% -> 3% of each run, Pallas kernels for 22% -> 22%
where the time goes in v3:
time: 123 us; the launch traced here: 122 us
  starting transfers between devices  65.1 us (53%)
  Pallas kernels  29.3 us (24%)
  waiting for transfers between devices  19 us (15%)
  between operations  3.35 us (3%)
  local copies, waits for them, and re-layouts  3.22 us (3%)
  other arithmetic  2.26 us (2%)
    ppermute x18, starting transfers between devices, to_neighbour(): return lax.ppermute(face, ('gx', 'gy'), pairs)  49.2 us
    pallas_call x29, Pallas kernels, call(): pl.pallas_call(body, out_shape=[jax.ShapeDtypeStruct(shape, kind) for sha...  29.3 us
    ppermute x11, starting transfers between devices, swap(): return lax.ppermute(array, axis, [(i, i ^ turn) for i in range(count)])  12.3 us
    ppermute x18, waiting for transfers between devices, to_neighbour(): return lax.ppermute(face, ('gx', 'gy'), pairs)  9.59 us
    ppermute x11, waiting for transfers between devices, swap(): return lax.ppermute(array, axis, [(i, i ^ turn) for i in range(count)])  5.9 us
    ppermute x3, starting transfers between devices, local(): part = lax.ppermute(part, ('sta', 'gy'), pairs)  3.55 us
    ppermute x3, waiting for transfers between devices, local(): part = lax.ppermute(part, ('sta', 'gy'), pairs)  3.54 us
  transfers between devices with their start and end apart: 32, of which 15 were waited for; matrix products, arithmetic and copies ran while one was open for 3% of the time, Pallas kernels for 22%

profile of v3, /device:TPU:0, one launch (start us, length us, event | category | flops | bytes accessed | tf_op | source)
XLA Modules:
  0.0 122.3 jit_solution(18286555458398358507)
XLA Ops:
  0.0 2.9 %collective-permute-start = (bf16[8,6,8,8,128]{4,3,2,1,0:T(8,128)(2,1)}, bf16[8,6,8,8,128]{4,3,2,1,0:T(8,128)(2,1)}, u32[]{:S(2)}, u32[]{:S(2)}) collective-permute-start(bf16[8,6,8,8,128]{4,3,2,1,0:T(8,128)(2,1)} %bitcast.55), channel_id=1, source_target_pairs={{0,16},{16,0},{1,17},{17,1},{2,18},{18,2},{3,19},{19,3},{4,20},{20... | collective-permute-start | bytes 2359304 | tf_op jit(solution)/shard_map/ppermute | solution.py:333
  2.9 1.3 %dynamic-slice_bitcast_fusion = (f32[6,8,8,128]{3,2,1,0:T(8,128)S(1)}, f32[6,8,8,128]{3,2,1,0:T(8,128)S(1)}, f32[6,8,8,128]{3,2,1,0:T(8,128)S(1)}, f32[6,8,8,128]{3,2,1,0:T(8,128)S(1)}) fusion(f32[1,4,9,8,8,128]{5,4,3,2,1,0:T(8,128)} %param.8, s32[]{:T(128)S(6)} %select_n.63, s32[]{:T(128)S(6)} %add.103, s32[]{:T(128)S(6)} %select_n.61, s32[]{:T(128)S(6)} %select_n.56, ...), kind=kLoop, calls=%fused_computation.5 | loop fusion | bytes 1572884 | tf_op jit(solution)/shard_map/slice | solution.py:365
  5.1 1.0 collective-permute-start.4
  6.6 1.1 dynamic-slice_bitcast_fusion.4
  12.3 1.6 %collective-permute-start.2 = (f32[3,8,8,128]{3,2,1,0:T(8,128)S(1)}, f32[3,8,8,128]{3,2,1,0:T(8,128)S(1)}, u32[]{:S(2)}, u32[]{:S(2)}) collective-permute-start(f32[3,8,8,128]{3,2,1,0:T(8,128)S(1)} %get-tuple-element.268), channel_id=1, source_target_pairs={{0,2},{1,3},{2,0},{3,1},{4,6},{5,7},{6,4},{7,5},{8,10},{9,11},{10,... | collective-permute-start | bytes 294920 | tf_op jit(solution)/shard_map/ppermute | solution.py:333
  13.9 3.5 %collective-permute-done.5.refs_2_ = f32[7,8,8,128]{3,2,1,0:T(8,128)S(1)} collective-permute-done((f32[7,8,8,128]{3,2,1,0:T(8,128)S(1)}, f32[7,8,8,128]{3,2,1,0:T(8,128)S(1)}, u32[]{:S(2)}, u32[]{:S(2)}) %collective-permute-start.5) | collective-permute-done | bytes 229408 | tf_op jit(solution)/shard_map/ppermute | solution.py:333
  17.3 1.0 shard_map.83
  18.4 3.5 %collective-permute-start.7 = (f32[4,2,32,128]{3,2,1,0:T(8,128)S(1)}, f32[4,2,32,128]{3,2,1,0:T(8,128)S(1)}, u32[]{:S(2)}, u32[]{:S(2)}) collective-permute-start(f32[4,2,32,128]{3,2,1,0:T(8,128)S(1)} %get-tuple-element.138), channel_id=1, source_target_pairs={{0,4},{2,6},{4,0},{5,9},{6,2},{7,11},{8,12},{9,5},{10,14},{11,7},{... | collective-permute-start | bytes 393224 | tf_op jit(solution)/shard_map/ppermute | solution.py:349
  22.7 2.3 %collective-permute-start.1 = (f32[3,8,8,128]{3,2,1,0:T(8,128)S(1)}, f32[3,8,8,128]{3,2,1,0:T(8,128)S(1)}, u32[]{:S(2)}, u32[]{:S(2)}) collective-permute-start(f32[3,8,8,128]{3,2,1,0:T(8,128)S(1)} %get-tuple-element.269), channel_id=1, source_target_pairs={{0,1},{1,0},{2,3},{3,2},{4,5},{5,4},{6,7},{7,6},{8,9},{9,8},{10,11... | collective-permute-start | bytes 294920 | tf_op jit(solution)/shard_map/ppermute | solution.py:333
  25.0 0.9 collective-permute-done.1.refs_1_
  26.7 1.1 shard_map.85
  27.8 1.1 shard_map.84
  29.0 1.5 %multiply_add_fusion.refs_32_ = f32[8,6,8,8,128]{4,3,2,1,0:T(8,128)S(1)} fusion(bf16[8,6,8,8,128]{4,3,2,1,0:T(8,128)(2,1)} %collective-permute-done, bf16[8,6,8,8,128]{4,3,2,1,0:T(8,128)(2,1)S(1)} %bitcast.56, f32[8]{0:T(128)S(1)} %get-tuple-element.262, f32[8]{0:T(128)S(1)} %get-tuple-element.261), kind=kLoop, calls=%fused_computation | loop fusion | flops 1966080 | bytes 3145792 | tf_op jit(solution)/shard_map/add | solution.py:419
  30.5 1.7 %collective-permute-start.22 = (f32[8,6,8,8,128]{4,3,2,1,0:T(8,128)S(1)}, f32[8,6,8,8,128]{4,3,2,1,0:T(8,128)S(1)}, u32[]{:S(2)}, u32[]{:S(2)}) collective-permute-start(f32[8,6,8,8,128]{4,3,2,1,0:T(8,128)S(1)} %multiply_add_fusion.refs_32_), channel_id=1, source_target_pairs={{0,2},{1,3},{2,0},{3,1},{4,6},{5,7},{6,4},{7,5},{8,10},{9,11},{10,... | collective-permute-start | bytes 4718600 | tf_op jit(solution)/shard_map/ppermute | solution.py:333
  32.8 7.6 %collective-permute-start.9 = (bf16[18,32,128]{2,1,0:T(8,128)(2,1)S(1)}, bf16[18,32,128]{2,1,0:T(8,128)(2,1)S(1)}, u32[]{:S(2)}, u32[]{:S(2)}) collective-permute-start(bf16[18,32,128]{2,1,0:T(8,128)(2,1)S(1)} %get-tuple-element.153), channel_id=1, source_target_pairs={{0,4},{2,6},{4,0},{5,9},{6,2},{7,11},{8,12},{9,5},{10,14},{11,7},{... | collective-permute-start | bytes 442376 | tf_op jit(solution)/shard_map/ppermute | solution.py:349
  41.3 1.0 shard_map.88
  43.6 1.0 shard_map.87
  44.6 6.3 %collective-permute-start.11 = (bf16[18,32,128]{2,1,0:T(8,128)(2,1)S(1)}, bf16[18,32,128]{2,1,0:T(8,128)(2,1)S(1)}, u32[]{:S(2)}, u32[]{:S(2)}) collective-permute-start(bf16[18,32,128]{2,1,0:T(8,128)(2,1)S(1)} %get-tuple-element.167), channel_id=1, source_target_pairs={{0,4},{2,6},{4,0},{5,9},{6,2},{7,11},{8,12},{9,5},{10,14},{11,7},{... | collective-permute-start | bytes 442376 | tf_op jit(solution)/shard_map/ppermute | solution.py:349
  51.7 1.1 shard_map.91
  53.4 1.8 %collective-permute-done.11.halo = bf16[18,32,128]{2,1,0:T(8,128)(2,1)S(1)} collective-permute-done((bf16[18,32,128]{2,1,0:T(8,128)(2,1)S(1)}, bf16[18,32,128]{2,1,0:T(8,128)(2,1)S(1)}, u32[]{:S(2)}, u32[]{:S(2)}) %collective-permute-start.11) | collective-permute-done | bytes 147488 | tf_op jit(solution)/shard_map/ppermute | solution.py:349
  55.2 1.0 shard_map.90
  56.3 3.6 %collective-permute-start.13 = (bf16[18,32,128]{2,1,0:T(8,128)(2,1)S(1)}, bf16[18,32,128]{2,1,0:T(8,128)(2,1)S(1)}, u32[]{:S(2)}, u32[]{:S(2)}) collective-permute-start(bf16[18,32,128]{2,1,0:T(8,128)(2,1)S(1)} %get-tuple-element.181), channel_id=1, source_target_pairs={{0,4},{2,6},{4,0},{5,9},{6,2},{7,11},{8,12},{9,5},{10,14},{11,7},{... | collective-permute-start | bytes 442376 | tf_op jit(solution)/shard_map/ppermute | solution.py:349
  60.7 1.0 shard_map.94
  62.5 1.3 %collective-permute-done.13.halo = bf16[18,32,128]{2,1,0:T(8,128)(2,1)S(1)} collective-permute-done((bf16[18,32,128]{2,1,0:T(8,128)(2,1)S(1)}, bf16[18,32,128]{2,1,0:T(8,128)(2,1)S(1)}, u32[]{:S(2)}, u32[]{:S(2)}) %collective-permute-start.13) | collective-permute-done | bytes 147488 | tf_op jit(solution)/shard_map/ppermute | solution.py:349
  63.8 1.0 shard_map.93
  64.8 3.3 %collective-permute-start.15 = (bf16[18,32,128]{2,1,0:T(8,128)(2,1)S(1)}, bf16[18,32,128]{2,1,0:T(8,128)(2,1)S(1)}, u32[]{:S(2)}, u32[]{:S(2)}) collective-permute-start(bf16[18,32,128]{2,1,0:T(8,128)(2,1)S(1)} %get-tuple-element.195), channel_id=1, source_target_pairs={{0,4},{2,6},{4,0},{5,9},{6,2},{7,11},{8,12},{9,5},{10,14},{11,7},{... | collective-permute-start | bytes 442376 | tf_op jit(solution)/shard_map/ppermute | solution.py:349
  68.9 1.0 shard_map.97
  70.6 1.2 collective-permute-done.15.halo
  71.8 1.0 shard_map.96
  72.9 3.5 %collective-permute-start.17 = (bf16[18,32,128]{2,1,0:T(8,128)(2,1)S(1)}, bf16[18,32,128]{2,1,0:T(8,128)(2,1)S(1)}, u32[]{:S(2)}, u32[]{:S(2)}) collective-permute-start(bf16[18,32,128]{2,1,0:T(8,128)(2,1)S(1)} %get-tuple-element.209), channel_id=1, source_target_pairs={{0,4},{2,6},{4,0},{5,9},{6,2},{7,11},{8,12},{9,5},{10,14},{11,7},{... | collective-permute-start | bytes 442376 | tf_op jit(solution)/shard_map/ppermute | solution.py:349
  77.2 1.0 shard_map.100
  78.9 1.0 collective-permute-done.17.halo
  79.9 1.0 shard_map.99
  81.0 3.9 %collective-permute-start.19 = (bf16[18,32,128]{2,1,0:T(8,128)(2,1)S(1)}, bf16[18,32,128]{2,1,0:T(8,128)(2,1)S(1)}, u32[]{:S(2)}, u32[]{:S(2)}) collective-permute-start(bf16[18,32,128]{2,1,0:T(8,128)(2,1)S(1)} %get-tuple-element.223), channel_id=1, source_target_pairs={{0,4},{2,6},{4,0},{5,9},{6,2},{7,11},{8,12},{9,5},{10,14},{11,7},{... | collective-permute-start | bytes 442376 | tf_op jit(solution)/shard_map/ppermute | solution.py:349
  85.7 1.0 shard_map.103
  86.7 1.3 %collective-permute-done.19.halo = bf16[18,32,128]{2,1,0:T(8,128)(2,1)S(1)} collective-permute-done((bf16[18,32,128]{2,1,0:T(8,128)(2,1)S(1)}, bf16[18,32,128]{2,1,0:T(8,128)(2,1)S(1)}, u32[]{:S(2)}, u32[]{:S(2)}) %collective-permute-start.19) | collective-permute-done | bytes 147488 | tf_op jit(solution)/shard_map/ppermute | solution.py:349
  88.0 1.0 shard_map.102
  91.1 5.9 %collective-permute-start.21 = (bf16[18,32,128]{2,1,0:T(8,128)(2,1)S(1)}, bf16[18,32,128]{2,1,0:T(8,128)(2,1)S(1)}, u32[]{:S(2)}, u32[]{:S(2)}) collective-permute-start(bf16[18,32,128]{2,1,0:T(8,128)(2,1)S(1)} %get-tuple-element.237), channel_id=1, source_target_pairs={{0,4},{2,6},{4,0},{5,9},{6,2},{7,11},{8,12},{9,5},{10,14},{11,7},{... | collective-permute-start | bytes 442376 | tf_op jit(solution)/shard_map/ppermute | solution.py:349
  97.0 1.5 %shard_map.106 = (f32[6,2,32,128]{3,2,1,0:T(8,128)S(1)}, f32[6,2,32,128]{3,2,1,0:T(8,128)S(1)}, f32[3,2,32,128]{3,2,1,0:T(8,128)}, f32[3,4,32,128]{3,2,1,0:T(8,128)S(1)}, bf16[18,32,128]{2,1,0:T(8,128)(2,1)S(1)}) custom-call(s32[6]{0:T(128)S(1)} %stack.38.place, f32[4,8]{1,0:T(4,128)S(1)} %bitcast.50, f32[3,4,32,128]{3,2,1,0:T(8,128)S(1)} %get-tuple-element.234.refs_1_.vel, ...), custom_call_target="tpu_custom_call" | custom-call | flops 1000000 | bytes 2000000 | tf_op jit(solution)/shard_map/pallas_call | solution.py:31
  99.2 0.9 collective-permute-done.21.halo
  100.1 1.5 %shard_map.105 = (f32[6,2,32,128]{3,2,1,0:T(8,128)S(1)}, f32[6,2,32,128]{3,2,1,0:T(8,128)S(1)}, f32[3,2,32,128]{3,2,1,0:T(8,128)}, f32[3,4,32,128]{3,2,1,0:T(8,128)S(1)}, bf16[18,32,128]{2,1,0:T(8,128)(2,1)S(1)}) custom-call(s32[6]{0:T(128)S(1)} %stack.38.place, f32[4,8]{1,0:T(4,128)S(1)} %bitcast.51, f32[3,4,32,128]{3,2,1,0:T(8,128)S(1)} %get-tuple-element.233.refs_0_.vel, ...), custom_call_target="tpu_custom_call" | custom-call | flops 1000000 | bytes 2000000 | tf_op jit(solution)/shard_map/pallas_call | solution.py:31
  101.6 5.6 %collective-permute-start.24 = (bf16[18,32,128]{2,1,0:T(8,128)(2,1)S(1)}, bf16[18,32,128]{2,1,0:T(8,128)(2,1)S(1)}, u32[]{:S(2)}, u32[]{:S(2)}) collective-permute-start(bf16[18,32,128]{2,1,0:T(8,128)(2,1)S(1)} %get-tuple-element.255), channel_id=1, source_target_pairs={{0,4},{2,6},{4,0},{5,9},{6,2},{7,11},{8,12},{9,5},{10,14},{11,7},{... | collective-permute-start | bytes 442376 | tf_op jit(solution)/shard_map/ppermute | solution.py:349
  108.8 1.6 %collective-permute-done.24.halo = bf16[18,32,128]{2,1,0:T(8,128)(2,1)S(1)} collective-permute-done((bf16[18,32,128]{2,1,0:T(8,128)(2,1)S(1)}, bf16[18,32,128]{2,1,0:T(8,128)(2,1)S(1)}, u32[]{:S(2)}, u32[]{:S(2)}) %collective-permute-start.24) | collective-permute-done | bytes 147488 | tf_op jit(solution)/shard_map/ppermute | solution.py:349
  111.1 1.9 %shard_map.110 = f32[4,2,8,8,128]{4,3,2,1,0:T(8,128)S(1)} custom-call(s32[6]{0:T(128)S(1)} %stack.38.place, f32[4,8]{1,0:T(4,128)S(1)} %bitcast.54, f32[6,2,32,128]{3,2,1,0:T(8,128)S(1)} %get-tuple-element.151.refs_0_, f32[6,2,32,128]{3,2,1,0:T(8,128)S(1)} %get-tuple-element.152.refs_1_, f32[6,2,32,128]{3,2,1,0:T(8,128)S(1)} %get-tuple-element.158.refs_2_, ...), custom_call_target="tpu_custom_call" | custom-call | flops 1000000 | bytes 2000000 | tf_op jit(solution)/shard_map/pallas_call | solution.py:31
  113.2 1.3 %collective-permute-done.28 = f32[2,2,8,8,128]{4,3,2,1,0:T(8,128)S(1)} collective-permute-done((f32[2,2,8,8,128]{4,3,2,1,0:T(8,128)S(1)}, f32[2,2,8,8,128]{4,3,2,1,0:T(8,128)S(1)}, u32[]{:S(2)}, u32[]{:S(2)}) %collective-permute-start.28) | collective-permute-done | bytes 131104 | tf_op jit(solution)/shard_map/ppermute | solution.py:333
  115.1 2.6 %collective-permute-start.29 = (f32[2,4,8,128]{3,2,1,0:T(8,128)S(1)}, f32[2,4,8,128]{3,2,1,0:T(8,128)S(1)}, u32[]{:S(2)}, u32[]{:S(2)}) collective-permute-start(f32[2,4,8,128]{3,2,1,0:T(8,128)S(1)} %get-tuple-element.275), channel_id=1, source_target_pairs={{0,18},{1,19},{2,16},{3,17},{16,2},{17,3},{18,0},{19,1},{4,22},{5,... | collective-permute-start | bytes 98312 | tf_op jit(solution)/shard_map/ppermute | solution.py:479
  118.5 1.4 %collective-permute-done.29 = f32[2,4,8,128]{3,2,1,0:T(8,128)S(1)} collective-permute-done((f32[2,4,8,128]{3,2,1,0:T(8,128)S(1)}, f32[2,4,8,128]{3,2,1,0:T(8,128)S(1)}, u32[]{:S(2)}, u32[]{:S(2)}) %collective-permute-start.29) | collective-permute-done | bytes 32800 | tf_op jit(solution)/shard_map/ppermute | solution.py:479
  119.9 1.7 %collective-permute-done.31 = f32[2,4,8,128]{3,2,1,0:T(8,128)S(1)} collective-permute-done((f32[2,4,8,128]{3,2,1,0:T(8,128)S(1)}, f32[2,4,8,128]{3,2,1,0:T(8,128)S(1)}, u32[]{:S(2)}, u32[]{:S(2)}) %collective-permute-start.31) | collective-permute-done | bytes 32800 | tf_op jit(solution)/shard_map/ppermute | solution.py:479
  (75 shorter events, 21.2 us)
Async XLA Ops:
  0.0 8.6 %copy-start = (s32[1,4]{1,0:T(1,128)S(1)}, s32[1,4]{1,0:T(1,128)}, u32[]{:S(2)}) copy-start(s32[1,4]{1,0:T(1,128)} %param.13) | copy-start | bytes 52
  0.0 4.2 %copy-start.3 = (s32[8,8,128]{2,1,0:T(8,128)S(1)}, s32[8,8,128]{2,1,0:T(8,128)}, u32[]{:S(2)}) copy-start(s32[8,8,128]{2,1,0:T(8,128)} %param.10) | copy-start | bytes 98308
  0.0 29.0 %collective-permute-start = (bf16[8,6,8,8,128]{4,3,2,1,0:T(8,128)(2,1)}, bf16[8,6,8,8,128]{4,3,2,1,0:T(8,128)(2,1)}, u32[]{:S(2)}, u32[]{:S(2)}) collective-permute-start(bf16[8,6,8,8,128]{4,3,2,1,0:T(8,128)(2,1)} %bitcast.55), channel_id=1, source_target_pairs={{0,16},{16,0},{1,17},{17,1},{2,18},{18,2},{3,19},{19,3},{4,20},{20... | collective-permute-start | bytes 2359304 | tf_op jit(solution)/shard_map/ppermute | solution.py:333
  4.2 18.3 %copy-start.6 = (s32[2,8,2]{1,2,0:T(2,128)S(1)}, s32[2,8,2]{1,2,0:T(2,128)}, u32[]{:S(2)}) copy-start(s32[2,8,2]{1,2,0:T(2,128)} %param.14) | copy-start | bytes 388
  4.3 18.3 %copy-start.4 = (f32[16,3]{0,1:T(4,128)S(1)}, f32[16,3]{0,1:T(4,128)}, u32[]{:S(2)}) copy-start(f32[16,3]{0,1:T(4,128)} %param.11) | copy-start | bytes 580
  4.3 20.7 %copy-start.5 = (s32[2,8]{1,0:T(2,128)S(1)}, s32[2,8]{1,0:T(2,128)}, u32[]{:S(2)}) copy-start(s32[2,8]{1,0:T(2,128)} %param.15) | copy-start | bytes 196
  4.4 22.3 %copy-start.1 = (f32[1,4,8]{2,1,0:T(4,128)S(1)}, f32[1,4,8]{2,1,0:T(4,128)}, u32[]{:S(2)}) copy-start(f32[1,4,8]{2,1,0:T(4,128)} %param.12) | copy-start | bytes 388
  4.4 7.9 %collective-permute-start.6 = (f32[7,8,8,128]{3,2,1,0:T(8,128)S(1)}, f32[7,8,8,128]{3,2,1,0:T(8,128)S(1)}, u32[]{:S(2)}, u32[]{:S(2)}) collective-permute-start(f32[7,8,8,128]{3,2,1,0:T(8,128)S(1)} %get-tuple-element.277), channel_id=1, source_target_pairs={{0,3},{1,2},{2,1},{3,0},{4,7},{5,6},{6,5},{7,4},{8,11},{9,10},{10,... | collective-permute-start | bytes 688136 | tf_op jit(solution)/shard_map/ppermute | solution.py:333
  5.1 8.7 %collective-permute-start.4 = (f32[7,8,8,128]{3,2,1,0:T(8,128)S(1)}, f32[7,8,8,128]{3,2,1,0:T(8,128)S(1)}, u32[]{:S(2)}, u32[]{:S(2)}) collective-permute-start(f32[7,8,8,128]{3,2,1,0:T(8,128)S(1)} %get-tuple-element.278), channel_id=1, source_target_pairs={{0,1},{1,0},{2,3},{3,2},{4,5},{5,4},{6,7},{7,6},{8,9},{9,8},{10,11... | collective-permute-start | bytes 688136 | tf_op jit(solution)/shard_map/ppermute | solution.py:333
  6.1 11.3 %collective-permute-start.5 = (f32[7,8,8,128]{3,2,1,0:T(8,128)S(1)}, f32[7,8,8,128]{3,2,1,0:T(8,128)S(1)}, u32[]{:S(2)}, u32[]{:S(2)}) collective-permute-start(f32[7,8,8,128]{3,2,1,0:T(8,128)S(1)} %get-tuple-element.279), channel_id=1, source_target_pairs={{0,2},{1,3},{2,0},{3,1},{4,6},{5,7},{6,4},{7,5},{8,10},{9,11},{10,... | collective-permute-start | bytes 688136 | tf_op jit(solution)/shard_map/ppermute | solution.py:333
  7.6 15.0 %collective-permute-start.3 = (f32[3,8,8,128]{3,2,1,0:T(8,128)S(1)}, f32[3,8,8,128]{3,2,1,0:T(8,128)S(1)}, u32[]{:S(2)}, u32[]{:S(2)}) collective-permute-start(f32[3,8,8,128]{3,2,1,0:T(8,128)S(1)} %get-tuple-element.267), channel_id=1, source_target_pairs={{0,3},{1,2},{2,1},{3,0},{4,7},{5,6},{6,5},{7,4},{8,11},{9,10},{10,... | collective-permute-start | bytes 294920 | tf_op jit(solution)/shard_map/ppermute | solution.py:333
  12.3 12.7 %collective-permute-start.2 = (f32[3,8,8,128]{3,2,1,0:T(8,128)S(1)}, f32[3,8,8,128]{3,2,1,0:T(8,128)S(1)}, u32[]{:S(2)}, u32[]{:S(2)}) collective-permute-start(f32[3,8,8,128]{3,2,1,0:T(8,128)S(1)} %get-tuple-element.268), channel_id=1, source_target_pairs={{0,2},{1,3},{2,0},{3,1},{4,6},{5,7},{6,4},{7,5},{8,10},{9,11},{10,... | collective-permute-start | bytes 294920 | tf_op jit(solution)/shard_map/ppermute | solution.py:333
  17.3 11.7 %copy-start.2 = (bf16[1,8,6,8,8,128]{5,4,3,2,1,0:T(8,128)(2,1)S(1)}, bf16[1,8,6,8,8,128]{5,4,3,2,1,0:T(8,128)(2,1)}, u32[]{:S(2)}) copy-start(bf16[1,8,6,8,8,128]{5,4,3,2,1,0:T(8,128)(2,1)} %param.9) | copy-start | bytes 2359300
  18.4 9.5 %collective-permute-start.7 = (f32[4,2,32,128]{3,2,1,0:T(8,128)S(1)}, f32[4,2,32,128]{3,2,1,0:T(8,128)S(1)}, u32[]{:S(2)}, u32[]{:S(2)}) collective-permute-start(f32[4,2,32,128]{3,2,1,0:T(8,128)S(1)} %get-tuple-element.138), channel_id=1, source_target_pairs={{0,4},{2,6},{4,0},{5,9},{6,2},{7,11},{8,12},{9,5},{10,14},{11,7},{... | collective-permute-start | bytes 393224 | tf_op jit(solution)/shard_map/ppermute | solution.py:349
  21.9 4.8 %collective-permute-start.8 = (f32[4,2,32,128]{3,2,1,0:T(8,128)S(1)}, f32[4,2,32,128]{3,2,1,0:T(8,128)S(1)}, u32[]{:S(2)}, u32[]{:S(2)}) collective-permute-start(f32[4,2,32,128]{3,2,1,0:T(8,128)S(1)} %get-tuple-element.143), channel_id=1, source_target_pairs={{1,5},{3,7},{4,8},{5,1},{6,10},{7,3},{8,4},{9,13},{10,6},{11,15},{... | collective-permute-start | bytes 393224 | tf_op jit(solution)/shard_map/ppermute | solution.py:349
  22.7 3.3 %collective-permute-start.1 = (f32[3,8,8,128]{3,2,1,0:T(8,128)S(1)}, f32[3,8,8,128]{3,2,1,0:T(8,128)S(1)}, u32[]{:S(2)}, u32[]{:S(2)}) collective-permute-start(f32[3,8,8,128]{3,2,1,0:T(8,128)S(1)} %get-tuple-element.269), channel_id=1, source_target_pairs={{0,1},{1,0},{2,3},{3,2},{4,5},{5,4},{6,7},{7,6},{8,9},{9,8},{10,11... | collective-permute-start | bytes 294920 | tf_op jit(solution)/shard_map/ppermute | solution.py:333
  30.5 59.3 %collective-permute-start.22 = (f32[8,6,8,8,128]{4,3,2,1,0:T(8,128)S(1)}, f32[8,6,8,8,128]{4,3,2,1,0:T(8,128)S(1)}, u32[]{:S(2)}, u32[]{:S(2)}) collective-permute-start(f32[8,6,8,8,128]{4,3,2,1,0:T(8,128)S(1)} %multiply_add_fusion.refs_32_), channel_id=1, source_target_pairs={{0,2},{1,3},{2,0},{3,1},{4,6},{5,7},{6,4},{7,5},{8,10},{9,11},{10,... | collective-permute-start | bytes 4718600 | tf_op jit(solution)/shard_map/ppermute | solution.py:333
  32.2 9.1 %collective-permute-start.10 = (bf16[18,32,128]{2,1,0:T(8,128)(2,1)S(1)}, bf16[18,32,128]{2,1,0:T(8,128)(2,1)S(1)}, u32[]{:S(2)}, u32[]{:S(2)}) collective-permute-start(bf16[18,32,128]{2,1,0:T(8,128)(2,1)S(1)} %get-tuple-element.159), channel_id=1, source_target_pairs={{1,5},{3,7},{4,8},{5,1},{6,10},{7,3},{8,4},{9,13},{10,6},{11,15},{... | collective-permute-start | bytes 442376 | tf_op jit(solution)/shard_map/ppermute | solution.py:349
  32.8 10.8 %collective-permute-start.9 = (bf16[18,32,128]{2,1,0:T(8,128)(2,1)S(1)}, bf16[18,32,128]{2,1,0:T(8,128)(2,1)S(1)}, u32[]{:S(2)}, u32[]{:S(2)}) collective-permute-start(bf16[18,32,128]{2,1,0:T(8,128)(2,1)S(1)} %get-tuple-element.153), channel_id=1, source_target_pairs={{0,4},{2,6},{4,0},{5,9},{6,2},{7,11},{8,12},{9,5},{10,14},{11,7},{... | collective-permute-start | bytes 442376 | tf_op jit(solution)/shard_map/ppermute | solution.py:349
  42.3 9.4 %collective-permute-start.12 = (bf16[18,32,128]{2,1,0:T(8,128)(2,1)S(1)}, bf16[18,32,128]{2,1,0:T(8,128)(2,1)S(1)}, u32[]{:S(2)}, u32[]{:S(2)}) collective-permute-start(bf16[18,32,128]{2,1,0:T(8,128)(2,1)S(1)} %get-tuple-element.173), channel_id=1, source_target_pairs={{1,5},{3,7},{4,8},{5,1},{6,10},{7,3},{8,4},{9,13},{10,6},{11,15},{... | collective-permute-start | bytes 442376 | tf_op jit(solution)/shard_map/ppermute | solution.py:349
  44.6 10.6 %collective-permute-start.11 = (bf16[18,32,128]{2,1,0:T(8,128)(2,1)S(1)}, bf16[18,32,128]{2,1,0:T(8,128)(2,1)S(1)}, u32[]{:S(2)}, u32[]{:S(2)}) collective-permute-start(bf16[18,32,128]{2,1,0:T(8,128)(2,1)S(1)} %get-tuple-element.167), channel_id=1, source_target_pairs={{0,4},{2,6},{4,0},{5,9},{6,2},{7,11},{8,12},{9,5},{10,14},{11,7},{... | collective-permute-start | bytes 442376 | tf_op jit(solution)/shard_map/ppermute | solution.py:349
  52.8 8.0 %collective-permute-start.14 = (bf16[18,32,128]{2,1,0:T(8,128)(2,1)S(1)}, bf16[18,32,128]{2,1,0:T(8,128)(2,1)S(1)}, u32[]{:S(2)}, u32[]{:S(2)}) collective-permute-start(bf16[18,32,128]{2,1,0:T(8,128)(2,1)S(1)} %get-tuple-element.187), channel_id=1, source_target_pairs={{1,5},{3,7},{4,8},{5,1},{6,10},{7,3},{8,4},{9,13},{10,6},{11,15},{... | collective-permute-start | bytes 442376 | tf_op jit(solution)/shard_map/ppermute | solution.py:349
  56.3 7.5 %collective-permute-start.13 = (bf16[18,32,128]{2,1,0:T(8,128)(2,1)S(1)}, bf16[18,32,128]{2,1,0:T(8,128)(2,1)S(1)}, u32[]{:S(2)}, u32[]{:S(2)}) collective-permute-start(bf16[18,32,128]{2,1,0:T(8,128)(2,1)S(1)} %get-tuple-element.181), channel_id=1, source_target_pairs={{0,4},{2,6},{4,0},{5,9},{6,2},{7,11},{8,12},{9,5},{10,14},{11,7},{... | collective-permute-start | bytes 442376 | tf_op jit(solution)/shard_map/ppermute | solution.py:349
  61.8 7.1 %collective-permute-start.16 = (bf16[18,32,128]{2,1,0:T(8,128)(2,1)S(1)}, bf16[18,32,128]{2,1,0:T(8,128)(2,1)S(1)}, u32[]{:S(2)}, u32[]{:S(2)}) collective-permute-start(bf16[18,32,128]{2,1,0:T(8,128)(2,1)S(1)} %get-tuple-element.201), channel_id=1, source_target_pairs={{1,5},{3,7},{4,8},{5,1},{6,10},{7,3},{8,4},{9,13},{10,6},{11,15},{... | collective-permute-start | bytes 442376 | tf_op jit(solution)/shard_map/ppermute | solution.py:349
  64.8 7.0 %collective-permute-start.15 = (bf16[18,32,128]{2,1,0:T(8,128)(2,1)S(1)}, bf16[18,32,128]{2,1,0:T(8,128)(2,1)S(1)}, u32[]{:S(2)}, u32[]{:S(2)}) collective-permute-start(bf16[18,32,128]{2,1,0:T(8,128)(2,1)S(1)} %get-tuple-element.195), channel_id=1, source_target_pairs={{0,4},{2,6},{4,0},{5,9},{6,2},{7,11},{8,12},{9,5},{10,14},{11,7},{... | collective-permute-start | bytes 442376 | tf_op jit(solution)/shard_map/ppermute | solution.py:349
  70.0 7.2 %collective-permute-start.18 = (bf16[18,32,128]{2,1,0:T(8,128)(2,1)S(1)}, bf16[18,32,128]{2,1,0:T(8,128)(2,1)S(1)}, u32[]{:S(2)}, u32[]{:S(2)}) collective-permute-start(bf16[18,32,128]{2,1,0:T(8,128)(2,1)S(1)} %get-tuple-element.215), channel_id=1, source_target_pairs={{1,5},{3,7},{4,8},{5,1},{6,10},{7,3},{8,4},{9,13},{10,6},{11,15},{... | collective-permute-start | bytes 442376 | tf_op jit(solution)/shard_map/ppermute | solution.py:349
  72.9 7.0 %collective-permute-start.17 = (bf16[18,32,128]{2,1,0:T(8,128)(2,1)S(1)}, bf16[18,32,128]{2,1,0:T(8,128)(2,1)S(1)}, u32[]{:S(2)}, u32[]{:S(2)}) collective-permute-start(bf16[18,32,128]{2,1,0:T(8,128)(2,1)S(1)} %get-tuple-element.209), channel_id=1, source_target_pairs={{0,4},{2,6},{4,0},{5,9},{6,2},{7,11},{8,12},{9,5},{10,14},{11,7},{... | collective-permute-start | bytes 442376 | tf_op jit(solution)/shard_map/ppermute | solution.py:349
  78.3 7.4 %collective-permute-start.20 = (bf16[18,32,128]{2,1,0:T(8,128)(2,1)S(1)}, bf16[18,32,128]{2,1,0:T(8,128)(2,1)S(1)}, u32[]{:S(2)}, u32[]{:S(2)}) collective-permute-start(bf16[18,32,128]{2,1,0:T(8,128)(2,1)S(1)} %get-tuple-element.229), channel_id=1, source_target_pairs={{1,5},{3,7},{4,8},{5,1},{6,10},{7,3},{8,4},{9,13},{10,6},{11,15},{... | collective-permute-start | bytes 442376 | tf_op jit(solution)/shard_map/ppermute | solution.py:349
  81.0 7.1 %collective-permute-start.19 = (bf16[18,32,128]{2,1,0:T(8,128)(2,1)S(1)}, bf16[18,32,128]{2,1,0:T(8,128)(2,1)S(1)}, u32[]{:S(2)}, u32[]{:S(2)}) collective-permute-start(bf16[18,32,128]{2,1,0:T(8,128)(2,1)S(1)} %get-tuple-element.223), channel_id=1, source_target_pairs={{0,4},{2,6},{4,0},{5,9},{6,2},{7,11},{8,12},{9,5},{10,14},{11,7},{... | collective-permute-start | bytes 442376 | tf_op jit(solution)/shard_map/ppermute | solution.py:349
  89.9 21.2 %collective-permute-start.26 = (f32[8,6,8,8,128]{4,3,2,1,0:T(8,128)S(1)}, f32[8,6,8,8,128]{4,3,2,1,0:T(8,128)S(1)}, u32[]{:S(2)}, u32[]{:S(2)}) collective-permute-start(f32[8,6,8,8,128]{4,3,2,1,0:T(8,128)S(1)} %multiply_add_fusion.refs_32_), channel_id=1, source_target_pairs={{0,1},{1,0},{2,3},{3,2},{4,5},{5,4},{6,7},{7,6},{8,9},{9,8},{10,11... | collective-permute-start | bytes 4718600 | tf_op jit(solution)/shard_map/ppermute | solution.py:333
  89.9 21.2 %collective-permute-start.27 = (f32[8,6,8,8,128]{4,3,2,1,0:T(8,128)S(1)}, f32[8,6,8,8,128]{4,3,2,1,0:T(8,128)S(1)}, u32[]{:S(2)}, u32[]{:S(2)}) collective-permute-start(f32[8,6,8,8,128]{4,3,2,1,0:T(8,128)S(1)} %collective-permute-done.22.refs_34_), channel_id=1, source_target_pairs={{0,1},{1,0},{2,3},{3,2},{4,5},{5,4},{6,7},{7,6},{8,9},{9,8},{10,11... | collective-permute-start | bytes 4718600 | tf_op jit(solution)/shard_map/ppermute | solution.py:333
  90.4 6.6 %collective-permute-start.23 = (bf16[18,32,128]{2,1,0:T(8,128)(2,1)S(1)}, bf16[18,32,128]{2,1,0:T(8,128)(2,1)S(1)}, u32[]{:S(2)}, u32[]{:S(2)}) collective-permute-start(bf16[18,32,128]{2,1,0:T(8,128)(2,1)S(1)} %get-tuple-element.247), channel_id=1, source_target_pairs={{1,5},{3,7},{4,8},{5,1},{6,10},{7,3},{8,4},{9,13},{10,6},{11,15},{... | collective-permute-start | bytes 442376 | tf_op jit(solution)/shard_map/ppermute | solution.py:349
  91.1 9.0 %collective-permute-start.21 = (bf16[18,32,128]{2,1,0:T(8,128)(2,1)S(1)}, bf16[18,32,128]{2,1,0:T(8,128)(2,1)S(1)}, u32[]{:S(2)}, u32[]{:S(2)}) collective-permute-start(bf16[18,32,128]{2,1,0:T(8,128)(2,1)S(1)} %get-tuple-element.237), channel_id=1, source_target_pairs={{0,4},{2,6},{4,0},{5,9},{6,2},{7,11},{8,12},{9,5},{10,14},{11,7},{... | collective-permute-start | bytes 442376 | tf_op jit(solution)/shard_map/ppermute | solution.py:349
  98.5 9.5 %collective-permute-start.25 = (bf16[18,32,128]{2,1,0:T(8,128)(2,1)S(1)}, bf16[18,32,128]{2,1,0:T(8,128)(2,1)S(1)}, u32[]{:S(2)}, u32[]{:S(2)}) collective-permute-start(bf16[18,32,128]{2,1,0:T(8,128)(2,1)S(1)} %get-tuple-element.257), channel_id=1, source_target_pairs={{1,5},{3,7},{4,8},{5,1},{6,10},{7,3},{8,4},{9,13},{10,6},{11,15},{... | collective-permute-start | bytes 442376 | tf_op jit(solution)/shard_map/ppermute | solution.py:349
  101.6 8.7 %collective-permute-start.24 = (bf16[18,32,128]{2,1,0:T(8,128)(2,1)S(1)}, bf16[18,32,128]{2,1,0:T(8,128)(2,1)S(1)}, u32[]{:S(2)}, u32[]{:S(2)}) collective-permute-start(bf16[18,32,128]{2,1,0:T(8,128)(2,1)S(1)} %get-tuple-element.255), channel_id=1, source_target_pairs={{0,4},{2,6},{4,0},{5,9},{6,2},{7,11},{8,12},{9,5},{10,14},{11,7},{... | collective-permute-start | bytes 442376 | tf_op jit(solution)/shard_map/ppermute | solution.py:349
  113.1 1.4 %collective-permute-start.28 = (f32[2,2,8,8,128]{4,3,2,1,0:T(8,128)S(1)}, f32[2,2,8,8,128]{4,3,2,1,0:T(8,128)S(1)}, u32[]{:S(2)}, u32[]{:S(2)}) collective-permute-start(f32[2,2,8,8,128]{4,3,2,1,0:T(8,128)S(1)} %pad_maximum_fusion.4), channel_id=1, source_target_pairs={{0,1},{1,0},{2,3},{3,2},{4,5},{5,4},{6,7},{7,6},{8,9},{9,8},{10,11... | collective-permute-start | bytes 393224 | tf_op jit(solution)/shard_map/ppermute | solution.py:333
  114.5 4.0 %collective-permute-start.30 = (f32[2,4,8,128]{3,2,1,0:T(8,128)S(1)}, f32[2,4,8,128]{3,2,1,0:T(8,128)S(1)}, u32[]{:S(2)}, u32[]{:S(2)}) collective-permute-start(f32[2,4,8,128]{3,2,1,0:T(8,128)S(1)} %dynamic-slice_bitcast_fusion.9), channel_id=1, source_target_pairs={{0,16},{1,17},{2,18},{3,19},{16,0},{17,1},{18,2},{19,3},{4,20},{5,... | collective-permute-start | bytes 98312 | tf_op jit(solution)/shard_map/ppermute | solution.py:479
  115.1 4.8 %collective-permute-start.29 = (f32[2,4,8,128]{3,2,1,0:T(8,128)S(1)}, f32[2,4,8,128]{3,2,1,0:T(8,128)S(1)}, u32[]{:S(2)}, u32[]{:S(2)}) collective-permute-start(f32[2,4,8,128]{3,2,1,0:T(8,128)S(1)} %get-tuple-element.275), channel_id=1, source_target_pairs={{0,18},{1,19},{2,16},{3,17},{16,2},{17,3},{18,0},{19,1},{4,22},{5,... | collective-permute-start | bytes 98312 | tf_op jit(solution)/shard_map/ppermute | solution.py:479
  117.7 3.9 %collective-permute-start.31 = (f32[2,4,8,128]{3,2,1,0:T(8,128)S(1)}, f32[2,4,8,128]{3,2,1,0:T(8,128)S(1)}, u32[]{:S(2)}, u32[]{:S(2)}) collective-permute-start(f32[2,4,8,128]{3,2,1,0:T(8,128)S(1)} %get-tuple-element.276), channel_id=1, source_target_pairs={{0,2},{1,3},{2,0},{3,1},{16,18},{17,19},{18,16},{19,17},{4,6},{5,7... | collective-permute-start | bytes 98312 | tf_op jit(solution)/shard_map/ppermute | solution.py:479

commit v4 on v3

--- a/solution.py
+++ b/solution.py
@@ -17,7 +17,6 @@
 REACH = 2
 DEEP = 2 * REACH
 ALONG_X = (0, 3, 4)
-ME, FLIP, HAS_HIGH, HAS_LOW, SPOT_X, SPOT_Y = range(6)
 NEAR_ROWS = 2
 PACKED = DEEP + NEAR_ROWS
 
@@ -93,71 +92,61 @@
 MIRRORED_STRESS = (3, 4)
 
 
-def sign_of(place):
-    return 1.0 - 2.0 * place[FLIP].astype(F32)
-
-
-def row_of(place, side, out, tile_x):
+def position():
+    slab, me = lax.axis_index("gx"), lax.axis_index("gy")
+    return slab, me, (slab + me) % 2
+
+
+def sign_of(flip):
+    return 1.0 - 2.0 * flip.astype(F32)
+
+
+def row_of(flip, side, out, tile_x):
     x = tile_x // 2 - 1 - out if side else tile_x // 2 + out
-    return x + place[FLIP] * (tile_x - 1 - 2 * x)
-
-
-def interleave(place, tiles, comp, row, held):
+    return x + flip * (tile_x - 1 - 2 * x)
+
+
+def interleave(me, tiles, comp, row, held):
     tile_y = tiles[0].shape[2]
     for turn, tile in enumerate(tiles):
-        held[pl.ds(pl.multiple_of((place[ME] ^ turn) * tile_y, tile_y), tile_y), :] = tile[comp, row]
+        held[pl.ds(pl.multiple_of((me ^ turn) * tile_y, tile_y), tile_y), :] = tile[comp, row]
     count = held.shape[0] // SUBLANES
     return jnp.concatenate([held[pl.ds(p, SUBLANES, stride=count), :] for p in range(count)], 0)
 
 
-def assemble_stress(place, *refs):
-    count = len(refs) - 9
-    tiles, sides, held = refs[:count], (refs[count : count + 4], refs[count + 4 : -1]), refs[-1]
+def assemble(*refs):
+    count = len(refs) - 11
+    tiles, sides, held = refs[:count], (refs[count : count + 5], refs[count + 5 : -1]), refs[-1]
     tile_x = tiles[0].shape[1]
-    sign = sign_of(place)
-    for side, (middle, edge, cells, face) in enumerate(sides):
+    _, me, flip = position()
+    sign = sign_of(flip)
+    face_comps = tuple(3 + comp for comp in ALONG_X) + (9,)
+    for side, (vel, middle, edge, cells, face) in enumerate(sides):
         for out in range(DEEP):
-            row = row_of(place, side, out, tile_x)
+            row = row_of(flip, side, out, tile_x)
             part, at = (middle, out) if out < REACH else (edge, out - REACH)
-            for comp in range(7):
-                value = interleave(place, tiles, comp, row, held.at[(out * 7 + comp) % held.shape[0]])
-                if comp in MIRRORED_STRESS:
+            for comp in range(10):
+                value = interleave(me, tiles, comp, row, held.at[(out * 10 + comp) % held.shape[0]])
+                if comp in MIRRORED_VEL or comp - 3 in MIRRORED_STRESS:
                     value = sign * value
-                if comp < 6:
-                    part[comp, at] = value
+                if comp < 3:
+                    vel[comp, out] = value
+                elif comp < 9:
+                    part[comp - 3, at] = value
                 else:
                     cells[out] = value
-                if out >= REACH and comp in ALONG_X + (6,):
-                    face[(ALONG_X + (6,)).index(comp), out - REACH] = value
-
-
-def assemble_vel(place, *refs):
-    count = len(refs) - 3
-    tiles, vels, held = refs[:count], refs[count:-1], refs[-1]
-    tile_x = tiles[0].shape[1]
-    sign = sign_of(place)
-    for side, vel in enumerate(vels):
-        for out in range(DEEP):
-            row = row_of(place, side, out, tile_x)
-            for comp in range(3):
-                value = interleave(place, tiles, comp, row, held.at[(out * 3 + comp) % held.shape[0]])
-                vel[comp, out] = sign * value if comp in MIRRORED_VEL else value
-
-
-def push(place, side, amount, stress_row, vel, light, vel_out, sent):
-    shape = vel.shape[2:]
-    spot = (lax.broadcasted_iota(jnp.int32, shape, 0) == place[SPOT_Y]) & (
-        lax.broadcasted_iota(jnp.int32, shape, 1) == 0
-    )
-    spot = jnp.where(spot, UNIT * amount, 0.0)
+                if out >= REACH and comp in face_comps:
+                    face[face_comps.index(comp), out - REACH] = value
+
+
+def push(side, spots, amount, stress_row, vel, light, vel_out, sent):
     rows = [functools.partial(stress_row, comp) for comp in range(6)]
     deep = along_depth([rows[comp](out) for out in range(DEEP) for comp in (4, 5, 2)])
     for out in range(DEEP):
         force_x = across_and_along(rows[0], out, side, rows[3](out)) + deep[3 * out]
         force_y = across_and_along(rows[3], out, side, rows[1](out)) + deep[3 * out + 1]
         force_z = across_and_along(rows[4], out, side, rows[5](out)) + deep[3 * out + 2]
-        here = place[SPOT_X] == (-1 - out if side else out)
-        force_z = force_z + jnp.where(here, 1.0, 0.0) * spot
+        force_z = force_z + amount * spots[out]
         near = DEEP - 1 - out
         for comp, force in enumerate((force_x, force_y, force_z)):
             fresh = vel[comp, out] + light[out] * force
@@ -179,15 +168,31 @@
     return halo[comp * PACKED + NEAR_ROWS + near].astype(F32)
 
 
-def first(side, place, table, residual, vel, middle, other, edge, cells, halo, *outs):
-    vel_out, sent, light, lame, shear, halo_out = outs
+def first(side, table, residual, rec_cell, vel, middle, other, edge, cells, halo, *outs):
+    vel_out, sent, light, lame, shear, halo_out, spots, amounts = outs
+    size_y, depth = vel.shape[2:]
+    planes = size_y // SUBLANES
+    slab, me, flip = position()
+    cell = rec_cell[0, me]
+    spot_x, spot_y = cell // size_y - slab * (2 * DEEP), cell % size_y
+    spot_x = spot_x + flip * (2 * DEEP - 1 - 2 * spot_x)
+    spot_y = (spot_y % planes) * SUBLANES + spot_y // planes
+    at_spot = (lax.broadcasted_iota(jnp.int32, (size_y, depth), 0) == spot_y) & (
+        lax.broadcasted_iota(jnp.int32, (size_y, depth), 1) == 0
+    )
+    for out in range(DEEP):
+        here = spot_x == (DEEP - 1 - out if side else DEEP + out)
+        spots[out] = jnp.where(at_spot, jnp.where(here, UNIT * AMPLITUDE, 0.0), 0.0)
+    for moment in range(residual.shape[2]):
+        amounts[moment] = jnp.full((size_y, depth), residual[0, me, moment], F32)
+    _, inside = partner(slab, me, lax.axis_size("gx"), side)
     count = table.shape[0]
     for out in range(DEEP + REACH):
         if out < DEEP:
             number, share = cells[out], 1.0
         else:
             number = halo[len(ALONG_X), REACH - 1 - (out - DEEP)]
-            share = jnp.where(place[HAS_LOW if side else HAS_HIGH] > 0, 1.0, 0.0)
+            share = jnp.where(inside, 1.0, 0.0)
         parts = [jnp.full(number.shape, table[0, c], F32) for c in range(3)]
         for m in range(1, count):
             hit = number == float(m)
@@ -200,8 +205,7 @@
         for near in range(REACH):
             value = halo[at, REACH - 1 - near]
             halo_out[at, near] = -value if ALONG_X[at] in MIRRORED_STRESS else value
-    amount = AMPLITUDE * residual[place[ME], 0]
-    push(place, side, amount, stress_rows(middle, other, edge, halo_out), vel, light, vel_out, sent)
+    push(side, spots, amounts[0], stress_rows(middle, other, edge, halo_out), vel, light, vel_out, sent)
 
 
 def stress_rows(middle, other, edge, halo):
@@ -252,11 +256,11 @@
     }
 
 
-def outer(side, moment, last, place, residual, vel, halo, edge, *refs):
+def outer(side, moment, last, vel, halo, edge, *refs):
     if last:
         (rates_out,) = refs
     else:
-        old_halo, middle, other, light, lame, shear, rates_out, edge_out, halo_out, vel_out, sent = refs
+        old_halo, middle, other, light, lame, shear, spots, amounts, rates_out, edge_out, halo_out, vel_out, sent = refs
 
     def rows(comp):
         return lambda out: vel[comp, out] if out < DEEP else from_halo(halo, comp, out - DEEP)
@@ -278,11 +282,11 @@
             for at, comp in enumerate(ALONG_X):
                 halo_out[at, out - DEEP] = fresh[comp]
     if not last:
-        amount = AMPLITUDE * residual[place[ME], moment + 1]
-        push(place, side, amount, stress_rows(middle, other, edge_out, halo_out), vel, light, vel_out, sent)
-
-
-def inner(last, place, *refs):
+        rows = stress_rows(middle, other, edge_out, halo_out)
+        push(side, spots, amounts[moment + 1], rows, vel, light, vel_out, sent)
+
+
+def inner(last, *refs):
     vels = refs[:2]
     if last:
         rates_out = refs[2:]
@@ -303,27 +307,29 @@
                     middles_out[side][comp, out] = value
 
 
-def correlate(moments, pieces, place, residual, *refs):
-    rates, sources, terms = refs[: 4 * moments], refs[4 * moments : 4 * moments + pieces], refs[-1]
+def correlate(moments, pieces, residual, *refs):
+    count = len(moments)
+    rates, sources, rest = refs[: 4 * count], refs[4 * count : 4 * count + pieces], refs[4 * count + pieces :]
+    before, terms = rest[:-1], rest[-1]
     tile_x, tile_y = sources[0].shape[2:4]
-    sign = sign_of(place)
+    _, me, flip = position()
+    sign = sign_of(flip)
     for turn in range(pieces):
-        spot = pl.ds(pl.multiple_of((place[ME] ^ turn) * tile_y, tile_y), tile_y)
+        spot = pl.ds(pl.multiple_of((me ^ turn) * tile_y, tile_y), tile_y)
         for side in range(2):
             for out in range(DEEP):
-                row = row_of(place, side, out, tile_x)
-                lam = mu = None
-                for moment in range(moments):
-                    weight = (KERNEL_SCALE / UNIT) * residual[place[ME], moment]
-                    held = rates[4 * moment + 2 * (out // REACH) + side]
+                row = row_of(flip, side, out, tile_x)
+                lam, mu = (before[0][turn, 0, row], before[0][turn, 1, row]) if before else (0.0, 0.0)
+                for at, moment in enumerate(moments):
+                    weight = (KERNEL_SCALE / UNIT) * residual[0, me, moment]
+                    held = rates[4 * at + 2 * (out // REACH) + side]
                     rate = [held[c, out % REACH, spot, :] for c in range(6)]
                     source = [sources[turn][moment, c, row] for c in range(6)]
                     bulk = (source[0] + source[1] + source[2]) * (rate[0] + rate[1] + rate[2])
                     diag = source[0] * rate[0] + source[1] * rate[1] + source[2] * rate[2]
                     off = sign * (source[3] * rate[3] + source[4] * rate[4]) + source[5] * rate[5]
-                    bulk, both = weight * bulk, (2.0 * weight) * (diag + off)
-                    lam = bulk if lam is None else lam + bulk
-                    mu = both if mu is None else mu + both
+                    lam = lam + weight * bulk
+                    mu = mu + (2.0 * weight) * (diag + off)
                 terms[turn, 0, row] = lam
                 terms[turn, 1, row] = mu
 
@@ -349,6 +355,10 @@
     return lax.ppermute(face, ("gx", "gy"), pairs)
 
 
+def sources_first(pieces):
+    return sorted((turn for turn in range(1, pieces) if turn & (turn - 1) == 0), reverse=True)
+
+
 def local(rec_state, source_strain, material, material_table, residual, rec_cell, listed, src_pick):
     state = rec_state[0]
     receivers, _, tile_x, tile_y, depth = state.shape
@@ -356,27 +366,16 @@
     assert receivers == pieces and tile_x == 2 * DEEP
     assert pieces & (pieces - 1) == 0 and groups & (groups - 1) == 0
     size_y = pieces * tile_y
-    group, slab, me = lax.axis_index("sta"), lax.axis_index("gx"), lax.axis_index("gy")
+    group, me = lax.axis_index("sta"), lax.axis_index("gy")
     moments = residual.shape[2]
 
     numbers = material.astype(F32)[None]
-    picked = [lax.dynamic_index_in_dim(state, me ^ turn, 0, keepdims=False) for turn in range(pieces)]
     order = sorted(range(pieces), reverse=True)
-    stresses = {turn: jnp.concatenate([picked[turn][3:], numbers], 0) for turn in order}
-    stresses = {turn: swap(stresses[turn], "gy", turn) if turn else stresses[turn] for turn in order}
-    speeds = {turn: swap(picked[turn][:3], "gy", turn) if turn else picked[turn][:3] for turn in order}
-    strains = [swap(source_strain[0], "sta", turn) if turn else source_strain[0] for turn in range(groups)]
-
-    cell = lax.dynamic_index_in_dim(rec_cell[0], me, 0, keepdims=False)
-    flip = (slab + me) % 2
-    spot_x = cell // size_y - slab * tile_x
-    spot_x = spot_x + flip * (tile_x - 1 - 2 * spot_x) - tile_x // 2
-    inside = [partner(slab, me, slabs, side)[1] for side in range(2)]
-    planes = size_y // SUBLANES
-    spot_y = cell % size_y
-    spot_y = (spot_y % planes) * SUBLANES + spot_y // planes
-    place = jnp.stack([me, flip, *inside, spot_x, spot_y]).astype(jnp.int32)
-    rows = residual[0]
+    picked = {turn: lax.dynamic_index_in_dim(state, me ^ turn, 0, keepdims=False) for turn in order}
+    own, picked = lax.optimization_barrier((source_strain[0], picked))
+    chunks = {turn: jnp.concatenate([picked[turn], numbers], 0) for turn in order}
+    chunks = [swap(chunks[turn], "gy", turn) if turn else chunks[turn] for turn in range(pieces)]
+    strains = [swap(own, "sta", turn) if turn else own for turn in range(groups)]
 
     def shape(*lead, kind=F32):
         return lead + (size_y, depth), kind
@@ -384,44 +383,38 @@
     vel_shape, pair_shape = shape(3, DEEP), shape(6, REACH)
     halo_shape, sent_shape = shape(3, REACH), shape(3 * PACKED, kind=BF16)
 
-    held = [pltpu.VMEM((8, size_y, depth), F32)]
     results = call(
-        assemble_stress,
-        [pair_shape, pair_shape, shape(DEEP), shape(4, REACH)] * 2,
-        ([place], [stresses[turn] for turn in range(pieces)]),
-        held,
+        assemble,
+        [vel_shape, pair_shape, pair_shape, shape(DEEP), shape(4, REACH)] * 2,
+        ([], chunks),
+        [pltpu.VMEM((8, size_y, depth), F32)],
     )
-    middles, edges, cells, faces = ([results[at], results[4 + at]] for at in range(4))
+    vels, middles, edges, cells, faces = ([results[at], results[5 + at]] for at in range(5))
     halos = [to_neighbour(faces[side], side) for side in range(2)]
-    vels = call(
-        assemble_vel, [vel_shape] * 2, ([place], [speeds[turn] for turn in range(pieces)]), held
-    )
-
-    sent, lights, lames, shears, old_halos = ([None, None] for _ in range(5))
-    fresh = [None, None]
-    for side in range(2):
-        fresh[side], sent[side], lights[side], lames[side], shears[side], old_halos[side] = call(
-            functools.partial(first, side),
-            [vel_shape, sent_shape, shape(DEEP), shape(DEEP + REACH), shape(DEEP + REACH), halo_shape],
-            (
-                [place, material_table, rows],
-                [vels[side], middles[side], middles[1 - side], edges[side], cells[side], halos[side]],
-            ),
-        )
-        sent[side] = to_neighbour(sent[side], side)
-    vels = fresh
-
-    strains, vels = lax.optimization_barrier((strains, vels))
+
+    strains, cells = lax.optimization_barrier((strains, cells))
     weights = lax.dynamic_slice_in_dim(listed, group, 1, 2)[:, :, 0].astype(F32)
     combined = 0.0
     for turn in range(groups):
         factor = jnp.sum(weights * (src_pick == (group ^ turn)).astype(F32), 0)
         combined = combined + factor[:, None, None, None, None] * strains[turn].astype(F32)
-    width = pieces // 2
-    found = {0: combined}
-    if width:
-        found[width] = swap(combined, "gy", width)
-        width //= 2
+
+    sent, lights, lames, shears, old_halos, spots, amounts = ([None, None] for _ in range(7))
+    fresh = [None, None]
+    for side in range(2):
+        results = call(
+            functools.partial(first, side),
+            [vel_shape, sent_shape, shape(DEEP), shape(DEEP + REACH), shape(DEEP + REACH), halo_shape]
+            + [shape(DEEP), shape(moments)],
+            (
+                [material_table, residual, rec_cell],
+                [vels[side], middles[side], middles[1 - side], edges[side], cells[side], halos[side]],
+            ),
+        )
+        fresh[side], sent[side], lights[side], lames[side], shears[side], old_halos[side] = results[:6]
+        spots[side], amounts[side] = results[6:]
+        sent[side] = to_neighbour(sent[side], side)
+    vels = fresh
 
     rates = []
     for moment in range(moments):
@@ -429,36 +422,47 @@
         results = call(
             functools.partial(inner, last),
             [pair_shape] * (2 if last else 4),
-            ([place], vels if last else vels + middles + lames + shears),
+            ([], vels if last else vels + middles + lames + shears),
         )
         rates += results[:2]
         if not last:
             middles = results[2:]
-        if moment == 3 * moments // 4:
+        if moment == 5 * moments // 8:
             found, middles = lax.optimization_barrier((found, middles))
-            while width:
-                for turn in list(found):
-                    found[turn ^ width] = swap(found[turn], "gy", width)
-                width //= 2
+            for turn in range(pieces):
+                if turn not in found:
+                    low = turn & -turn
+                    found[turn] = swap(found[turn ^ low], "gy", low)
+        if last:
+            (terms,) = call(
+                functools.partial(correlate, list(range(moment)), pieces),
+                [((pieces, 2, tile_x, tile_y, depth), F32)],
+                ([residual], rates[: 4 * moment] + [found[turn] for turn in range(pieces)]),
+            )
+            terms, vels = lax.optimization_barrier((terms, vels))
         fresh = [None, None]
         for side in range(2):
             arrays = [vels[side], sent[side], edges[side]]
             outs = [pair_shape]
             if not last:
                 arrays += [old_halos[side], middles[side], middles[1 - side]]
-                arrays += [lights[side], lames[side], shears[side]]
+                arrays += [lights[side], lames[side], shears[side], spots[side], amounts[side]]
                 outs += [pair_shape, halo_shape, vel_shape, sent_shape]
-            results = call(functools.partial(outer, side, moment, last), outs, ([place, rows], arrays))
+            results = call(functools.partial(outer, side, moment, last), outs, ([], arrays))
             rates.append(results[0])
             if not last:
                 edges[side], old_halos[side], fresh[side] = results[1:4]
                 sent[side] = to_neighbour(results[4], side)
+        if moment == 0:
+            combined, rates[-1] = lax.optimization_barrier((combined, rates[-1]))
+            found = {turn: swap(combined, "gy", turn) for turn in sources_first(pieces)}
+            found[0] = combined
         vels = fresh
 
     (terms,) = call(
-        functools.partial(correlate, moments, pieces),
+        functools.partial(correlate, [moments - 1], pieces),
         [((pieces, 2, tile_x, tile_y, depth), F32)],
-        ([place, rows], rates + [found[turn] for turn in range(pieces)]),
+        ([residual], rates[-4:] + [found[turn] for turn in range(pieces)] + [terms]),
     )
     held = {turn: terms[turn] for turn in range(pieces)}
     if pieces > 1:

time: 123 us -> 117 us (0.951)
  waiting for transfers between devices: 19 us -> 34 us
  Pallas kernels: 29.3 us -> 15.1 us
  between operations: 3.35 us -> 0.57 us
  starting transfers between devices: 65.1 us -> 62.6 us
  local copies, waits for them, and re-layouts: 3.22 us -> 1.46 us
    pallas_call x29, Pallas kernels: 29.3 us -> 15.1 us  [call(): pl.pallas_call(body, out_shape=[jax.ShapeDtypeStruct(shape, kind) for sha...]
    ppermute x11 -> x8, waiting for transfers between devices: 5.9 us -> 16.2 us  [swap(): return lax.ppermute(array, axis, [(i, i ^ turn) for i in range(count)])]
    ppermute x18, waiting for transfers between devices: 9.59 us -> 15.5 us  [to_neighbour(): return lax.ppermute(face, ('gx', 'gy'), pairs)]
    ppermute x11 -> x8, starting transfers between devices: 12.3 us -> 9.32 us  [swap(): return lax.ppermute(array, axis, [(i, i ^ turn) for i in range(count)])]
    slice x2 -> x0, local copies, waits for them, and re-layouts: 2.33 us -> none  [the longest x1 1.27 us: local(): picked[turn][3:]]
    squeeze x0 -> x1, local copies, waits for them, and re-layouts: none -> 1.31 us  [local(): lax.dynamic_index_in_dim(state, me ^ turn, 0, keepdims=False)]
  transfers between devices with their start and end apart: 32 -> 29, of which waited for: 15 -> 13; matrix products, arithmetic and copies ran while one was open for 3% -> 2% of each run, Pallas kernels for 22% -> 12%
where the time goes in v4:
time: 117 us; the launch traced here: 116 us
  starting transfers between devices  62.6 us (54%)
  waiting for transfers between devices  34 us (29%)
  Pallas kernels  15.1 us (13%)
  other arithmetic  2.56 us (2%)
  local copies, waits for them, and re-layouts  1.46 us (1%)
    ppermute x18, starting transfers between devices, to_neighbour(): return lax.ppermute(face, ('gx', 'gy'), pairs)  49.7 us
    ppermute x8, waiting for transfers between devices, swap(): return lax.ppermute(array, axis, [(i, i ^ turn) for i in range(count)])  16.2 us
    ppermute x18, waiting for transfers between devices, to_neighbour(): return lax.ppermute(face, ('gx', 'gy'), pairs)  15.5 us
    pallas_call x29, Pallas kernels, call(): pl.pallas_call(body, out_shape=[jax.ShapeDtypeStruct(shape, kind) for sha...  15.1 us
    ppermute x8, starting transfers between devices, swap(): return lax.ppermute(array, axis, [(i, i ^ turn) for i in range(count)])  9.32 us
    ppermute x3, starting transfers between devices, local(): part = lax.ppermute(part, ('sta', 'gy'), pairs)  3.55 us
    ppermute x3, waiting for transfers between devices, local(): part = lax.ppermute(part, ('sta', 'gy'), pairs)  2.4 us
  transfers between devices with their start and end apart: 29, of which 13 were waited for; matrix products, arithmetic and copies ran while one was open for 2% of the time, Pallas kernels for 12%

profile of v4, /device:TPU:0, one launch (start us, length us, event | category | flops | bytes accessed | tf_op | source)
XLA Modules:
  0.0 116.4 jit_solution(12990828014425372045)
XLA Ops:
  0.0 1.3 %dynamic-slice_bitcast_fusion = (f32[9,8,8,128]{3,2,1,0:T(8,128)S(1)}, f32[9,8,8,128]{3,2,1,0:T(8,128)S(1)}, f32[9,8,8,128]{3,2,1,0:T(8,128)S(1)}, f32[9,8,8,128]{3,2,1,0:T(8,128)S(1)}) fusion(f32[1,4,9,8,8,128]{5,4,3,2,1,0:T(8,128)} %param.8, s32[]{:T(128)S(6)} %select_n.27, s32[]{:T(128)S(6)} %select_n.25, s32[]{:T(128)S(6)} %select_n.24, s32[]{:T(128)S(6)} %select_n.26), kind=kLoop, calls=%fused_computation.5 | loop fusion | bytes 2359312 | tf_op jit(solution)/shard_map/jit(dynamic_index_in_dim)/squeeze | solution.py:374
  1.3 3.0 %collective-permute-start.3 = (bf16[8,6,8,8,128]{4,3,2,1,0:T(8,128)(2,1)}, bf16[8,6,8,8,128]{4,3,2,1,0:T(8,128)(2,1)}, u32[]{:S(2)}, u32[]{:S(2)}) collective-permute-start(bf16[8,6,8,8,128]{4,3,2,1,0:T(8,128)(2,1)} %bitcast), channel_id=1, source_target_pairs={{0,16},{16,0},{1,17},{17,1},{2,18},{18,2},{3,19},{19,3},{4,20},{20... | collective-permute-start | bytes 2359304 | tf_op jit(solution)/shard_map/ppermute | solution.py:339
  4.6 1.6 %collective-permute-start.1 = (f32[10,8,8,128]{3,2,1,0:T(8,128)S(1)}, f32[10,8,8,128]{3,2,1,0:T(8,128)S(1)}, u32[]{:S(2)}, u32[]{:S(2)}) collective-permute-start(f32[10,8,8,128]{3,2,1,0:T(8,128)S(1)} %get-tuple-element.305), channel_id=1, source_target_pairs={{0,2},{1,3},{2,0},{3,1},{4,6},{5,7},{6,4},{7,5},{8,10},{9,11},{10,... | collective-permute-start | bytes 983048 | tf_op jit(solution)/shard_map/ppermute | solution.py:339
  6.5 8.7 %collective-permute-done.1.refs_2_ = f32[10,8,8,128]{3,2,1,0:T(8,128)S(1)} collective-permute-done((f32[10,8,8,128]{3,2,1,0:T(8,128)S(1)}, f32[10,8,8,128]{3,2,1,0:T(8,128)S(1)}, u32[]{:S(2)}, u32[]{:S(2)}) %collective-permute-start.1) | collective-permute-done | bytes 327712 | tf_op jit(solution)/shard_map/ppermute | solution.py:339
  15.2 6.1 %collective-permute-done.2.refs_3_ = f32[10,8,8,128]{3,2,1,0:T(8,128)S(1)} collective-permute-done((f32[10,8,8,128]{3,2,1,0:T(8,128)S(1)}, f32[10,8,8,128]{3,2,1,0:T(8,128)S(1)}, u32[]{:S(2)}, u32[]{:S(2)}) %collective-permute-start.2) | collective-permute-done | bytes 327712 | tf_op jit(solution)/shard_map/ppermute | solution.py:339
  21.3 0.7 shard_map.82
  22.0 0.7 collective-permute-start.6
  22.8 6.3 %collective-permute-start.4 = (f32[4,2,32,128]{3,2,1,0:T(8,128)S(1)}, f32[4,2,32,128]{3,2,1,0:T(8,128)S(1)}, u32[]{:S(2)}, u32[]{:S(2)}) collective-permute-start(f32[4,2,32,128]{3,2,1,0:T(8,128)S(1)} %get-tuple-element.160), channel_id=1, source_target_pairs={{0,4},{2,6},{4,0},{5,9},{6,2},{7,11},{8,12},{9,5},{10,14},{11,7},{... | collective-permute-start | bytes 393224 | tf_op jit(solution)/shard_map/ppermute | solution.py:355
  29.1 1.1 shard_map.84
  30.3 0.7 collective-permute-start.8
  31.0 1.7 %multiply_add_fusion.refs_28_.refs_4_ = f32[8,6,8,8,128]{4,3,2,1,0:T(8,128)S(1)} fusion(bf16[8,6,8,8,128]{4,3,2,1,0:T(8,128)(2,1)} %collective-permute-done.3, bf16[8,6,8,8,128]{4,3,2,1,0:T(8,128)(2,1)} %bitcast, f32[8]{0:T(128)S(1)} %get-tuple-element.292, f32[8]{0:T(128)S(1)} %get-tuple-element.291), kind=kLoop, calls=%fused_computation | loop fusion | flops 1966080 | bytes 3145792 | tf_op jit(solution)/shard_map/add | solution.py:400
  32.7 1.1 shard_map.83
  34.6 2.7 %collective-permute-start.16 = (f32[8,6,8,8,128]{4,3,2,1,0:T(8,128)S(1)}, f32[8,6,8,8,128]{4,3,2,1,0:T(8,128)S(1)}, u32[]{:S(2)}, u32[]{:S(2)}) collective-permute-start(f32[8,6,8,8,128]{4,3,2,1,0:T(8,128)S(1)} %multiply_add_fusion.refs_28_.refs_4_), channel_id=1, source_target_pairs={{0,1},{1,0},{2,3},{3,2},{4,5},{5,4},{6,7},{7,6},{8,9},{9,8},{10,11... | collective-permute-start | bytes 4718600 | tf_op jit(solution)/shard_map/ppermute | solution.py:339
  37.3 1.5 %collective-permute-start.17 = (f32[8,6,8,8,128]{4,3,2,1,0:T(8,128)S(1)}, f32[8,6,8,8,128]{4,3,2,1,0:T(8,128)S(1)}, u32[]{:S(2)}, u32[]{:S(2)}) collective-permute-start(f32[8,6,8,8,128]{4,3,2,1,0:T(8,128)S(1)} %multiply_add_fusion.refs_28_.refs_4_), channel_id=1, source_target_pairs={{0,2},{1,3},{2,0},{3,1},{4,6},{5,7},{6,4},{7,5},{8,10},{9,11},{10,... | collective-permute-start | bytes 4718600 | tf_op jit(solution)/shard_map/ppermute | solution.py:339
  38.8 3.8 %collective-permute-start.5 = (bf16[18,32,128]{2,1,0:T(8,128)(2,1)S(1)}, bf16[18,32,128]{2,1,0:T(8,128)(2,1)S(1)}, u32[]{:S(2)}, u32[]{:S(2)}) collective-permute-start(bf16[18,32,128]{2,1,0:T(8,128)(2,1)S(1)} %get-tuple-element.162), channel_id=1, source_target_pairs={{0,4},{2,6},{4,0},{5,9},{6,2},{7,11},{8,12},{9,5},{10,14},{11,7},{... | collective-permute-start | bytes 442376 | tf_op jit(solution)/shard_map/ppermute | solution.py:355
  42.6 0.7 collective-permute-start.10
  43.3 2.6 %collective-permute-done.5.halo = bf16[18,32,128]{2,1,0:T(8,128)(2,1)S(1)} collective-permute-done((bf16[18,32,128]{2,1,0:T(8,128)(2,1)S(1)}, bf16[18,32,128]{2,1,0:T(8,128)(2,1)S(1)}, u32[]{:S(2)}, u32[]{:S(2)}) %collective-permute-start.5) | collective-permute-done | bytes 147488 | tf_op jit(solution)/shard_map/ppermute | solution.py:355
  46.3 3.8 %collective-permute-start.7 = (bf16[18,32,128]{2,1,0:T(8,128)(2,1)S(1)}, bf16[18,32,128]{2,1,0:T(8,128)(2,1)S(1)}, u32[]{:S(2)}, u32[]{:S(2)}) collective-permute-start(bf16[18,32,128]{2,1,0:T(8,128)(2,1)S(1)} %get-tuple-element.179), channel_id=1, source_target_pairs={{0,4},{2,6},{4,0},{5,9},{6,2},{7,11},{8,12},{9,5},{10,14},{11,7},{... | collective-permute-start | bytes 442376 | tf_op jit(solution)/shard_map/ppermute | solution.py:355
  50.9 0.7 collective-permute-start.12
  51.5 1.8 %collective-permute-done.7.halo = bf16[18,32,128]{2,1,0:T(8,128)(2,1)S(1)} collective-permute-done((bf16[18,32,128]{2,1,0:T(8,128)(2,1)S(1)}, bf16[18,32,128]{2,1,0:T(8,128)(2,1)S(1)}, u32[]{:S(2)}, u32[]{:S(2)}) %collective-permute-start.7) | collective-permute-done | bytes 147488 | tf_op jit(solution)/shard_map/ppermute | solution.py:355
  53.8 3.8 %collective-permute-start.9 = (bf16[18,32,128]{2,1,0:T(8,128)(2,1)S(1)}, bf16[18,32,128]{2,1,0:T(8,128)(2,1)S(1)}, u32[]{:S(2)}, u32[]{:S(2)}) collective-permute-start(bf16[18,32,128]{2,1,0:T(8,128)(2,1)S(1)} %get-tuple-element.191), channel_id=1, source_target_pairs={{0,4},{2,6},{4,0},{5,9},{6,2},{7,11},{8,12},{9,5},{10,14},{11,7},{... | collective-permute-start | bytes 442376 | tf_op jit(solution)/shard_map/ppermute | solution.py:355
  58.4 0.7 collective-permute-start.14
  59.0 1.8 %collective-permute-done.9.halo = bf16[18,32,128]{2,1,0:T(8,128)(2,1)S(1)} collective-permute-done((bf16[18,32,128]{2,1,0:T(8,128)(2,1)S(1)}, bf16[18,32,128]{2,1,0:T(8,128)(2,1)S(1)}, u32[]{:S(2)}, u32[]{:S(2)}) %collective-permute-start.9) | collective-permute-done | bytes 147488 | tf_op jit(solution)/shard_map/ppermute | solution.py:355
  61.3 4.2 %collective-permute-start.11 = (bf16[18,32,128]{2,1,0:T(8,128)(2,1)S(1)}, bf16[18,32,128]{2,1,0:T(8,128)(2,1)S(1)}, u32[]{:S(2)}, u32[]{:S(2)}) collective-permute-start(bf16[18,32,128]{2,1,0:T(8,128)(2,1)S(1)} %get-tuple-element.201), channel_id=1, source_target_pairs={{0,4},{2,6},{4,0},{5,9},{6,2},{7,11},{8,12},{9,5},{10,14},{11,7},{... | collective-permute-start | bytes 442376 | tf_op jit(solution)/shard_map/ppermute | solution.py:355
  66.2 0.7 collective-permute-start.18
  66.9 2.7 %collective-permute-done.11.halo = bf16[18,32,128]{2,1,0:T(8,128)(2,1)S(1)} collective-permute-done((bf16[18,32,128]{2,1,0:T(8,128)(2,1)S(1)}, bf16[18,32,128]{2,1,0:T(8,128)(2,1)S(1)}, u32[]{:S(2)}, u32[]{:S(2)}) %collective-permute-start.11) | collective-permute-done | bytes 147488 | tf_op jit(solution)/shard_map/ppermute | solution.py:355
  70.1 4.5 %collective-permute-start.13 = (bf16[18,32,128]{2,1,0:T(8,128)(2,1)S(1)}, bf16[18,32,128]{2,1,0:T(8,128)(2,1)S(1)}, u32[]{:S(2)}, u32[]{:S(2)}) collective-permute-start(bf16[18,32,128]{2,1,0:T(8,128)(2,1)S(1)} %get-tuple-element.211), channel_id=1, source_target_pairs={{0,4},{2,6},{4,0},{5,9},{6,2},{7,11},{8,12},{9,5},{10,14},{11,7},{... | collective-permute-start | bytes 442376 | tf_op jit(solution)/shard_map/ppermute | solution.py:355
  75.3 2.4 %collective-permute-done.13.halo = bf16[18,32,128]{2,1,0:T(8,128)(2,1)S(1)} collective-permute-done((bf16[18,32,128]{2,1,0:T(8,128)(2,1)S(1)}, bf16[18,32,128]{2,1,0:T(8,128)(2,1)S(1)}, u32[]{:S(2)}, u32[]{:S(2)}) %collective-permute-start.13) | collective-permute-done | bytes 147488 | tf_op jit(solution)/shard_map/ppermute | solution.py:355
  78.5 0.7 collective-permute-start.20
  79.2 8.1 %collective-permute-start.15 = (bf16[18,32,128]{2,1,0:T(8,128)(2,1)S(1)}, bf16[18,32,128]{2,1,0:T(8,128)(2,1)S(1)}, u32[]{:S(2)}, u32[]{:S(2)}) collective-permute-start(bf16[18,32,128]{2,1,0:T(8,128)(2,1)S(1)} %get-tuple-element.221), channel_id=1, source_target_pairs={{0,4},{2,6},{4,0},{5,9},{6,2},{7,11},{8,12},{9,5},{10,14},{11,7},{... | collective-permute-start | bytes 442376 | tf_op jit(solution)/shard_map/ppermute | solution.py:355
  87.7 0.7 collective-permute-start.21
  88.4 1.9 %collective-permute-done.15.halo = bf16[18,32,128]{2,1,0:T(8,128)(2,1)S(1)} collective-permute-done((bf16[18,32,128]{2,1,0:T(8,128)(2,1)S(1)}, bf16[18,32,128]{2,1,0:T(8,128)(2,1)S(1)}, u32[]{:S(2)}, u32[]{:S(2)}) %collective-permute-start.15) | collective-permute-done | bytes 147488 | tf_op jit(solution)/shard_map/ppermute | solution.py:355
  90.8 4.4 %collective-permute-start.19 = (bf16[18,32,128]{2,1,0:T(8,128)(2,1)S(1)}, bf16[18,32,128]{2,1,0:T(8,128)(2,1)S(1)}, u32[]{:S(2)}, u32[]{:S(2)}) collective-permute-start(bf16[18,32,128]{2,1,0:T(8,128)(2,1)S(1)} %get-tuple-element.237), channel_id=1, source_target_pairs={{0,4},{2,6},{4,0},{5,9},{6,2},{7,11},{8,12},{9,5},{10,14},{11,7},{... | collective-permute-start | bytes 442376 | tf_op jit(solution)/shard_map/ppermute | solution.py:355
  95.5 1.0 shard_map.105
  96.5 0.7 collective-permute-start.24
  97.1 1.2 %collective-permute-done.19.halo = bf16[18,32,128]{2,1,0:T(8,128)(2,1)S(1)} collective-permute-done((bf16[18,32,128]{2,1,0:T(8,128)(2,1)S(1)}, bf16[18,32,128]{2,1,0:T(8,128)(2,1)S(1)}, u32[]{:S(2)}, u32[]{:S(2)}) %collective-permute-start.19) | collective-permute-done | bytes 147488 | tf_op jit(solution)/shard_map/ppermute | solution.py:355
  98.4 0.9 shard_map.104
  99.3 4.9 %collective-permute-start.23 = (bf16[18,32,128]{2,1,0:T(8,128)(2,1)S(1)}, bf16[18,32,128]{2,1,0:T(8,128)(2,1)S(1)}, u32[]{:S(2)}, u32[]{:S(2)}) collective-permute-start(bf16[18,32,128]{2,1,0:T(8,128)(2,1)S(1)} %get-tuple-element.285), channel_id=1, source_target_pairs={{0,4},{2,6},{4,0},{5,9},{6,2},{7,11},{8,12},{9,5},{10,14},{11,7},{... | collective-permute-start | bytes 442376 | tf_op jit(solution)/shard_map/ppermute | solution.py:355
  104.5 1.7 %shard_map.107.refs_8_ = f32[4,2,8,8,128]{4,3,2,1,0:T(8,128)S(1)} custom-call(f32[1,4,8]{2,1,0:T(4,128)S(1)} %copy-done, f32[6,2,32,128]{3,2,1,0:T(8,128)S(1)} %get-tuple-element.253.refs_0_, f32[6,2,32,128]{3,2,1,0:T(8,128)S(1)} %get-tuple-element.254.refs_1_, f32[6,2,32,128]{3,2,1,0:T(8,128)S(1)} %get-tuple-element.255.refs_2_, ...), custom_call_target="tpu_custom_call" | custom-call | flops 1000000 | bytes 2000000 | tf_op jit(solution)/shard_map/pallas_call | solution.py:30
  106.4 0.9 collective-permute-done.23.halo
  107.5 0.7 shard_map.110
  108.4 1.3 %collective-permute-done.25 = f32[2,2,8,8,128]{4,3,2,1,0:T(8,128)S(1)} collective-permute-done((f32[2,2,8,8,128]{4,3,2,1,0:T(8,128)S(1)}, f32[2,2,8,8,128]{4,3,2,1,0:T(8,128)S(1)}, u32[]{:S(2)}, u32[]{:S(2)}) %collective-permute-start.25) | collective-permute-done | bytes 131104 | tf_op jit(solution)/shard_map/ppermute | solution.py:339
  109.8 0.5 collective-permute-start.26
  110.3 1.5 %collective-permute-start.28 = (f32[2,4,8,128]{3,2,1,0:T(8,128)S(1)}, f32[2,4,8,128]{3,2,1,0:T(8,128)S(1)}, u32[]{:S(2)}, u32[]{:S(2)}) collective-permute-start(f32[2,4,8,128]{3,2,1,0:T(8,128)S(1)} %get-tuple-element.302), channel_id=1, source_target_pairs={{0,2},{1,3},{2,0},{3,1},{16,18},{17,19},{18,16},{19,17},{4,6},{5,7... | collective-permute-start | bytes 98312 | tf_op jit(solution)/shard_map/ppermute | solution.py:483
  111.8 1.5 %collective-permute-start.27 = (f32[2,4,8,128]{3,2,1,0:T(8,128)S(1)}, f32[2,4,8,128]{3,2,1,0:T(8,128)S(1)}, u32[]{:S(2)}, u32[]{:S(2)}) collective-permute-start(f32[2,4,8,128]{3,2,1,0:T(8,128)S(1)} %dynamic-slice_bitcast_fusion.5), channel_id=1, source_target_pairs={{0,16},{1,17},{2,18},{3,19},{16,0},{17,1},{18,2},{19,3},{4,20},{5,... | collective-permute-start | bytes 98312 | tf_op jit(solution)/shard_map/ppermute | solution.py:483
  113.3 1.3 %collective-permute-done.26 = f32[2,4,8,128]{3,2,1,0:T(8,128)S(1)} collective-permute-done((f32[2,4,8,128]{3,2,1,0:T(8,128)S(1)}, f32[2,4,8,128]{3,2,1,0:T(8,128)S(1)}, u32[]{:S(2)}, u32[]{:S(2)}) %collective-permute-start.26) | collective-permute-done | bytes 32800 | tf_op jit(solution)/shard_map/ppermute | solution.py:483
  114.7 1.1 collective-permute-done.27
  115.7 0.6 bitcast_add_fusion
  (64 shorter events, 8.7 us)
Async XLA Ops:
  0.0 4.3 %copy-start.2 = (s32[8,8,128]{2,1,0:T(8,128)S(1)}, s32[8,8,128]{2,1,0:T(8,128)}, u32[]{:S(2)}) copy-start(s32[8,8,128]{2,1,0:T(8,128)} %param.10) | copy-start | bytes 98308
  1.3 27.8 %collective-permute-start.3 = (bf16[8,6,8,8,128]{4,3,2,1,0:T(8,128)(2,1)}, bf16[8,6,8,8,128]{4,3,2,1,0:T(8,128)(2,1)}, u32[]{:S(2)}, u32[]{:S(2)}) collective-permute-start(bf16[8,6,8,8,128]{4,3,2,1,0:T(8,128)(2,1)} %bitcast), channel_id=1, source_target_pairs={{0,16},{16,0},{1,17},{17,1},{2,18},{18,2},{3,19},{19,3},{4,20},{20... | collective-permute-start | bytes 2359304 | tf_op jit(solution)/shard_map/ppermute | solution.py:339
  4.3 18.3 %copy-start.5 = (s32[2,8,2]{1,2,0:T(2,128)S(1)}, s32[2,8,2]{1,2,0:T(2,128)}, u32[]{:S(2)}) copy-start(s32[2,8,2]{1,2,0:T(2,128)} %param.14) | copy-start | bytes 388
  4.3 18.3 %copy-start.3 = (f32[16,3]{0,1:T(4,128)S(1)}, f32[16,3]{0,1:T(4,128)}, u32[]{:S(2)}) copy-start(f32[16,3]{0,1:T(4,128)} %param.11) | copy-start | bytes 580
  4.3 18.4 %copy-start.4 = (s32[2,8]{1,0:T(2,128)S(1)}, s32[2,8]{1,0:T(2,128)}, u32[]{:S(2)}) copy-start(s32[2,8]{1,0:T(2,128)} %param.15) | copy-start | bytes 196
  4.4 24.8 %copy-start = (f32[1,4,8]{2,1,0:T(4,128)S(1)}, f32[1,4,8]{2,1,0:T(4,128)}, u32[]{:S(2)}) copy-start(f32[1,4,8]{2,1,0:T(4,128)} %residual.7) | copy-start | bytes 388
  4.4 24.8 %copy-start.1 = (s32[1,4]{1,0:T(1,128)S(1)}, s32[1,4]{1,0:T(1,128)}, u32[]{:S(2)}) copy-start(s32[1,4]{1,0:T(1,128)} %rec_cell.3) | copy-start | bytes 52
  4.5 1.9 %collective-permute-start = (f32[10,8,8,128]{3,2,1,0:T(8,128)S(1)}, f32[10,8,8,128]{3,2,1,0:T(8,128)S(1)}, u32[]{:S(2)}, u32[]{:S(2)}) collective-permute-start(f32[10,8,8,128]{3,2,1,0:T(8,128)S(1)} %get-tuple-element.304), channel_id=1, source_target_pairs={{0,1},{1,0},{2,3},{3,2},{4,5},{5,4},{6,7},{7,6},{8,9},{9,8},{10,11... | collective-permute-start | bytes 983048 | tf_op jit(solution)/shard_map/ppermute | solution.py:339
  4.6 10.6 %collective-permute-start.1 = (f32[10,8,8,128]{3,2,1,0:T(8,128)S(1)}, f32[10,8,8,128]{3,2,1,0:T(8,128)S(1)}, u32[]{:S(2)}, u32[]{:S(2)}) collective-permute-start(f32[10,8,8,128]{3,2,1,0:T(8,128)S(1)} %get-tuple-element.305), channel_id=1, source_target_pairs={{0,2},{1,3},{2,0},{3,1},{4,6},{5,7},{6,4},{7,5},{8,10},{9,11},{10,... | collective-permute-start | bytes 983048 | tf_op jit(solution)/shard_map/ppermute | solution.py:339
  6.2 15.1 %collective-permute-start.2 = (f32[10,8,8,128]{3,2,1,0:T(8,128)S(1)}, f32[10,8,8,128]{3,2,1,0:T(8,128)S(1)}, u32[]{:S(2)}, u32[]{:S(2)}) collective-permute-start(f32[10,8,8,128]{3,2,1,0:T(8,128)S(1)} %get-tuple-element.303), channel_id=1, source_target_pairs={{0,3},{1,2},{2,1},{3,0},{4,7},{5,6},{6,5},{7,4},{8,11},{9,10},{10,... | collective-permute-start | bytes 983048 | tf_op jit(solution)/shard_map/ppermute | solution.py:339
  22.0 7.1 %collective-permute-start.6 = (f32[4,2,32,128]{3,2,1,0:T(8,128)S(1)}, f32[4,2,32,128]{3,2,1,0:T(8,128)S(1)}, u32[]{:S(2)}, u32[]{:S(2)}) collective-permute-start(f32[4,2,32,128]{3,2,1,0:T(8,128)S(1)} %get-tuple-element.167), channel_id=1, source_target_pairs={{1,5},{3,7},{4,8},{5,1},{6,10},{7,3},{8,4},{9,13},{10,6},{11,15},{... | collective-permute-start | bytes 393224 | tf_op jit(solution)/shard_map/ppermute | solution.py:355
  22.8 9.9 %collective-permute-start.4 = (f32[4,2,32,128]{3,2,1,0:T(8,128)S(1)}, f32[4,2,32,128]{3,2,1,0:T(8,128)S(1)}, u32[]{:S(2)}, u32[]{:S(2)}) collective-permute-start(f32[4,2,32,128]{3,2,1,0:T(8,128)S(1)} %get-tuple-element.160), channel_id=1, source_target_pairs={{0,4},{2,6},{4,0},{5,9},{6,2},{7,11},{8,12},{9,5},{10,14},{11,7},{... | collective-permute-start | bytes 393224 | tf_op jit(solution)/shard_map/ppermute | solution.py:355
  30.3 3.8 %collective-permute-start.8 = (bf16[18,32,128]{2,1,0:T(8,128)(2,1)S(1)}, bf16[18,32,128]{2,1,0:T(8,128)(2,1)S(1)}, u32[]{:S(2)}, u32[]{:S(2)}) collective-permute-start(bf16[18,32,128]{2,1,0:T(8,128)(2,1)S(1)} %get-tuple-element.182), channel_id=1, source_target_pairs={{1,5},{3,7},{4,8},{5,1},{6,10},{7,3},{8,4},{9,13},{10,6},{11,15},{... | collective-permute-start | bytes 442376 | tf_op jit(solution)/shard_map/ppermute | solution.py:355
  34.6 43.8 %collective-permute-start.16 = (f32[8,6,8,8,128]{4,3,2,1,0:T(8,128)S(1)}, f32[8,6,8,8,128]{4,3,2,1,0:T(8,128)S(1)}, u32[]{:S(2)}, u32[]{:S(2)}) collective-permute-start(f32[8,6,8,8,128]{4,3,2,1,0:T(8,128)S(1)} %multiply_add_fusion.refs_28_.refs_4_), channel_id=1, source_target_pairs={{0,1},{1,0},{2,3},{3,2},{4,5},{5,4},{6,7},{7,6},{8,9},{9,8},{10,11... | collective-permute-start | bytes 4718600 | tf_op jit(solution)/shard_map/ppermute | solution.py:339
  37.3 41.1 %collective-permute-start.17 = (f32[8,6,8,8,128]{4,3,2,1,0:T(8,128)S(1)}, f32[8,6,8,8,128]{4,3,2,1,0:T(8,128)S(1)}, u32[]{:S(2)}, u32[]{:S(2)}) collective-permute-start(f32[8,6,8,8,128]{4,3,2,1,0:T(8,128)S(1)} %multiply_add_fusion.refs_28_.refs_4_), channel_id=1, source_target_pairs={{0,2},{1,3},{2,0},{3,1},{4,6},{5,7},{6,4},{7,5},{8,10},{9,11},{10,... | collective-permute-start | bytes 4718600 | tf_op jit(solution)/shard_map/ppermute | solution.py:339
  38.8 7.0 %collective-permute-start.5 = (bf16[18,32,128]{2,1,0:T(8,128)(2,1)S(1)}, bf16[18,32,128]{2,1,0:T(8,128)(2,1)S(1)}, u32[]{:S(2)}, u32[]{:S(2)}) collective-permute-start(bf16[18,32,128]{2,1,0:T(8,128)(2,1)S(1)} %get-tuple-element.162), channel_id=1, source_target_pairs={{0,4},{2,6},{4,0},{5,9},{6,2},{7,11},{8,12},{9,5},{10,14},{11,7},{... | collective-permute-start | bytes 442376 | tf_op jit(solution)/shard_map/ppermute | solution.py:355
  42.6 7.7 %collective-permute-start.10 = (bf16[18,32,128]{2,1,0:T(8,128)(2,1)S(1)}, bf16[18,32,128]{2,1,0:T(8,128)(2,1)S(1)}, u32[]{:S(2)}, u32[]{:S(2)}) collective-permute-start(bf16[18,32,128]{2,1,0:T(8,128)(2,1)S(1)} %get-tuple-element.194), channel_id=1, source_target_pairs={{1,5},{3,7},{4,8},{5,1},{6,10},{7,3},{8,4},{9,13},{10,6},{11,15},{... | collective-permute-start | bytes 442376 | tf_op jit(solution)/shard_map/ppermute | solution.py:355
  46.3 7.0 %collective-permute-start.7 = (bf16[18,32,128]{2,1,0:T(8,128)(2,1)S(1)}, bf16[18,32,128]{2,1,0:T(8,128)(2,1)S(1)}, u32[]{:S(2)}, u32[]{:S(2)}) collective-permute-start(bf16[18,32,128]{2,1,0:T(8,128)(2,1)S(1)} %get-tuple-element.179), channel_id=1, source_target_pairs={{0,4},{2,6},{4,0},{5,9},{6,2},{7,11},{8,12},{9,5},{10,14},{11,7},{... | collective-permute-start | bytes 442376 | tf_op jit(solution)/shard_map/ppermute | solution.py:355
  50.9 7.0 %collective-permute-start.12 = (bf16[18,32,128]{2,1,0:T(8,128)(2,1)S(1)}, bf16[18,32,128]{2,1,0:T(8,128)(2,1)S(1)}, u32[]{:S(2)}, u32[]{:S(2)}) collective-permute-start(bf16[18,32,128]{2,1,0:T(8,128)(2,1)S(1)} %get-tuple-element.204), channel_id=1, source_target_pairs={{1,5},{3,7},{4,8},{5,1},{6,10},{7,3},{8,4},{9,13},{10,6},{11,15},{... | collective-permute-start | bytes 442376 | tf_op jit(solution)/shard_map/ppermute | solution.py:355
  53.8 7.0 %collective-permute-start.9 = (bf16[18,32,128]{2,1,0:T(8,128)(2,1)S(1)}, bf16[18,32,128]{2,1,0:T(8,128)(2,1)S(1)}, u32[]{:S(2)}, u32[]{:S(2)}) collective-permute-start(bf16[18,32,128]{2,1,0:T(8,128)(2,1)S(1)} %get-tuple-element.191), channel_id=1, source_target_pairs={{0,4},{2,6},{4,0},{5,9},{6,2},{7,11},{8,12},{9,5},{10,14},{11,7},{... | collective-permute-start | bytes 442376 | tf_op jit(solution)/shard_map/ppermute | solution.py:355
  58.4 7.4 %collective-permute-start.14 = (bf16[18,32,128]{2,1,0:T(8,128)(2,1)S(1)}, bf16[18,32,128]{2,1,0:T(8,128)(2,1)S(1)}, u32[]{:S(2)}, u32[]{:S(2)}) collective-permute-start(bf16[18,32,128]{2,1,0:T(8,128)(2,1)S(1)} %get-tuple-element.214), channel_id=1, source_target_pairs={{1,5},{3,7},{4,8},{5,1},{6,10},{7,3},{8,4},{9,13},{10,6},{11,15},{... | collective-permute-start | bytes 442376 | tf_op jit(solution)/shard_map/ppermute | solution.py:355
  61.3 8.3 %collective-permute-start.11 = (bf16[18,32,128]{2,1,0:T(8,128)(2,1)S(1)}, bf16[18,32,128]{2,1,0:T(8,128)(2,1)S(1)}, u32[]{:S(2)}, u32[]{:S(2)}) collective-permute-start(bf16[18,32,128]{2,1,0:T(8,128)(2,1)S(1)} %get-tuple-element.201), channel_id=1, source_target_pairs={{0,4},{2,6},{4,0},{5,9},{6,2},{7,11},{8,12},{9,5},{10,14},{11,7},{... | collective-permute-start | bytes 442376 | tf_op jit(solution)/shard_map/ppermute | solution.py:355
  66.2 8.6 %collective-permute-start.18 = (bf16[18,32,128]{2,1,0:T(8,128)(2,1)S(1)}, bf16[18,32,128]{2,1,0:T(8,128)(2,1)S(1)}, u32[]{:S(2)}, u32[]{:S(2)}) collective-permute-start(bf16[18,32,128]{2,1,0:T(8,128)(2,1)S(1)} %get-tuple-element.228), channel_id=1, source_target_pairs={{1,5},{3,7},{4,8},{5,1},{6,10},{7,3},{8,4},{9,13},{10,6},{11,15},{... | collective-permute-start | bytes 442376 | tf_op jit(solution)/shard_map/ppermute | solution.py:355
  70.1 7.6 %collective-permute-start.13 = (bf16[18,32,128]{2,1,0:T(8,128)(2,1)S(1)}, bf16[18,32,128]{2,1,0:T(8,128)(2,1)S(1)}, u32[]{:S(2)}, u32[]{:S(2)}) collective-permute-start(bf16[18,32,128]{2,1,0:T(8,128)(2,1)S(1)} %get-tuple-element.211), channel_id=1, source_target_pairs={{0,4},{2,6},{4,0},{5,9},{6,2},{7,11},{8,12},{9,5},{10,14},{11,7},{... | collective-permute-start | bytes 442376 | tf_op jit(solution)/shard_map/ppermute | solution.py:355
  78.4 26.0 %collective-permute-start.22 = (f32[8,6,8,8,128]{4,3,2,1,0:T(8,128)S(1)}, f32[8,6,8,8,128]{4,3,2,1,0:T(8,128)S(1)}, u32[]{:S(2)}, u32[]{:S(2)}) collective-permute-start(f32[8,6,8,8,128]{4,3,2,1,0:T(8,128)S(1)} %collective-permute-done.17.refs_30_.refs_6_), channel_id=1, source_target_pairs={{0,1},{1,0},{2,3},{3,2},{4,5},{5,4},{6,7},{7,6},{8,9},{9,8},{10,11... | collective-permute-start | bytes 4718600 | tf_op jit(solution)/shard_map/ppermute | solution.py:339
  78.5 8.7 %collective-permute-start.20 = (bf16[18,32,128]{2,1,0:T(8,128)(2,1)S(1)}, bf16[18,32,128]{2,1,0:T(8,128)(2,1)S(1)}, u32[]{:S(2)}, u32[]{:S(2)}) collective-permute-start(bf16[18,32,128]{2,1,0:T(8,128)(2,1)S(1)} %get-tuple-element.240), channel_id=1, source_target_pairs={{1,5},{3,7},{4,8},{5,1},{6,10},{7,3},{8,4},{9,13},{10,6},{11,15},{... | collective-permute-start | bytes 442376 | tf_op jit(solution)/shard_map/ppermute | solution.py:355
  79.2 11.2 %collective-permute-start.15 = (bf16[18,32,128]{2,1,0:T(8,128)(2,1)S(1)}, bf16[18,32,128]{2,1,0:T(8,128)(2,1)S(1)}, u32[]{:S(2)}, u32[]{:S(2)}) collective-permute-start(bf16[18,32,128]{2,1,0:T(8,128)(2,1)S(1)} %get-tuple-element.221), channel_id=1, source_target_pairs={{0,4},{2,6},{4,0},{5,9},{6,2},{7,11},{8,12},{9,5},{10,14},{11,7},{... | collective-permute-start | bytes 442376 | tf_op jit(solution)/shard_map/ppermute | solution.py:355
  87.7 7.8 %collective-permute-start.21 = (bf16[18,32,128]{2,1,0:T(8,128)(2,1)S(1)}, bf16[18,32,128]{2,1,0:T(8,128)(2,1)S(1)}, u32[]{:S(2)}, u32[]{:S(2)}) collective-permute-start(bf16[18,32,128]{2,1,0:T(8,128)(2,1)S(1)} %get-tuple-element.247), channel_id=1, source_target_pairs={{1,5},{3,7},{4,8},{5,1},{6,10},{7,3},{8,4},{9,13},{10,6},{11,15},{... | collective-permute-start | bytes 442376 | tf_op jit(solution)/shard_map/ppermute | solution.py:355
  90.8 7.6 %collective-permute-start.19 = (bf16[18,32,128]{2,1,0:T(8,128)(2,1)S(1)}, bf16[18,32,128]{2,1,0:T(8,128)(2,1)S(1)}, u32[]{:S(2)}, u32[]{:S(2)}) collective-permute-start(bf16[18,32,128]{2,1,0:T(8,128)(2,1)S(1)} %get-tuple-element.237), channel_id=1, source_target_pairs={{0,4},{2,6},{4,0},{5,9},{6,2},{7,11},{8,12},{9,5},{10,14},{11,7},{... | collective-permute-start | bytes 442376 | tf_op jit(solution)/shard_map/ppermute | solution.py:355
  96.5 9.7 %collective-permute-start.24 = (bf16[18,32,128]{2,1,0:T(8,128)(2,1)S(1)}, bf16[18,32,128]{2,1,0:T(8,128)(2,1)S(1)}, u32[]{:S(2)}, u32[]{:S(2)}) collective-permute-start(bf16[18,32,128]{2,1,0:T(8,128)(2,1)S(1)} %get-tuple-element.288), channel_id=1, source_target_pairs={{1,5},{3,7},{4,8},{5,1},{6,10},{7,3},{8,4},{9,13},{10,6},{11,15},{... | collective-permute-start | bytes 442376 | tf_op jit(solution)/shard_map/ppermute | solution.py:355
  99.3 8.0 %collective-permute-start.23 = (bf16[18,32,128]{2,1,0:T(8,128)(2,1)S(1)}, bf16[18,32,128]{2,1,0:T(8,128)(2,1)S(1)}, u32[]{:S(2)}, u32[]{:S(2)}) collective-permute-start(bf16[18,32,128]{2,1,0:T(8,128)(2,1)S(1)} %get-tuple-element.285), channel_id=1, source_target_pairs={{0,4},{2,6},{4,0},{5,9},{6,2},{7,11},{8,12},{9,5},{10,14},{11,7},{... | collective-permute-start | bytes 442376 | tf_op jit(solution)/shard_map/ppermute | solution.py:355
  108.3 1.4 %collective-permute-start.25 = (f32[2,2,8,8,128]{4,3,2,1,0:T(8,128)S(1)}, f32[2,2,8,8,128]{4,3,2,1,0:T(8,128)S(1)}, u32[]{:S(2)}, u32[]{:S(2)}) collective-permute-start(f32[2,2,8,8,128]{4,3,2,1,0:T(8,128)S(1)} %pad_maximum_fusion.4), channel_id=1, source_target_pairs={{0,1},{1,0},{2,3},{3,2},{4,5},{5,4},{6,7},{7,6},{8,9},{9,8},{10,11... | collective-permute-start | bytes 393224 | tf_op jit(solution)/shard_map/ppermute | solution.py:339
  109.8 4.9 %collective-permute-start.26 = (f32[2,4,8,128]{3,2,1,0:T(8,128)S(1)}, f32[2,4,8,128]{3,2,1,0:T(8,128)S(1)}, u32[]{:S(2)}, u32[]{:S(2)}) collective-permute-start(f32[2,4,8,128]{3,2,1,0:T(8,128)S(1)} %get-tuple-element.301), channel_id=1, source_target_pairs={{0,18},{1,19},{2,16},{3,17},{16,2},{17,3},{18,0},{19,1},{4,22},{5,... | collective-permute-start | bytes 98312 | tf_op jit(solution)/shard_map/ppermute | solution.py:483
  110.3 4.4 %collective-permute-start.28 = (f32[2,4,8,128]{3,2,1,0:T(8,128)S(1)}, f32[2,4,8,128]{3,2,1,0:T(8,128)S(1)}, u32[]{:S(2)}, u32[]{:S(2)}) collective-permute-start(f32[2,4,8,128]{3,2,1,0:T(8,128)S(1)} %get-tuple-element.302), channel_id=1, source_target_pairs={{0,2},{1,3},{2,0},{3,1},{16,18},{17,19},{18,16},{19,17},{4,6},{5,7... | collective-permute-start | bytes 98312 | tf_op jit(solution)/shard_map/ppermute | solution.py:483
  111.8 3.9 %collective-permute-start.27 = (f32[2,4,8,128]{3,2,1,0:T(8,128)S(1)}, f32[2,4,8,128]{3,2,1,0:T(8,128)S(1)}, u32[]{:S(2)}, u32[]{:S(2)}) collective-permute-start(f32[2,4,8,128]{3,2,1,0:T(8,128)S(1)} %dynamic-slice_bitcast_fusion.5), channel_id=1, source_target_pairs={{0,16},{1,17},{2,18},{3,19},{16,0},{17,1},{18,2},{19,3},{4,20},{5,... | collective-permute-start | bytes 98312 | tf_op jit(solution)/shard_map/ppermute | solution.py:483

commit v5 on v4

--- a/solution.py
+++ b/solution.py
@@ -309,9 +309,8 @@
 
 def correlate(moments, pieces, residual, *refs):
     count = len(moments)
-    rates, sources, rest = refs[: 4 * count], refs[4 * count : 4 * count + pieces], refs[4 * count + pieces :]
-    before, terms = rest[:-1], rest[-1]
-    tile_x, tile_y = sources[0].shape[2:4]
+    rates, sources, before, terms = refs[: 4 * count], refs[4 * count], refs[4 * count + 1 : -1], refs[-1]
+    tile_x, tile_y = sources.shape[3:5]
     _, me, flip = position()
     sign = sign_of(flip)
     for turn in range(pieces):
@@ -324,7 +323,7 @@
                     weight = (KERNEL_SCALE / UNIT) * residual[0, me, moment]
                     held = rates[4 * at + 2 * (out // REACH) + side]
                     rate = [held[c, out % REACH, spot, :] for c in range(6)]
-                    source = [sources[turn][moment, c, row] for c in range(6)]
+                    source = [sources[me ^ turn, moment, c, row] for c in range(6)]
                     bulk = (source[0] + source[1] + source[2]) * (rate[0] + rate[1] + rate[2])
                     diag = source[0] * rate[0] + source[1] * rate[1] + source[2] * rate[2]
                     off = sign * (source[3] * rate[3] + source[4] * rate[4]) + source[5] * rate[5]
@@ -355,10 +354,6 @@
     return lax.ppermute(face, ("gx", "gy"), pairs)
 
 
-def sources_first(pieces):
-    return sorted((turn for turn in range(1, pieces) if turn & (turn - 1) == 0), reverse=True)
-
-
 def local(rec_state, source_strain, material, material_table, residual, rec_cell, listed, src_pick):
     state = rec_state[0]
     receivers, _, tile_x, tile_y, depth = state.shape
@@ -398,6 +393,7 @@
     for turn in range(groups):
         factor = jnp.sum(weights * (src_pick == (group ^ turn)).astype(F32), 0)
         combined = combined + factor[:, None, None, None, None] * strains[turn].astype(F32)
+    gathered = lax.all_gather(combined, "gy", axis=0)
 
     sent, lights, lames, shears, old_halos, spots, amounts = ([None, None] for _ in range(7))
     fresh = [None, None]
@@ -427,17 +423,11 @@
         rates += results[:2]
         if not last:
             middles = results[2:]
-        if moment == 5 * moments // 8:
-            found, middles = lax.optimization_barrier((found, middles))
-            for turn in range(pieces):
-                if turn not in found:
-                    low = turn & -turn
-                    found[turn] = swap(found[turn ^ low], "gy", low)
         if last:
             (terms,) = call(
                 functools.partial(correlate, list(range(moment)), pieces),
                 [((pieces, 2, tile_x, tile_y, depth), F32)],
-                ([residual], rates[: 4 * moment] + [found[turn] for turn in range(pieces)]),
+                ([residual], rates[: 4 * moment] + [gathered]),
             )
             terms, vels = lax.optimization_barrier((terms, vels))
         fresh = [None, None]
@@ -453,16 +443,12 @@
             if not last:
                 edges[side], old_halos[side], fresh[side] = results[1:4]
                 sent[side] = to_neighbour(results[4], side)
-        if moment == 0:
-            combined, rates[-1] = lax.optimization_barrier((combined, rates[-1]))
-            found = {turn: swap(combined, "gy", turn) for turn in sources_first(pieces)}
-            found[0] = combined
         vels = fresh
 
     (terms,) = call(
         functools.partial(correlate, [moments - 1], pieces),
         [((pieces, 2, tile_x, tile_y, depth), F32)],
-        ([residual], rates[-4:] + [found[turn] for turn in range(pieces)] + [terms]),
+        ([residual], rates[-4:] + [gathered, terms]),
     )
     held = {turn: terms[turn] for turn in range(pieces)}
     if pieces > 1:

time: 117 us -> 148 us (1.26)
  local copies, waits for them, and re-layouts: 1.46 us -> 25.6 us
  between operations: 0.57 us -> 14 us
  starting transfers between devices: 62.6 us -> 54.3 us
  Pallas kernels: 15.1 us -> 17.2 us
  waiting for transfers between devices: 34 us -> 32.2 us
    unnamed x13 -> x85, local copies, waits for them, and re-layouts: 0.12 us -> 24.3 us
    ppermute x8 -> x5, starting transfers between devices: 9.32 us -> 5.01 us  [swap(): return lax.ppermute(array, axis, [(i, i ^ turn) for i in range(count)])]
    ppermute x18, starting transfers between devices: 49.7 us -> 45.7 us  [to_neighbour(): return lax.ppermute(face, ('gx', 'gy'), pairs)]
    ppermute x18, waiting for transfers between devices: 15.5 us -> 12.2 us  [to_neighbour(): return lax.ppermute(face, ('gx', 'gy'), pairs)]
    pallas_call x29, Pallas kernels: 15.1 us -> 17.2 us  [call(): pl.pallas_call(body, out_shape=[jax.ShapeDtypeStruct(shape, kind) for sha...]
    ppermute x8 -> x5, waiting for transfers between devices: 16.2 us -> 16.3 us  [swap(): return lax.ppermute(array, axis, [(i, i ^ turn) for i in range(count)])]
  transfers between devices with their start and end apart: 29 -> 27, of which waited for: 13 -> 15; matrix products, arithmetic and copies ran while one was open for 2% -> 0% of each run, Pallas kernels for 12% -> 10%
where the time goes in v5:
time: 148 us; the launch traced here: 147 us
  starting transfers between devices  54.3 us (37%)
  waiting for transfers between devices  32.2 us (22%)
  local copies, waits for them, and re-layouts  25.6 us (17%)
  Pallas kernels  17.2 us (12%)
  between operations  14 us (9%)
  other arithmetic  3.8 us (3%)
    ppermute x18, starting transfers between devices, to_neighbour(): return lax.ppermute(face, ('gx', 'gy'), pairs)  45.7 us
    unnamed x85, local copies, waits for them, and re-layouts  24.3 us
    pallas_call x29, Pallas kernels, call(): pl.pallas_call(body, out_shape=[jax.ShapeDtypeStruct(shape, kind) for sha...  17.2 us
    ppermute x5, waiting for transfers between devices, swap(): return lax.ppermute(array, axis, [(i, i ^ turn) for i in range(count)])  16.3 us
    ppermute x18, waiting for transfers between devices, to_neighbour(): return lax.ppermute(face, ('gx', 'gy'), pairs)  12.2 us
    ppermute x5, starting transfers between devices, swap(): return lax.ppermute(array, axis, [(i, i ^ turn) for i in range(count)])  5.01 us
    ppermute x3, waiting for transfers between devices, local(): part = lax.ppermute(part, ('sta', 'gy'), pairs)  3.7 us
    ppermute x3, starting transfers between devices, local(): part = lax.ppermute(part, ('sta', 'gy'), pairs)  3.55 us
  transfers between devices with their start and end apart: 27, of which 15 were waited for; matrix products, arithmetic and copies ran while one was open for 0% of the time, Pallas kernels for 10%

profile of v5, /device:TPU:0, one launch (start us, length us, event | category | flops | bytes accessed | tf_op | source)
XLA Modules:
  0.0 147.1 jit_solution(2511763006324768862)
XLA Ops:
  6.5 1.3 dynamic-slice_bitcast_fusion
  7.9 3.0 %collective-permute-start.3 = (bf16[8,6,8,8,128]{4,3,2,1,0:T(8,128)(2,1)}, bf16[8,6,8,8,128]{4,3,2,1,0:T(8,128)(2,1)}, u32[]{:S(2)}, u32[]{:S(2)}) collective-permute-start(bf16[8,6,8,8,128]{4,3,2,1,0:T(8,128)(2,1)} %bitcast), channel_id=1, source_target_pairs={{0,16},{16,0},{1,17},{17,1},{2,18},{18,2},{3,19},{19,3},{4,20},{20... | collective-permute-start | bytes 2359304 | tf_op jit(solution)/shard_map/ppermute | solution.py:338
  11.1 1.6 %collective-permute-start.1 = (f32[10,8,8,128]{3,2,1,0:T(8,128)S(1)}, f32[10,8,8,128]{3,2,1,0:T(8,128)S(1)}, u32[]{:S(2)}, u32[]{:S(2)}) collective-permute-start(f32[10,8,8,128]{3,2,1,0:T(8,128)S(1)} %get-tuple-element.291), channel_id=1, source_target_pairs={{0,2},{1,3},{2,0},{3,1},{4,6},{5,7},{6,4},{7,5},{8,10},{9,11},{10,... | collective-permute-start | bytes 983048 | tf_op jit(solution)/shard_map/ppermute | solution.py:338
  13.0 8.7 %collective-permute-done.1.refs_2_ = f32[10,8,8,128]{3,2,1,0:T(8,128)S(1)} collective-permute-done((f32[10,8,8,128]{3,2,1,0:T(8,128)S(1)}, f32[10,8,8,128]{3,2,1,0:T(8,128)S(1)}, u32[]{:S(2)}, u32[]{:S(2)}) %collective-permute-start.1) | collective-permute-done | bytes 327712 | tf_op jit(solution)/shard_map/ppermute | solution.py:338
  21.7 6.1 %collective-permute-done.2.refs_3_ = f32[10,8,8,128]{3,2,1,0:T(8,128)S(1)} collective-permute-done((f32[10,8,8,128]{3,2,1,0:T(8,128)S(1)}, f32[10,8,8,128]{3,2,1,0:T(8,128)S(1)}, u32[]{:S(2)}, u32[]{:S(2)}) %collective-permute-start.2) | collective-permute-done | bytes 327712 | tf_op jit(solution)/shard_map/ppermute | solution.py:338
  28.7 3.0 %multiply_add_fusion = f32[8,6,8,8,128]{4,3,2,1,0:T(8,128)} fusion(bf16[8,6,8,8,128]{4,3,2,1,0:T(8,128)(2,1)} %collective-permute-done.3, bf16[8,6,8,8,128]{4,3,2,1,0:T(8,128)(2,1)} %bitcast, f32[8]{0:T(128)S(1)} %get-tuple-element.278, f32[8]{0:T(128)S(1)} %get-tuple-element.277), kind=kLoop, calls=%fused_computation | loop fusion | flops 1966080 | bytes 3145792 | tf_op jit(solution)/shard_map/add | solution.py:395
  32.5 6.5 %collective-permute-start.4 = (f32[4,2,32,128]{3,2,1,0:T(8,128)S(1)}, f32[4,2,32,128]{3,2,1,0:T(8,128)S(1)}, u32[]{:S(2)}, u32[]{:S(2)}) collective-permute-start(f32[4,2,32,128]{3,2,1,0:T(8,128)S(1)} %get-tuple-element.153), channel_id=1, source_target_pairs={{0,4},{2,6},{4,0},{5,9},{6,2},{7,11},{8,12},{9,5},{10,14},{11,7},{... | collective-permute-start | bytes 393224 | tf_op jit(solution)/shard_map/ppermute | solution.py:354
  39.2 1.1 shard_map.84
  41.0 1.0 collective-permute-done.4.halo
  42.0 1.1 shard_map.83
  43.2 5.1 %collective-permute-start.5 = (bf16[18,32,128]{2,1,0:T(8,128)(2,1)S(1)}, bf16[18,32,128]{2,1,0:T(8,128)(2,1)S(1)}, u32[]{:S(2)}, u32[]{:S(2)}) collective-permute-start(bf16[18,32,128]{2,1,0:T(8,128)(2,1)S(1)} %get-tuple-element.155), channel_id=1, source_target_pairs={{0,4},{2,6},{4,0},{5,9},{6,2},{7,11},{8,12},{9,5},{10,14},{11,7},{... | collective-permute-start | bytes 442376 | tf_op jit(solution)/shard_map/ppermute | solution.py:354
  49.6 1.7 %collective-permute-done.5.halo = bf16[18,32,128]{2,1,0:T(8,128)(2,1)S(1)} collective-permute-done((bf16[18,32,128]{2,1,0:T(8,128)(2,1)S(1)}, bf16[18,32,128]{2,1,0:T(8,128)(2,1)S(1)}, u32[]{:S(2)}, u32[]{:S(2)}) %collective-permute-start.5) | collective-permute-done | bytes 147488 | tf_op jit(solution)/shard_map/ppermute | solution.py:354
  51.8 3.9 %collective-permute-start.7 = (bf16[18,32,128]{2,1,0:T(8,128)(2,1)S(1)}, bf16[18,32,128]{2,1,0:T(8,128)(2,1)S(1)}, u32[]{:S(2)}, u32[]{:S(2)}) collective-permute-start(bf16[18,32,128]{2,1,0:T(8,128)(2,1)S(1)} %get-tuple-element.172), channel_id=1, source_target_pairs={{0,4},{2,6},{4,0},{5,9},{6,2},{7,11},{8,12},{9,5},{10,14},{11,7},{... | collective-permute-start | bytes 442376 | tf_op jit(solution)/shard_map/ppermute | solution.py:354
  57.1 2.0 %collective-permute-done.7.halo = bf16[18,32,128]{2,1,0:T(8,128)(2,1)S(1)} collective-permute-done((bf16[18,32,128]{2,1,0:T(8,128)(2,1)S(1)}, bf16[18,32,128]{2,1,0:T(8,128)(2,1)S(1)}, u32[]{:S(2)}, u32[]{:S(2)}) %collective-permute-start.7) | collective-permute-done | bytes 147488 | tf_op jit(solution)/shard_map/ppermute | solution.py:354
  59.6 4.2 %collective-permute-start.9 = (bf16[18,32,128]{2,1,0:T(8,128)(2,1)S(1)}, bf16[18,32,128]{2,1,0:T(8,128)(2,1)S(1)}, u32[]{:S(2)}, u32[]{:S(2)}) collective-permute-start(bf16[18,32,128]{2,1,0:T(8,128)(2,1)S(1)} %get-tuple-element.184), channel_id=1, source_target_pairs={{0,4},{2,6},{4,0},{5,9},{6,2},{7,11},{8,12},{9,5},{10,14},{11,7},{... | collective-permute-start | bytes 442376 | tf_op jit(solution)/shard_map/ppermute | solution.py:354
  65.2 2.9 %collective-permute-done.9.halo = bf16[18,32,128]{2,1,0:T(8,128)(2,1)S(1)} collective-permute-done((bf16[18,32,128]{2,1,0:T(8,128)(2,1)S(1)}, bf16[18,32,128]{2,1,0:T(8,128)(2,1)S(1)}, u32[]{:S(2)}, u32[]{:S(2)}) %collective-permute-start.9) | collective-permute-done | bytes 147488 | tf_op jit(solution)/shard_map/ppermute | solution.py:354
  68.5 4.1 %collective-permute-start.11 = (bf16[18,32,128]{2,1,0:T(8,128)(2,1)S(1)}, bf16[18,32,128]{2,1,0:T(8,128)(2,1)S(1)}, u32[]{:S(2)}, u32[]{:S(2)}) collective-permute-start(bf16[18,32,128]{2,1,0:T(8,128)(2,1)S(1)} %get-tuple-element.194), channel_id=1, source_target_pairs={{0,4},{2,6},{4,0},{5,9},{6,2},{7,11},{8,12},{9,5},{10,14},{11,7},{... | collective-permute-start | bytes 442376 | tf_op jit(solution)/shard_map/ppermute | solution.py:354
  75.4 1.6 %collective-permute-done.11.halo = bf16[18,32,128]{2,1,0:T(8,128)(2,1)S(1)} collective-permute-done((bf16[18,32,128]{2,1,0:T(8,128)(2,1)S(1)}, bf16[18,32,128]{2,1,0:T(8,128)(2,1)S(1)}, u32[]{:S(2)}, u32[]{:S(2)}) %collective-permute-start.11) | collective-permute-done | bytes 147488 | tf_op jit(solution)/shard_map/ppermute | solution.py:354
  78.1 4.1 %collective-permute-start.13 = (bf16[18,32,128]{2,1,0:T(8,128)(2,1)S(1)}, bf16[18,32,128]{2,1,0:T(8,128)(2,1)S(1)}, u32[]{:S(2)}, u32[]{:S(2)}) collective-permute-start(bf16[18,32,128]{2,1,0:T(8,128)(2,1)S(1)} %get-tuple-element.204), channel_id=1, source_target_pairs={{0,4},{2,6},{4,0},{5,9},{6,2},{7,11},{8,12},{9,5},{10,14},{11,7},{... | collective-permute-start | bytes 442376 | tf_op jit(solution)/shard_map/ppermute | solution.py:354
  85.0 1.0 collective-permute-done.13.halo
  87.1 3.6 %collective-permute-start.15 = (bf16[18,32,128]{2,1,0:T(8,128)(2,1)S(1)}, bf16[18,32,128]{2,1,0:T(8,128)(2,1)S(1)}, u32[]{:S(2)}, u32[]{:S(2)}) collective-permute-start(bf16[18,32,128]{2,1,0:T(8,128)(2,1)S(1)} %get-tuple-element.214), channel_id=1, source_target_pairs={{0,4},{2,6},{4,0},{5,9},{6,2},{7,11},{8,12},{9,5},{10,14},{11,7},{... | collective-permute-start | bytes 442376 | tf_op jit(solution)/shard_map/ppermute | solution.py:354
  92.8 1.3 collective-permute-done.15.halo
  95.3 3.6 %collective-permute-start.17 = (bf16[18,32,128]{2,1,0:T(8,128)(2,1)S(1)}, bf16[18,32,128]{2,1,0:T(8,128)(2,1)S(1)}, u32[]{:S(2)}, u32[]{:S(2)}) collective-permute-start(bf16[18,32,128]{2,1,0:T(8,128)(2,1)S(1)} %get-tuple-element.224), channel_id=1, source_target_pairs={{0,4},{2,6},{4,0},{5,9},{6,2},{7,11},{8,12},{9,5},{10,14},{11,7},{... | collective-permute-start | bytes 442376 | tf_op jit(solution)/shard_map/ppermute | solution.py:354
  99.2 1.1 shard_map.105
  100.3 1.3 collective-permute-start.21
  102.3 1.1 shard_map.104
  104.1 3.6 %collective-permute-start.20 = (bf16[18,32,128]{2,1,0:T(8,128)(2,1)}, bf16[18,32,128]{2,1,0:T(8,128)(2,1)}, u32[]{:S(2)}, u32[]{:S(2)}) collective-permute-start(bf16[18,32,128]{2,1,0:T(8,128)(2,1)} %get-tuple-element.271), channel_id=1, source_target_pairs={{0,4},{2,6},{4,0},{5,9},{6,2},{7,11},{8,12},{9,5},{10,14},{11,7},{... | collective-permute-start | bytes 442376 | tf_op jit(solution)/shard_map/ppermute | solution.py:354
  109.3 2.8 %copy-done = f32[32,6,8,8,128]{4,3,2,1,0:T(8,128)S(1)} copy-done((f32[32,6,8,8,128]{4,3,2,1,0:T(8,128)S(1)}, f32[32,6,8,8,128]{4,3,2,1,0:T(8,128)}, u32[]{:S(2)}) %copy-start) | copy-done | bytes 6291480
  112.1 0.9 copy-done.3
  113.0 0.9 copy-done.5
  114.0 0.9 copy-done.7
  114.9 0.9 copy-done.9
  115.8 0.9 copy-done.11
  116.7 0.9 copy-done.13
  117.7 0.9 copy-done.15
  119.5 0.9 copy-done.19
  120.5 0.9 copy-done.21
  121.4 0.9 copy-done.23
  122.3 0.9 copy-done.25
  123.2 0.9 copy-done.27
  124.2 0.9 copy-done.29
  126.0 1.7 %shard_map.107.refs_5_ = f32[4,2,8,8,128]{4,3,2,1,0:T(8,128)S(1)} custom-call(f32[1,4,8]{2,1,0:T(4,128)S(1)} %copy-done.36, f32[6,2,32,128]{3,2,1,0:T(8,128)S(1)} %get-tuple-element.240.refs_0_, f32[6,2,32,128]{3,2,1,0:T(8,128)S(1)} %get-tuple-element.241.refs_1_, f32[6,2,32,128]{3,2,1,0:T(8,128)S(1)} %get-tuple-element.242.refs_2_, ...), custom_call_target="tpu_custom_call" | custom-call | flops 1000000 | bytes 2000000 | tf_op jit(solution)/shard_map/pallas_call | solution.py:30
  127.7 1.3 shard_map.109.refs_3_
  129.0 1.1 shard_map.108.refs_2_
  131.0 1.3 collective-permute-done.22
  132.4 2.8 %collective-permute-start.23 = (f32[2,4,8,128]{3,2,1,0:T(8,128)S(1)}, f32[2,4,8,128]{3,2,1,0:T(8,128)S(1)}, u32[]{:S(2)}, u32[]{:S(2)}) collective-permute-start(f32[2,4,8,128]{3,2,1,0:T(8,128)S(1)} %get-tuple-element.287), channel_id=1, source_target_pairs={{0,18},{1,19},{2,16},{3,17},{16,2},{17,3},{18,0},{19,1},{4,22},{5,... | collective-permute-start | bytes 98312 | tf_op jit(solution)/shard_map/ppermute | solution.py:469
  135.9 1.3 collective-permute-done.23
  137.3 1.9 %collective-permute-done.25 = f32[2,4,8,128]{3,2,1,0:T(8,128)S(1)} collective-permute-done((f32[2,4,8,128]{3,2,1,0:T(8,128)S(1)}, f32[2,4,8,128]{3,2,1,0:T(8,128)S(1)}, u32[]{:S(2)}, u32[]{:S(2)}) %collective-permute-start.25) | collective-permute-done | bytes 32800 | tf_op jit(solution)/shard_map/ppermute | solution.py:469
  (133 shorter events, 27.0 us)
Async XLA Ops:
  6.5 4.4 %copy-start.38 = (s32[8,8,128]{2,1,0:T(8,128)S(1)}, s32[8,8,128]{2,1,0:T(8,128)}, u32[]{:S(2)}) copy-start(s32[8,8,128]{2,1,0:T(8,128)} %param.10) | copy-start | bytes 98308
  6.5 102.8 %all-gather.3.cloned.1.call-start = ((), (), s32[]{:S(2)}) async-start(), calls=%async_computation | async-start | bytes 7864320 | tf_op jit(solution)/shard_map/all_gather | solution.py:396
  7.9 5.1 %copy-start.41 = (s32[2,8,2]{1,2,0:T(2,128)S(1)}, s32[2,8,2]{1,2,0:T(2,128)}, u32[]{:S(2)}) copy-start(s32[2,8,2]{1,2,0:T(2,128)} %param.14) | copy-start | bytes 388
  7.9 5.1 %copy-start.40 = (s32[2,8]{1,0:T(2,128)S(1)}, s32[2,8]{1,0:T(2,128)}, u32[]{:S(2)}) copy-start(s32[2,8]{1,0:T(2,128)} %param.15) | copy-start | bytes 196
  7.9 20.9 %collective-permute-start.3 = (bf16[8,6,8,8,128]{4,3,2,1,0:T(8,128)(2,1)}, bf16[8,6,8,8,128]{4,3,2,1,0:T(8,128)(2,1)}, u32[]{:S(2)}, u32[]{:S(2)}) collective-permute-start(bf16[8,6,8,8,128]{4,3,2,1,0:T(8,128)(2,1)} %bitcast), channel_id=1, source_target_pairs={{0,16},{16,0},{1,17},{17,1},{2,18},{18,2},{3,19},{19,3},{4,20},{20... | collective-permute-start | bytes 2359304 | tf_op jit(solution)/shard_map/ppermute | solution.py:338
  11.1 2.0 %collective-permute-start = (f32[10,8,8,128]{3,2,1,0:T(8,128)S(1)}, f32[10,8,8,128]{3,2,1,0:T(8,128)S(1)}, u32[]{:S(2)}, u32[]{:S(2)}) collective-permute-start(f32[10,8,8,128]{3,2,1,0:T(8,128)S(1)} %get-tuple-element.290), channel_id=1, source_target_pairs={{0,1},{1,0},{2,3},{3,2},{4,5},{5,4},{6,7},{7,6},{8,9},{9,8},{10,11... | collective-permute-start | bytes 983048 | tf_op jit(solution)/shard_map/ppermute | solution.py:338
  11.1 10.6 %collective-permute-start.1 = (f32[10,8,8,128]{3,2,1,0:T(8,128)S(1)}, f32[10,8,8,128]{3,2,1,0:T(8,128)S(1)}, u32[]{:S(2)}, u32[]{:S(2)}) collective-permute-start(f32[10,8,8,128]{3,2,1,0:T(8,128)S(1)} %get-tuple-element.291), channel_id=1, source_target_pairs={{0,2},{1,3},{2,0},{3,1},{4,6},{5,7},{6,4},{7,5},{8,10},{9,11},{10,... | collective-permute-start | bytes 983048 | tf_op jit(solution)/shard_map/ppermute | solution.py:338
  12.7 15.1 %collective-permute-start.2 = (f32[10,8,8,128]{3,2,1,0:T(8,128)S(1)}, f32[10,8,8,128]{3,2,1,0:T(8,128)S(1)}, u32[]{:S(2)}, u32[]{:S(2)}) collective-permute-start(f32[10,8,8,128]{3,2,1,0:T(8,128)S(1)} %get-tuple-element.289), channel_id=1, source_target_pairs={{0,3},{1,2},{2,1},{3,0},{4,7},{5,6},{6,5},{7,4},{8,11},{9,10},{10,... | collective-permute-start | bytes 983048 | tf_op jit(solution)/shard_map/ppermute | solution.py:338
  31.7 7.4 %copy-start.39 = (f32[16,3]{0,1:T(4,128)S(1)}, f32[16,3]{0,1:T(4,128)}, u32[]{:S(2)}) copy-start(f32[16,3]{0,1:T(4,128)} %param.11) | copy-start | bytes 580
  31.7 7.5 %copy-start.36 = (f32[1,4,8]{2,1,0:T(4,128)S(1)}, f32[1,4,8]{2,1,0:T(4,128)}, u32[]{:S(2)}) copy-start(f32[1,4,8]{2,1,0:T(4,128)} %residual.7) | copy-start | bytes 388
  31.7 7.5 %copy-start.37 = (s32[1,4]{1,0:T(1,128)S(1)}, s32[1,4]{1,0:T(1,128)}, u32[]{:S(2)}) copy-start(s32[1,4]{1,0:T(1,128)} %rec_cell.3) | copy-start | bytes 52
  31.7 7.5 %collective-permute-start.6 = (f32[4,2,32,128]{3,2,1,0:T(8,128)S(1)}, f32[4,2,32,128]{3,2,1,0:T(8,128)S(1)}, u32[]{:S(2)}, u32[]{:S(2)}) collective-permute-start(f32[4,2,32,128]{3,2,1,0:T(8,128)S(1)} %get-tuple-element.160), channel_id=1, source_target_pairs={{1,5},{3,7},{4,8},{5,1},{6,10},{7,3},{8,4},{9,13},{10,6},{11,15},{... | collective-permute-start | bytes 393224 | tf_op jit(solution)/shard_map/ppermute | solution.py:354
  32.5 9.5 %collective-permute-start.4 = (f32[4,2,32,128]{3,2,1,0:T(8,128)S(1)}, f32[4,2,32,128]{3,2,1,0:T(8,128)S(1)}, u32[]{:S(2)}, u32[]{:S(2)}) collective-permute-start(f32[4,2,32,128]{3,2,1,0:T(8,128)S(1)} %get-tuple-element.153), channel_id=1, source_target_pairs={{0,4},{2,6},{4,0},{5,9},{6,2},{7,11},{8,12},{9,5},{10,14},{11,7},{... | collective-permute-start | bytes 393224 | tf_op jit(solution)/shard_map/ppermute | solution.py:354
  40.4 8.1 %collective-permute-start.8 = (bf16[18,32,128]{2,1,0:T(8,128)(2,1)S(1)}, bf16[18,32,128]{2,1,0:T(8,128)(2,1)S(1)}, u32[]{:S(2)}, u32[]{:S(2)}) collective-permute-start(bf16[18,32,128]{2,1,0:T(8,128)(2,1)S(1)} %get-tuple-element.175), channel_id=1, source_target_pairs={{1,5},{3,7},{4,8},{5,1},{6,10},{7,3},{8,4},{9,13},{10,6},{11,15},{... | collective-permute-start | bytes 442376 | tf_op jit(solution)/shard_map/ppermute | solution.py:354
  43.2 8.2 %collective-permute-start.5 = (bf16[18,32,128]{2,1,0:T(8,128)(2,1)S(1)}, bf16[18,32,128]{2,1,0:T(8,128)(2,1)S(1)}, u32[]{:S(2)}, u32[]{:S(2)}) collective-permute-start(bf16[18,32,128]{2,1,0:T(8,128)(2,1)S(1)} %get-tuple-element.155), channel_id=1, source_target_pairs={{0,4},{2,6},{4,0},{5,9},{6,2},{7,11},{8,12},{9,5},{10,14},{11,7},{... | collective-permute-start | bytes 442376 | tf_op jit(solution)/shard_map/ppermute | solution.py:354
  49.0 7.0 %collective-permute-start.10 = (bf16[18,32,128]{2,1,0:T(8,128)(2,1)S(1)}, bf16[18,32,128]{2,1,0:T(8,128)(2,1)S(1)}, u32[]{:S(2)}, u32[]{:S(2)}) collective-permute-start(bf16[18,32,128]{2,1,0:T(8,128)(2,1)S(1)} %get-tuple-element.187), channel_id=1, source_target_pairs={{1,5},{3,7},{4,8},{5,1},{6,10},{7,3},{8,4},{9,13},{10,6},{11,15},{... | collective-permute-start | bytes 442376 | tf_op jit(solution)/shard_map/ppermute | solution.py:354
  51.8 7.3 %collective-permute-start.7 = (bf16[18,32,128]{2,1,0:T(8,128)(2,1)S(1)}, bf16[18,32,128]{2,1,0:T(8,128)(2,1)S(1)}, u32[]{:S(2)}, u32[]{:S(2)}) collective-permute-start(bf16[18,32,128]{2,1,0:T(8,128)(2,1)S(1)} %get-tuple-element.172), channel_id=1, source_target_pairs={{0,4},{2,6},{4,0},{5,9},{6,2},{7,11},{8,12},{9,5},{10,14},{11,7},{... | collective-permute-start | bytes 442376 | tf_op jit(solution)/shard_map/ppermute | solution.py:354
  56.4 7.6 %collective-permute-start.12 = (bf16[18,32,128]{2,1,0:T(8,128)(2,1)S(1)}, bf16[18,32,128]{2,1,0:T(8,128)(2,1)S(1)}, u32[]{:S(2)}, u32[]{:S(2)}) collective-permute-start(bf16[18,32,128]{2,1,0:T(8,128)(2,1)S(1)} %get-tuple-element.197), channel_id=1, source_target_pairs={{1,5},{3,7},{4,8},{5,1},{6,10},{7,3},{8,4},{9,13},{10,6},{11,15},{... | collective-permute-start | bytes 442376 | tf_op jit(solution)/shard_map/ppermute | solution.py:354
  59.6 8.5 %collective-permute-start.9 = (bf16[18,32,128]{2,1,0:T(8,128)(2,1)S(1)}, bf16[18,32,128]{2,1,0:T(8,128)(2,1)S(1)}, u32[]{:S(2)}, u32[]{:S(2)}) collective-permute-start(bf16[18,32,128]{2,1,0:T(8,128)(2,1)S(1)} %get-tuple-element.184), channel_id=1, source_target_pairs={{0,4},{2,6},{4,0},{5,9},{6,2},{7,11},{8,12},{9,5},{10,14},{11,7},{... | collective-permute-start | bytes 442376 | tf_op jit(solution)/shard_map/ppermute | solution.py:354
  64.5 9.0 %collective-permute-start.14 = (bf16[18,32,128]{2,1,0:T(8,128)(2,1)S(1)}, bf16[18,32,128]{2,1,0:T(8,128)(2,1)S(1)}, u32[]{:S(2)}, u32[]{:S(2)}) collective-permute-start(bf16[18,32,128]{2,1,0:T(8,128)(2,1)S(1)} %get-tuple-element.207), channel_id=1, source_target_pairs={{1,5},{3,7},{4,8},{5,1},{6,10},{7,3},{8,4},{9,13},{10,6},{11,15},{... | collective-permute-start | bytes 442376 | tf_op jit(solution)/shard_map/ppermute | solution.py:354
  68.5 8.5 %collective-permute-start.11 = (bf16[18,32,128]{2,1,0:T(8,128)(2,1)S(1)}, bf16[18,32,128]{2,1,0:T(8,128)(2,1)S(1)}, u32[]{:S(2)}, u32[]{:S(2)}) collective-permute-start(bf16[18,32,128]{2,1,0:T(8,128)(2,1)S(1)} %get-tuple-element.194), channel_id=1, source_target_pairs={{0,4},{2,6},{4,0},{5,9},{6,2},{7,11},{8,12},{9,5},{10,14},{11,7},{... | collective-permute-start | bytes 442376 | tf_op jit(solution)/shard_map/ppermute | solution.py:354
  74.7 9.1 %collective-permute-start.16 = (bf16[18,32,128]{2,1,0:T(8,128)(2,1)S(1)}, bf16[18,32,128]{2,1,0:T(8,128)(2,1)S(1)}, u32[]{:S(2)}, u32[]{:S(2)}) collective-permute-start(bf16[18,32,128]{2,1,0:T(8,128)(2,1)S(1)} %get-tuple-element.217), channel_id=1, source_target_pairs={{1,5},{3,7},{4,8},{5,1},{6,10},{7,3},{8,4},{9,13},{10,6},{11,15},{... | collective-permute-start | bytes 442376 | tf_op jit(solution)/shard_map/ppermute | solution.py:354
  78.1 7.8 %collective-permute-start.13 = (bf16[18,32,128]{2,1,0:T(8,128)(2,1)S(1)}, bf16[18,32,128]{2,1,0:T(8,128)(2,1)S(1)}, u32[]{:S(2)}, u32[]{:S(2)}) collective-permute-start(bf16[18,32,128]{2,1,0:T(8,128)(2,1)S(1)} %get-tuple-element.204), channel_id=1, source_target_pairs={{0,4},{2,6},{4,0},{5,9},{6,2},{7,11},{8,12},{9,5},{10,14},{11,7},{... | collective-permute-start | bytes 442376 | tf_op jit(solution)/shard_map/ppermute | solution.py:354
  84.3 6.4 %copy-start.12 = (f32[6,2,32,128]{3,2,1,0:T(8,128)}, f32[6,2,32,128]{3,2,1,0:T(8,128)S(1)}, u32[]{:S(2)}) copy-start(f32[6,2,32,128]{3,2,1,0:T(8,128)S(1)} %get-tuple-element.259.refs_19_) | copy-start | bytes 589828
  84.3 7.4 %collective-permute-start.18 = (bf16[18,32,128]{2,1,0:T(8,128)(2,1)S(1)}, bf16[18,32,128]{2,1,0:T(8,128)(2,1)S(1)}, u32[]{:S(2)}, u32[]{:S(2)}) collective-permute-start(bf16[18,32,128]{2,1,0:T(8,128)(2,1)S(1)} %get-tuple-element.227), channel_id=1, source_target_pairs={{1,5},{3,7},{4,8},{5,1},{6,10},{7,3},{8,4},{9,13},{10,6},{11,15},{... | collective-permute-start | bytes 442376 | tf_op jit(solution)/shard_map/ppermute | solution.py:354
  87.1 7.0 %collective-permute-start.15 = (bf16[18,32,128]{2,1,0:T(8,128)(2,1)S(1)}, bf16[18,32,128]{2,1,0:T(8,128)(2,1)S(1)}, u32[]{:S(2)}, u32[]{:S(2)}) collective-permute-start(bf16[18,32,128]{2,1,0:T(8,128)(2,1)S(1)} %get-tuple-element.214), channel_id=1, source_target_pairs={{0,4},{2,6},{4,0},{5,9},{6,2},{7,11},{8,12},{9,5},{10,14},{11,7},{... | collective-permute-start | bytes 442376 | tf_op jit(solution)/shard_map/ppermute | solution.py:354
  91.7 7.5 %copy-start.16 = (f32[6,2,32,128]{3,2,1,0:T(8,128)}, f32[6,2,32,128]{3,2,1,0:T(8,128)S(1)}, u32[]{:S(2)}) copy-start(f32[6,2,32,128]{3,2,1,0:T(8,128)S(1)} %get-tuple-element.260.refs_20_) | copy-start | bytes 589828
  92.1 6.8 %copy-start.20 = (f32[6,2,32,128]{3,2,1,0:T(8,128)}, f32[6,2,32,128]{3,2,1,0:T(8,128)S(1)}, u32[]{:S(2)}) copy-start(f32[6,2,32,128]{3,2,1,0:T(8,128)S(1)} %get-tuple-element.263.refs_23_) | copy-start | bytes 589828
  92.1 7.0 %collective-permute-start.19 = (bf16[18,32,128]{2,1,0:T(8,128)(2,1)S(1)}, bf16[18,32,128]{2,1,0:T(8,128)(2,1)S(1)}, u32[]{:S(2)}, u32[]{:S(2)}) collective-permute-start(bf16[18,32,128]{2,1,0:T(8,128)(2,1)S(1)} %get-tuple-element.234), channel_id=1, source_target_pairs={{1,5},{3,7},{4,8},{5,1},{6,10},{7,3},{8,4},{9,13},{10,6},{11,15},{... | collective-permute-start | bytes 442376 | tf_op jit(solution)/shard_map/ppermute | solution.py:354
  95.3 7.0 %collective-permute-start.17 = (bf16[18,32,128]{2,1,0:T(8,128)(2,1)S(1)}, bf16[18,32,128]{2,1,0:T(8,128)(2,1)S(1)}, u32[]{:S(2)}, u32[]{:S(2)}) collective-permute-start(bf16[18,32,128]{2,1,0:T(8,128)(2,1)S(1)} %get-tuple-element.224), channel_id=1, source_target_pairs={{0,4},{2,6},{4,0},{5,9},{6,2},{7,11},{8,12},{9,5},{10,14},{11,7},{... | collective-permute-start | bytes 442376 | tf_op jit(solution)/shard_map/ppermute | solution.py:354
  99.2 4.3 %copy-start.24 = (f32[6,2,32,128]{3,2,1,0:T(8,128)}, f32[6,2,32,128]{3,2,1,0:T(8,128)S(1)}, u32[]{:S(2)}) copy-start(f32[6,2,32,128]{3,2,1,0:T(8,128)S(1)} %get-tuple-element.264.refs_24_) | copy-start | bytes 589828
  99.2 4.9 %copy-start.26 = (f32[6,2,32,128]{3,2,1,0:T(8,128)}, f32[6,2,32,128]{3,2,1,0:T(8,128)S(1)}, u32[]{:S(2)}) copy-start(f32[6,2,32,128]{3,2,1,0:T(8,128)S(1)} %get-tuple-element.265.refs_25_) | copy-start | bytes 589828
  100.3 7.4 %copy-start.28 = (f32[6,2,32,128]{3,2,1,0:T(8,128)}, f32[6,2,32,128]{3,2,1,0:T(8,128)S(1)}, u32[]{:S(2)}) copy-start(f32[6,2,32,128]{3,2,1,0:T(8,128)S(1)} %get-tuple-element.267.refs_27_) | copy-start | bytes 589828
  100.3 27.4 %collective-permute-start.21 = (bf16[18,32,128]{2,1,0:T(8,128)(2,1)}, bf16[18,32,128]{2,1,0:T(8,128)(2,1)}, u32[]{:S(2)}, u32[]{:S(2)}) collective-permute-start(bf16[18,32,128]{2,1,0:T(8,128)(2,1)} %get-tuple-element.274), channel_id=1, source_target_pairs={{1,5},{3,7},{4,8},{5,1},{6,10},{7,3},{8,4},{9,13},{10,6},{11,15},{... | collective-permute-start | bytes 442376 | tf_op jit(solution)/shard_map/ppermute | solution.py:354
  104.1 24.9 %collective-permute-start.20 = (bf16[18,32,128]{2,1,0:T(8,128)(2,1)}, bf16[18,32,128]{2,1,0:T(8,128)(2,1)}, u32[]{:S(2)}, u32[]{:S(2)}) collective-permute-start(bf16[18,32,128]{2,1,0:T(8,128)(2,1)} %get-tuple-element.271), channel_id=1, source_target_pairs={{0,4},{2,6},{4,0},{5,9},{6,2},{7,11},{8,12},{9,5},{10,14},{11,7},{... | collective-permute-start | bytes 442376 | tf_op jit(solution)/shard_map/ppermute | solution.py:354
  109.3 2.8 %copy-start = (f32[32,6,8,8,128]{4,3,2,1,0:T(8,128)S(1)}, f32[32,6,8,8,128]{4,3,2,1,0:T(8,128)}, u32[]{:S(2)}) copy-start(f32[32,6,8,8,128]{4,3,2,1,0:T(8,128)} %all-gather.3.cloned.1.call-done) | copy-start | bytes 18874372
  112.1 0.9 copy-start.3
  113.0 0.9 copy-start.5
  114.0 0.9 copy-start.7
  114.9 0.9 copy-start.9
  123.2 0.9 copy-start.27
  126.0 4.1 %copy-start.1 = (f32[32,6,8,8,128]{4,3,2,1,0:T(8,128)S(1)}, f32[32,6,8,8,128]{4,3,2,1,0:T(8,128)}, u32[]{:S(2)}) copy-start(f32[32,6,8,8,128]{4,3,2,1,0:T(8,128)} %all-gather.3.cloned.1.call-done) | copy-start | bytes 18874372
  127.7 2.4 %copy-start.33 = (f32[6,2,32,128]{3,2,1,0:T(8,128)S(1)}, f32[6,2,32,128]{3,2,1,0:T(8,128)}, u32[]{:S(2)}) copy-start(f32[6,2,32,128]{3,2,1,0:T(8,128)} %copy-done.32) | copy-start | bytes 589828
  127.7 2.4 %copy-start.35 = (f32[6,2,32,128]{3,2,1,0:T(8,128)S(1)}, f32[6,2,32,128]{3,2,1,0:T(8,128)}, u32[]{:S(2)}) copy-start(f32[6,2,32,128]{3,2,1,0:T(8,128)} %copy-done.34) | copy-start | bytes 589828
  130.9 1.4 collective-permute-start.22
  132.4 4.9 %collective-permute-start.23 = (f32[2,4,8,128]{3,2,1,0:T(8,128)S(1)}, f32[2,4,8,128]{3,2,1,0:T(8,128)S(1)}, u32[]{:S(2)}, u32[]{:S(2)}) collective-permute-start(f32[2,4,8,128]{3,2,1,0:T(8,128)S(1)} %get-tuple-element.287), channel_id=1, source_target_pairs={{0,18},{1,19},{2,16},{3,17},{16,2},{17,3},{18,0},{19,1},{4,22},{5,... | collective-permute-start | bytes 98312 | tf_op jit(solution)/shard_map/ppermute | solution.py:469
  135.2 3.9 %collective-permute-start.25 = (f32[2,4,8,128]{3,2,1,0:T(8,128)S(1)}, f32[2,4,8,128]{3,2,1,0:T(8,128)S(1)}, u32[]{:S(2)}, u32[]{:S(2)}) collective-permute-start(f32[2,4,8,128]{3,2,1,0:T(8,128)S(1)} %get-tuple-element.288), channel_id=1, source_target_pairs={{0,2},{1,3},{2,0},{3,1},{16,18},{17,19},{18,16},{19,17},{4,6},{5,7... | collective-permute-start | bytes 98312 | tf_op jit(solution)/shard_map/ppermute | solution.py:469
  135.7 3.9 %collective-permute-start.24 = (f32[2,4,8,128]{3,2,1,0:T(8,128)S(1)}, f32[2,4,8,128]{3,2,1,0:T(8,128)S(1)}, u32[]{:S(2)}, u32[]{:S(2)}) collective-permute-start(f32[2,4,8,128]{3,2,1,0:T(8,128)S(1)} %dynamic-slice_bitcast_fusion.5), channel_id=1, source_target_pairs={{0,16},{1,17},{2,18},{3,19},{16,0},{17,1},{18,2},{19,3},{4,20},{5,... | collective-permute-start | bytes 98312 | tf_op jit(solution)/shard_map/ppermute | solution.py:469
  (21 other events, 16.8 us)
Sparse Core Ops, SparseCore 0:
  31.9 47.8 all-gather.2

commit v6 on v5

--- a/solution.py
+++ b/solution.py
@@ -17,7 +17,7 @@
 REACH = 2
 DEEP = 2 * REACH
 ALONG_X = (0, 3, 4)
-NEAR_ROWS = 2
+NEAR_ROWS = 1
 PACKED = DEEP + NEAR_ROWS
 
 VMEM = pl.BlockSpec(memory_space=pltpu.VMEM)
@@ -309,8 +309,9 @@
 
 def correlate(moments, pieces, residual, *refs):
     count = len(moments)
-    rates, sources, before, terms = refs[: 4 * count], refs[4 * count], refs[4 * count + 1 : -1], refs[-1]
-    tile_x, tile_y = sources.shape[3:5]
+    rates, sources, rest = refs[: 4 * count], refs[4 * count : 4 * count + pieces], refs[4 * count + pieces :]
+    before, terms = rest[:-1], rest[-1]
+    tile_x, tile_y = sources[0].shape[2:4]
     _, me, flip = position()
     sign = sign_of(flip)
     for turn in range(pieces):
@@ -323,7 +324,7 @@
                     weight = (KERNEL_SCALE / UNIT) * residual[0, me, moment]
                     held = rates[4 * at + 2 * (out // REACH) + side]
                     rate = [held[c, out % REACH, spot, :] for c in range(6)]
-                    source = [sources[me ^ turn, moment, c, row] for c in range(6)]
+                    source = [sources[turn][moment, c, row] for c in range(6)]
                     bulk = (source[0] + source[1] + source[2]) * (rate[0] + rate[1] + rate[2])
                     diag = source[0] * rate[0] + source[1] * rate[1] + source[2] * rate[2]
                     off = sign * (source[3] * rate[3] + source[4] * rate[4]) + source[5] * rate[5]
@@ -354,6 +355,17 @@
     return lax.ppermute(face, ("gx", "gy"), pairs)
 
 
+def exchange_plan(pieces, moments):
+    result, known, width = {}, [0], pieces // 2
+    while width:
+        for turn in known:
+            moment = 0 if len(known) == 1 else 3 * moments // 4
+            result.setdefault(moment, []).append((turn ^ width, width))
+        known = known + [turn ^ width for turn in known]
+        width //= 2
+    return result
+
+
 def local(rec_state, source_strain, material, material_table, residual, rec_cell, listed, src_pick):
     state = rec_state[0]
     receivers, _, tile_x, tile_y, depth = state.shape
@@ -393,7 +405,6 @@
     for turn in range(groups):
         factor = jnp.sum(weights * (src_pick == (group ^ turn)).astype(F32), 0)
         combined = combined + factor[:, None, None, None, None] * strains[turn].astype(F32)
-    gathered = lax.all_gather(combined, "gy", axis=0)
 
     sent, lights, lames, shears, old_halos, spots, amounts = ([None, None] for _ in range(7))
     fresh = [None, None]
@@ -412,6 +423,7 @@
         sent[side] = to_neighbour(sent[side], side)
     vels = fresh
 
+    found, exchanges = {0: combined}, exchange_plan(pieces, moments)
     rates = []
     for moment in range(moments):
         last = moment == moments - 1
@@ -423,11 +435,15 @@
         rates += results[:2]
         if not last:
             middles = results[2:]
+        if moment in exchanges:
+            found, rates[-1] = lax.optimization_barrier((found, rates[-1]))
+            for turn, width in exchanges[moment]:
+                found[turn] = swap(found[turn ^ width], "gy", width)
         if last:
             (terms,) = call(
                 functools.partial(correlate, list(range(moment)), pieces),
                 [((pieces, 2, tile_x, tile_y, depth), F32)],
-                ([residual], rates[: 4 * moment] + [gathered]),
+                ([residual], rates[: 4 * moment] + [found[turn] for turn in range(pieces)]),
             )
             terms, vels = lax.optimization_barrier((terms, vels))
         fresh = [None, None]
@@ -448,7 +464,7 @@
     (terms,) = call(
         functools.partial(correlate, [moments - 1], pieces),
         [((pieces, 2, tile_x, tile_y, depth), F32)],
-        ([residual], rates[-4:] + [gathered, terms]),
+        ([residual], rates[-4:] + [found[turn] for turn in range(pieces)] + [terms]),
     )
     held = {turn: terms[turn] for turn in range(pieces)}
     if pieces > 1:

time: 148 us -> 113 us (0.76)
  local copies, waits for them, and re-layouts: 25.6 us -> 1.6 us
  between operations: 14 us -> 0.49 us
  starting transfers between devices: 54.3 us -> 58.7 us
  Pallas kernels: 17.2 us -> 15.2 us
  waiting for transfers between devices: 32.2 us -> 33.9 us
    unnamed x85 -> x13, local copies, waits for them, and re-layouts: 24.3 us -> 0.19 us
    ppermute x18, waiting for transfers between devices: 12.2 us -> 15.3 us  [to_neighbour(): return lax.ppermute(face, ('gx', 'gy'), pairs)]
    ppermute x18, starting transfers between devices: 45.7 us -> 48.4 us  [to_neighbour(): return lax.ppermute(face, ('gx', 'gy'), pairs)]
    add x1, other arithmetic: 2.96 us -> 0.37 us  [local(): combined + factor[:, None, None, None, None] * strains[turn].astype(F32)]
    pallas_call x29, Pallas kernels: 17.2 us -> 15.2 us  [call(): pl.pallas_call(body, out_shape=[jax.ShapeDtypeStruct(shape, kind) for sha...]
    ppermute x5 -> x8, starting transfers between devices: 5.01 us -> 6.77 us  [swap(): return lax.ppermute(array, axis, [(i, i ^ turn) for i in range(count)])]
    ppermute x5 -> x8, waiting for transfers between devices: 16.3 us -> 15.6 us  [swap(): return lax.ppermute(array, axis, [(i, i ^ turn) for i in range(count)])]
  transfers between devices with their start and end apart: 27 -> 29, of which waited for: 15 -> 15; matrix products, arithmetic and copies ran while one was open for 0% -> 2% of each run, Pallas kernels for 10% -> 11%
where the time goes in v6:
time: 113 us; the launch traced here: 112 us
  starting transfers between devices  58.7 us (52%)
  waiting for transfers between devices  33.9 us (30%)
  Pallas kernels  15.2 us (13%)
  other arithmetic  2.57 us (2%)
  local copies, waits for them, and re-layouts  1.6 us (1%)
    ppermute x18, starting transfers between devices, to_neighbour(): return lax.ppermute(face, ('gx', 'gy'), pairs)  48.4 us
    ppermute x8, waiting for transfers between devices, swap(): return lax.ppermute(array, axis, [(i, i ^ turn) for i in range(count)])  15.6 us
    ppermute x18, waiting for transfers between devices, to_neighbour(): return lax.ppermute(face, ('gx', 'gy'), pairs)  15.3 us
    pallas_call x29, Pallas kernels, call(): pl.pallas_call(body, out_shape=[jax.ShapeDtypeStruct(shape, kind) for sha...  15.2 us
    ppermute x8, starting transfers between devices, swap(): return lax.ppermute(array, axis, [(i, i ^ turn) for i in range(count)])  6.77 us
    ppermute x3, starting transfers between devices, local(): part = lax.ppermute(part, ('sta', 'gy'), pairs)  3.55 us
    ppermute x3, waiting for transfers between devices, local(): part = lax.ppermute(part, ('sta', 'gy'), pairs)  2.93 us
  transfers between devices with their start and end apart: 29, of which 15 were waited for; matrix products, arithmetic and copies ran while one was open for 2% of the time, Pallas kernels for 11%

profile of v6, /device:TPU:0, one launch (start us, length us, event | category | flops | bytes accessed | tf_op | source)
XLA Modules:
  0.0 112.4 jit_solution(10187456204838520236)
XLA Ops:
  0.0 1.4 %dynamic-slice_bitcast_fusion = (f32[9,8,8,128]{3,2,1,0:T(8,128)S(1)}, f32[9,8,8,128]{3,2,1,0:T(8,128)S(1)}, f32[9,8,8,128]{3,2,1,0:T(8,128)S(1)}, f32[9,8,8,128]{3,2,1,0:T(8,128)S(1)}) fusion(f32[1,4,9,8,8,128]{5,4,3,2,1,0:T(8,128)} %param.8, s32[]{:T(128)S(6)} %select_n.27, s32[]{:T(128)S(6)} %select_n.25, s32[]{:T(128)S(6)} %select_n.24, s32[]{:T(128)S(6)} %select_n.26), kind=kLoop, calls=%fused_computation.5 | loop fusion | bytes 2359312 | tf_op jit(solution)/shard_map/jit(dynamic_index_in_dim)/squeeze | solution.py:381
  1.5 2.9 %collective-permute-start.3 = (bf16[8,6,8,8,128]{4,3,2,1,0:T(8,128)(2,1)S(1)}, bf16[8,6,8,8,128]{4,3,2,1,0:T(8,128)(2,1)S(1)}, u32[]{:S(2)}, u32[]{:S(2)}) collective-permute-start(bf16[8,6,8,8,128]{4,3,2,1,0:T(8,128)(2,1)S(1)} %bitcast.20), channel_id=1, source_target_pairs={{0,16},{16,0},{1,17},{17,1},{2,18},{18,2},{3,19},{19,3},{4,20},{20... | collective-permute-start | bytes 2359304 | tf_op jit(solution)/shard_map/ppermute | solution.py:339
  4.4 0.8 pad_maximum_fusion
  5.3 0.7 collective-permute-start.2
  5.9 1.0 collective-permute-start
  7.5 0.7 fusion.2
  8.2 7.2 %collective-permute-done.2.refs_3_ = f32[10,8,8,128]{3,2,1,0:T(8,128)S(1)} collective-permute-done((f32[10,8,8,128]{3,2,1,0:T(8,128)}, f32[10,8,8,128]{3,2,1,0:T(8,128)S(1)}, u32[]{:S(2)}, u32[]{:S(2)}) %collective-permute-start.2) | collective-permute-done | bytes 327712 | tf_op jit(solution)/shard_map/ppermute | solution.py:339
  15.4 7.1 %collective-permute-done.1.refs_2_ = f32[10,8,8,128]{3,2,1,0:T(8,128)S(1)} collective-permute-done((f32[10,8,8,128]{3,2,1,0:T(8,128)S(1)}, f32[10,8,8,128]{3,2,1,0:T(8,128)S(1)}, u32[]{:S(2)}, u32[]{:S(2)}) %collective-permute-start.1) | collective-permute-done | bytes 327712 | tf_op jit(solution)/shard_map/ppermute | solution.py:339
  22.5 0.7 shard_map.82
  23.2 3.5 %collective-permute-start.4 = (f32[4,2,32,128]{3,2,1,0:T(8,128)S(1)}, f32[4,2,32,128]{3,2,1,0:T(8,128)S(1)}, u32[]{:S(2)}, u32[]{:S(2)}) collective-permute-start(f32[4,2,32,128]{3,2,1,0:T(8,128)S(1)} %get-tuple-element.158), channel_id=1, source_target_pairs={{0,4},{2,6},{4,0},{5,9},{6,2},{7,11},{8,12},{9,5},{10,14},{11,7},{... | collective-permute-start | bytes 393224 | tf_op jit(solution)/shard_map/ppermute | solution.py:355
  26.7 0.7 collective-permute-start.6
  27.8 2.3 %collective-permute-done.4.halo = f32[4,2,32,128]{3,2,1,0:T(8,128)S(1)} collective-permute-done((f32[4,2,32,128]{3,2,1,0:T(8,128)S(1)}, f32[4,2,32,128]{3,2,1,0:T(8,128)S(1)}, u32[]{:S(2)}, u32[]{:S(2)}) %collective-permute-start.4) | collective-permute-done | bytes 131104 | tf_op jit(solution)/shard_map/ppermute | solution.py:355
  30.1 1.1 %shard_map.83 = (f32[3,4,32,128]{3,2,1,0:T(8,128)S(1)}, bf16[15,32,128]{2,1,0:T(8,128)(2,1)S(1)}, f32[4,32,128]{2,1,0:T(8,128)S(1)}, f32[6,32,128]{2,1,0:T(8,128...) custom-call(f32[16,3]{1,0:T(8,128)S(1)} %copy.9.table, ...), custom_call_target="tpu_custom_call" | custom-call | flops 1000000 | bytes 2000000 | tf_op jit(solution)/shard_map/pallas_call | solution.py:30
  31.2 1.1 %shard_map.84 = (f32[3,4,32,128]{3,2,1,0:T(8,128)S(1)}, bf16[15,32,128]{2,1,0:T(8,128)(2,1)S(1)}, f32[4,32,128]{2,1,0:T(8,128)S(1)}, f32[6,32,128]{2,1,0:T(8,128...) custom-call(f32[16,3]{1,0:T(8,128)S(1)} %copy.9.table, ...), custom_call_target="tpu_custom_call" | custom-call | flops 1000000 | bytes 2000000 | tf_op jit(solution)/shard_map/pallas_call | solution.py:30
  32.6 1.0 collective-permute-start.20
  33.7 0.7 collective-permute-start.8
  34.3 8.6 %collective-permute-start.5 = (bf16[15,32,128]{2,1,0:T(8,128)(2,1)S(1)}, bf16[15,32,128]{2,1,0:T(8,128)(2,1)S(1)}, u32[]{:S(2)}, u32[]{:S(2)}) collective-permute-start(bf16[15,32,128]{2,1,0:T(8,128)(2,1)S(1)} %get-tuple-element.160), channel_id=1, source_target_pairs={{0,4},{2,6},{4,0},{5,9},{6,2},{7,11},{8,12},{9,5},{10,14},{11,7},{... | collective-permute-start | bytes 368648 | tf_op jit(solution)/shard_map/ppermute | solution.py:355
  43.4 0.7 collective-permute-start.10
  44.1 1.8 %collective-permute-done.5.halo = bf16[15,32,128]{2,1,0:T(8,128)(2,1)S(1)} collective-permute-done((bf16[15,32,128]{2,1,0:T(8,128)(2,1)S(1)}, bf16[15,32,128]{2,1,0:T(8,128)(2,1)S(1)}, u32[]{:S(2)}, u32[]{:S(2)}) %collective-permute-start.5) | collective-permute-done | bytes 122912 | tf_op jit(solution)/shard_map/ppermute | solution.py:355
  46.4 5.4 %collective-permute-start.7 = (bf16[15,32,128]{2,1,0:T(8,128)(2,1)S(1)}, bf16[15,32,128]{2,1,0:T(8,128)(2,1)S(1)}, u32[]{:S(2)}, u32[]{:S(2)}) collective-permute-start(bf16[15,32,128]{2,1,0:T(8,128)(2,1)S(1)} %get-tuple-element.177), channel_id=1, source_target_pairs={{0,4},{2,6},{4,0},{5,9},{6,2},{7,11},{8,12},{9,5},{10,14},{11,7},{... | collective-permute-start | bytes 368648 | tf_op jit(solution)/shard_map/ppermute | solution.py:355
  52.5 0.7 collective-permute-start.12
  53.2 1.9 %collective-permute-done.7.halo = bf16[15,32,128]{2,1,0:T(8,128)(2,1)S(1)} collective-permute-done((bf16[15,32,128]{2,1,0:T(8,128)(2,1)S(1)}, bf16[15,32,128]{2,1,0:T(8,128)(2,1)S(1)}, u32[]{:S(2)}, u32[]{:S(2)}) %collective-permute-start.7) | collective-permute-done | bytes 122912 | tf_op jit(solution)/shard_map/ppermute | solution.py:355
  55.6 3.7 %collective-permute-start.9 = (bf16[15,32,128]{2,1,0:T(8,128)(2,1)S(1)}, bf16[15,32,128]{2,1,0:T(8,128)(2,1)S(1)}, u32[]{:S(2)}, u32[]{:S(2)}) collective-permute-start(bf16[15,32,128]{2,1,0:T(8,128)(2,1)S(1)} %get-tuple-element.189), channel_id=1, source_target_pairs={{0,4},{2,6},{4,0},{5,9},{6,2},{7,11},{8,12},{9,5},{10,14},{11,7},{... | collective-permute-start | bytes 368648 | tf_op jit(solution)/shard_map/ppermute | solution.py:355
  60.0 0.7 collective-permute-start.14
  60.7 1.7 %collective-permute-done.9.halo = bf16[15,32,128]{2,1,0:T(8,128)(2,1)S(1)} collective-permute-done((bf16[15,32,128]{2,1,0:T(8,128)(2,1)S(1)}, bf16[15,32,128]{2,1,0:T(8,128)(2,1)S(1)}, u32[]{:S(2)}, u32[]{:S(2)}) %collective-permute-start.9) | collective-permute-done | bytes 122912 | tf_op jit(solution)/shard_map/ppermute | solution.py:355
  62.8 3.7 %collective-permute-start.11 = (bf16[15,32,128]{2,1,0:T(8,128)(2,1)S(1)}, bf16[15,32,128]{2,1,0:T(8,128)(2,1)S(1)}, u32[]{:S(2)}, u32[]{:S(2)}) collective-permute-start(bf16[15,32,128]{2,1,0:T(8,128)(2,1)S(1)} %get-tuple-element.199), channel_id=1, source_target_pairs={{0,4},{2,6},{4,0},{5,9},{6,2},{7,11},{8,12},{9,5},{10,14},{11,7},{... | collective-permute-start | bytes 368648 | tf_op jit(solution)/shard_map/ppermute | solution.py:355
  67.3 0.7 collective-permute-start.16
  67.9 1.7 %collective-permute-done.11.halo = bf16[15,32,128]{2,1,0:T(8,128)(2,1)S(1)} collective-permute-done((bf16[15,32,128]{2,1,0:T(8,128)(2,1)S(1)}, bf16[15,32,128]{2,1,0:T(8,128)(2,1)S(1)}, u32[]{:S(2)}, u32[]{:S(2)}) %collective-permute-start.11) | collective-permute-done | bytes 122912 | tf_op jit(solution)/shard_map/ppermute | solution.py:355
  70.1 3.7 %collective-permute-start.13 = (bf16[15,32,128]{2,1,0:T(8,128)(2,1)S(1)}, bf16[15,32,128]{2,1,0:T(8,128)(2,1)S(1)}, u32[]{:S(2)}, u32[]{:S(2)}) collective-permute-start(bf16[15,32,128]{2,1,0:T(8,128)(2,1)S(1)} %get-tuple-element.209), channel_id=1, source_target_pairs={{0,4},{2,6},{4,0},{5,9},{6,2},{7,11},{8,12},{9,5},{10,14},{11,7},{... | collective-permute-start | bytes 368648 | tf_op jit(solution)/shard_map/ppermute | solution.py:355
  74.5 0.7 collective-permute-start.18
  75.2 1.7 %collective-permute-done.13.halo = bf16[15,32,128]{2,1,0:T(8,128)(2,1)S(1)} collective-permute-done((bf16[15,32,128]{2,1,0:T(8,128)(2,1)S(1)}, bf16[15,32,128]{2,1,0:T(8,128)(2,1)S(1)}, u32[]{:S(2)}, u32[]{:S(2)}) %collective-permute-start.13) | collective-permute-done | bytes 122912 | tf_op jit(solution)/shard_map/ppermute | solution.py:355
  77.3 3.7 %collective-permute-start.15 = (bf16[15,32,128]{2,1,0:T(8,128)(2,1)S(1)}, bf16[15,32,128]{2,1,0:T(8,128)(2,1)S(1)}, u32[]{:S(2)}, u32[]{:S(2)}) collective-permute-start(bf16[15,32,128]{2,1,0:T(8,128)(2,1)S(1)} %get-tuple-element.219), channel_id=1, source_target_pairs={{0,4},{2,6},{4,0},{5,9},{6,2},{7,11},{8,12},{9,5},{10,14},{11,7},{... | collective-permute-start | bytes 368648 | tf_op jit(solution)/shard_map/ppermute | solution.py:355
  81.8 2.3 %collective-permute-done.15.halo = bf16[15,32,128]{2,1,0:T(8,128)(2,1)S(1)} collective-permute-done((bf16[15,32,128]{2,1,0:T(8,128)(2,1)S(1)}, bf16[15,32,128]{2,1,0:T(8,128)(2,1)S(1)}, u32[]{:S(2)}, u32[]{:S(2)}) %collective-permute-start.15) | collective-permute-done | bytes 122912 | tf_op jit(solution)/shard_map/ppermute | solution.py:355
  85.4 0.7 collective-permute-start.19
  86.0 5.3 %collective-permute-start.17 = (bf16[15,32,128]{2,1,0:T(8,128)(2,1)S(1)}, bf16[15,32,128]{2,1,0:T(8,128)(2,1)S(1)}, u32[]{:S(2)}, u32[]{:S(2)}) collective-permute-start(bf16[15,32,128]{2,1,0:T(8,128)(2,1)S(1)} %get-tuple-element.229), channel_id=1, source_target_pairs={{0,4},{2,6},{4,0},{5,9},{6,2},{7,11},{8,12},{9,5},{10,14},{11,7},{... | collective-permute-start | bytes 368648 | tf_op jit(solution)/shard_map/ppermute | solution.py:355
  91.4 0.9 shard_map.105
  92.3 0.7 collective-permute-start.24
  93.0 1.2 %collective-permute-done.17.halo = bf16[15,32,128]{2,1,0:T(8,128)(2,1)S(1)} collective-permute-done((bf16[15,32,128]{2,1,0:T(8,128)(2,1)S(1)}, bf16[15,32,128]{2,1,0:T(8,128)(2,1)S(1)}, u32[]{:S(2)}, u32[]{:S(2)}) %collective-permute-start.17) | collective-permute-done | bytes 122912 | tf_op jit(solution)/shard_map/ppermute | solution.py:355
  94.2 0.9 shard_map.104
  95.2 4.9 %collective-permute-start.23 = (bf16[15,32,128]{2,1,0:T(8,128)(2,1)S(1)}, bf16[15,32,128]{2,1,0:T(8,128)(2,1)S(1)}, u32[]{:S(2)}, u32[]{:S(2)}) collective-permute-start(bf16[15,32,128]{2,1,0:T(8,128)(2,1)S(1)} %get-tuple-element.281), channel_id=1, source_target_pairs={{0,4},{2,6},{4,0},{5,9},{6,2},{7,11},{8,12},{9,5},{10,14},{11,7},{... | collective-permute-start | bytes 368648 | tf_op jit(solution)/shard_map/ppermute | solution.py:355
  100.3 1.7 %shard_map.107.refs_8_ = f32[4,2,8,8,128]{4,3,2,1,0:T(8,128)S(1)} custom-call(f32[1,4,8]{2,1,0:T(4,128)S(1)} %copy-done, f32[6,2,32,128]{3,2,1,0:T(8,128)S(1)} %get-tuple-element.245.refs_0_, f32[6,2,32,128]{3,2,1,0:T(8,128)S(1)} %get-tuple-element.249.refs_1_, f32[6,2,32,128]{3,2,1,0:T(8,128)S(1)} %get-tuple-element.250.refs_2_, ...), custom_call_target="tpu_custom_call" | custom-call | flops 1000000 | bytes 2000000 | tf_op jit(solution)/shard_map/pallas_call | solution.py:30
  103.1 0.7 shard_map.110
  103.9 1.3 %collective-permute-done.25 = f32[2,2,8,8,128]{4,3,2,1,0:T(8,128)S(1)} collective-permute-done((f32[2,2,8,8,128]{4,3,2,1,0:T(8,128)S(1)}, f32[2,2,8,8,128]{4,3,2,1,0:T(8,128)S(1)}, u32[]{:S(2)}, u32[]{:S(2)}) %collective-permute-start.25) | collective-permute-done | bytes 131104 | tf_op jit(solution)/shard_map/ppermute | solution.py:339
  105.9 2.0 %collective-permute-start.26 = (f32[2,4,8,128]{3,2,1,0:T(8,128)S(1)}, f32[2,4,8,128]{3,2,1,0:T(8,128)S(1)}, u32[]{:S(2)}, u32[]{:S(2)}) collective-permute-start(f32[2,4,8,128]{3,2,1,0:T(8,128)S(1)} %get-tuple-element.297), channel_id=1, source_target_pairs={{0,18},{1,19},{2,16},{3,17},{16,2},{17,3},{18,0},{19,1},{4,22},{5,... | collective-permute-start | bytes 98312 | tf_op jit(solution)/shard_map/ppermute | solution.py:485
  107.9 1.0 collective-permute-start.28
  108.9 0.7 collective-permute-done.27
  109.6 1.2 %collective-permute-done.26 = f32[2,4,8,128]{3,2,1,0:T(8,128)S(1)} collective-permute-done((f32[2,4,8,128]{3,2,1,0:T(8,128)S(1)}, f32[2,4,8,128]{3,2,1,0:T(8,128)S(1)}, u32[]{:S(2)}, u32[]{:S(2)}) %collective-permute-start.26) | collective-permute-done | bytes 32800 | tf_op jit(solution)/shard_map/ppermute | solution.py:485
  110.8 1.0 collective-permute-done.28
  (64 shorter events, 11.5 us)
Async XLA Ops:
  0.0 1.5 %copy-start.2 = (bf16[1,8,6,8,8,128]{5,4,3,2,1,0:T(8,128)(2,1)S(1)}, bf16[1,8,6,8,8,128]{5,4,3,2,1,0:T(8,128)(2,1)}, u32[]{:S(2)}) copy-start(bf16[1,8,6,8,8,128]{5,4,3,2,1,0:T(8,128)(2,1)} %param.9) | copy-start | bytes 2359300
  0.0 4.4 %copy-start.3 = (s32[8,8,128]{2,1,0:T(8,128)S(1)}, s32[8,8,128]{2,1,0:T(8,128)}, u32[]{:S(2)}) copy-start(s32[8,8,128]{2,1,0:T(8,128)} %param.10) | copy-start | bytes 98308
  1.4 6.0 %copy-start.4 = (f32[16,3]{0,1:T(4,128)S(1)}, f32[16,3]{0,1:T(4,128)}, u32[]{:S(2)}) copy-start(f32[16,3]{0,1:T(4,128)} %param.11) | copy-start | bytes 580
  1.4 6.8 %copy-start.5 = (s32[2,8]{1,0:T(2,128)S(1)}, s32[2,8]{1,0:T(2,128)}, u32[]{:S(2)}) copy-start(s32[2,8]{1,0:T(2,128)} %param.15) | copy-start | bytes 196
  1.5 25.9 %collective-permute-start.3 = (bf16[8,6,8,8,128]{4,3,2,1,0:T(8,128)(2,1)S(1)}, bf16[8,6,8,8,128]{4,3,2,1,0:T(8,128)(2,1)S(1)}, u32[]{:S(2)}, u32[]{:S(2)}) collective-permute-start(bf16[8,6,8,8,128]{4,3,2,1,0:T(8,128)(2,1)S(1)} %bitcast.20), channel_id=1, source_target_pairs={{0,16},{16,0},{1,17},{17,1},{2,18},{18,2},{3,19},{19,3},{4,20},{20... | collective-permute-start | bytes 2359304 | tf_op jit(solution)/shard_map/ppermute | solution.py:339
  5.3 10.2 %collective-permute-start.2 = (f32[10,8,8,128]{3,2,1,0:T(8,128)}, f32[10,8,8,128]{3,2,1,0:T(8,128)S(1)}, u32[]{:S(2)}, u32[]{:S(2)}) collective-permute-start(f32[10,8,8,128]{3,2,1,0:T(8,128)} %get-tuple-element.299), channel_id=1, source_target_pairs={{0,3},{1,2},{2,1},{3,0},{4,7},{5,6},{6,5},{7,4},{8,11},{9,10},{10,... | collective-permute-start | bytes 983048 | tf_op jit(solution)/shard_map/ppermute | solution.py:339
  5.9 9.5 %collective-permute-start = (f32[10,8,8,128]{3,2,1,0:T(8,128)S(1)}, f32[10,8,8,128]{3,2,1,0:T(8,128)S(1)}, u32[]{:S(2)}, u32[]{:S(2)}) collective-permute-start(f32[10,8,8,128]{3,2,1,0:T(8,128)S(1)} %get-tuple-element.300), channel_id=1, source_target_pairs={{0,1},{1,0},{2,3},{3,2},{4,5},{5,4},{6,7},{7,6},{8,9},{9,8},{10,11... | collective-permute-start | bytes 983048 | tf_op jit(solution)/shard_map/ppermute | solution.py:339
  6.9 15.6 %collective-permute-start.1 = (f32[10,8,8,128]{3,2,1,0:T(8,128)S(1)}, f32[10,8,8,128]{3,2,1,0:T(8,128)S(1)}, u32[]{:S(2)}, u32[]{:S(2)}) collective-permute-start(f32[10,8,8,128]{3,2,1,0:T(8,128)S(1)} %get-tuple-element.301), channel_id=1, source_target_pairs={{0,2},{1,3},{2,0},{3,1},{4,6},{5,7},{6,4},{7,5},{8,10},{9,11},{10,... | collective-permute-start | bytes 983048 | tf_op jit(solution)/shard_map/ppermute | solution.py:339
  23.2 6.9 %collective-permute-start.4 = (f32[4,2,32,128]{3,2,1,0:T(8,128)S(1)}, f32[4,2,32,128]{3,2,1,0:T(8,128)S(1)}, u32[]{:S(2)}, u32[]{:S(2)}) collective-permute-start(f32[4,2,32,128]{3,2,1,0:T(8,128)S(1)} %get-tuple-element.158), channel_id=1, source_target_pairs={{0,4},{2,6},{4,0},{5,9},{6,2},{7,11},{8,12},{9,5},{10,14},{11,7},{... | collective-permute-start | bytes 393224 | tf_op jit(solution)/shard_map/ppermute | solution.py:355
  26.7 4.5 %collective-permute-start.6 = (f32[4,2,32,128]{3,2,1,0:T(8,128)S(1)}, f32[4,2,32,128]{3,2,1,0:T(8,128)S(1)}, u32[]{:S(2)}, u32[]{:S(2)}) collective-permute-start(f32[4,2,32,128]{3,2,1,0:T(8,128)S(1)} %get-tuple-element.165), channel_id=1, source_target_pairs={{1,5},{3,7},{4,8},{5,1},{6,10},{7,3},{8,4},{9,13},{10,6},{11,15},{... | collective-permute-start | bytes 393224 | tf_op jit(solution)/shard_map/ppermute | solution.py:355
  27.4 2.7 %copy-start = (f32[1,4,8]{2,1,0:T(4,128)S(1)}, f32[1,4,8]{2,1,0:T(4,128)}, u32[]{:S(2)}) copy-start(f32[1,4,8]{2,1,0:T(4,128)} %residual.7) | copy-start | bytes 388
  27.4 2.7 %copy-start.1 = (s32[1,4]{1,0:T(1,128)S(1)}, s32[1,4]{1,0:T(1,128)}, u32[]{:S(2)}) copy-start(s32[1,4]{1,0:T(1,128)} %rec_cell.3) | copy-start | bytes 52
  32.6 52.2 %collective-permute-start.20 = (f32[8,6,8,8,128]{4,3,2,1,0:T(8,128)S(1)}, f32[8,6,8,8,128]{4,3,2,1,0:T(8,128)S(1)}, u32[]{:S(2)}, u32[]{:S(2)}) collective-permute-start(f32[8,6,8,8,128]{4,3,2,1,0:T(8,128)S(1)} %multiply_add_fusion.refs_28_.refs_4_), channel_id=1, source_target_pairs={{0,2},{1,3},{2,0},{3,1},{4,6},{5,7},{6,4},{7,5},{8,10},{9,11},{10,... | collective-permute-start | bytes 4718600 | tf_op jit(solution)/shard_map/ppermute | solution.py:339
  33.7 9.3 %collective-permute-start.8 = (bf16[15,32,128]{2,1,0:T(8,128)(2,1)S(1)}, bf16[15,32,128]{2,1,0:T(8,128)(2,1)S(1)}, u32[]{:S(2)}, u32[]{:S(2)}) collective-permute-start(bf16[15,32,128]{2,1,0:T(8,128)(2,1)S(1)} %get-tuple-element.180), channel_id=1, source_target_pairs={{1,5},{3,7},{4,8},{5,1},{6,10},{7,3},{8,4},{9,13},{10,6},{11,15},{... | collective-permute-start | bytes 368648 | tf_op jit(solution)/shard_map/ppermute | solution.py:355
  34.3 11.6 %collective-permute-start.5 = (bf16[15,32,128]{2,1,0:T(8,128)(2,1)S(1)}, bf16[15,32,128]{2,1,0:T(8,128)(2,1)S(1)}, u32[]{:S(2)}, u32[]{:S(2)}) collective-permute-start(bf16[15,32,128]{2,1,0:T(8,128)(2,1)S(1)} %get-tuple-element.160), channel_id=1, source_target_pairs={{0,4},{2,6},{4,0},{5,9},{6,2},{7,11},{8,12},{9,5},{10,14},{11,7},{... | collective-permute-start | bytes 368648 | tf_op jit(solution)/shard_map/ppermute | solution.py:355
  43.4 8.6 %collective-permute-start.10 = (bf16[15,32,128]{2,1,0:T(8,128)(2,1)S(1)}, bf16[15,32,128]{2,1,0:T(8,128)(2,1)S(1)}, u32[]{:S(2)}, u32[]{:S(2)}) collective-permute-start(bf16[15,32,128]{2,1,0:T(8,128)(2,1)S(1)} %get-tuple-element.192), channel_id=1, source_target_pairs={{1,5},{3,7},{4,8},{5,1},{6,10},{7,3},{8,4},{9,13},{10,6},{11,15},{... | collective-permute-start | bytes 368648 | tf_op jit(solution)/shard_map/ppermute | solution.py:355
  46.4 8.7 %collective-permute-start.7 = (bf16[15,32,128]{2,1,0:T(8,128)(2,1)S(1)}, bf16[15,32,128]{2,1,0:T(8,128)(2,1)S(1)}, u32[]{:S(2)}, u32[]{:S(2)}) collective-permute-start(bf16[15,32,128]{2,1,0:T(8,128)(2,1)S(1)} %get-tuple-element.177), channel_id=1, source_target_pairs={{0,4},{2,6},{4,0},{5,9},{6,2},{7,11},{8,12},{9,5},{10,14},{11,7},{... | collective-permute-start | bytes 368648 | tf_op jit(solution)/shard_map/ppermute | solution.py:355
  52.5 7.0 %collective-permute-start.12 = (bf16[15,32,128]{2,1,0:T(8,128)(2,1)S(1)}, bf16[15,32,128]{2,1,0:T(8,128)(2,1)S(1)}, u32[]{:S(2)}, u32[]{:S(2)}) collective-permute-start(bf16[15,32,128]{2,1,0:T(8,128)(2,1)S(1)} %get-tuple-element.202), channel_id=1, source_target_pairs={{1,5},{3,7},{4,8},{5,1},{6,10},{7,3},{8,4},{9,13},{10,6},{11,15},{... | collective-permute-start | bytes 368648 | tf_op jit(solution)/shard_map/ppermute | solution.py:355
  55.6 6.8 %collective-permute-start.9 = (bf16[15,32,128]{2,1,0:T(8,128)(2,1)S(1)}, bf16[15,32,128]{2,1,0:T(8,128)(2,1)S(1)}, u32[]{:S(2)}, u32[]{:S(2)}) collective-permute-start(bf16[15,32,128]{2,1,0:T(8,128)(2,1)S(1)} %get-tuple-element.189), channel_id=1, source_target_pairs={{0,4},{2,6},{4,0},{5,9},{6,2},{7,11},{8,12},{9,5},{10,14},{11,7},{... | collective-permute-start | bytes 368648 | tf_op jit(solution)/shard_map/ppermute | solution.py:355
  60.0 6.8 %collective-permute-start.14 = (bf16[15,32,128]{2,1,0:T(8,128)(2,1)S(1)}, bf16[15,32,128]{2,1,0:T(8,128)(2,1)S(1)}, u32[]{:S(2)}, u32[]{:S(2)}) collective-permute-start(bf16[15,32,128]{2,1,0:T(8,128)(2,1)S(1)} %get-tuple-element.212), channel_id=1, source_target_pairs={{1,5},{3,7},{4,8},{5,1},{6,10},{7,3},{8,4},{9,13},{10,6},{11,15},{... | collective-permute-start | bytes 368648 | tf_op jit(solution)/shard_map/ppermute | solution.py:355
  62.8 6.8 %collective-permute-start.11 = (bf16[15,32,128]{2,1,0:T(8,128)(2,1)S(1)}, bf16[15,32,128]{2,1,0:T(8,128)(2,1)S(1)}, u32[]{:S(2)}, u32[]{:S(2)}) collective-permute-start(bf16[15,32,128]{2,1,0:T(8,128)(2,1)S(1)} %get-tuple-element.199), channel_id=1, source_target_pairs={{0,4},{2,6},{4,0},{5,9},{6,2},{7,11},{8,12},{9,5},{10,14},{11,7},{... | collective-permute-start | bytes 368648 | tf_op jit(solution)/shard_map/ppermute | solution.py:355
  67.3 6.8 %collective-permute-start.16 = (bf16[15,32,128]{2,1,0:T(8,128)(2,1)S(1)}, bf16[15,32,128]{2,1,0:T(8,128)(2,1)S(1)}, u32[]{:S(2)}, u32[]{:S(2)}) collective-permute-start(bf16[15,32,128]{2,1,0:T(8,128)(2,1)S(1)} %get-tuple-element.222), channel_id=1, source_target_pairs={{1,5},{3,7},{4,8},{5,1},{6,10},{7,3},{8,4},{9,13},{10,6},{11,15},{... | collective-permute-start | bytes 368648 | tf_op jit(solution)/shard_map/ppermute | solution.py:355
  70.1 6.8 %collective-permute-start.13 = (bf16[15,32,128]{2,1,0:T(8,128)(2,1)S(1)}, bf16[15,32,128]{2,1,0:T(8,128)(2,1)S(1)}, u32[]{:S(2)}, u32[]{:S(2)}) collective-permute-start(bf16[15,32,128]{2,1,0:T(8,128)(2,1)S(1)} %get-tuple-element.209), channel_id=1, source_target_pairs={{0,4},{2,6},{4,0},{5,9},{6,2},{7,11},{8,12},{9,5},{10,14},{11,7},{... | collective-permute-start | bytes 368648 | tf_op jit(solution)/shard_map/ppermute | solution.py:355
  74.5 6.8 %collective-permute-start.18 = (bf16[15,32,128]{2,1,0:T(8,128)(2,1)S(1)}, bf16[15,32,128]{2,1,0:T(8,128)(2,1)S(1)}, u32[]{:S(2)}, u32[]{:S(2)}) collective-permute-start(bf16[15,32,128]{2,1,0:T(8,128)(2,1)S(1)} %get-tuple-element.232), channel_id=1, source_target_pairs={{1,5},{3,7},{4,8},{5,1},{6,10},{7,3},{8,4},{9,13},{10,6},{11,15},{... | collective-permute-start | bytes 368648 | tf_op jit(solution)/shard_map/ppermute | solution.py:355
  77.3 6.8 %collective-permute-start.15 = (bf16[15,32,128]{2,1,0:T(8,128)(2,1)S(1)}, bf16[15,32,128]{2,1,0:T(8,128)(2,1)S(1)}, u32[]{:S(2)}, u32[]{:S(2)}) collective-permute-start(bf16[15,32,128]{2,1,0:T(8,128)(2,1)S(1)} %get-tuple-element.219), channel_id=1, source_target_pairs={{0,4},{2,6},{4,0},{5,9},{6,2},{7,11},{8,12},{9,5},{10,14},{11,7},{... | collective-permute-start | bytes 368648 | tf_op jit(solution)/shard_map/ppermute | solution.py:355
  84.8 15.5 %collective-permute-start.21 = (f32[8,6,8,8,128]{4,3,2,1,0:T(8,128)S(1)}, f32[8,6,8,8,128]{4,3,2,1,0:T(8,128)S(1)}, u32[]{:S(2)}, u32[]{:S(2)}) collective-permute-start(f32[8,6,8,8,128]{4,3,2,1,0:T(8,128)S(1)} %multiply_add_fusion.refs_28_.refs_4_), channel_id=1, source_target_pairs={{0,1},{1,0},{2,3},{3,2},{4,5},{5,4},{6,7},{7,6},{8,9},{9,8},{10,11... | collective-permute-start | bytes 4718600 | tf_op jit(solution)/shard_map/ppermute | solution.py:339
  84.9 15.4 %collective-permute-start.22 = (f32[8,6,8,8,128]{4,3,2,1,0:T(8,128)S(1)}, f32[8,6,8,8,128]{4,3,2,1,0:T(8,128)S(1)}, u32[]{:S(2)}, u32[]{:S(2)}) collective-permute-start(f32[8,6,8,8,128]{4,3,2,1,0:T(8,128)S(1)} %collective-permute-done.20.refs_30_.refs_6_), channel_id=1, source_target_pairs={{0,1},{1,0},{2,3},{3,2},{4,5},{5,4},{6,7},{7,6},{8,9},{9,8},{10,11... | collective-permute-start | bytes 4718600 | tf_op jit(solution)/shard_map/ppermute | solution.py:339
  85.4 6.0 %collective-permute-start.19 = (bf16[15,32,128]{2,1,0:T(8,128)(2,1)S(1)}, bf16[15,32,128]{2,1,0:T(8,128)(2,1)S(1)}, u32[]{:S(2)}, u32[]{:S(2)}) collective-permute-start(bf16[15,32,128]{2,1,0:T(8,128)(2,1)S(1)} %get-tuple-element.239), channel_id=1, source_target_pairs={{1,5},{3,7},{4,8},{5,1},{6,10},{7,3},{8,4},{9,13},{10,6},{11,15},{... | collective-permute-start | bytes 368648 | tf_op jit(solution)/shard_map/ppermute | solution.py:355
  86.0 8.2 %collective-permute-start.17 = (bf16[15,32,128]{2,1,0:T(8,128)(2,1)S(1)}, bf16[15,32,128]{2,1,0:T(8,128)(2,1)S(1)}, u32[]{:S(2)}, u32[]{:S(2)}) collective-permute-start(bf16[15,32,128]{2,1,0:T(8,128)(2,1)S(1)} %get-tuple-element.229), channel_id=1, source_target_pairs={{0,4},{2,6},{4,0},{5,9},{6,2},{7,11},{8,12},{9,5},{10,14},{11,7},{... | collective-permute-start | bytes 368648 | tf_op jit(solution)/shard_map/ppermute | solution.py:355
  92.3 9.7 %collective-permute-start.24 = (bf16[15,32,128]{2,1,0:T(8,128)(2,1)S(1)}, bf16[15,32,128]{2,1,0:T(8,128)(2,1)S(1)}, u32[]{:S(2)}, u32[]{:S(2)}) collective-permute-start(bf16[15,32,128]{2,1,0:T(8,128)(2,1)S(1)} %get-tuple-element.284), channel_id=1, source_target_pairs={{1,5},{3,7},{4,8},{5,1},{6,10},{7,3},{8,4},{9,13},{10,6},{11,15},{... | collective-permute-start | bytes 368648 | tf_op jit(solution)/shard_map/ppermute | solution.py:355
  95.2 7.7 %collective-permute-start.23 = (bf16[15,32,128]{2,1,0:T(8,128)(2,1)S(1)}, bf16[15,32,128]{2,1,0:T(8,128)(2,1)S(1)}, u32[]{:S(2)}, u32[]{:S(2)}) collective-permute-start(bf16[15,32,128]{2,1,0:T(8,128)(2,1)S(1)} %get-tuple-element.281), channel_id=1, source_target_pairs={{0,4},{2,6},{4,0},{5,9},{6,2},{7,11},{8,12},{9,5},{10,14},{11,7},{... | collective-permute-start | bytes 368648 | tf_op jit(solution)/shard_map/ppermute | solution.py:355
  103.9 1.4 %collective-permute-start.25 = (f32[2,2,8,8,128]{4,3,2,1,0:T(8,128)S(1)}, f32[2,2,8,8,128]{4,3,2,1,0:T(8,128)S(1)}, u32[]{:S(2)}, u32[]{:S(2)}) collective-permute-start(f32[2,2,8,8,128]{4,3,2,1,0:T(8,128)S(1)} %pad_maximum_fusion.4), channel_id=1, source_target_pairs={{0,1},{1,0},{2,3},{3,2},{4,5},{5,4},{6,7},{7,6},{8,9},{9,8},{10,11... | collective-permute-start | bytes 393224 | tf_op jit(solution)/shard_map/ppermute | solution.py:339
  105.3 4.2 %collective-permute-start.27 = (f32[2,4,8,128]{3,2,1,0:T(8,128)S(1)}, f32[2,4,8,128]{3,2,1,0:T(8,128)S(1)}, u32[]{:S(2)}, u32[]{:S(2)}) collective-permute-start(f32[2,4,8,128]{3,2,1,0:T(8,128)S(1)} %dynamic-slice_bitcast_fusion.5), channel_id=1, source_target_pairs={{0,16},{1,17},{2,18},{3,19},{16,0},{17,1},{18,2},{19,3},{4,20},{5,... | collective-permute-start | bytes 98312 | tf_op jit(solution)/shard_map/ppermute | solution.py:485
  105.9 4.9 %collective-permute-start.26 = (f32[2,4,8,128]{3,2,1,0:T(8,128)S(1)}, f32[2,4,8,128]{3,2,1,0:T(8,128)S(1)}, u32[]{:S(2)}, u32[]{:S(2)}) collective-permute-start(f32[2,4,8,128]{3,2,1,0:T(8,128)S(1)} %get-tuple-element.297), channel_id=1, source_target_pairs={{0,18},{1,19},{2,16},{3,17},{16,2},{17,3},{18,0},{19,1},{4,22},{5,... | collective-permute-start | bytes 98312 | tf_op jit(solution)/shard_map/ppermute | solution.py:485
  107.9 3.9 %collective-permute-start.28 = (f32[2,4,8,128]{3,2,1,0:T(8,128)S(1)}, f32[2,4,8,128]{3,2,1,0:T(8,128)S(1)}, u32[]{:S(2)}, u32[]{:S(2)}) collective-permute-start(f32[2,4,8,128]{3,2,1,0:T(8,128)S(1)} %get-tuple-element.298), channel_id=1, source_target_pairs={{0,2},{1,3},{2,0},{3,1},{16,18},{17,19},{18,16},{19,17},{4,6},{5,7... | collective-permute-start | bytes 98312 | tf_op jit(solution)/shard_map/ppermute | solution.py:485

commit v7 on v5

--- a/solution.py
+++ b/solution.py
@@ -17,7 +17,7 @@
 REACH = 2
 DEEP = 2 * REACH
 ALONG_X = (0, 3, 4)
-NEAR_ROWS = 2
+NEAR_ROWS = 1
 PACKED = DEEP + NEAR_ROWS
 
 VMEM = pl.BlockSpec(memory_space=pltpu.VMEM)
@@ -307,30 +307,32 @@
                     middles_out[side][comp, out] = value
 
 
-def correlate(moments, pieces, residual, *refs):
-    count = len(moments)
-    rates, sources, before, terms = refs[: 4 * count], refs[4 * count], refs[4 * count + 1 : -1], refs[-1]
-    tile_x, tile_y = sources.shape[3:5]
+def correlate(jobs, moments, residual, *refs):
+    count = 4 * moments
+    rates, sources, before, terms = refs[:count], refs[count : count + len(jobs)], refs[count + len(jobs) : -1], refs[-1]
+    tile_x, tile_y = sources[0].shape[2:4]
     _, me, flip = position()
     sign = sign_of(flip)
-    for turn in range(pieces):
+    for job, turn in enumerate(jobs):
         spot = pl.ds(pl.multiple_of((me ^ turn) * tile_y, tile_y), tile_y)
         for side in range(2):
             for out in range(DEEP):
                 row = row_of(flip, side, out, tile_x)
-                lam, mu = (before[0][turn, 0, row], before[0][turn, 1, row]) if before else (0.0, 0.0)
-                for at, moment in enumerate(moments):
+                lam = mu = 0.0
+                if before and job < before[0].shape[0]:
+                    lam, mu = before[0][job, 0, row], before[0][job, 1, row]
+                for moment in jobs[turn]:
                     weight = (KERNEL_SCALE / UNIT) * residual[0, me, moment]
-                    held = rates[4 * at + 2 * (out // REACH) + side]
+                    held = rates[4 * moment + 2 * (out // REACH) + side]
                     rate = [held[c, out % REACH, spot, :] for c in range(6)]
-                    source = [sources[me ^ turn, moment, c, row] for c in range(6)]
+                    source = [sources[job][moment, c, row] for c in range(6)]
                     bulk = (source[0] + source[1] + source[2]) * (rate[0] + rate[1] + rate[2])
                     diag = source[0] * rate[0] + source[1] * rate[1] + source[2] * rate[2]
                     off = sign * (source[3] * rate[3] + source[4] * rate[4]) + source[5] * rate[5]
                     lam = lam + weight * bulk
                     mu = mu + (2.0 * weight) * (diag + off)
-                terms[turn, 0, row] = lam
-                terms[turn, 1, row] = mu
+                terms[job, 0, row] = lam
+                terms[job, 1, row] = mu
 
 
 def swap(array, axis, turn):
@@ -393,7 +395,9 @@
     for turn in range(groups):
         factor = jnp.sum(weights * (src_pick == (group ^ turn)).astype(F32), 0)
         combined = combined + factor[:, None, None, None, None] * strains[turn].astype(F32)
-    gathered = lax.all_gather(combined, "gy", axis=0)
+    combined, halos = lax.optimization_barrier((combined, halos))
+    found = {turn: swap(combined, "gy", turn) for turn in range(pieces - 1, 0, -1) if turn & (turn - 1) == 0}
+    found[0] = combined
 
     sent, lights, lames, shears, old_halos, spots, amounts = ([None, None] for _ in range(7))
     fresh = [None, None]
@@ -423,11 +427,19 @@
         rates += results[:2]
         if not last:
             middles = results[2:]
+        if moment == 3 * moments // 4:
+            ready, rates[-1] = lax.optimization_barrier((found, rates[-1]))
+            for turn in range(pieces):
+                if turn not in found:
+                    low = turn & -turn
+                    found[turn] = swap(ready[turn ^ low], "gy", low)
         if last:
+            early, late = list(range(pieces)), []
+            jobs = {turn: list(range(moment)) for turn in early}
             (terms,) = call(
-                functools.partial(correlate, list(range(moment)), pieces),
-                [((pieces, 2, tile_x, tile_y, depth), F32)],
-                ([residual], rates[: 4 * moment] + [gathered]),
+                functools.partial(correlate, jobs, moment),
+                [((len(jobs), 2, tile_x, tile_y, depth), F32)],
+                ([residual], rates[: 4 * moment] + [found[turn] for turn in jobs]),
             )
             terms, vels = lax.optimization_barrier((terms, vels))
         fresh = [None, None]
@@ -445,12 +457,13 @@
                 sent[side] = to_neighbour(results[4], side)
         vels = fresh
 
+    jobs = {turn: [moments - 1] if turn in early else list(range(moments)) for turn in early + late}
     (terms,) = call(
-        functools.partial(correlate, [moments - 1], pieces),
+        functools.partial(correlate, jobs, moments),
         [((pieces, 2, tile_x, tile_y, depth), F32)],
-        ([residual], rates[-4:] + [gathered, terms]),
+        ([residual], rates + [found[turn] for turn in jobs] + [terms]),
     )
-    held = {turn: terms[turn] for turn in range(pieces)}
+    held = {turn: terms[at] for at, turn in enumerate(jobs)}
     if pieces > 1:
         keep = [turn for turn in held if not turn & 1]
         got = swap(jnp.stack([held[turn ^ 1] for turn in keep]), "gy", 1)

time: 148 us -> 126 us (0.85)
  between operations: 14 us -> 0.55 us
  local copies, waits for them, and re-layouts: 25.6 us -> 14.7 us
  starting transfers between devices: 54.3 us -> 58 us
    unnamed x85 -> x49, local copies, waits for them, and re-layouts: 24.3 us -> 13.3 us
    ppermute x5 -> x8, starting transfers between devices: 5.01 us -> 7.74 us  [swap(): return lax.ppermute(array, axis, [(i, i ^ turn) for i in range(count)])]
    ppermute x18, waiting for transfers between devices: 12.2 us -> 14 us  [to_neighbour(): return lax.ppermute(face, ('gx', 'gy'), pairs)]
    ppermute x5 -> x8, waiting for transfers between devices: 16.3 us -> 16.2 us  [swap(): return lax.ppermute(array, axis, [(i, i ^ turn) for i in range(count)])]
  transfers between devices with their start and end apart: 27 -> 29, of which waited for: 15 -> 14; matrix products, arithmetic and copies ran while one was open for 0% -> 2% of each run, Pallas kernels for 10% -> 12%
where the time goes in v7:
time: 126 us; the launch traced here: 125 us
  starting transfers between devices  58 us (46%)
  waiting for transfers between devices  33.1 us (26%)
  Pallas kernels  16.6 us (13%)
  local copies, waits for them, and re-layouts  14.7 us (12%)
  other arithmetic  2.34 us (2%)
    ppermute x18, starting transfers between devices, to_neighbour(): return lax.ppermute(face, ('gx', 'gy'), pairs)  46.7 us
    pallas_call x29, Pallas kernels, call(): pl.pallas_call(body, out_shape=[jax.ShapeDtypeStruct(shape, kind) for sha...  16.6 us
    ppermute x8, waiting for transfers between devices, swap(): return lax.ppermute(array, axis, [(i, i ^ turn) for i in range(count)])  16.2 us
    ppermute x18, waiting for transfers between devices, to_neighbour(): return lax.ppermute(face, ('gx', 'gy'), pairs)  14 us
    unnamed x49, local copies, waits for them, and re-layouts  13.3 us
    ppermute x8, starting transfers between devices, swap(): return lax.ppermute(array, axis, [(i, i ^ turn) for i in range(count)])  7.74 us
    ppermute x3, starting transfers between devices, local(): part = lax.ppermute(part, ('sta', 'gy'), pairs)  3.55 us
    ppermute x3, waiting for transfers between devices, local(): part = lax.ppermute(part, ('sta', 'gy'), pairs)  2.88 us
  transfers between devices with their start and end apart: 29, of which 14 were waited for; matrix products, arithmetic and copies ran while one was open for 2% of the time, Pallas kernels for 12%

profile of v7, /device:TPU:0, one launch (start us, length us, event | category | flops | bytes accessed | tf_op | source)
XLA Modules:
  0.0 125.3 jit_solution(2626444043584410852)
XLA Ops:
  0.0 1.4 %dynamic-slice_bitcast_fusion = (f32[9,8,8,128]{3,2,1,0:T(8,128)S(1)}, f32[9,8,8,128]{3,2,1,0:T(8,128)S(1)}, f32[9,8,8,128]{3,2,1,0:T(8,128)S(1)}, f32[9,8,8,128]{3,2,1,0:T(8,128)S(1)}) fusion(f32[1,4,9,8,8,128]{5,4,3,2,1,0:T(8,128)} %param.8, s32[]{:T(128)S(6)} %select_n.27, s32[]{:T(128)S(6)} %select_n.25, s32[]{:T(128)S(6)} %select_n.24, s32[]{:T(128)S(6)} %select_n.26), kind=kLoop, calls=%fused_computation.5 | loop fusion | bytes 2359312 | tf_op jit(solution)/shard_map/jit(dynamic_index_in_dim)/squeeze | solution.py:371
  1.5 2.9 %collective-permute-start.3 = (bf16[8,6,8,8,128]{4,3,2,1,0:T(8,128)(2,1)S(1)}, bf16[8,6,8,8,128]{4,3,2,1,0:T(8,128)(2,1)}, u32[]{:S(2)}, u32[]{:S(2)}) collective-permute-start(bf16[8,6,8,8,128]{4,3,2,1,0:T(8,128)(2,1)S(1)} %bitcast.20), channel_id=1, source_target_pairs={{0,16},{16,0},{1,17},{17,1},{2,18},{18,2},{3,19},{19,3},{4,20},{20... | collective-permute-start | bytes 2359304 | tf_op jit(solution)/shard_map/ppermute | solution.py:340
  4.6 0.7 collective-permute-start.2
  5.3 1.0 collective-permute-start
  6.8 7.7 %collective-permute-done.2.refs_3_ = f32[10,8,8,128]{3,2,1,0:T(8,128)S(1)} collective-permute-done((f32[10,8,8,128]{3,2,1,0:T(8,128)S(1)}, f32[10,8,8,128]{3,2,1,0:T(8,128)S(1)}, u32[]{:S(2)}, u32[]{:S(2)}) %collective-permute-start.2) | collective-permute-done | bytes 327712 | tf_op jit(solution)/shard_map/ppermute | solution.py:340
  14.6 7.1 %collective-permute-done.1.refs_2_ = f32[10,8,8,128]{3,2,1,0:T(8,128)S(1)} collective-permute-done((f32[10,8,8,128]{3,2,1,0:T(8,128)S(1)}, f32[10,8,8,128]{3,2,1,0:T(8,128)S(1)}, u32[]{:S(2)}, u32[]{:S(2)}) %collective-permute-start.1) | collective-permute-done | bytes 327712 | tf_op jit(solution)/shard_map/ppermute | solution.py:340
  21.7 0.7 shard_map.82
  23.1 0.7 copy-done.3
  26.3 3.5 %collective-permute-start.4 = (f32[4,2,32,128]{3,2,1,0:T(8,128)S(1)}, f32[4,2,32,128]{3,2,1,0:T(8,128)S(1)}, u32[]{:S(2)}, u32[]{:S(2)}) collective-permute-start(f32[4,2,32,128]{3,2,1,0:T(8,128)S(1)} %get-tuple-element.160), channel_id=1, source_target_pairs={{0,4},{2,6},{4,0},{5,9},{6,2},{7,11},{8,12},{9,5},{10,14},{11,7},{... | collective-permute-start | bytes 393224 | tf_op jit(solution)/shard_map/ppermute | solution.py:356
  30.5 1.5 %multiply_add_fusion.refs_28_.refs_32_ = f32[8,6,8,8,128]{4,3,2,1,0:T(8,128)S(1)} fusion(bf16[8,6,8,8,128]{4,3,2,1,0:T(8,128)(2,1)} %collective-permute-done.3, bf16[8,6,8,8,128]{4,3,2,1,0:T(8,128)(2,1)S(1)} %bitcast.21, f32[8]{0:T(128)S(1)} %get-tuple-element.288, f32[8]{0:T(128)S(1)} %get-tuple-element.287), kind=kLoop, calls=%fused_computation | loop fusion | flops 1966080 | bytes 3145792 | tf_op jit(solution)/shard_map/add | solution.py:397
  32.0 1.1 collective-permute-done.4.halo
  34.5 1.0 collective-permute-start.19
  35.5 1.5 %collective-permute-start.18 = (f32[8,6,8,8,128]{4,3,2,1,0:T(8,128)S(1)}, f32[8,6,8,8,128]{4,3,2,1,0:T(8,128)}, u32[]{:S(2)}, u32[]{:S(2)}) collective-permute-start(f32[8,6,8,8,128]{4,3,2,1,0:T(8,128)S(1)} %multiply_add_fusion.refs_28_.refs_32_), channel_id=1, source_target_pairs={{0,1},{1,0},{2,3},{3,2},{4,5},{5,4},{6,7},{7,6},{8,9},{9,8},{10,11... | collective-permute-start | bytes 4718600 | tf_op jit(solution)/shard_map/ppermute | solution.py:340
  36.9 0.8 copy.9.table
  37.7 0.9 copy-done.4
  38.6 0.9 copy-done.9
  39.6 0.9 copy-done.13
  40.5 0.8 copy-done.17
  41.3 1.1 shard_map.84
  43.1 0.9 copy-done.1
  44.0 0.9 copy-done.7
  45.0 0.9 copy-done.11
  45.9 0.8 copy-done.15
  46.7 1.1 shard_map.83
  47.8 7.8 %collective-permute-start.6 = (bf16[15,32,128]{2,1,0:T(8,128)(2,1)S(1)}, bf16[15,32,128]{2,1,0:T(8,128)(2,1)S(1)}, u32[]{:S(2)}, u32[]{:S(2)}) collective-permute-start(bf16[15,32,128]{2,1,0:T(8,128)(2,1)S(1)} %get-tuple-element.175), channel_id=1, source_target_pairs={{0,4},{2,6},{4,0},{5,9},{6,2},{7,11},{8,12},{9,5},{10,14},{11,7},{... | collective-permute-start | bytes 368648 | tf_op jit(solution)/shard_map/ppermute | solution.py:356
  57.1 1.5 %collective-permute-done.6.halo = bf16[15,32,128]{2,1,0:T(8,128)(2,1)S(1)} collective-permute-done((bf16[15,32,128]{2,1,0:T(8,128)(2,1)S(1)}, bf16[15,32,128]{2,1,0:T(8,128)(2,1)S(1)}, u32[]{:S(2)}, u32[]{:S(2)}) %collective-permute-start.6) | collective-permute-done | bytes 122912 | tf_op jit(solution)/shard_map/ppermute | solution.py:356
  59.0 3.9 %collective-permute-start.8 = (bf16[15,32,128]{2,1,0:T(8,128)(2,1)S(1)}, bf16[15,32,128]{2,1,0:T(8,128)(2,1)S(1)}, u32[]{:S(2)}, u32[]{:S(2)}) collective-permute-start(bf16[15,32,128]{2,1,0:T(8,128)(2,1)S(1)} %get-tuple-element.193), channel_id=1, source_target_pairs={{0,4},{2,6},{4,0},{5,9},{6,2},{7,11},{8,12},{9,5},{10,14},{11,7},{... | collective-permute-start | bytes 368648 | tf_op jit(solution)/shard_map/ppermute | solution.py:356
  64.3 1.5 %collective-permute-done.8.halo = bf16[15,32,128]{2,1,0:T(8,128)(2,1)S(1)} collective-permute-done((bf16[15,32,128]{2,1,0:T(8,128)(2,1)S(1)}, bf16[15,32,128]{2,1,0:T(8,128)(2,1)S(1)}, u32[]{:S(2)}, u32[]{:S(2)}) %collective-permute-start.8) | collective-permute-done | bytes 122912 | tf_op jit(solution)/shard_map/ppermute | solution.py:356
  66.2 4.2 %collective-permute-start.10 = (bf16[15,32,128]{2,1,0:T(8,128)(2,1)S(1)}, bf16[15,32,128]{2,1,0:T(8,128)(2,1)S(1)}, u32[]{:S(2)}, u32[]{:S(2)}) collective-permute-start(bf16[15,32,128]{2,1,0:T(8,128)(2,1)S(1)} %get-tuple-element.207), channel_id=1, source_target_pairs={{0,4},{2,6},{4,0},{5,9},{6,2},{7,11},{8,12},{9,5},{10,14},{11,7},{... | collective-permute-start | bytes 368648 | tf_op jit(solution)/shard_map/ppermute | solution.py:356
  71.7 2.4 %collective-permute-done.10.halo = bf16[15,32,128]{2,1,0:T(8,128)(2,1)S(1)} collective-permute-done((bf16[15,32,128]{2,1,0:T(8,128)(2,1)S(1)}, bf16[15,32,128]{2,1,0:T(8,128)(2,1)S(1)}, u32[]{:S(2)}, u32[]{:S(2)}) %collective-permute-start.10) | collective-permute-done | bytes 122912 | tf_op jit(solution)/shard_map/ppermute | solution.py:356
  74.5 4.1 %collective-permute-start.12 = (bf16[15,32,128]{2,1,0:T(8,128)(2,1)S(1)}, bf16[15,32,128]{2,1,0:T(8,128)(2,1)S(1)}, u32[]{:S(2)}, u32[]{:S(2)}) collective-permute-start(bf16[15,32,128]{2,1,0:T(8,128)(2,1)S(1)} %get-tuple-element.221), channel_id=1, source_target_pairs={{0,4},{2,6},{4,0},{5,9},{6,2},{7,11},{8,12},{9,5},{10,14},{11,7},{... | collective-permute-start | bytes 368648 | tf_op jit(solution)/shard_map/ppermute | solution.py:356
  80.1 2.2 %collective-permute-done.12.halo = bf16[15,32,128]{2,1,0:T(8,128)(2,1)S(1)} collective-permute-done((bf16[15,32,128]{2,1,0:T(8,128)(2,1)S(1)}, bf16[15,32,128]{2,1,0:T(8,128)(2,1)S(1)}, u32[]{:S(2)}, u32[]{:S(2)}) %collective-permute-start.12) | collective-permute-done | bytes 122912 | tf_op jit(solution)/shard_map/ppermute | solution.py:356
  82.7 3.6 %collective-permute-start.14 = (bf16[15,32,128]{2,1,0:T(8,128)(2,1)S(1)}, bf16[15,32,128]{2,1,0:T(8,128)(2,1)S(1)}, u32[]{:S(2)}, u32[]{:S(2)}) collective-permute-start(bf16[15,32,128]{2,1,0:T(8,128)(2,1)S(1)} %get-tuple-element.235), channel_id=1, source_target_pairs={{0,4},{2,6},{4,0},{5,9},{6,2},{7,11},{8,12},{9,5},{10,14},{11,7},{... | collective-permute-start | bytes 368648 | tf_op jit(solution)/shard_map/ppermute | solution.py:356
  87.8 1.7 %collective-permute-done.14.halo = bf16[15,32,128]{2,1,0:T(8,128)(2,1)S(1)} collective-permute-done((bf16[15,32,128]{2,1,0:T(8,128)(2,1)S(1)}, bf16[15,32,128]{2,1,0:T(8,128)(2,1)S(1)}, u32[]{:S(2)}, u32[]{:S(2)}) %collective-permute-start.14) | collective-permute-done | bytes 122912 | tf_op jit(solution)/shard_map/ppermute | solution.py:356
  90.0 3.6 %collective-permute-start.16 = (bf16[15,32,128]{2,1,0:T(8,128)(2,1)S(1)}, bf16[15,32,128]{2,1,0:T(8,128)(2,1)S(1)}, u32[]{:S(2)}, u32[]{:S(2)}) collective-permute-start(bf16[15,32,128]{2,1,0:T(8,128)(2,1)S(1)} %get-tuple-element.249), channel_id=1, source_target_pairs={{0,4},{2,6},{4,0},{5,9},{6,2},{7,11},{8,12},{9,5},{10,14},{11,7},{... | collective-permute-start | bytes 368648 | tf_op jit(solution)/shard_map/ppermute | solution.py:356
  94.3 2.4 %collective-permute-done.16.halo = bf16[15,32,128]{2,1,0:T(8,128)(2,1)S(1)} collective-permute-done((bf16[15,32,128]{2,1,0:T(8,128)(2,1)S(1)}, bf16[15,32,128]{2,1,0:T(8,128)(2,1)S(1)}, u32[]{:S(2)}, u32[]{:S(2)}) %collective-permute-start.16) | collective-permute-done | bytes 122912 | tf_op jit(solution)/shard_map/ppermute | solution.py:356
  98.2 5.0 %collective-permute-start.20 = (bf16[15,32,128]{2,1,0:T(8,128)(2,1)S(1)}, bf16[15,32,128]{2,1,0:T(8,128)(2,1)S(1)}, u32[]{:S(2)}, u32[]{:S(2)}) collective-permute-start(bf16[15,32,128]{2,1,0:T(8,128)(2,1)S(1)} %get-tuple-element.265), channel_id=1, source_target_pairs={{0,4},{2,6},{4,0},{5,9},{6,2},{7,11},{8,12},{9,5},{10,14},{11,7},{... | collective-permute-start | bytes 368648 | tf_op jit(solution)/shard_map/ppermute | solution.py:356
  103.2 0.9 shard_map.105
  104.8 1.2 collective-permute-done.20.halo
  106.1 0.9 shard_map.104
  107.0 4.8 %collective-permute-start.23 = (bf16[15,32,128]{2,1,0:T(8,128)(2,1)S(1)}, bf16[15,32,128]{2,1,0:T(8,128)(2,1)S(1)}, u32[]{:S(2)}, u32[]{:S(2)}) collective-permute-start(bf16[15,32,128]{2,1,0:T(8,128)(2,1)S(1)} %get-tuple-element.281), channel_id=1, source_target_pairs={{0,4},{2,6},{4,0},{5,9},{6,2},{7,11},{8,12},{9,5},{10,14},{11,7},{... | collective-permute-start | bytes 368648 | tf_op jit(solution)/shard_map/ppermute | solution.py:356
  112.1 2.6 %shard_map.107.refs_36_ = f32[4,2,8,8,128]{4,3,2,1,0:T(8,128)S(1)} custom-call(f32[1,4,8]{2,1,0:T(4,128)S(1)} %copy-done.18, f32[6,2,32,128]{3,2,1,0:T(8,128)S(1)} %get-tuple-element.173.refs_0_, f32[6,2,32,128]{3,2,1,0:T(8,128)S(1)} %get-tuple-element.174.refs_1_, f32[6,2,32,128]{3,2,1,0:T(8,128)S(1)} %get-tuple-element.182.refs_2_, ...), custom_call_target="tpu_custom_call" | custom-call | flops 1000000 | bytes 2000000 | tf_op jit(solution)/shard_map/pallas_call | solution.py:30
  115.1 1.6 %shard_map.110 = f32[4,2,8,8,128]{4,3,2,1,0:T(8,128)S(1)} custom-call(f32[1,4,8]{2,1,0:T(4,128)S(1)} %copy-done.18, f32[6,2,32,128]{3,2,1,0:T(8,128)S(1)} %get-tuple-element.173.refs_0_, f32[6,2,32,128]{3,2,1,0:T(8,128)S(1)} %get-tuple-element.174.refs_1_, f32[6,2,32,128]{3,2,1,0:T(8,128)S(1)} %get-tuple-element.182.refs_2_, ...), custom_call_target="tpu_custom_call" | custom-call | flops 1000000 | bytes 2000000 | tf_op jit(solution)/shard_map/pallas_call | solution.py:30
  116.9 1.3 %collective-permute-done.25 = f32[2,2,8,8,128]{4,3,2,1,0:T(8,128)S(1)} collective-permute-done((f32[2,2,8,8,128]{4,3,2,1,0:T(8,128)S(1)}, f32[2,2,8,8,128]{4,3,2,1,0:T(8,128)S(1)}, u32[]{:S(2)}, u32[]{:S(2)}) %collective-permute-start.25) | collective-permute-done | bytes 131104 | tf_op jit(solution)/shard_map/ppermute | solution.py:340
  118.8 1.9 %collective-permute-start.26 = (f32[2,4,8,128]{3,2,1,0:T(8,128)S(1)}, f32[2,4,8,128]{3,2,1,0:T(8,128)S(1)}, u32[]{:S(2)}, u32[]{:S(2)}) collective-permute-start(f32[2,4,8,128]{3,2,1,0:T(8,128)S(1)} %get-tuple-element.297), channel_id=1, source_target_pairs={{0,18},{1,19},{2,16},{3,17},{16,2},{17,3},{18,0},{19,1},{4,22},{5,... | collective-permute-start | bytes 98312 | tf_op jit(solution)/shard_map/ppermute | solution.py:482
  120.8 1.0 collective-permute-start.28
  122.4 1.2 collective-permute-done.26
  123.7 1.0 collective-permute-done.28
  (100 shorter events, 21.1 us)
Async XLA Ops:
  0.0 1.5 %copy-start.20 = (bf16[1,8,6,8,8,128]{5,4,3,2,1,0:T(8,128)(2,1)S(1)}, bf16[1,8,6,8,8,128]{5,4,3,2,1,0:T(8,128)(2,1)}, u32[]{:S(2)}) copy-start(bf16[1,8,6,8,8,128]{5,4,3,2,1,0:T(8,128)(2,1)} %param.9) | copy-start | bytes 2359300
  0.0 4.4 %copy-start.21 = (s32[8,8,128]{2,1,0:T(8,128)S(1)}, s32[8,8,128]{2,1,0:T(8,128)}, u32[]{:S(2)}) copy-start(s32[8,8,128]{2,1,0:T(8,128)} %param.10) | copy-start | bytes 98308
  1.4 5.4 %copy-start.23 = (s32[2,8,2]{1,2,0:T(2,128)S(1)}, s32[2,8,2]{1,2,0:T(2,128)}, u32[]{:S(2)}) copy-start(s32[2,8,2]{1,2,0:T(2,128)} %param.14) | copy-start | bytes 388
  1.4 5.4 %copy-start.22 = (s32[2,8]{1,0:T(2,128)S(1)}, s32[2,8]{1,0:T(2,128)}, u32[]{:S(2)}) copy-start(s32[2,8]{1,0:T(2,128)} %param.15) | copy-start | bytes 196
  1.5 29.0 %collective-permute-start.3 = (bf16[8,6,8,8,128]{4,3,2,1,0:T(8,128)(2,1)S(1)}, bf16[8,6,8,8,128]{4,3,2,1,0:T(8,128)(2,1)}, u32[]{:S(2)}, u32[]{:S(2)}) collective-permute-start(bf16[8,6,8,8,128]{4,3,2,1,0:T(8,128)(2,1)S(1)} %bitcast.20), channel_id=1, source_target_pairs={{0,16},{16,0},{1,17},{17,1},{2,18},{18,2},{3,19},{19,3},{4,20},{20... | collective-permute-start | bytes 2359304 | tf_op jit(solution)/shard_map/ppermute | solution.py:340
  4.6 10.0 %collective-permute-start.2 = (f32[10,8,8,128]{3,2,1,0:T(8,128)S(1)}, f32[10,8,8,128]{3,2,1,0:T(8,128)S(1)}, u32[]{:S(2)}, u32[]{:S(2)}) collective-permute-start(f32[10,8,8,128]{3,2,1,0:T(8,128)S(1)} %get-tuple-element.299), channel_id=1, source_target_pairs={{0,3},{1,2},{2,1},{3,0},{4,7},{5,6},{6,5},{7,4},{8,11},{9,10},{10,... | collective-permute-start | bytes 983048 | tf_op jit(solution)/shard_map/ppermute | solution.py:340
  5.3 9.3 %collective-permute-start = (f32[10,8,8,128]{3,2,1,0:T(8,128)S(1)}, f32[10,8,8,128]{3,2,1,0:T(8,128)S(1)}, u32[]{:S(2)}, u32[]{:S(2)}) collective-permute-start(f32[10,8,8,128]{3,2,1,0:T(8,128)S(1)} %get-tuple-element.300), channel_id=1, source_target_pairs={{0,1},{1,0},{2,3},{3,2},{4,5},{5,4},{6,7},{7,6},{8,9},{9,8},{10,11... | collective-permute-start | bytes 983048 | tf_op jit(solution)/shard_map/ppermute | solution.py:340
  6.3 15.4 %collective-permute-start.1 = (f32[10,8,8,128]{3,2,1,0:T(8,128)S(1)}, f32[10,8,8,128]{3,2,1,0:T(8,128)S(1)}, u32[]{:S(2)}, u32[]{:S(2)}) collective-permute-start(f32[10,8,8,128]{3,2,1,0:T(8,128)S(1)} %get-tuple-element.301), channel_id=1, source_target_pairs={{0,2},{1,3},{2,0},{3,1},{4,6},{5,7},{6,4},{7,5},{8,10},{9,11},{10,... | collective-permute-start | bytes 983048 | tf_op jit(solution)/shard_map/ppermute | solution.py:340
  22.4 0.7 copy-start
  23.1 0.7 copy-start.3
  24.4 0.7 copy-start.8
  26.3 6.8 %collective-permute-start.4 = (f32[4,2,32,128]{3,2,1,0:T(8,128)S(1)}, f32[4,2,32,128]{3,2,1,0:T(8,128)S(1)}, u32[]{:S(2)}, u32[]{:S(2)}) collective-permute-start(f32[4,2,32,128]{3,2,1,0:T(8,128)S(1)} %get-tuple-element.160), channel_id=1, source_target_pairs={{0,4},{2,6},{4,0},{5,9},{6,2},{7,11},{8,12},{9,5},{10,14},{11,7},{... | collective-permute-start | bytes 393224 | tf_op jit(solution)/shard_map/ppermute | solution.py:356
  29.8 4.0 %collective-permute-start.5 = (f32[4,2,32,128]{3,2,1,0:T(8,128)S(1)}, f32[4,2,32,128]{3,2,1,0:T(8,128)S(1)}, u32[]{:S(2)}, u32[]{:S(2)}) collective-permute-start(f32[4,2,32,128]{3,2,1,0:T(8,128)S(1)} %get-tuple-element.161), channel_id=1, source_target_pairs={{1,5},{3,7},{4,8},{5,1},{6,10},{7,3},{8,4},{9,13},{10,6},{11,15},{... | collective-permute-start | bytes 393224 | tf_op jit(solution)/shard_map/ppermute | solution.py:356
  30.5 7.2 %copy-start.18 = (f32[1,4,8]{2,1,0:T(4,128)S(1)}, f32[1,4,8]{2,1,0:T(4,128)}, u32[]{:S(2)}) copy-start(f32[1,4,8]{2,1,0:T(4,128)} %residual.7) | copy-start | bytes 388
  30.5 7.2 %copy-start.19 = (s32[1,4]{1,0:T(1,128)S(1)}, s32[1,4]{1,0:T(1,128)}, u32[]{:S(2)}) copy-start(s32[1,4]{1,0:T(1,128)} %rec_cell.3) | copy-start | bytes 52
  34.5 62.9 %collective-permute-start.19 = (f32[8,6,8,8,128]{4,3,2,1,0:T(8,128)S(1)}, f32[8,6,8,8,128]{4,3,2,1,0:T(8,128)S(1)}, u32[]{:S(2)}, u32[]{:S(2)}) collective-permute-start(f32[8,6,8,8,128]{4,3,2,1,0:T(8,128)S(1)} %multiply_add_fusion.refs_28_.refs_32_), channel_id=1, source_target_pairs={{0,2},{1,3},{2,0},{3,1},{4,6},{5,7},{6,4},{7,5},{8,10},{9,11},{10,... | collective-permute-start | bytes 4718600 | tf_op jit(solution)/shard_map/ppermute | solution.py:340
  35.5 62.0 %collective-permute-start.18 = (f32[8,6,8,8,128]{4,3,2,1,0:T(8,128)S(1)}, f32[8,6,8,8,128]{4,3,2,1,0:T(8,128)}, u32[]{:S(2)}, u32[]{:S(2)}) collective-permute-start(f32[8,6,8,8,128]{4,3,2,1,0:T(8,128)S(1)} %multiply_add_fusion.refs_28_.refs_32_), channel_id=1, source_target_pairs={{0,1},{1,0},{2,3},{3,2},{4,5},{5,4},{6,7},{7,6},{8,9},{9,8},{10,11... | collective-permute-start | bytes 4718600 | tf_op jit(solution)/shard_map/ppermute | solution.py:340
  37.7 0.9 copy-start.4
  38.6 0.9 copy-start.9
  39.6 0.9 copy-start.13
  40.5 0.8 copy-start.17
  41.3 14.6 %copy-start.5 = (f32[6,2,32,128]{3,2,1,0:T(8,128)S(1)}, f32[6,2,32,128]{3,2,1,0:T(8,128)}, u32[]{:S(2)}) copy-start(f32[6,2,32,128]{3,2,1,0:T(8,128)} %copy-done.3) | copy-start | bytes 589828
  42.4 13.5 %collective-permute-start.7 = (bf16[15,32,128]{2,1,0:T(8,128)(2,1)S(1)}, bf16[15,32,128]{2,1,0:T(8,128)(2,1)S(1)}, u32[]{:S(2)}, u32[]{:S(2)}) collective-permute-start(bf16[15,32,128]{2,1,0:T(8,128)(2,1)S(1)} %get-tuple-element.183), channel_id=1, source_target_pairs={{1,5},{3,7},{4,8},{5,1},{6,10},{7,3},{8,4},{9,13},{10,6},{11,15},{... | collective-permute-start | bytes 368648 | tf_op jit(solution)/shard_map/ppermute | solution.py:356
  43.1 0.9 copy-start.1
  44.0 0.9 copy-start.7
  45.0 0.9 copy-start.11
  45.9 0.8 copy-start.15
  47.8 10.7 %copy-start.2 = (f32[6,2,32,128]{3,2,1,0:T(8,128)S(1)}, f32[6,2,32,128]{3,2,1,0:T(8,128)}, u32[]{:S(2)}) copy-start(f32[6,2,32,128]{3,2,1,0:T(8,128)} %copy-done) | copy-start | bytes 589828
  47.8 10.7 %collective-permute-start.6 = (bf16[15,32,128]{2,1,0:T(8,128)(2,1)S(1)}, bf16[15,32,128]{2,1,0:T(8,128)(2,1)S(1)}, u32[]{:S(2)}, u32[]{:S(2)}) collective-permute-start(bf16[15,32,128]{2,1,0:T(8,128)(2,1)S(1)} %get-tuple-element.175), channel_id=1, source_target_pairs={{0,4},{2,6},{4,0},{5,9},{6,2},{7,11},{8,12},{9,5},{10,14},{11,7},{... | collective-permute-start | bytes 368648 | tf_op jit(solution)/shard_map/ppermute | solution.py:356
  56.4 6.7 %collective-permute-start.9 = (bf16[15,32,128]{2,1,0:T(8,128)(2,1)S(1)}, bf16[15,32,128]{2,1,0:T(8,128)(2,1)S(1)}, u32[]{:S(2)}, u32[]{:S(2)}) collective-permute-start(bf16[15,32,128]{2,1,0:T(8,128)(2,1)S(1)} %get-tuple-element.199), channel_id=1, source_target_pairs={{1,5},{3,7},{4,8},{5,1},{6,10},{7,3},{8,4},{9,13},{10,6},{11,15},{... | collective-permute-start | bytes 368648 | tf_op jit(solution)/shard_map/ppermute | solution.py:356
  59.0 6.8 %collective-permute-start.8 = (bf16[15,32,128]{2,1,0:T(8,128)(2,1)S(1)}, bf16[15,32,128]{2,1,0:T(8,128)(2,1)S(1)}, u32[]{:S(2)}, u32[]{:S(2)}) collective-permute-start(bf16[15,32,128]{2,1,0:T(8,128)(2,1)S(1)} %get-tuple-element.193), channel_id=1, source_target_pairs={{0,4},{2,6},{4,0},{5,9},{6,2},{7,11},{8,12},{9,5},{10,14},{11,7},{... | collective-permute-start | bytes 368648 | tf_op jit(solution)/shard_map/ppermute | solution.py:356
  63.6 7.0 %collective-permute-start.11 = (bf16[15,32,128]{2,1,0:T(8,128)(2,1)S(1)}, bf16[15,32,128]{2,1,0:T(8,128)(2,1)S(1)}, u32[]{:S(2)}, u32[]{:S(2)}) collective-permute-start(bf16[15,32,128]{2,1,0:T(8,128)(2,1)S(1)} %get-tuple-element.213), channel_id=1, source_target_pairs={{1,5},{3,7},{4,8},{5,1},{6,10},{7,3},{8,4},{9,13},{10,6},{11,15},{... | collective-permute-start | bytes 368648 | tf_op jit(solution)/shard_map/ppermute | solution.py:356
  66.2 7.9 %collective-permute-start.10 = (bf16[15,32,128]{2,1,0:T(8,128)(2,1)S(1)}, bf16[15,32,128]{2,1,0:T(8,128)(2,1)S(1)}, u32[]{:S(2)}, u32[]{:S(2)}) collective-permute-start(bf16[15,32,128]{2,1,0:T(8,128)(2,1)S(1)} %get-tuple-element.207), channel_id=1, source_target_pairs={{0,4},{2,6},{4,0},{5,9},{6,2},{7,11},{8,12},{9,5},{10,14},{11,7},{... | collective-permute-start | bytes 368648 | tf_op jit(solution)/shard_map/ppermute | solution.py:356
  71.1 7.8 %collective-permute-start.13 = (bf16[15,32,128]{2,1,0:T(8,128)(2,1)S(1)}, bf16[15,32,128]{2,1,0:T(8,128)(2,1)S(1)}, u32[]{:S(2)}, u32[]{:S(2)}) collective-permute-start(bf16[15,32,128]{2,1,0:T(8,128)(2,1)S(1)} %get-tuple-element.227), channel_id=1, source_target_pairs={{1,5},{3,7},{4,8},{5,1},{6,10},{7,3},{8,4},{9,13},{10,6},{11,15},{... | collective-permute-start | bytes 368648 | tf_op jit(solution)/shard_map/ppermute | solution.py:356
  74.5 7.7 %collective-permute-start.12 = (bf16[15,32,128]{2,1,0:T(8,128)(2,1)S(1)}, bf16[15,32,128]{2,1,0:T(8,128)(2,1)S(1)}, u32[]{:S(2)}, u32[]{:S(2)}) collective-permute-start(bf16[15,32,128]{2,1,0:T(8,128)(2,1)S(1)} %get-tuple-element.221), channel_id=1, source_target_pairs={{0,4},{2,6},{4,0},{5,9},{6,2},{7,11},{8,12},{9,5},{10,14},{11,7},{... | collective-permute-start | bytes 368648 | tf_op jit(solution)/shard_map/ppermute | solution.py:356
  79.4 7.2 %collective-permute-start.15 = (bf16[15,32,128]{2,1,0:T(8,128)(2,1)S(1)}, bf16[15,32,128]{2,1,0:T(8,128)(2,1)S(1)}, u32[]{:S(2)}, u32[]{:S(2)}) collective-permute-start(bf16[15,32,128]{2,1,0:T(8,128)(2,1)S(1)} %get-tuple-element.241), channel_id=1, source_target_pairs={{1,5},{3,7},{4,8},{5,1},{6,10},{7,3},{8,4},{9,13},{10,6},{11,15},{... | collective-permute-start | bytes 368648 | tf_op jit(solution)/shard_map/ppermute | solution.py:356
  82.7 6.8 %collective-permute-start.14 = (bf16[15,32,128]{2,1,0:T(8,128)(2,1)S(1)}, bf16[15,32,128]{2,1,0:T(8,128)(2,1)S(1)}, u32[]{:S(2)}, u32[]{:S(2)}) collective-permute-start(bf16[15,32,128]{2,1,0:T(8,128)(2,1)S(1)} %get-tuple-element.235), channel_id=1, source_target_pairs={{0,4},{2,6},{4,0},{5,9},{6,2},{7,11},{8,12},{9,5},{10,14},{11,7},{... | collective-permute-start | bytes 368648 | tf_op jit(solution)/shard_map/ppermute | solution.py:356
  87.1 6.8 %collective-permute-start.17 = (bf16[15,32,128]{2,1,0:T(8,128)(2,1)S(1)}, bf16[15,32,128]{2,1,0:T(8,128)(2,1)S(1)}, u32[]{:S(2)}, u32[]{:S(2)}) collective-permute-start(bf16[15,32,128]{2,1,0:T(8,128)(2,1)S(1)} %get-tuple-element.255), channel_id=1, source_target_pairs={{1,5},{3,7},{4,8},{5,1},{6,10},{7,3},{8,4},{9,13},{10,6},{11,15},{... | collective-permute-start | bytes 368648 | tf_op jit(solution)/shard_map/ppermute | solution.py:356
  90.0 6.8 %collective-permute-start.16 = (bf16[15,32,128]{2,1,0:T(8,128)(2,1)S(1)}, bf16[15,32,128]{2,1,0:T(8,128)(2,1)S(1)}, u32[]{:S(2)}, u32[]{:S(2)}) collective-permute-start(bf16[15,32,128]{2,1,0:T(8,128)(2,1)S(1)} %get-tuple-element.249), channel_id=1, source_target_pairs={{0,4},{2,6},{4,0},{5,9},{6,2},{7,11},{8,12},{9,5},{10,14},{11,7},{... | collective-permute-start | bytes 368648 | tf_op jit(solution)/shard_map/ppermute | solution.py:356
  97.4 14.6 %collective-permute-start.22 = (f32[8,6,8,8,128]{4,3,2,1,0:T(8,128)S(1)}, f32[8,6,8,8,128]{4,3,2,1,0:T(8,128)S(1)}, u32[]{:S(2)}, u32[]{:S(2)}) collective-permute-start(f32[8,6,8,8,128]{4,3,2,1,0:T(8,128)S(1)} %collective-permute-done.19.refs_30_.refs_34_), channel_id=1, source_target_pairs={{0,1},{1,0},{2,3},{3,2},{4,5},{5,4},{6,7},{7,6},{8,9},{9,8},{10,11... | collective-permute-start | bytes 4718600 | tf_op jit(solution)/shard_map/ppermute | solution.py:340
  97.5 5.7 %collective-permute-start.21 = (bf16[15,32,128]{2,1,0:T(8,128)(2,1)S(1)}, bf16[15,32,128]{2,1,0:T(8,128)(2,1)S(1)}, u32[]{:S(2)}, u32[]{:S(2)}) collective-permute-start(bf16[15,32,128]{2,1,0:T(8,128)(2,1)S(1)} %get-tuple-element.271), channel_id=1, source_target_pairs={{1,5},{3,7},{4,8},{5,1},{6,10},{7,3},{8,4},{9,13},{10,6},{11,15},{... | collective-permute-start | bytes 368648 | tf_op jit(solution)/shard_map/ppermute | solution.py:356
  98.2 7.9 %collective-permute-start.20 = (bf16[15,32,128]{2,1,0:T(8,128)(2,1)S(1)}, bf16[15,32,128]{2,1,0:T(8,128)(2,1)S(1)}, u32[]{:S(2)}, u32[]{:S(2)}) collective-permute-start(bf16[15,32,128]{2,1,0:T(8,128)(2,1)S(1)} %get-tuple-element.265), channel_id=1, source_target_pairs={{0,4},{2,6},{4,0},{5,9},{6,2},{7,11},{8,12},{9,5},{10,14},{11,7},{... | collective-permute-start | bytes 368648 | tf_op jit(solution)/shard_map/ppermute | solution.py:356
  104.2 10.5 %collective-permute-start.24 = (bf16[15,32,128]{2,1,0:T(8,128)(2,1)S(1)}, bf16[15,32,128]{2,1,0:T(8,128)(2,1)S(1)}, u32[]{:S(2)}, u32[]{:S(2)}) collective-permute-start(bf16[15,32,128]{2,1,0:T(8,128)(2,1)S(1)} %get-tuple-element.284), channel_id=1, source_target_pairs={{1,5},{3,7},{4,8},{5,1},{6,10},{7,3},{8,4},{9,13},{10,6},{11,15},{... | collective-permute-start | bytes 368648 | tf_op jit(solution)/shard_map/ppermute | solution.py:356
  107.0 7.9 %collective-permute-start.23 = (bf16[15,32,128]{2,1,0:T(8,128)(2,1)S(1)}, bf16[15,32,128]{2,1,0:T(8,128)(2,1)S(1)}, u32[]{:S(2)}, u32[]{:S(2)}) collective-permute-start(bf16[15,32,128]{2,1,0:T(8,128)(2,1)S(1)} %get-tuple-element.281), channel_id=1, source_target_pairs={{0,4},{2,6},{4,0},{5,9},{6,2},{7,11},{8,12},{9,5},{10,14},{11,7},{... | collective-permute-start | bytes 368648 | tf_op jit(solution)/shard_map/ppermute | solution.py:356
  116.8 1.4 %collective-permute-start.25 = (f32[2,2,8,8,128]{4,3,2,1,0:T(8,128)S(1)}, f32[2,2,8,8,128]{4,3,2,1,0:T(8,128)S(1)}, u32[]{:S(2)}, u32[]{:S(2)}) collective-permute-start(f32[2,2,8,8,128]{4,3,2,1,0:T(8,128)S(1)} %pad_maximum_fusion.4), channel_id=1, source_target_pairs={{0,1},{1,0},{2,3},{3,2},{4,5},{5,4},{6,7},{7,6},{8,9},{9,8},{10,11... | collective-permute-start | bytes 393224 | tf_op jit(solution)/shard_map/ppermute | solution.py:340
  118.2 4.2 %collective-permute-start.27 = (f32[2,4,8,128]{3,2,1,0:T(8,128)S(1)}, f32[2,4,8,128]{3,2,1,0:T(8,128)S(1)}, u32[]{:S(2)}, u32[]{:S(2)}) collective-permute-start(f32[2,4,8,128]{3,2,1,0:T(8,128)S(1)} %dynamic-slice_bitcast_fusion.5), channel_id=1, source_target_pairs={{0,16},{1,17},{2,18},{3,19},{16,0},{17,1},{18,2},{19,3},{4,20},{5,... | collective-permute-start | bytes 98312 | tf_op jit(solution)/shard_map/ppermute | solution.py:482
  118.8 4.8 %collective-permute-start.26 = (f32[2,4,8,128]{3,2,1,0:T(8,128)S(1)}, f32[2,4,8,128]{3,2,1,0:T(8,128)S(1)}, u32[]{:S(2)}, u32[]{:S(2)}) collective-permute-start(f32[2,4,8,128]{3,2,1,0:T(8,128)S(1)} %get-tuple-element.297), channel_id=1, source_target_pairs={{0,18},{1,19},{2,16},{3,17},{16,2},{17,3},{18,0},{19,1},{4,22},{5,... | collective-permute-start | bytes 98312 | tf_op jit(solution)/shard_map/ppermute | solution.py:482
  120.8 3.9 %collective-permute-start.28 = (f32[2,4,8,128]{3,2,1,0:T(8,128)S(1)}, f32[2,4,8,128]{3,2,1,0:T(8,128)S(1)}, u32[]{:S(2)}, u32[]{:S(2)}) collective-permute-start(f32[2,4,8,128]{3,2,1,0:T(8,128)S(1)} %get-tuple-element.298), channel_id=1, source_target_pairs={{0,2},{1,3},{2,0},{3,1},{16,18},{17,19},{18,16},{19,17},{4,6},{5,7... | collective-permute-start | bytes 98312 | tf_op jit(solution)/shard_map/ppermute | solution.py:482
  (5 other events, 3.2 us)

commit v8 on v7

--- a/solution.py
+++ b/solution.py
@@ -22,20 +22,22 @@
 
 VMEM = pl.BlockSpec(memory_space=pltpu.VMEM)
 SMEM = pl.BlockSpec(memory_space=pltpu.SMEM)
+HBM = pl.BlockSpec(memory_space=pltpu.HBM)
 F32, BF16 = jnp.float32, jnp.bfloat16
 
 
 def call(body, outs, ins, scratch=(), flops=1_000_000):
-    scalars, arrays = ins
+    scalars, arrays, *far = ins
+    far = far[0] if far else []
     return list(pl.pallas_call(
         body,
         out_shape=[jax.ShapeDtypeStruct(shape, kind) for shape, kind in outs],
-        in_specs=[SMEM] * len(scalars) + [VMEM] * len(arrays),
+        in_specs=[SMEM] * len(scalars) + [VMEM] * len(arrays) + [HBM] * len(far),
         out_specs=[VMEM] * len(outs),
         scratch_shapes=list(scratch),
         compiler_params=pltpu.CompilerParams(vmem_limit_bytes=6 * 1024 * 1024),
         cost_estimate=pl.CostEstimate(flops=flops, bytes_accessed=2_000_000, transcendentals=0),
-    )(*scalars, *arrays))
+    )(*scalars, *arrays, *far))
 
 
 def band(depth):
@@ -308,31 +310,59 @@
 
 
 def correlate(jobs, moments, residual, *refs):
-    count = 4 * moments
-    rates, sources, before, terms = refs[:count], refs[count : count + len(jobs)], refs[count + len(jobs) : -1], refs[-1]
+    rates, refs = refs[: 4 * moments], refs[4 * moments :]
+    terms, slots, arrived = refs[-3:]
+    sources, before = refs[-3 - len(jobs) : -3], refs[: -3 - len(jobs)]
     tile_x, tile_y = sources[0].shape[2:4]
     _, me, flip = position()
     sign = sign_of(flip)
-    for job, turn in enumerate(jobs):
-        spot = pl.ds(pl.multiple_of((me ^ turn) * tile_y, tile_y), tile_y)
-        for side in range(2):
-            for out in range(DEEP):
-                row = row_of(flip, side, out, tile_x)
-                lam = mu = 0.0
-                if before and job < before[0].shape[0]:
-                    lam, mu = before[0][job, 0, row], before[0][job, 1, row]
-                for moment in jobs[turn]:
-                    weight = (KERNEL_SCALE / UNIT) * residual[0, me, moment]
+    steps = sorted({moment for wanted in jobs.values() for moment in wanted})
+    work = {step: [job for job, turn in enumerate(jobs) if step in jobs[turn]] for step in steps}
+
+    def fetch(at, job):
+        slot = at % 2
+        return pltpu.make_async_copy(sources[job].at[steps[at]], slots.at[slot, job], arrived.at[slot, job])
+
+    for job in work[steps[0]]:
+        fetch(0, job).start()
+    done = set()
+    for at, moment in enumerate(steps):
+        if at + 1 < len(steps):
+            for job in work[steps[at + 1]]:
+                fetch(at + 1, job).start()
+        weight = (KERNEL_SCALE / UNIT) * residual[0, me, moment]
+        for job in work[moment]:
+            fetch(at, job).wait()
+            turn = list(jobs)[job]
+            spot = pl.ds(pl.multiple_of((me ^ turn) * tile_y, tile_y), tile_y)
+            for side in range(2):
+                for out in range(DEEP):
+                    row = row_of(flip, side, out, tile_x)
                     held = rates[4 * moment + 2 * (out // REACH) + side]
                     rate = [held[c, out % REACH, spot, :] for c in range(6)]
-                    source = [sources[job][moment, c, row] for c in range(6)]
+                    source = [slots[at % 2, job, c, row] for c in range(6)]
                     bulk = (source[0] + source[1] + source[2]) * (rate[0] + rate[1] + rate[2])
                     diag = source[0] * rate[0] + source[1] * rate[1] + source[2] * rate[2]
                     off = sign * (source[3] * rate[3] + source[4] * rate[4]) + source[5] * rate[5]
-                    lam = lam + weight * bulk
-                    mu = mu + (2.0 * weight) * (diag + off)
-                terms[job, 0, row] = lam
-                terms[job, 1, row] = mu
+                    lam, mu = weight * bulk, (2.0 * weight) * (diag + off)
+                    if job in done:
+                        lam, mu = terms[job, 0, row] + lam, terms[job, 1, row] + mu
+                    elif before and job < before[0].shape[0]:
+                        lam, mu = before[0][job, 0, row] + lam, before[0][job, 1, row] + mu
+                    terms[job, 0, row] = lam
+                    terms[job, 1, row] = mu
+            done.add(job)
+
+
+def correlated(jobs, moments, residual, rates, found, before):
+    one = found[0].shape[1:]
+    (terms,) = call(
+        functools.partial(correlate, jobs, moments),
+        [((len(jobs), 2) + one[1:], F32)],
+        ([residual], rates + before, [found[turn] for turn in jobs]),
+        [pltpu.VMEM((2, len(jobs)) + one, F32), pltpu.SemaphoreType.DMA((2, len(jobs)))],
+    )
+    return terms
 
 
 def swap(array, axis, turn):
@@ -436,11 +466,7 @@
         if last:
             early, late = list(range(pieces)), []
             jobs = {turn: list(range(moment)) for turn in early}
-            (terms,) = call(
-                functools.partial(correlate, jobs, moment),
-                [((len(jobs), 2, tile_x, tile_y, depth), F32)],
-                ([residual], rates[: 4 * moment] + [found[turn] for turn in jobs]),
-            )
+            terms = correlated(jobs, moment, residual, rates[: 4 * moment], found, [])
             terms, vels = lax.optimization_barrier((terms, vels))
         fresh = [None, None]
         for side in range(2):
@@ -458,11 +484,7 @@
         vels = fresh
 
     jobs = {turn: [moments - 1] if turn in early else list(range(moments)) for turn in early + late}
-    (terms,) = call(
-        functools.partial(correlate, jobs, moments),
-        [((pieces, 2, tile_x, tile_y, depth), F32)],
-        ([residual], rates + [found[turn] for turn in jobs] + [terms]),
-    )
+    terms = correlated(jobs, moments, residual, rates, found, [terms])
     held = {turn: terms[at] for at, turn in enumerate(jobs)}
     if pieces > 1:
         keep = [turn for turn in held if not turn & 1]

time: 126 us -> 132 us (1.048)
  Pallas kernels: 16.6 us -> 22.2 us
    pallas_call x29, Pallas kernels: 16.6 us -> 22.2 us  [call(): pl.pallas_call(body, out_shape=[jax.ShapeDtypeStruct(shape, kind) for sha...]
  transfers between devices with their start and end apart: 29 -> 29, of which waited for: 14 -> 14; matrix products, arithmetic and copies ran while one was open for 2% -> 2% of each run, Pallas kernels for 12% -> 15%
where the time goes in v8:
time: 132 us; the launch traced here: 131 us
  starting transfers between devices  58.2 us (44%)
  waiting for transfers between devices  33.2 us (25%)
  Pallas kernels  22.2 us (17%)
  local copies, waits for them, and re-layouts  14.7 us (11%)
  other arithmetic  2.34 us (2%)
    ppermute x18, starting transfers between devices, to_neighbour(): return lax.ppermute(face, ('gx', 'gy'), pairs)  46.9 us
    pallas_call x29, Pallas kernels, call(): pl.pallas_call(body, out_shape=[jax.ShapeDtypeStruct(shape, kind) for sha...  22.2 us
    ppermute x8, waiting for transfers between devices, swap(): return lax.ppermute(array, axis, [(i, i ^ turn) for i in range(count)])  16.2 us
    ppermute x18, waiting for transfers between devices, to_neighbour(): return lax.ppermute(face, ('gx', 'gy'), pairs)  14 us
    unnamed x49, local copies, waits for them, and re-layouts  13.3 us
    ppermute x8, starting transfers between devices, swap(): return lax.ppermute(array, axis, [(i, i ^ turn) for i in range(count)])  7.74 us
    ppermute x3, starting transfers between devices, local(): part = lax.ppermute(part, ('sta', 'gy'), pairs)  3.55 us
    ppermute x3, waiting for transfers between devices, local(): part = lax.ppermute(part, ('sta', 'gy'), pairs)  2.93 us
  transfers between devices with their start and end apart: 29, of which 14 were waited for; matrix products, arithmetic and copies ran while one was open for 2% of the time, Pallas kernels for 15%

profile of v8, /device:TPU:0, one launch (start us, length us, event | category | flops | bytes accessed | tf_op | source)
XLA Modules:
  0.0 131.2 jit_solution(4128301438281305531)
XLA Ops:
  0.0 1.4 %dynamic-slice_bitcast_fusion = (f32[9,8,8,128]{3,2,1,0:T(8,128)S(1)}, f32[9,8,8,128]{3,2,1,0:T(8,128)S(1)}, f32[9,8,8,128]{3,2,1,0:T(8,128)S(1)}, f32[9,8,8,128]{3,2,1,0:T(8,128)S(1)}) fusion(f32[1,4,9,8,8,128]{5,4,3,2,1,0:T(8,128)} %param.8, s32[]{:T(128)S(6)} %select_n.27, s32[]{:T(128)S(6)} %select_n.25, s32[]{:T(128)S(6)} %select_n.24, s32[]{:T(128)S(6)} %select_n.26), kind=kLoop, calls=%fused_computation.5 | loop fusion | bytes 2359312 | tf_op jit(solution)/shard_map/jit(dynamic_index_in_dim)/squeeze | solution.py:401
  1.5 2.9 %collective-permute-start.3 = (bf16[8,6,8,8,128]{4,3,2,1,0:T(8,128)(2,1)S(1)}, bf16[8,6,8,8,128]{4,3,2,1,0:T(8,128)(2,1)}, u32[]{:S(2)}, u32[]{:S(2)}) collective-permute-start(bf16[8,6,8,8,128]{4,3,2,1,0:T(8,128)(2,1)S(1)} %bitcast.20), channel_id=1, source_target_pairs={{0,16},{16,0},{1,17},{17,1},{2,18},{18,2},{3,19},{19,3},{4,20},{20... | collective-permute-start | bytes 2359304 | tf_op jit(solution)/shard_map/ppermute | solution.py:370
  4.6 0.7 collective-permute-start.2
  5.3 1.0 collective-permute-start
  6.8 7.7 %collective-permute-done.2.refs_3_ = f32[10,8,8,128]{3,2,1,0:T(8,128)S(1)} collective-permute-done((f32[10,8,8,128]{3,2,1,0:T(8,128)S(1)}, f32[10,8,8,128]{3,2,1,0:T(8,128)S(1)}, u32[]{:S(2)}, u32[]{:S(2)}) %collective-permute-start.2) | collective-permute-done | bytes 327712 | tf_op jit(solution)/shard_map/ppermute | solution.py:370
  14.6 7.1 %collective-permute-done.1.refs_2_ = f32[10,8,8,128]{3,2,1,0:T(8,128)S(1)} collective-permute-done((f32[10,8,8,128]{3,2,1,0:T(8,128)S(1)}, f32[10,8,8,128]{3,2,1,0:T(8,128)S(1)}, u32[]{:S(2)}, u32[]{:S(2)}) %collective-permute-start.1) | collective-permute-done | bytes 327712 | tf_op jit(solution)/shard_map/ppermute | solution.py:370
  21.7 0.7 shard_map.82
  26.3 3.5 %collective-permute-start.4 = (f32[4,2,32,128]{3,2,1,0:T(8,128)S(1)}, f32[4,2,32,128]{3,2,1,0:T(8,128)S(1)}, u32[]{:S(2)}, u32[]{:S(2)}) collective-permute-start(f32[4,2,32,128]{3,2,1,0:T(8,128)S(1)} %get-tuple-element.160), channel_id=1, source_target_pairs={{0,4},{2,6},{4,0},{5,9},{6,2},{7,11},{8,12},{9,5},{10,14},{11,7},{... | collective-permute-start | bytes 393224 | tf_op jit(solution)/shard_map/ppermute | solution.py:386
  30.5 1.5 %multiply_add_fusion.refs_28_.refs_33_ = f32[8,6,8,8,128]{4,3,2,1,0:T(8,128)S(1)} fusion(bf16[8,6,8,8,128]{4,3,2,1,0:T(8,128)(2,1)} %collective-permute-done.3, bf16[8,6,8,8,128]{4,3,2,1,0:T(8,128)(2,1)S(1)} %bitcast.21, f32[8]{0:T(128)S(1)} %get-tuple-element.288, f32[8]{0:T(128)S(1)} %get-tuple-element.287), kind=kLoop, calls=%fused_computation | loop fusion | flops 1966080 | bytes 3145792 | tf_op jit(solution)/shard_map/add | solution.py:427
  32.0 1.1 collective-permute-done.4.halo
  34.5 1.0 collective-permute-start.19
  35.5 1.5 %collective-permute-start.18 = (f32[8,6,8,8,128]{4,3,2,1,0:T(8,128)S(1)}, f32[8,6,8,8,128]{4,3,2,1,0:T(8,128)}, u32[]{:S(2)}, u32[]{:S(2)}) collective-permute-start(f32[8,6,8,8,128]{4,3,2,1,0:T(8,128)S(1)} %multiply_add_fusion.refs_28_.refs_33_), channel_id=1, source_target_pairs={{0,1},{1,0},{2,3},{3,2},{4,5},{5,4},{6,7},{7,6},{8,9},{9,8},{10,11... | collective-permute-start | bytes 4718600 | tf_op jit(solution)/shard_map/ppermute | solution.py:370
  36.9 0.8 copy.9.table
  37.7 0.9 copy-done.4
  38.6 0.9 copy-done.9
  39.6 0.9 copy-done.13
  40.5 0.8 copy-done.17
  41.3 1.1 shard_map.84
  43.1 0.9 copy-done.1
  44.0 0.9 copy-done.7
  45.0 0.9 copy-done.11
  45.9 0.8 copy-done.15
  46.7 1.1 shard_map.83
  47.8 7.8 %collective-permute-start.6 = (bf16[15,32,128]{2,1,0:T(8,128)(2,1)S(1)}, bf16[15,32,128]{2,1,0:T(8,128)(2,1)S(1)}, u32[]{:S(2)}, u32[]{:S(2)}) collective-permute-start(bf16[15,32,128]{2,1,0:T(8,128)(2,1)S(1)} %get-tuple-element.175), channel_id=1, source_target_pairs={{0,4},{2,6},{4,0},{5,9},{6,2},{7,11},{8,12},{9,5},{10,14},{11,7},{... | collective-permute-start | bytes 368648 | tf_op jit(solution)/shard_map/ppermute | solution.py:386
  57.1 1.5 %collective-permute-done.6.halo = bf16[15,32,128]{2,1,0:T(8,128)(2,1)S(1)} collective-permute-done((bf16[15,32,128]{2,1,0:T(8,128)(2,1)S(1)}, bf16[15,32,128]{2,1,0:T(8,128)(2,1)S(1)}, u32[]{:S(2)}, u32[]{:S(2)}) %collective-permute-start.6) | collective-permute-done | bytes 122912 | tf_op jit(solution)/shard_map/ppermute | solution.py:386
  59.0 3.9 %collective-permute-start.8 = (bf16[15,32,128]{2,1,0:T(8,128)(2,1)S(1)}, bf16[15,32,128]{2,1,0:T(8,128)(2,1)S(1)}, u32[]{:S(2)}, u32[]{:S(2)}) collective-permute-start(bf16[15,32,128]{2,1,0:T(8,128)(2,1)S(1)} %get-tuple-element.193), channel_id=1, source_target_pairs={{0,4},{2,6},{4,0},{5,9},{6,2},{7,11},{8,12},{9,5},{10,14},{11,7},{... | collective-permute-start | bytes 368648 | tf_op jit(solution)/shard_map/ppermute | solution.py:386
  64.3 1.5 %collective-permute-done.8.halo = bf16[15,32,128]{2,1,0:T(8,128)(2,1)S(1)} collective-permute-done((bf16[15,32,128]{2,1,0:T(8,128)(2,1)S(1)}, bf16[15,32,128]{2,1,0:T(8,128)(2,1)S(1)}, u32[]{:S(2)}, u32[]{:S(2)}) %collective-permute-start.8) | collective-permute-done | bytes 122912 | tf_op jit(solution)/shard_map/ppermute | solution.py:386
  66.2 4.2 %collective-permute-start.10 = (bf16[15,32,128]{2,1,0:T(8,128)(2,1)S(1)}, bf16[15,32,128]{2,1,0:T(8,128)(2,1)S(1)}, u32[]{:S(2)}, u32[]{:S(2)}) collective-permute-start(bf16[15,32,128]{2,1,0:T(8,128)(2,1)S(1)} %get-tuple-element.207), channel_id=1, source_target_pairs={{0,4},{2,6},{4,0},{5,9},{6,2},{7,11},{8,12},{9,5},{10,14},{11,7},{... | collective-permute-start | bytes 368648 | tf_op jit(solution)/shard_map/ppermute | solution.py:386
  71.7 2.3 %collective-permute-done.10.halo = bf16[15,32,128]{2,1,0:T(8,128)(2,1)S(1)} collective-permute-done((bf16[15,32,128]{2,1,0:T(8,128)(2,1)S(1)}, bf16[15,32,128]{2,1,0:T(8,128)(2,1)S(1)}, u32[]{:S(2)}, u32[]{:S(2)}) %collective-permute-start.10) | collective-permute-done | bytes 122912 | tf_op jit(solution)/shard_map/ppermute | solution.py:386
  74.5 4.1 %collective-permute-start.12 = (bf16[15,32,128]{2,1,0:T(8,128)(2,1)S(1)}, bf16[15,32,128]{2,1,0:T(8,128)(2,1)S(1)}, u32[]{:S(2)}, u32[]{:S(2)}) collective-permute-start(bf16[15,32,128]{2,1,0:T(8,128)(2,1)S(1)} %get-tuple-element.221), channel_id=1, source_target_pairs={{0,4},{2,6},{4,0},{5,9},{6,2},{7,11},{8,12},{9,5},{10,14},{11,7},{... | collective-permute-start | bytes 368648 | tf_op jit(solution)/shard_map/ppermute | solution.py:386
  80.1 2.2 %collective-permute-done.12.halo = bf16[15,32,128]{2,1,0:T(8,128)(2,1)S(1)} collective-permute-done((bf16[15,32,128]{2,1,0:T(8,128)(2,1)S(1)}, bf16[15,32,128]{2,1,0:T(8,128)(2,1)S(1)}, u32[]{:S(2)}, u32[]{:S(2)}) %collective-permute-start.12) | collective-permute-done | bytes 122912 | tf_op jit(solution)/shard_map/ppermute | solution.py:386
  82.7 3.6 %collective-permute-start.14 = (bf16[15,32,128]{2,1,0:T(8,128)(2,1)S(1)}, bf16[15,32,128]{2,1,0:T(8,128)(2,1)S(1)}, u32[]{:S(2)}, u32[]{:S(2)}) collective-permute-start(bf16[15,32,128]{2,1,0:T(8,128)(2,1)S(1)} %get-tuple-element.235), channel_id=1, source_target_pairs={{0,4},{2,6},{4,0},{5,9},{6,2},{7,11},{8,12},{9,5},{10,14},{11,7},{... | collective-permute-start | bytes 368648 | tf_op jit(solution)/shard_map/ppermute | solution.py:386
  87.7 1.7 %collective-permute-done.14.halo = bf16[15,32,128]{2,1,0:T(8,128)(2,1)S(1)} collective-permute-done((bf16[15,32,128]{2,1,0:T(8,128)(2,1)S(1)}, bf16[15,32,128]{2,1,0:T(8,128)(2,1)S(1)}, u32[]{:S(2)}, u32[]{:S(2)}) %collective-permute-start.14) | collective-permute-done | bytes 122912 | tf_op jit(solution)/shard_map/ppermute | solution.py:386
  89.9 3.6 %collective-permute-start.16 = (bf16[15,32,128]{2,1,0:T(8,128)(2,1)S(1)}, bf16[15,32,128]{2,1,0:T(8,128)(2,1)S(1)}, u32[]{:S(2)}, u32[]{:S(2)}) collective-permute-start(bf16[15,32,128]{2,1,0:T(8,128)(2,1)S(1)} %get-tuple-element.249), channel_id=1, source_target_pairs={{0,4},{2,6},{4,0},{5,9},{6,2},{7,11},{8,12},{9,5},{10,14},{11,7},{... | collective-permute-start | bytes 368648 | tf_op jit(solution)/shard_map/ppermute | solution.py:386
  94.3 2.4 %collective-permute-done.16.halo = bf16[15,32,128]{2,1,0:T(8,128)(2,1)S(1)} collective-permute-done((bf16[15,32,128]{2,1,0:T(8,128)(2,1)S(1)}, bf16[15,32,128]{2,1,0:T(8,128)(2,1)S(1)}, u32[]{:S(2)}, u32[]{:S(2)}) %collective-permute-start.16) | collective-permute-done | bytes 122912 | tf_op jit(solution)/shard_map/ppermute | solution.py:386
  98.2 5.0 %collective-permute-start.20 = (bf16[15,32,128]{2,1,0:T(8,128)(2,1)S(1)}, bf16[15,32,128]{2,1,0:T(8,128)(2,1)S(1)}, u32[]{:S(2)}, u32[]{:S(2)}) collective-permute-start(bf16[15,32,128]{2,1,0:T(8,128)(2,1)S(1)} %get-tuple-element.265), channel_id=1, source_target_pairs={{0,4},{2,6},{4,0},{5,9},{6,2},{7,11},{8,12},{9,5},{10,14},{11,7},{... | collective-permute-start | bytes 368648 | tf_op jit(solution)/shard_map/ppermute | solution.py:386
  103.2 0.9 shard_map.105
  104.8 1.2 collective-permute-done.20.halo
  106.1 0.9 shard_map.104
  107.0 5.0 %collective-permute-start.23 = (bf16[15,32,128]{2,1,0:T(8,128)(2,1)S(1)}, bf16[15,32,128]{2,1,0:T(8,128)(2,1)S(1)}, u32[]{:S(2)}, u32[]{:S(2)}) collective-permute-start(bf16[15,32,128]{2,1,0:T(8,128)(2,1)S(1)} %get-tuple-element.281), channel_id=1, source_target_pairs={{0,4},{2,6},{4,0},{5,9},{6,2},{7,11},{8,12},{9,5},{10,14},{11,7},{... | collective-permute-start | bytes 368648 | tf_op jit(solution)/shard_map/ppermute | solution.py:386
  112.3 7.8 %shard_map.107.refs_32_ = f32[4,2,8,8,128]{4,3,2,1,0:T(8,128)S(1)} custom-call(f32[1,4,8]{2,1,0:T(4,128)S(1)} %copy-done.18, f32[6,2,32,128]{3,2,1,0:T(8,128)S(1)} %get-tuple-element.173.refs_0_, f32[6,2,32,128]{3,2,1,0:T(8,128)S(1)} %get-tuple-element.174.refs_1_, f32[6,2,32,128]{3,2,1,0:T(8,128)S(1)} %get-tuple-element.182.refs_2_, ...), custom_call_target="tpu_custom_call" | custom-call | flops 1000000 | bytes 2000000 | tf_op jit(solution)/shard_map/pallas_call | solution.py:32
  120.5 2.0 %shard_map.110 = f32[4,2,8,8,128]{4,3,2,1,0:T(8,128)S(1)} custom-call(f32[1,4,8]{2,1,0:T(4,128)S(1)} %copy-done.18, f32[6,2,32,128]{3,2,1,0:T(8,128)S(1)} %get-tuple-element.173.refs_0_, f32[6,2,32,128]{3,2,1,0:T(8,128)S(1)} %get-tuple-element.174.refs_1_, f32[6,2,32,128]{3,2,1,0:T(8,128)S(1)} %get-tuple-element.182.refs_2_, ...), custom_call_target="tpu_custom_call" | custom-call | flops 1000000 | bytes 2000000 | tf_op jit(solution)/shard_map/pallas_call | solution.py:32
  122.7 1.3 %collective-permute-done.25 = f32[2,2,8,8,128]{4,3,2,1,0:T(8,128)S(1)} collective-permute-done((f32[2,2,8,8,128]{4,3,2,1,0:T(8,128)S(1)}, f32[2,2,8,8,128]{4,3,2,1,0:T(8,128)S(1)}, u32[]{:S(2)}, u32[]{:S(2)}) %collective-permute-start.25) | collective-permute-done | bytes 131104 | tf_op jit(solution)/shard_map/ppermute | solution.py:370
  124.6 2.0 %collective-permute-start.26 = (f32[2,4,8,128]{3,2,1,0:T(8,128)S(1)}, f32[2,4,8,128]{3,2,1,0:T(8,128)S(1)}, u32[]{:S(2)}, u32[]{:S(2)}) collective-permute-start(f32[2,4,8,128]{3,2,1,0:T(8,128)S(1)} %get-tuple-element.297), channel_id=1, source_target_pairs={{0,18},{1,19},{2,16},{3,17},{16,2},{17,3},{18,0},{19,1},{4,22},{5,... | collective-permute-start | bytes 98312 | tf_op jit(solution)/shard_map/ppermute | solution.py:504
  126.6 1.0 collective-permute-start.28
  127.6 0.7 collective-permute-done.27
  128.3 1.2 collective-permute-done.26
  129.5 1.0 collective-permute-done.28
  (100 shorter events, 21.1 us)
Async XLA Ops:
  0.0 1.5 %copy-start.20 = (bf16[1,8,6,8,8,128]{5,4,3,2,1,0:T(8,128)(2,1)S(1)}, bf16[1,8,6,8,8,128]{5,4,3,2,1,0:T(8,128)(2,1)}, u32[]{:S(2)}) copy-start(bf16[1,8,6,8,8,128]{5,4,3,2,1,0:T(8,128)(2,1)} %param.9) | copy-start | bytes 2359300
  0.0 4.4 %copy-start.21 = (s32[8,8,128]{2,1,0:T(8,128)S(1)}, s32[8,8,128]{2,1,0:T(8,128)}, u32[]{:S(2)}) copy-start(s32[8,8,128]{2,1,0:T(8,128)} %param.10) | copy-start | bytes 98308
  1.4 5.4 %copy-start.23 = (s32[2,8,2]{1,2,0:T(2,128)S(1)}, s32[2,8,2]{1,2,0:T(2,128)}, u32[]{:S(2)}) copy-start(s32[2,8,2]{1,2,0:T(2,128)} %param.14) | copy-start | bytes 388
  1.4 5.4 %copy-start.22 = (s32[2,8]{1,0:T(2,128)S(1)}, s32[2,8]{1,0:T(2,128)}, u32[]{:S(2)}) copy-start(s32[2,8]{1,0:T(2,128)} %param.15) | copy-start | bytes 196
  1.5 29.0 %collective-permute-start.3 = (bf16[8,6,8,8,128]{4,3,2,1,0:T(8,128)(2,1)S(1)}, bf16[8,6,8,8,128]{4,3,2,1,0:T(8,128)(2,1)}, u32[]{:S(2)}, u32[]{:S(2)}) collective-permute-start(bf16[8,6,8,8,128]{4,3,2,1,0:T(8,128)(2,1)S(1)} %bitcast.20), channel_id=1, source_target_pairs={{0,16},{16,0},{1,17},{17,1},{2,18},{18,2},{3,19},{19,3},{4,20},{20... | collective-permute-start | bytes 2359304 | tf_op jit(solution)/shard_map/ppermute | solution.py:370
  4.6 10.0 %collective-permute-start.2 = (f32[10,8,8,128]{3,2,1,0:T(8,128)S(1)}, f32[10,8,8,128]{3,2,1,0:T(8,128)S(1)}, u32[]{:S(2)}, u32[]{:S(2)}) collective-permute-start(f32[10,8,8,128]{3,2,1,0:T(8,128)S(1)} %get-tuple-element.299), channel_id=1, source_target_pairs={{0,3},{1,2},{2,1},{3,0},{4,7},{5,6},{6,5},{7,4},{8,11},{9,10},{10,... | collective-permute-start | bytes 983048 | tf_op jit(solution)/shard_map/ppermute | solution.py:370
  5.3 9.3 %collective-permute-start = (f32[10,8,8,128]{3,2,1,0:T(8,128)S(1)}, f32[10,8,8,128]{3,2,1,0:T(8,128)S(1)}, u32[]{:S(2)}, u32[]{:S(2)}) collective-permute-start(f32[10,8,8,128]{3,2,1,0:T(8,128)S(1)} %get-tuple-element.300), channel_id=1, source_target_pairs={{0,1},{1,0},{2,3},{3,2},{4,5},{5,4},{6,7},{7,6},{8,9},{9,8},{10,11... | collective-permute-start | bytes 983048 | tf_op jit(solution)/shard_map/ppermute | solution.py:370
  6.3 15.4 %collective-permute-start.1 = (f32[10,8,8,128]{3,2,1,0:T(8,128)S(1)}, f32[10,8,8,128]{3,2,1,0:T(8,128)S(1)}, u32[]{:S(2)}, u32[]{:S(2)}) collective-permute-start(f32[10,8,8,128]{3,2,1,0:T(8,128)S(1)} %get-tuple-element.301), channel_id=1, source_target_pairs={{0,2},{1,3},{2,0},{3,1},{4,6},{5,7},{6,4},{7,5},{8,10},{9,11},{10,... | collective-permute-start | bytes 983048 | tf_op jit(solution)/shard_map/ppermute | solution.py:370
  22.4 0.7 copy-start
  23.1 0.7 copy-start.3
  24.4 0.7 copy-start.8
  26.3 6.8 %collective-permute-start.4 = (f32[4,2,32,128]{3,2,1,0:T(8,128)S(1)}, f32[4,2,32,128]{3,2,1,0:T(8,128)S(1)}, u32[]{:S(2)}, u32[]{:S(2)}) collective-permute-start(f32[4,2,32,128]{3,2,1,0:T(8,128)S(1)} %get-tuple-element.160), channel_id=1, source_target_pairs={{0,4},{2,6},{4,0},{5,9},{6,2},{7,11},{8,12},{9,5},{10,14},{11,7},{... | collective-permute-start | bytes 393224 | tf_op jit(solution)/shard_map/ppermute | solution.py:386
  29.8 4.0 %collective-permute-start.5 = (f32[4,2,32,128]{3,2,1,0:T(8,128)S(1)}, f32[4,2,32,128]{3,2,1,0:T(8,128)S(1)}, u32[]{:S(2)}, u32[]{:S(2)}) collective-permute-start(f32[4,2,32,128]{3,2,1,0:T(8,128)S(1)} %get-tuple-element.161), channel_id=1, source_target_pairs={{1,5},{3,7},{4,8},{5,1},{6,10},{7,3},{8,4},{9,13},{10,6},{11,15},{... | collective-permute-start | bytes 393224 | tf_op jit(solution)/shard_map/ppermute | solution.py:386
  30.5 7.2 %copy-start.18 = (f32[1,4,8]{2,1,0:T(4,128)S(1)}, f32[1,4,8]{2,1,0:T(4,128)}, u32[]{:S(2)}) copy-start(f32[1,4,8]{2,1,0:T(4,128)} %residual.7) | copy-start | bytes 388
  30.5 7.2 %copy-start.19 = (s32[1,4]{1,0:T(1,128)S(1)}, s32[1,4]{1,0:T(1,128)}, u32[]{:S(2)}) copy-start(s32[1,4]{1,0:T(1,128)} %rec_cell.3) | copy-start | bytes 52
  34.5 62.9 %collective-permute-start.19 = (f32[8,6,8,8,128]{4,3,2,1,0:T(8,128)S(1)}, f32[8,6,8,8,128]{4,3,2,1,0:T(8,128)S(1)}, u32[]{:S(2)}, u32[]{:S(2)}) collective-permute-start(f32[8,6,8,8,128]{4,3,2,1,0:T(8,128)S(1)} %multiply_add_fusion.refs_28_.refs_33_), channel_id=1, source_target_pairs={{0,2},{1,3},{2,0},{3,1},{4,6},{5,7},{6,4},{7,5},{8,10},{9,11},{10,... | collective-permute-start | bytes 4718600 | tf_op jit(solution)/shard_map/ppermute | solution.py:370
  35.5 61.9 %collective-permute-start.18 = (f32[8,6,8,8,128]{4,3,2,1,0:T(8,128)S(1)}, f32[8,6,8,8,128]{4,3,2,1,0:T(8,128)}, u32[]{:S(2)}, u32[]{:S(2)}) collective-permute-start(f32[8,6,8,8,128]{4,3,2,1,0:T(8,128)S(1)} %multiply_add_fusion.refs_28_.refs_33_), channel_id=1, source_target_pairs={{0,1},{1,0},{2,3},{3,2},{4,5},{5,4},{6,7},{7,6},{8,9},{9,8},{10,11... | collective-permute-start | bytes 4718600 | tf_op jit(solution)/shard_map/ppermute | solution.py:370
  37.7 0.9 copy-start.4
  38.6 0.9 copy-start.9
  39.6 0.9 copy-start.13
  40.5 0.8 copy-start.17
  41.3 14.6 %copy-start.5 = (f32[6,2,32,128]{3,2,1,0:T(8,128)S(1)}, f32[6,2,32,128]{3,2,1,0:T(8,128)}, u32[]{:S(2)}) copy-start(f32[6,2,32,128]{3,2,1,0:T(8,128)} %copy-done.3) | copy-start | bytes 589828
  42.4 13.5 %collective-permute-start.7 = (bf16[15,32,128]{2,1,0:T(8,128)(2,1)S(1)}, bf16[15,32,128]{2,1,0:T(8,128)(2,1)S(1)}, u32[]{:S(2)}, u32[]{:S(2)}) collective-permute-start(bf16[15,32,128]{2,1,0:T(8,128)(2,1)S(1)} %get-tuple-element.183), channel_id=1, source_target_pairs={{1,5},{3,7},{4,8},{5,1},{6,10},{7,3},{8,4},{9,13},{10,6},{11,15},{... | collective-permute-start | bytes 368648 | tf_op jit(solution)/shard_map/ppermute | solution.py:386
  43.1 0.9 copy-start.1
  44.0 0.9 copy-start.7
  45.0 0.9 copy-start.11
  45.9 0.8 copy-start.15
  47.8 10.7 %copy-start.2 = (f32[6,2,32,128]{3,2,1,0:T(8,128)S(1)}, f32[6,2,32,128]{3,2,1,0:T(8,128)}, u32[]{:S(2)}) copy-start(f32[6,2,32,128]{3,2,1,0:T(8,128)} %copy-done) | copy-start | bytes 589828
  47.8 10.7 %collective-permute-start.6 = (bf16[15,32,128]{2,1,0:T(8,128)(2,1)S(1)}, bf16[15,32,128]{2,1,0:T(8,128)(2,1)S(1)}, u32[]{:S(2)}, u32[]{:S(2)}) collective-permute-start(bf16[15,32,128]{2,1,0:T(8,128)(2,1)S(1)} %get-tuple-element.175), channel_id=1, source_target_pairs={{0,4},{2,6},{4,0},{5,9},{6,2},{7,11},{8,12},{9,5},{10,14},{11,7},{... | collective-permute-start | bytes 368648 | tf_op jit(solution)/shard_map/ppermute | solution.py:386
  56.4 6.7 %collective-permute-start.9 = (bf16[15,32,128]{2,1,0:T(8,128)(2,1)S(1)}, bf16[15,32,128]{2,1,0:T(8,128)(2,1)S(1)}, u32[]{:S(2)}, u32[]{:S(2)}) collective-permute-start(bf16[15,32,128]{2,1,0:T(8,128)(2,1)S(1)} %get-tuple-element.199), channel_id=1, source_target_pairs={{1,5},{3,7},{4,8},{5,1},{6,10},{7,3},{8,4},{9,13},{10,6},{11,15},{... | collective-permute-start | bytes 368648 | tf_op jit(solution)/shard_map/ppermute | solution.py:386
  59.0 6.8 %collective-permute-start.8 = (bf16[15,32,128]{2,1,0:T(8,128)(2,1)S(1)}, bf16[15,32,128]{2,1,0:T(8,128)(2,1)S(1)}, u32[]{:S(2)}, u32[]{:S(2)}) collective-permute-start(bf16[15,32,128]{2,1,0:T(8,128)(2,1)S(1)} %get-tuple-element.193), channel_id=1, source_target_pairs={{0,4},{2,6},{4,0},{5,9},{6,2},{7,11},{8,12},{9,5},{10,14},{11,7},{... | collective-permute-start | bytes 368648 | tf_op jit(solution)/shard_map/ppermute | solution.py:386
  63.6 7.0 %collective-permute-start.11 = (bf16[15,32,128]{2,1,0:T(8,128)(2,1)S(1)}, bf16[15,32,128]{2,1,0:T(8,128)(2,1)S(1)}, u32[]{:S(2)}, u32[]{:S(2)}) collective-permute-start(bf16[15,32,128]{2,1,0:T(8,128)(2,1)S(1)} %get-tuple-element.213), channel_id=1, source_target_pairs={{1,5},{3,7},{4,8},{5,1},{6,10},{7,3},{8,4},{9,13},{10,6},{11,15},{... | collective-permute-start | bytes 368648 | tf_op jit(solution)/shard_map/ppermute | solution.py:386
  66.2 7.9 %collective-permute-start.10 = (bf16[15,32,128]{2,1,0:T(8,128)(2,1)S(1)}, bf16[15,32,128]{2,1,0:T(8,128)(2,1)S(1)}, u32[]{:S(2)}, u32[]{:S(2)}) collective-permute-start(bf16[15,32,128]{2,1,0:T(8,128)(2,1)S(1)} %get-tuple-element.207), channel_id=1, source_target_pairs={{0,4},{2,6},{4,0},{5,9},{6,2},{7,11},{8,12},{9,5},{10,14},{11,7},{... | collective-permute-start | bytes 368648 | tf_op jit(solution)/shard_map/ppermute | solution.py:386
  71.1 7.8 %collective-permute-start.13 = (bf16[15,32,128]{2,1,0:T(8,128)(2,1)S(1)}, bf16[15,32,128]{2,1,0:T(8,128)(2,1)S(1)}, u32[]{:S(2)}, u32[]{:S(2)}) collective-permute-start(bf16[15,32,128]{2,1,0:T(8,128)(2,1)S(1)} %get-tuple-element.227), channel_id=1, source_target_pairs={{1,5},{3,7},{4,8},{5,1},{6,10},{7,3},{8,4},{9,13},{10,6},{11,15},{... | collective-permute-start | bytes 368648 | tf_op jit(solution)/shard_map/ppermute | solution.py:386
  74.5 7.7 %collective-permute-start.12 = (bf16[15,32,128]{2,1,0:T(8,128)(2,1)S(1)}, bf16[15,32,128]{2,1,0:T(8,128)(2,1)S(1)}, u32[]{:S(2)}, u32[]{:S(2)}) collective-permute-start(bf16[15,32,128]{2,1,0:T(8,128)(2,1)S(1)} %get-tuple-element.221), channel_id=1, source_target_pairs={{0,4},{2,6},{4,0},{5,9},{6,2},{7,11},{8,12},{9,5},{10,14},{11,7},{... | collective-permute-start | bytes 368648 | tf_op jit(solution)/shard_map/ppermute | solution.py:386
  79.4 7.2 %collective-permute-start.15 = (bf16[15,32,128]{2,1,0:T(8,128)(2,1)S(1)}, bf16[15,32,128]{2,1,0:T(8,128)(2,1)S(1)}, u32[]{:S(2)}, u32[]{:S(2)}) collective-permute-start(bf16[15,32,128]{2,1,0:T(8,128)(2,1)S(1)} %get-tuple-element.241), channel_id=1, source_target_pairs={{1,5},{3,7},{4,8},{5,1},{6,10},{7,3},{8,4},{9,13},{10,6},{11,15},{... | collective-permute-start | bytes 368648 | tf_op jit(solution)/shard_map/ppermute | solution.py:386
  82.7 6.8 %collective-permute-start.14 = (bf16[15,32,128]{2,1,0:T(8,128)(2,1)S(1)}, bf16[15,32,128]{2,1,0:T(8,128)(2,1)S(1)}, u32[]{:S(2)}, u32[]{:S(2)}) collective-permute-start(bf16[15,32,128]{2,1,0:T(8,128)(2,1)S(1)} %get-tuple-element.235), channel_id=1, source_target_pairs={{0,4},{2,6},{4,0},{5,9},{6,2},{7,11},{8,12},{9,5},{10,14},{11,7},{... | collective-permute-start | bytes 368648 | tf_op jit(solution)/shard_map/ppermute | solution.py:386
  87.1 6.8 %collective-permute-start.17 = (bf16[15,32,128]{2,1,0:T(8,128)(2,1)S(1)}, bf16[15,32,128]{2,1,0:T(8,128)(2,1)S(1)}, u32[]{:S(2)}, u32[]{:S(2)}) collective-permute-start(bf16[15,32,128]{2,1,0:T(8,128)(2,1)S(1)} %get-tuple-element.255), channel_id=1, source_target_pairs={{1,5},{3,7},{4,8},{5,1},{6,10},{7,3},{8,4},{9,13},{10,6},{11,15},{... | collective-permute-start | bytes 368648 | tf_op jit(solution)/shard_map/ppermute | solution.py:386
  89.9 6.8 %collective-permute-start.16 = (bf16[15,32,128]{2,1,0:T(8,128)(2,1)S(1)}, bf16[15,32,128]{2,1,0:T(8,128)(2,1)S(1)}, u32[]{:S(2)}, u32[]{:S(2)}) collective-permute-start(bf16[15,32,128]{2,1,0:T(8,128)(2,1)S(1)} %get-tuple-element.249), channel_id=1, source_target_pairs={{0,4},{2,6},{4,0},{5,9},{6,2},{7,11},{8,12},{9,5},{10,14},{11,7},{... | collective-permute-start | bytes 368648 | tf_op jit(solution)/shard_map/ppermute | solution.py:386
  97.4 14.8 %collective-permute-start.22 = (f32[8,6,8,8,128]{4,3,2,1,0:T(8,128)S(1)}, f32[8,6,8,8,128]{4,3,2,1,0:T(8,128)S(1)}, u32[]{:S(2)}, u32[]{:S(2)}) collective-permute-start(f32[8,6,8,8,128]{4,3,2,1,0:T(8,128)S(1)} %collective-permute-done.19.refs_30_.refs_35_), channel_id=1, source_target_pairs={{0,1},{1,0},{2,3},{3,2},{4,5},{5,4},{6,7},{7,6},{8,9},{9,8},{10,11... | collective-permute-start | bytes 4718600 | tf_op jit(solution)/shard_map/ppermute | solution.py:370
  97.5 5.7 %collective-permute-start.21 = (bf16[15,32,128]{2,1,0:T(8,128)(2,1)S(1)}, bf16[15,32,128]{2,1,0:T(8,128)(2,1)S(1)}, u32[]{:S(2)}, u32[]{:S(2)}) collective-permute-start(bf16[15,32,128]{2,1,0:T(8,128)(2,1)S(1)} %get-tuple-element.271), channel_id=1, source_target_pairs={{1,5},{3,7},{4,8},{5,1},{6,10},{7,3},{8,4},{9,13},{10,6},{11,15},{... | collective-permute-start | bytes 368648 | tf_op jit(solution)/shard_map/ppermute | solution.py:386
  98.2 7.9 %collective-permute-start.20 = (bf16[15,32,128]{2,1,0:T(8,128)(2,1)S(1)}, bf16[15,32,128]{2,1,0:T(8,128)(2,1)S(1)}, u32[]{:S(2)}, u32[]{:S(2)}) collective-permute-start(bf16[15,32,128]{2,1,0:T(8,128)(2,1)S(1)} %get-tuple-element.265), channel_id=1, source_target_pairs={{0,4},{2,6},{4,0},{5,9},{6,2},{7,11},{8,12},{9,5},{10,14},{11,7},{... | collective-permute-start | bytes 368648 | tf_op jit(solution)/shard_map/ppermute | solution.py:386
  104.2 16.0 %collective-permute-start.24 = (bf16[15,32,128]{2,1,0:T(8,128)(2,1)S(1)}, bf16[15,32,128]{2,1,0:T(8,128)(2,1)S(1)}, u32[]{:S(2)}, u32[]{:S(2)}) collective-permute-start(bf16[15,32,128]{2,1,0:T(8,128)(2,1)S(1)} %get-tuple-element.284), channel_id=1, source_target_pairs={{1,5},{3,7},{4,8},{5,1},{6,10},{7,3},{8,4},{9,13},{10,6},{11,15},{... | collective-permute-start | bytes 368648 | tf_op jit(solution)/shard_map/ppermute | solution.py:386
  107.0 13.3 %collective-permute-start.23 = (bf16[15,32,128]{2,1,0:T(8,128)(2,1)S(1)}, bf16[15,32,128]{2,1,0:T(8,128)(2,1)S(1)}, u32[]{:S(2)}, u32[]{:S(2)}) collective-permute-start(bf16[15,32,128]{2,1,0:T(8,128)(2,1)S(1)} %get-tuple-element.281), channel_id=1, source_target_pairs={{0,4},{2,6},{4,0},{5,9},{6,2},{7,11},{8,12},{9,5},{10,14},{11,7},{... | collective-permute-start | bytes 368648 | tf_op jit(solution)/shard_map/ppermute | solution.py:386
  122.6 1.4 %collective-permute-start.25 = (f32[2,2,8,8,128]{4,3,2,1,0:T(8,128)S(1)}, f32[2,2,8,8,128]{4,3,2,1,0:T(8,128)S(1)}, u32[]{:S(2)}, u32[]{:S(2)}) collective-permute-start(f32[2,2,8,8,128]{4,3,2,1,0:T(8,128)S(1)} %pad_maximum_fusion.4), channel_id=1, source_target_pairs={{0,1},{1,0},{2,3},{3,2},{4,5},{5,4},{6,7},{7,6},{8,9},{9,8},{10,11... | collective-permute-start | bytes 393224 | tf_op jit(solution)/shard_map/ppermute | solution.py:370
  124.0 4.2 %collective-permute-start.27 = (f32[2,4,8,128]{3,2,1,0:T(8,128)S(1)}, f32[2,4,8,128]{3,2,1,0:T(8,128)S(1)}, u32[]{:S(2)}, u32[]{:S(2)}) collective-permute-start(f32[2,4,8,128]{3,2,1,0:T(8,128)S(1)} %dynamic-slice_bitcast_fusion.5), channel_id=1, source_target_pairs={{0,16},{1,17},{2,18},{3,19},{16,0},{17,1},{18,2},{19,3},{4,20},{5,... | collective-permute-start | bytes 98312 | tf_op jit(solution)/shard_map/ppermute | solution.py:504
  124.6 4.9 %collective-permute-start.26 = (f32[2,4,8,128]{3,2,1,0:T(8,128)S(1)}, f32[2,4,8,128]{3,2,1,0:T(8,128)S(1)}, u32[]{:S(2)}, u32[]{:S(2)}) collective-permute-start(f32[2,4,8,128]{3,2,1,0:T(8,128)S(1)} %get-tuple-element.297), channel_id=1, source_target_pairs={{0,18},{1,19},{2,16},{3,17},{16,2},{17,3},{18,0},{19,1},{4,22},{5,... | collective-permute-start | bytes 98312 | tf_op jit(solution)/shard_map/ppermute | solution.py:504
  126.6 3.9 %collective-permute-start.28 = (f32[2,4,8,128]{3,2,1,0:T(8,128)S(1)}, f32[2,4,8,128]{3,2,1,0:T(8,128)S(1)}, u32[]{:S(2)}, u32[]{:S(2)}) collective-permute-start(f32[2,4,8,128]{3,2,1,0:T(8,128)S(1)} %get-tuple-element.298), channel_id=1, source_target_pairs={{0,2},{1,3},{2,0},{3,1},{16,18},{17,19},{18,16},{19,17},{4,6},{5,7... | collective-permute-start | bytes 98312 | tf_op jit(solution)/shard_map/ppermute | solution.py:504
  (5 other events, 3.2 us)

commit v9 on v7

--- a/solution.py
+++ b/solution.py
@@ -335,6 +335,24 @@
                 terms[job, 1, row] = mu
 
 
+def combine(groups, listed, src_pick, *refs):
+    strains, out = refs[:groups], refs[groups]
+    group = lax.axis_index("sta")
+    moments, comps = out.shape[:2]
+    for moment in range(moments):
+        factors = []
+        for turn in range(groups):
+            factor = 0
+            for at in range(src_pick.shape[0]):
+                factor += jnp.where(src_pick[at, moment] == (group ^ turn), listed[at, moment, group], 0)
+            factors.append(factor.astype(F32))
+        for comp in range(comps):
+            total = 0.0
+            for factor, strain in zip(factors, strains):
+                total = total + factor * strain[moment, comp].astype(F32)
+            out[moment, comp] = total
+
+
 def swap(array, axis, turn):
     count = lax.axis_size(axis)
     return lax.ppermute(array, axis, [(i, i ^ turn) for i in range(count)])
@@ -369,7 +387,8 @@
     numbers = material.astype(F32)[None]
     order = sorted(range(pieces), reverse=True)
     picked = {turn: lax.dynamic_index_in_dim(state, me ^ turn, 0, keepdims=False) for turn in order}
-    own, picked = lax.optimization_barrier((source_strain[0], picked))
+    own = source_strain[0].reshape(source_strain.shape[1:3] + (tile_x * tile_y, depth))
+    own, picked = lax.optimization_barrier((own, picked))
     chunks = {turn: jnp.concatenate([picked[turn], numbers], 0) for turn in order}
     chunks = [swap(chunks[turn], "gy", turn) if turn else chunks[turn] for turn in range(pieces)]
     strains = [swap(own, "sta", turn) if turn else own for turn in range(groups)]
@@ -390,11 +409,10 @@
     halos = [to_neighbour(faces[side], side) for side in range(2)]
 
     strains, cells = lax.optimization_barrier((strains, cells))
-    weights = lax.dynamic_slice_in_dim(listed, group, 1, 2)[:, :, 0].astype(F32)
-    combined = 0.0
-    for turn in range(groups):
-        factor = jnp.sum(weights * (src_pick == (group ^ turn)).astype(F32), 0)
-        combined = combined + factor[:, None, None, None, None] * strains[turn].astype(F32)
+    (combined,) = call(
+        functools.partial(combine, groups), [(own.shape, F32)], ([listed, src_pick], strains)
+    )
+    combined = combined.reshape(own.shape[:2] + (tile_x, tile_y, depth))
     combined, halos = lax.optimization_barrier((combined, halos))
     found = {turn: swap(combined, "gy", turn) for turn in range(pieces - 1, 0, -1) if turn & (turn - 1) == 0}
     found[0] = combined

time: 126 us -> 124 us (0.984)
  waiting for transfers between devices: 33.1 us -> 29.2 us
  starting transfers between devices: 58 us -> 61.4 us
  local copies, waits for them, and re-layouts: 14.7 us -> 12.4 us
  Pallas kernels: 16.6 us -> 18.7 us
  other arithmetic: 2.34 us -> 0.81 us
    ppermute x18, waiting for transfers between devices: 14 us -> 10.9 us  [to_neighbour(): return lax.ppermute(face, ('gx', 'gy'), pairs)]
    ppermute x8, starting transfers between devices: 7.74 us -> 10.7 us  [swap(): return lax.ppermute(array, axis, [(i, i ^ turn) for i in range(count)])]
    unnamed x49 -> x42, local copies, waits for them, and re-layouts: 13.3 us -> 11 us
    pallas_call x29 -> x30, Pallas kernels: 16.6 us -> 18.7 us  [call(): pl.pallas_call(body, out_shape=[jax.ShapeDtypeStruct(shape, kind) for sha...]
    add x1 -> x0, other arithmetic: 1.5 us -> none  [local(): combined + factor[:, None, None, None, None] * strains[turn].astype(F32)]
  transfers between devices with their start and end apart: 29 -> 29, of which waited for: 14 -> 13; matrix products, arithmetic and copies ran while one was open for 2% -> 1% of each run, Pallas kernels for 12% -> 14%
where the time goes in v9:
time: 124 us; the launch traced here: 123 us
  starting transfers between devices  61.4 us (50%)
  waiting for transfers between devices  29.2 us (24%)
  Pallas kernels  18.7 us (15%)
  local copies, waits for them, and re-layouts  12.4 us (10%)
    ppermute x18, starting transfers between devices, to_neighbour(): return lax.ppermute(face, ('gx', 'gy'), pairs)  47.2 us
    pallas_call x30, Pallas kernels, call(): pl.pallas_call(body, out_shape=[jax.ShapeDtypeStruct(shape, kind) for sha...  18.7 us
    ppermute x8, waiting for transfers between devices, swap(): return lax.ppermute(array, axis, [(i, i ^ turn) for i in range(count)])  15.8 us
    unnamed x42, local copies, waits for them, and re-layouts  11 us
    ppermute x18, waiting for transfers between devices, to_neighbour(): return lax.ppermute(face, ('gx', 'gy'), pairs)  10.9 us
    ppermute x8, starting transfers between devices, swap(): return lax.ppermute(array, axis, [(i, i ^ turn) for i in range(count)])  10.7 us
    ppermute x3, starting transfers between devices, local(): part = lax.ppermute(part, ('sta', 'gy'), pairs)  3.57 us
  transfers between devices with their start and end apart: 29, of which 13 were waited for; matrix products, arithmetic and copies ran while one was open for 1% of the time, Pallas kernels for 14%

profile of v9, /device:TPU:0, one launch (start us, length us, event | category | flops | bytes accessed | tf_op | source)
XLA Modules:
  0.0 123.0 jit_solution(8712054689407190983)
XLA Ops:
  0.0 1.4 %dynamic-slice_bitcast_fusion = (f32[9,8,8,128]{3,2,1,0:T(8,128)S(1)}, f32[9,8,8,128]{3,2,1,0:T(8,128)S(1)}, f32[9,8,8,128]{3,2,1,0:T(8,128)S(1)}, f32[9,8,8,128]{3,2,1,0:T(8,128)S(1)}) fusion(f32[1,4,9,8,8,128]{5,4,3,2,1,0:T(8,128)} %param.8, s32[]{:T(128)S(6)} %select_n.24, s32[]{:T(128)S(6)} %select_n.22, s32[]{:T(128)S(6)} %select_n.21, s32[]{:T(128)S(6)} %select_n.23), kind=kLoop, calls=%fused_computation.4 | loop fusion | bytes 2359312 | tf_op jit(solution)/shard_map/jit(dynamic_index_in_dim)/squeeze | solution.py:389
  1.5 2.9 %collective-permute-start.3 = (bf16[8,6,64,128]{3,2,1,0:T(8,128)(2,1)S(1)}, bf16[8,6,64,128]{3,2,1,0:T(8,128)(2,1)S(1)}, u32[]{:S(2)}, u32[]{:S(2)}) collective-permute-start(bf16[8,6,64,128]{3,2,1,0:T(8,128)(2,1)S(1)} %bitcast.24), channel_id=1, source_target_pairs={{0,16},{16,0},{1,17},{17,1},{2,18},{18,2},{3,19},{19,3},{4,20},{20... | collective-permute-start | bytes 2359304 | tf_op jit(solution)/shard_map/ppermute | solution.py:358
  4.7 1.6 %collective-permute-start.1 = (f32[10,8,8,128]{3,2,1,0:T(8,128)S(1)}, f32[10,8,8,128]{3,2,1,0:T(8,128)S(1)}, u32[]{:S(2)}, u32[]{:S(2)}) collective-permute-start(f32[10,8,8,128]{3,2,1,0:T(8,128)S(1)} %get-tuple-element.299), channel_id=1, source_target_pairs={{0,2},{1,3},{2,0},{3,1},{4,6},{5,7},{6,4},{7,5},{8,10},{9,11},{10,... | collective-permute-start | bytes 983048 | tf_op jit(solution)/shard_map/ppermute | solution.py:358
  6.5 8.7 %collective-permute-done.1.refs_2_ = f32[10,8,8,128]{3,2,1,0:T(8,128)S(1)} collective-permute-done((f32[10,8,8,128]{3,2,1,0:T(8,128)S(1)}, f32[10,8,8,128]{3,2,1,0:T(8,128)S(1)}, u32[]{:S(2)}, u32[]{:S(2)}) %collective-permute-start.1) | collective-permute-done | bytes 327712 | tf_op jit(solution)/shard_map/ppermute | solution.py:358
  15.3 6.1 %collective-permute-done.2.refs_3_ = f32[10,8,8,128]{3,2,1,0:T(8,128)S(1)} collective-permute-done((f32[10,8,8,128]{3,2,1,0:T(8,128)S(1)}, f32[10,8,8,128]{3,2,1,0:T(8,128)S(1)}, u32[]{:S(2)}, u32[]{:S(2)}) %collective-permute-start.2) | collective-permute-done | bytes 327712 | tf_op jit(solution)/shard_map/ppermute | solution.py:358
  21.4 1.4 %shard_map.82 = (f32[3,4,32,128]{3,2,1,0:T(8,128)S(1)}, f32[6,2,32,128]{3,2,1,0:T(8,128)S(1)}, f32[6,2,32,128]{3,2,1,0:T(8,128)S(1)}, f32[4,32,128]{2,1,0:T(8,12...) custom-call(f32[10,8,8,128]{3,2,1,0:T(8,128)S(1)} %get-tuple-element, ...), custom_call_target="tpu_custom_call" | custom-call | flops 1000000 | bytes 2000000 | tf_op jit(solution)/shard_map/pallas_call | solution.py:30
  22.7 0.7 copy-done.1
  23.4 0.7 copy-done.4
  24.8 0.7 copy-done.9
  26.7 3.5 %collective-permute-start.4 = (f32[4,2,32,128]{3,2,1,0:T(8,128)}, f32[4,2,32,128]{3,2,1,0:T(8,128)}, u32[]{:S(2)}, u32[]{:S(2)}) collective-permute-start(f32[4,2,32,128]{3,2,1,0:T(8,128)} %get-tuple-element.160), channel_id=1, source_target_pairs={{0,4},{2,6},{4,0},{5,9},{6,2},{7,11},{8,12},{9,5},{10,14},{11,7},{... | collective-permute-start | bytes 393224 | tf_op jit(solution)/shard_map/ppermute | solution.py:374
  30.2 1.3 %collective-permute-start.5 = (f32[4,2,32,128]{3,2,1,0:T(8,128)}, f32[4,2,32,128]{3,2,1,0:T(8,128)}, u32[]{:S(2)}, u32[]{:S(2)}) collective-permute-start(f32[4,2,32,128]{3,2,1,0:T(8,128)} %get-tuple-element.161), channel_id=1, source_target_pairs={{1,5},{3,7},{4,8},{5,1},{6,10},{7,3},{8,4},{9,13},{10,6},{11,15},{... | collective-permute-start | bytes 393224 | tf_op jit(solution)/shard_map/ppermute | solution.py:374
  31.6 0.7 copy-done.17
  32.3 0.9 shard_map.83
  33.9 2.5 %collective-permute-start.18 = (f32[8,6,8,8,128]{4,3,2,1,0:T(8,128)S(1)}, f32[8,6,8,8,128]{4,3,2,1,0:T(8,128)S(1)}, u32[]{:S(2)}, u32[]{:S(2)}) collective-permute-start(f32[8,6,8,8,128]{4,3,2,1,0:T(8,128)S(1)} %bitcast.20), channel_id=1, source_target_pairs={{0,1},{1,0},{2,3},{3,2},{4,5},{5,4},{6,7},{7,6},{8,9},{9,8},{10,11... | collective-permute-start | bytes 4718600 | tf_op jit(solution)/shard_map/ppermute | solution.py:358
  36.3 1.5 %collective-permute-start.19 = (f32[8,6,8,8,128]{4,3,2,1,0:T(8,128)S(1)}, f32[8,6,8,8,128]{4,3,2,1,0:T(8,128)}, u32[]{:S(2)}, u32[]{:S(2)}) collective-permute-start(f32[8,6,8,8,128]{4,3,2,1,0:T(8,128)S(1)} %bitcast.21), channel_id=1, source_target_pairs={{0,2},{1,3},{2,0},{3,1},{4,6},{5,7},{6,4},{7,5},{8,10},{9,11},{10,... | collective-permute-start | bytes 4718600 | tf_op jit(solution)/shard_map/ppermute | solution.py:358
  37.9 0.8 copy.10.table
  38.6 0.9 copy-done.5
  39.5 0.9 copy-done.10
  40.5 0.8 copy-done.14
  41.3 1.4 %shard_map.84 = (f32[3,4,32,128]{3,2,1,0:T(8,128)S(1)}, bf16[15,32,128]{2,1,0:T(8,128)(2,1)S(1)}, f32[4,32,128]{2,1,0:T(8,128)S(1)}, f32[6,32,128]{2,1,0:T(8,128...) custom-call(f32[16,3]{1,0:T(8,128)S(1)} %copy.10.table, ...), custom_call_target="tpu_custom_call" | custom-call | flops 1000000 | bytes 2000000 | tf_op jit(solution)/shard_map/pallas_call | solution.py:30
  42.7 4.1 %collective-permute-start.6 = (bf16[15,32,128]{2,1,0:T(8,128)(2,1)S(1)}, bf16[15,32,128]{2,1,0:T(8,128)(2,1)S(1)}, u32[]{:S(2)}, u32[]{:S(2)}) collective-permute-start(bf16[15,32,128]{2,1,0:T(8,128)(2,1)S(1)} %get-tuple-element.175), channel_id=1, source_target_pairs={{0,4},{2,6},{4,0},{5,9},{6,2},{7,11},{8,12},{9,5},{10,14},{11,7},{... | collective-permute-start | bytes 368648 | tf_op jit(solution)/shard_map/ppermute | solution.py:374
  46.8 0.9 copy-done.2
  47.7 0.9 copy-done.8
  48.6 0.8 copy-done.12
  49.5 1.3 %shard_map.85 = (f32[3,4,32,128]{3,2,1,0:T(8,128)S(1)}, bf16[15,32,128]{2,1,0:T(8,128)(2,1)S(1)}, f32[4,32,128]{2,1,0:T(8,128)S(1)}, f32[6,32,128]{2,1,0:T(8,128...) custom-call(f32[16,3]{1,0:T(8,128)S(1)} %copy.10.table, ...), custom_call_target="tpu_custom_call" | custom-call | flops 1000000 | bytes 2000000 | tf_op jit(solution)/shard_map/pallas_call | solution.py:30
  50.8 0.8 collective-permute-start.7
  52.3 5.2 %collective-permute-start.8 = (bf16[15,32,128]{2,1,0:T(8,128)(2,1)S(1)}, bf16[15,32,128]{2,1,0:T(8,128)(2,1)S(1)}, u32[]{:S(2)}, u32[]{:S(2)}) collective-permute-start(bf16[15,32,128]{2,1,0:T(8,128)(2,1)S(1)} %get-tuple-element.193), channel_id=1, source_target_pairs={{0,4},{2,6},{4,0},{5,9},{6,2},{7,11},{8,12},{9,5},{10,14},{11,7},{... | collective-permute-start | bytes 368648 | tf_op jit(solution)/shard_map/ppermute | solution.py:374
  58.9 1.5 %collective-permute-done.8.halo = bf16[15,32,128]{2,1,0:T(8,128)(2,1)S(1)} collective-permute-done((bf16[15,32,128]{2,1,0:T(8,128)(2,1)S(1)}, bf16[15,32,128]{2,1,0:T(8,128)(2,1)S(1)}, u32[]{:S(2)}, u32[]{:S(2)}) %collective-permute-start.8) | collective-permute-done | bytes 122912 | tf_op jit(solution)/shard_map/ppermute | solution.py:374
  60.8 3.9 %collective-permute-start.10 = (bf16[15,32,128]{2,1,0:T(8,128)(2,1)S(1)}, bf16[15,32,128]{2,1,0:T(8,128)(2,1)S(1)}, u32[]{:S(2)}, u32[]{:S(2)}) collective-permute-start(bf16[15,32,128]{2,1,0:T(8,128)(2,1)S(1)} %get-tuple-element.207), channel_id=1, source_target_pairs={{0,4},{2,6},{4,0},{5,9},{6,2},{7,11},{8,12},{9,5},{10,14},{11,7},{... | collective-permute-start | bytes 368648 | tf_op jit(solution)/shard_map/ppermute | solution.py:374
  66.1 1.5 %collective-permute-done.10.halo = bf16[15,32,128]{2,1,0:T(8,128)(2,1)S(1)} collective-permute-done((bf16[15,32,128]{2,1,0:T(8,128)(2,1)S(1)}, bf16[15,32,128]{2,1,0:T(8,128)(2,1)S(1)}, u32[]{:S(2)}, u32[]{:S(2)}) %collective-permute-start.10) | collective-permute-done | bytes 122912 | tf_op jit(solution)/shard_map/ppermute | solution.py:374
  68.0 4.1 %collective-permute-start.12 = (bf16[15,32,128]{2,1,0:T(8,128)(2,1)S(1)}, bf16[15,32,128]{2,1,0:T(8,128)(2,1)S(1)}, u32[]{:S(2)}, u32[]{:S(2)}) collective-permute-start(bf16[15,32,128]{2,1,0:T(8,128)(2,1)S(1)} %get-tuple-element.221), channel_id=1, source_target_pairs={{0,4},{2,6},{4,0},{5,9},{6,2},{7,11},{8,12},{9,5},{10,14},{11,7},{... | collective-permute-start | bytes 368648 | tf_op jit(solution)/shard_map/ppermute | solution.py:374
  73.5 1.5 %collective-permute-done.12.halo = bf16[15,32,128]{2,1,0:T(8,128)(2,1)S(1)} collective-permute-done((bf16[15,32,128]{2,1,0:T(8,128)(2,1)S(1)}, bf16[15,32,128]{2,1,0:T(8,128)(2,1)S(1)}, u32[]{:S(2)}, u32[]{:S(2)}) %collective-permute-start.12) | collective-permute-done | bytes 122912 | tf_op jit(solution)/shard_map/ppermute | solution.py:374
  75.4 4.9 %collective-permute-start.14 = (bf16[15,32,128]{2,1,0:T(8,128)(2,1)S(1)}, bf16[15,32,128]{2,1,0:T(8,128)(2,1)S(1)}, u32[]{:S(2)}, u32[]{:S(2)}) collective-permute-start(bf16[15,32,128]{2,1,0:T(8,128)(2,1)S(1)} %get-tuple-element.235), channel_id=1, source_target_pairs={{0,4},{2,6},{4,0},{5,9},{6,2},{7,11},{8,12},{9,5},{10,14},{11,7},{... | collective-permute-start | bytes 368648 | tf_op jit(solution)/shard_map/ppermute | solution.py:374
  81.7 2.2 %collective-permute-done.14.halo = bf16[15,32,128]{2,1,0:T(8,128)(2,1)S(1)} collective-permute-done((bf16[15,32,128]{2,1,0:T(8,128)(2,1)S(1)}, bf16[15,32,128]{2,1,0:T(8,128)(2,1)S(1)}, u32[]{:S(2)}, u32[]{:S(2)}) %collective-permute-start.14) | collective-permute-done | bytes 122912 | tf_op jit(solution)/shard_map/ppermute | solution.py:374
  84.4 4.0 %collective-permute-start.16 = (bf16[15,32,128]{2,1,0:T(8,128)(2,1)S(1)}, bf16[15,32,128]{2,1,0:T(8,128)(2,1)S(1)}, u32[]{:S(2)}, u32[]{:S(2)}) collective-permute-start(bf16[15,32,128]{2,1,0:T(8,128)(2,1)S(1)} %get-tuple-element.249), channel_id=1, source_target_pairs={{0,4},{2,6},{4,0},{5,9},{6,2},{7,11},{8,12},{9,5},{10,14},{11,7},{... | collective-permute-start | bytes 368648 | tf_op jit(solution)/shard_map/ppermute | solution.py:374
  89.8 1.5 %collective-permute-done.16.halo = bf16[15,32,128]{2,1,0:T(8,128)(2,1)S(1)} collective-permute-done((bf16[15,32,128]{2,1,0:T(8,128)(2,1)S(1)}, bf16[15,32,128]{2,1,0:T(8,128)(2,1)S(1)}, u32[]{:S(2)}, u32[]{:S(2)}) %collective-permute-start.16) | collective-permute-done | bytes 122912 | tf_op jit(solution)/shard_map/ppermute | solution.py:374
  92.5 6.8 %collective-permute-start.20 = (bf16[15,32,128]{2,1,0:T(8,128)(2,1)S(1)}, bf16[15,32,128]{2,1,0:T(8,128)(2,1)S(1)}, u32[]{:S(2)}, u32[]{:S(2)}) collective-permute-start(bf16[15,32,128]{2,1,0:T(8,128)(2,1)S(1)} %get-tuple-element.265), channel_id=1, source_target_pairs={{0,4},{2,6},{4,0},{5,9},{6,2},{7,11},{8,12},{9,5},{10,14},{11,7},{... | collective-permute-start | bytes 368648 | tf_op jit(solution)/shard_map/ppermute | solution.py:374
  100.0 2.2 %collective-permute-done.20.halo = bf16[15,32,128]{2,1,0:T(8,128)(2,1)S(1)} collective-permute-done((bf16[15,32,128]{2,1,0:T(8,128)(2,1)S(1)}, bf16[15,32,128]{2,1,0:T(8,128)(2,1)S(1)}, u32[]{:S(2)}, u32[]{:S(2)}) %collective-permute-start.20) | collective-permute-done | bytes 122912 | tf_op jit(solution)/shard_map/ppermute | solution.py:374
  102.2 0.9 shard_map.105
  103.1 3.9 %collective-permute-start.23 = (bf16[15,32,128]{2,1,0:T(8,128)(2,1)S(1)}, bf16[15,32,128]{2,1,0:T(8,128)(2,1)S(1)}, u32[]{:S(2)}, u32[]{:S(2)}) collective-permute-start(bf16[15,32,128]{2,1,0:T(8,128)(2,1)S(1)} %get-tuple-element.281), channel_id=1, source_target_pairs={{0,4},{2,6},{4,0},{5,9},{6,2},{7,11},{8,12},{9,5},{10,14},{11,7},{... | collective-permute-start | bytes 368648 | tf_op jit(solution)/shard_map/ppermute | solution.py:374
  107.0 0.9 shard_map.106
  108.9 2.6 %shard_map.108.refs_36_ = f32[4,2,8,8,128]{4,3,2,1,0:T(8,128)S(1)} custom-call(f32[1,4,8]{2,1,0:T(4,128)S(1)} %copy-done.15, f32[6,2,32,128]{3,2,1,0:T(8,128)S(1)} %get-tuple-element.173.refs_0_, f32[6,2,32,128]{3,2,1,0:T(8,128)S(1)} %get-tuple-element.174.refs_1_, f32[6,2,32,128]{3,2,1,0:T(8,128)S(1)} %get-tuple-element.182.refs_2_, ...), custom_call_target="tpu_custom_call" | custom-call | flops 1000000 | bytes 2000000 | tf_op jit(solution)/shard_map/pallas_call | solution.py:30
  111.9 1.6 %shard_map.111 = f32[4,2,8,8,128]{4,3,2,1,0:T(8,128)S(1)} custom-call(f32[1,4,8]{2,1,0:T(4,128)S(1)} %copy-done.15, f32[6,2,32,128]{3,2,1,0:T(8,128)S(1)} %get-tuple-element.173.refs_0_, f32[6,2,32,128]{3,2,1,0:T(8,128)S(1)} %get-tuple-element.174.refs_1_, f32[6,2,32,128]{3,2,1,0:T(8,128)S(1)} %get-tuple-element.182.refs_2_, ...), custom_call_target="tpu_custom_call" | custom-call | flops 1000000 | bytes 2000000 | tf_op jit(solution)/shard_map/pallas_call | solution.py:30
  113.6 1.7 %collective-permute-start.25 = (f32[2,2,8,8,128]{4,3,2,1,0:T(8,128)S(1)}, f32[2,2,8,8,128]{4,3,2,1,0:T(8,128)S(1)}, u32[]{:S(2)}, u32[]{:S(2)}) collective-permute-start(f32[2,2,8,8,128]{4,3,2,1,0:T(8,128)S(1)} %pad_maximum_fusion.4), channel_id=1, source_target_pairs={{0,1},{1,0},{2,3},{3,2},{4,5},{5,4},{6,7},{7,6},{8,9},{9,8},{10,11... | collective-permute-start | bytes 393224 | tf_op jit(solution)/shard_map/ppermute | solution.py:358
  115.3 1.0 collective-permute-done.25
  116.9 1.5 %collective-permute-start.26 = (f32[2,4,8,128]{3,2,1,0:T(8,128)S(1)}, f32[2,4,8,128]{3,2,1,0:T(8,128)S(1)}, u32[]{:S(2)}, u32[]{:S(2)}) collective-permute-start(f32[2,4,8,128]{3,2,1,0:T(8,128)S(1)} %get-tuple-element.295), channel_id=1, source_target_pairs={{0,18},{1,19},{2,16},{3,17},{16,2},{17,3},{18,0},{19,1},{4,22},{5,... | collective-permute-start | bytes 98312 | tf_op jit(solution)/shard_map/ppermute | solution.py:500
  118.4 1.5 %collective-permute-start.27 = (f32[2,4,8,128]{3,2,1,0:T(8,128)S(1)}, f32[2,4,8,128]{3,2,1,0:T(8,128)S(1)}, u32[]{:S(2)}, u32[]{:S(2)}) collective-permute-start(f32[2,4,8,128]{3,2,1,0:T(8,128)S(1)} %dynamic-slice_bitcast_fusion.5), channel_id=1, source_target_pairs={{0,16},{1,17},{2,18},{3,19},{16,0},{17,1},{18,2},{19,3},{4,20},{5,... | collective-permute-start | bytes 98312 | tf_op jit(solution)/shard_map/ppermute | solution.py:500
  120.3 1.4 %collective-permute-done.26 = f32[2,4,8,128]{3,2,1,0:T(8,128)S(1)} collective-permute-done((f32[2,4,8,128]{3,2,1,0:T(8,128)S(1)}, f32[2,4,8,128]{3,2,1,0:T(8,128)S(1)}, u32[]{:S(2)}, u32[]{:S(2)}) %collective-permute-start.26) | collective-permute-done | bytes 32800 | tf_op jit(solution)/shard_map/ppermute | solution.py:500
  (91 shorter events, 18.0 us)
Async XLA Ops:
  0.0 1.5 %copy-start = (bf16[1,8,6,8,8,128]{5,4,3,2,1,0:T(8,128)(2,1)S(1)}, bf16[1,8,6,8,8,128]{5,4,3,2,1,0:T(8,128)(2,1)}, u32[]{:S(2)}) copy-start(bf16[1,8,6,8,8,128]{5,4,3,2,1,0:T(8,128)(2,1)} %param.9) | copy-start | bytes 2359300
  0.0 4.4 %copy-start.18 = (s32[8,8,128]{2,1,0:T(8,128)S(1)}, s32[8,8,128]{2,1,0:T(8,128)}, u32[]{:S(2)}) copy-start(s32[8,8,128]{2,1,0:T(8,128)} %param.10) | copy-start | bytes 98308
  1.5 30.1 %collective-permute-start.3 = (bf16[8,6,64,128]{3,2,1,0:T(8,128)(2,1)S(1)}, bf16[8,6,64,128]{3,2,1,0:T(8,128)(2,1)S(1)}, u32[]{:S(2)}, u32[]{:S(2)}) collective-permute-start(bf16[8,6,64,128]{3,2,1,0:T(8,128)(2,1)S(1)} %bitcast.24), channel_id=1, source_target_pairs={{0,16},{16,0},{1,17},{17,1},{2,18},{18,2},{3,19},{19,3},{4,20},{20... | collective-permute-start | bytes 2359304 | tf_op jit(solution)/shard_map/ppermute | solution.py:358
  4.4 27.0 %copy-start.19 = (s32[2,8,2]{1,2,0:T(2,128)S(1)}, s32[2,8,2]{1,2,0:T(2,128)}, u32[]{:S(2)}) copy-start(s32[2,8,2]{1,2,0:T(2,128)} %param.14) | copy-start | bytes 388
  4.6 1.9 %collective-permute-start = (f32[10,8,8,128]{3,2,1,0:T(8,128)S(1)}, f32[10,8,8,128]{3,2,1,0:T(8,128)S(1)}, u32[]{:S(2)}, u32[]{:S(2)}) collective-permute-start(f32[10,8,8,128]{3,2,1,0:T(8,128)S(1)} %get-tuple-element.298), channel_id=1, source_target_pairs={{0,1},{1,0},{2,3},{3,2},{4,5},{5,4},{6,7},{7,6},{8,9},{9,8},{10,11... | collective-permute-start | bytes 983048 | tf_op jit(solution)/shard_map/ppermute | solution.py:358
  4.7 10.6 %collective-permute-start.1 = (f32[10,8,8,128]{3,2,1,0:T(8,128)S(1)}, f32[10,8,8,128]{3,2,1,0:T(8,128)S(1)}, u32[]{:S(2)}, u32[]{:S(2)}) collective-permute-start(f32[10,8,8,128]{3,2,1,0:T(8,128)S(1)} %get-tuple-element.299), channel_id=1, source_target_pairs={{0,2},{1,3},{2,0},{3,1},{4,6},{5,7},{6,4},{7,5},{8,10},{9,11},{10,... | collective-permute-start | bytes 983048 | tf_op jit(solution)/shard_map/ppermute | solution.py:358
  6.3 15.1 %collective-permute-start.2 = (f32[10,8,8,128]{3,2,1,0:T(8,128)S(1)}, f32[10,8,8,128]{3,2,1,0:T(8,128)S(1)}, u32[]{:S(2)}, u32[]{:S(2)}) collective-permute-start(f32[10,8,8,128]{3,2,1,0:T(8,128)S(1)} %get-tuple-element.297), channel_id=1, source_target_pairs={{0,3},{1,2},{2,1},{3,0},{4,7},{5,6},{6,5},{7,4},{8,11},{9,10},{10,... | collective-permute-start | bytes 983048 | tf_op jit(solution)/shard_map/ppermute | solution.py:358
  22.7 0.7 copy-start.1
  23.4 0.7 copy-start.4
  24.1 0.7 copy-start.7
  24.8 0.7 copy-start.9
  25.4 0.6 copy-start.11
  26.7 7.2 %collective-permute-start.4 = (f32[4,2,32,128]{3,2,1,0:T(8,128)}, f32[4,2,32,128]{3,2,1,0:T(8,128)}, u32[]{:S(2)}, u32[]{:S(2)}) collective-permute-start(f32[4,2,32,128]{3,2,1,0:T(8,128)} %get-tuple-element.160), channel_id=1, source_target_pairs={{0,4},{2,6},{4,0},{5,9},{6,2},{7,11},{8,12},{9,5},{10,14},{11,7},{... | collective-permute-start | bytes 393224 | tf_op jit(solution)/shard_map/ppermute | solution.py:374
  30.2 3.7 %collective-permute-start.5 = (f32[4,2,32,128]{3,2,1,0:T(8,128)}, f32[4,2,32,128]{3,2,1,0:T(8,128)}, u32[]{:S(2)}, u32[]{:S(2)}) collective-permute-start(f32[4,2,32,128]{3,2,1,0:T(8,128)} %get-tuple-element.161), channel_id=1, source_target_pairs={{1,5},{3,7},{4,8},{5,1},{6,10},{7,3},{8,4},{9,13},{10,6},{11,15},{... | collective-permute-start | bytes 393224 | tf_op jit(solution)/shard_map/ppermute | solution.py:374
  31.6 0.7 copy-start.17
  32.3 6.4 %copy-start.15 = (f32[1,4,8]{2,1,0:T(4,128)S(1)}, f32[1,4,8]{2,1,0:T(4,128)}, u32[]{:S(2)}) copy-start(f32[1,4,8]{2,1,0:T(4,128)} %residual.7) | copy-start | bytes 388
  32.3 6.4 %copy-start.16 = (s32[1,4]{1,0:T(1,128)S(1)}, s32[1,4]{1,0:T(1,128)}, u32[]{:S(2)}) copy-start(s32[1,4]{1,0:T(1,128)} %rec_cell.3) | copy-start | bytes 52
  33.9 58.6 %collective-permute-start.18 = (f32[8,6,8,8,128]{4,3,2,1,0:T(8,128)S(1)}, f32[8,6,8,8,128]{4,3,2,1,0:T(8,128)S(1)}, u32[]{:S(2)}, u32[]{:S(2)}) collective-permute-start(f32[8,6,8,8,128]{4,3,2,1,0:T(8,128)S(1)} %bitcast.20), channel_id=1, source_target_pairs={{0,1},{1,0},{2,3},{3,2},{4,5},{5,4},{6,7},{7,6},{8,9},{9,8},{10,11... | collective-permute-start | bytes 4718600 | tf_op jit(solution)/shard_map/ppermute | solution.py:358
  36.3 56.1 %collective-permute-start.19 = (f32[8,6,8,8,128]{4,3,2,1,0:T(8,128)S(1)}, f32[8,6,8,8,128]{4,3,2,1,0:T(8,128)}, u32[]{:S(2)}, u32[]{:S(2)}) collective-permute-start(f32[8,6,8,8,128]{4,3,2,1,0:T(8,128)S(1)} %bitcast.21), channel_id=1, source_target_pairs={{0,2},{1,3},{2,0},{3,1},{4,6},{5,7},{6,4},{7,5},{8,10},{9,11},{10,... | collective-permute-start | bytes 4718600 | tf_op jit(solution)/shard_map/ppermute | solution.py:358
  38.6 0.9 copy-start.5
  39.5 0.9 copy-start.10
  40.5 0.8 copy-start.14
  41.3 10.5 %copy-start.6 = (f32[6,2,32,128]{3,2,1,0:T(8,128)S(1)}, f32[6,2,32,128]{3,2,1,0:T(8,128)}, u32[]{:S(2)}) copy-start(f32[6,2,32,128]{3,2,1,0:T(8,128)} %copy-done.4) | copy-start | bytes 589828
  42.7 9.2 %collective-permute-start.6 = (bf16[15,32,128]{2,1,0:T(8,128)(2,1)S(1)}, bf16[15,32,128]{2,1,0:T(8,128)(2,1)S(1)}, u32[]{:S(2)}, u32[]{:S(2)}) collective-permute-start(bf16[15,32,128]{2,1,0:T(8,128)(2,1)S(1)} %get-tuple-element.175), channel_id=1, source_target_pairs={{0,4},{2,6},{4,0},{5,9},{6,2},{7,11},{8,12},{9,5},{10,14},{11,7},{... | collective-permute-start | bytes 368648 | tf_op jit(solution)/shard_map/ppermute | solution.py:374
  46.8 0.9 copy-start.2
  47.7 0.9 copy-start.8
  48.6 0.8 copy-start.12
  50.8 6.7 %copy-start.3 = (f32[6,2,32,128]{3,2,1,0:T(8,128)S(1)}, f32[6,2,32,128]{3,2,1,0:T(8,128)}, u32[]{:S(2)}) copy-start(f32[6,2,32,128]{3,2,1,0:T(8,128)} %copy-done.1) | copy-start | bytes 589828
  50.8 6.7 %collective-permute-start.7 = (bf16[15,32,128]{2,1,0:T(8,128)(2,1)S(1)}, bf16[15,32,128]{2,1,0:T(8,128)(2,1)S(1)}, u32[]{:S(2)}, u32[]{:S(2)}) collective-permute-start(bf16[15,32,128]{2,1,0:T(8,128)(2,1)S(1)} %get-tuple-element.183), channel_id=1, source_target_pairs={{1,5},{3,7},{4,8},{5,1},{6,10},{7,3},{8,4},{9,13},{10,6},{11,15},{... | collective-permute-start | bytes 368648 | tf_op jit(solution)/shard_map/ppermute | solution.py:374
  52.3 8.0 %collective-permute-start.8 = (bf16[15,32,128]{2,1,0:T(8,128)(2,1)S(1)}, bf16[15,32,128]{2,1,0:T(8,128)(2,1)S(1)}, u32[]{:S(2)}, u32[]{:S(2)}) collective-permute-start(bf16[15,32,128]{2,1,0:T(8,128)(2,1)S(1)} %get-tuple-element.193), channel_id=1, source_target_pairs={{0,4},{2,6},{4,0},{5,9},{6,2},{7,11},{8,12},{9,5},{10,14},{11,7},{... | collective-permute-start | bytes 368648 | tf_op jit(solution)/shard_map/ppermute | solution.py:374
  58.0 6.7 %collective-permute-start.9 = (bf16[15,32,128]{2,1,0:T(8,128)(2,1)S(1)}, bf16[15,32,128]{2,1,0:T(8,128)(2,1)S(1)}, u32[]{:S(2)}, u32[]{:S(2)}) collective-permute-start(bf16[15,32,128]{2,1,0:T(8,128)(2,1)S(1)} %get-tuple-element.199), channel_id=1, source_target_pairs={{1,5},{3,7},{4,8},{5,1},{6,10},{7,3},{8,4},{9,13},{10,6},{11,15},{... | collective-permute-start | bytes 368648 | tf_op jit(solution)/shard_map/ppermute | solution.py:374
  60.8 6.8 %collective-permute-start.10 = (bf16[15,32,128]{2,1,0:T(8,128)(2,1)S(1)}, bf16[15,32,128]{2,1,0:T(8,128)(2,1)S(1)}, u32[]{:S(2)}, u32[]{:S(2)}) collective-permute-start(bf16[15,32,128]{2,1,0:T(8,128)(2,1)S(1)} %get-tuple-element.207), channel_id=1, source_target_pairs={{0,4},{2,6},{4,0},{5,9},{6,2},{7,11},{8,12},{9,5},{10,14},{11,7},{... | collective-permute-start | bytes 368648 | tf_op jit(solution)/shard_map/ppermute | solution.py:374
  65.2 6.9 %collective-permute-start.11 = (bf16[15,32,128]{2,1,0:T(8,128)(2,1)S(1)}, bf16[15,32,128]{2,1,0:T(8,128)(2,1)S(1)}, u32[]{:S(2)}, u32[]{:S(2)}) collective-permute-start(bf16[15,32,128]{2,1,0:T(8,128)(2,1)S(1)} %get-tuple-element.213), channel_id=1, source_target_pairs={{1,5},{3,7},{4,8},{5,1},{6,10},{7,3},{8,4},{9,13},{10,6},{11,15},{... | collective-permute-start | bytes 368648 | tf_op jit(solution)/shard_map/ppermute | solution.py:374
  68.0 6.9 %collective-permute-start.12 = (bf16[15,32,128]{2,1,0:T(8,128)(2,1)S(1)}, bf16[15,32,128]{2,1,0:T(8,128)(2,1)S(1)}, u32[]{:S(2)}, u32[]{:S(2)}) collective-permute-start(bf16[15,32,128]{2,1,0:T(8,128)(2,1)S(1)} %get-tuple-element.221), channel_id=1, source_target_pairs={{0,4},{2,6},{4,0},{5,9},{6,2},{7,11},{8,12},{9,5},{10,14},{11,7},{... | collective-permute-start | bytes 368648 | tf_op jit(solution)/shard_map/ppermute | solution.py:374
  72.6 7.8 %collective-permute-start.13 = (bf16[15,32,128]{2,1,0:T(8,128)(2,1)S(1)}, bf16[15,32,128]{2,1,0:T(8,128)(2,1)S(1)}, u32[]{:S(2)}, u32[]{:S(2)}) collective-permute-start(bf16[15,32,128]{2,1,0:T(8,128)(2,1)S(1)} %get-tuple-element.227), channel_id=1, source_target_pairs={{1,5},{3,7},{4,8},{5,1},{6,10},{7,3},{8,4},{9,13},{10,6},{11,15},{... | collective-permute-start | bytes 368648 | tf_op jit(solution)/shard_map/ppermute | solution.py:374
  75.4 8.5 %collective-permute-start.14 = (bf16[15,32,128]{2,1,0:T(8,128)(2,1)S(1)}, bf16[15,32,128]{2,1,0:T(8,128)(2,1)S(1)}, u32[]{:S(2)}, u32[]{:S(2)}) collective-permute-start(bf16[15,32,128]{2,1,0:T(8,128)(2,1)S(1)} %get-tuple-element.235), channel_id=1, source_target_pairs={{0,4},{2,6},{4,0},{5,9},{6,2},{7,11},{8,12},{9,5},{10,14},{11,7},{... | collective-permute-start | bytes 368648 | tf_op jit(solution)/shard_map/ppermute | solution.py:374
  80.8 7.6 %collective-permute-start.15 = (bf16[15,32,128]{2,1,0:T(8,128)(2,1)S(1)}, bf16[15,32,128]{2,1,0:T(8,128)(2,1)S(1)}, u32[]{:S(2)}, u32[]{:S(2)}) collective-permute-start(bf16[15,32,128]{2,1,0:T(8,128)(2,1)S(1)} %get-tuple-element.241), channel_id=1, source_target_pairs={{1,5},{3,7},{4,8},{5,1},{6,10},{7,3},{8,4},{9,13},{10,6},{11,15},{... | collective-permute-start | bytes 368648 | tf_op jit(solution)/shard_map/ppermute | solution.py:374
  84.4 6.9 %collective-permute-start.16 = (bf16[15,32,128]{2,1,0:T(8,128)(2,1)S(1)}, bf16[15,32,128]{2,1,0:T(8,128)(2,1)S(1)}, u32[]{:S(2)}, u32[]{:S(2)}) collective-permute-start(bf16[15,32,128]{2,1,0:T(8,128)(2,1)S(1)} %get-tuple-element.249), channel_id=1, source_target_pairs={{0,4},{2,6},{4,0},{5,9},{6,2},{7,11},{8,12},{9,5},{10,14},{11,7},{... | collective-permute-start | bytes 368648 | tf_op jit(solution)/shard_map/ppermute | solution.py:374
  88.9 2.8 %collective-permute-start.17 = (bf16[15,32,128]{2,1,0:T(8,128)(2,1)S(1)}, bf16[15,32,128]{2,1,0:T(8,128)(2,1)S(1)}, u32[]{:S(2)}, u32[]{:S(2)}) collective-permute-start(bf16[15,32,128]{2,1,0:T(8,128)(2,1)S(1)} %get-tuple-element.255), channel_id=1, source_target_pairs={{1,5},{3,7},{4,8},{5,1},{6,10},{7,3},{8,4},{9,13},{10,6},{11,15},{... | collective-permute-start | bytes 368648 | tf_op jit(solution)/shard_map/ppermute | solution.py:374
  92.5 16.4 %collective-permute-start.22 = (f32[8,6,8,8,128]{4,3,2,1,0:T(8,128)}, f32[8,6,8,8,128]{4,3,2,1,0:T(8,128)S(1)}, u32[]{:S(2)}, u32[]{:S(2)}) collective-permute-start(f32[8,6,8,8,128]{4,3,2,1,0:T(8,128)} %collective-permute-done.19.refs_30_.refs_34_), channel_id=1, source_target_pairs={{0,1},{1,0},{2,3},{3,2},{4,5},{5,4},{6,7},{7,6},{8,9},{9,8},{10,11... | collective-permute-start | bytes 4718600 | tf_op jit(solution)/shard_map/ppermute | solution.py:358
  92.5 9.6 %collective-permute-start.20 = (bf16[15,32,128]{2,1,0:T(8,128)(2,1)S(1)}, bf16[15,32,128]{2,1,0:T(8,128)(2,1)S(1)}, u32[]{:S(2)}, u32[]{:S(2)}) collective-permute-start(bf16[15,32,128]{2,1,0:T(8,128)(2,1)S(1)} %get-tuple-element.265), channel_id=1, source_target_pairs={{0,4},{2,6},{4,0},{5,9},{6,2},{7,11},{8,12},{9,5},{10,14},{11,7},{... | collective-permute-start | bytes 368648 | tf_op jit(solution)/shard_map/ppermute | solution.py:374
  99.3 7.7 %collective-permute-start.21 = (bf16[15,32,128]{2,1,0:T(8,128)(2,1)S(1)}, bf16[15,32,128]{2,1,0:T(8,128)(2,1)S(1)}, u32[]{:S(2)}, u32[]{:S(2)}) collective-permute-start(bf16[15,32,128]{2,1,0:T(8,128)(2,1)S(1)} %get-tuple-element.271), channel_id=1, source_target_pairs={{1,5},{3,7},{4,8},{5,1},{6,10},{7,3},{8,4},{9,13},{10,6},{11,15},{... | collective-permute-start | bytes 368648 | tf_op jit(solution)/shard_map/ppermute | solution.py:374
  103.1 8.4 %collective-permute-start.23 = (bf16[15,32,128]{2,1,0:T(8,128)(2,1)S(1)}, bf16[15,32,128]{2,1,0:T(8,128)(2,1)S(1)}, u32[]{:S(2)}, u32[]{:S(2)}) collective-permute-start(bf16[15,32,128]{2,1,0:T(8,128)(2,1)S(1)} %get-tuple-element.281), channel_id=1, source_target_pairs={{0,4},{2,6},{4,0},{5,9},{6,2},{7,11},{8,12},{9,5},{10,14},{11,7},{... | collective-permute-start | bytes 368648 | tf_op jit(solution)/shard_map/ppermute | solution.py:374
  108.0 3.7 %collective-permute-start.24 = (bf16[15,32,128]{2,1,0:T(8,128)(2,1)S(1)}, bf16[15,32,128]{2,1,0:T(8,128)(2,1)S(1)}, u32[]{:S(2)}, u32[]{:S(2)}) collective-permute-start(bf16[15,32,128]{2,1,0:T(8,128)(2,1)S(1)} %get-tuple-element.284), channel_id=1, source_target_pairs={{1,5},{3,7},{4,8},{5,1},{6,10},{7,3},{8,4},{9,13},{10,6},{11,15},{... | collective-permute-start | bytes 368648 | tf_op jit(solution)/shard_map/ppermute | solution.py:374
  113.6 2.7 %collective-permute-start.25 = (f32[2,2,8,8,128]{4,3,2,1,0:T(8,128)S(1)}, f32[2,2,8,8,128]{4,3,2,1,0:T(8,128)S(1)}, u32[]{:S(2)}, u32[]{:S(2)}) collective-permute-start(f32[2,2,8,8,128]{4,3,2,1,0:T(8,128)S(1)} %pad_maximum_fusion.4), channel_id=1, source_target_pairs={{0,1},{1,0},{2,3},{3,2},{4,5},{5,4},{6,7},{7,6},{8,9},{9,8},{10,11... | collective-permute-start | bytes 393224 | tf_op jit(solution)/shard_map/ppermute | solution.py:358
  116.3 4.0 %collective-permute-start.28 = (f32[2,4,8,128]{3,2,1,0:T(8,128)S(1)}, f32[2,4,8,128]{3,2,1,0:T(8,128)S(1)}, u32[]{:S(2)}, u32[]{:S(2)}) collective-permute-start(f32[2,4,8,128]{3,2,1,0:T(8,128)S(1)} %get-tuple-element.296), channel_id=1, source_target_pairs={{0,2},{1,3},{2,0},{3,1},{16,18},{17,19},{18,16},{19,17},{4,6},{5,7... | collective-permute-start | bytes 98312 | tf_op jit(solution)/shard_map/ppermute | solution.py:500
  116.9 4.8 %collective-permute-start.26 = (f32[2,4,8,128]{3,2,1,0:T(8,128)S(1)}, f32[2,4,8,128]{3,2,1,0:T(8,128)S(1)}, u32[]{:S(2)}, u32[]{:S(2)}) collective-permute-start(f32[2,4,8,128]{3,2,1,0:T(8,128)S(1)} %get-tuple-element.295), channel_id=1, source_target_pairs={{0,18},{1,19},{2,16},{3,17},{16,2},{17,3},{18,0},{19,1},{4,22},{5,... | collective-permute-start | bytes 98312 | tf_op jit(solution)/shard_map/ppermute | solution.py:500
  118.4 3.9 %collective-permute-start.27 = (f32[2,4,8,128]{3,2,1,0:T(8,128)S(1)}, f32[2,4,8,128]{3,2,1,0:T(8,128)S(1)}, u32[]{:S(2)}, u32[]{:S(2)}) collective-permute-start(f32[2,4,8,128]{3,2,1,0:T(8,128)S(1)} %dynamic-slice_bitcast_fusion.5), channel_id=1, source_target_pairs={{0,16},{1,17},{2,18},{3,19},{16,0},{17,1},{18,2},{19,3},{4,20},{5,... | collective-permute-start | bytes 98312 | tf_op jit(solution)/shard_map/ppermute | solution.py:500
  (1 other events, 0.6 us)

commit v10 on v7

--- a/solution.py
+++ b/solution.py
@@ -25,7 +25,7 @@
 F32, BF16 = jnp.float32, jnp.bfloat16
 
 
-def call(body, outs, ins, scratch=(), flops=1_000_000):
+def call(body, outs, ins, scratch=(), flops=8_000_000_000):
     scalars, arrays = ins
     return list(pl.pallas_call(
         body,
@@ -395,10 +395,6 @@
     for turn in range(groups):
         factor = jnp.sum(weights * (src_pick == (group ^ turn)).astype(F32), 0)
         combined = combined + factor[:, None, None, None, None] * strains[turn].astype(F32)
-    combined, halos = lax.optimization_barrier((combined, halos))
-    found = {turn: swap(combined, "gy", turn) for turn in range(pieces - 1, 0, -1) if turn & (turn - 1) == 0}
-    found[0] = combined
-
     sent, lights, lames, shears, old_halos, spots, amounts = ([None, None] for _ in range(7))
     fresh = [None, None]
     for side in range(2):
@@ -416,7 +412,9 @@
         sent[side] = to_neighbour(sent[side], side)
     vels = fresh
 
-    rates = []
+    found, rates = {0: combined}, []
+    exchanges = {0: [pieces // 2], 1: [w for w in range(1, pieces // 2) if w & (w - 1) == 0]}
+    rest = [turn for turn in range(pieces) if turn & (turn - 1)]
     for moment in range(moments):
         last = moment == moments - 1
         results = call(
@@ -427,14 +425,17 @@
         rates += results[:2]
         if not last:
             middles = results[2:]
+        if moment in exchanges:
+            ready, rates[-1] = lax.optimization_barrier((combined, rates[-1]))
+            for turn in exchanges[moment]:
+                found[turn] = swap(ready, "gy", turn)
         if moment == 3 * moments // 4:
-            ready, rates[-1] = lax.optimization_barrier((found, rates[-1]))
-            for turn in range(pieces):
-                if turn not in found:
-                    low = turn & -turn
-                    found[turn] = swap(ready[turn ^ low], "gy", low)
+            found, rates[-1] = lax.optimization_barrier((found, rates[-1]))
+            for turn in rest:
+                low = turn & -turn
+                found[turn] = swap(found[turn ^ low], "gy", low)
         if last:
-            early, late = list(range(pieces)), []
+            early, late = [turn for turn in range(pieces) if turn not in rest], rest
             jobs = {turn: list(range(moment)) for turn in early}
             (terms,) = call(
                 functools.partial(correlate, jobs, moment),

time: 126 us -> 113 us (0.90)
  local copies, waits for them, and re-layouts: 14.7 us -> 1.44 us
  waiting for transfers between devices: 33.1 us -> 29.7 us
  other arithmetic: 2.34 us -> 4.51 us
  Pallas kernels: 16.6 us -> 17.9 us
    unnamed x49 -> x11, local copies, waits for them, and re-layouts: 13.3 us -> 0.1 us
    ppermute x8, waiting for transfers between devices: 16.2 us -> 14.2 us  [swap(): return lax.ppermute(array, axis, [(i, i ^ turn) for i in range(count)])]
    ppermute x18, waiting for transfers between devices: 14 us -> 12.5 us  [to_neighbour(): return lax.ppermute(face, ('gx', 'gy'), pairs)]
    add x1, other arithmetic: 1.5 us -> 2.91 us  [local(): combined + factor[:, None, None, None, None] * strains[turn].astype(F32)]
    pallas_call x29, Pallas kernels: 16.6 us -> 17.9 us  [call(): pl.pallas_call(body, out_shape=[jax.ShapeDtypeStruct(shape, kind) for sha...]
  transfers between devices with their start and end apart: 29 -> 29, of which waited for: 14 -> 13; matrix products, arithmetic and copies ran while one was open for 2% -> 3% of each run, Pallas kernels for 12% -> 14%
where the time goes in v10:
time: 113 us; the launch traced here: 112 us
  starting transfers between devices  58.2 us (52%)
  waiting for transfers between devices  29.7 us (26%)
  Pallas kernels  17.9 us (16%)
  other arithmetic  4.51 us (4%)
  local copies, waits for them, and re-layouts  1.44 us (1%)
    ppermute x18, starting transfers between devices, to_neighbour(): return lax.ppermute(face, ('gx', 'gy'), pairs)  47.6 us
    pallas_call x29, Pallas kernels, call(): pl.pallas_call(body, out_shape=[jax.ShapeDtypeStruct(shape, kind) for sha...  17.9 us
    ppermute x8, waiting for transfers between devices, swap(): return lax.ppermute(array, axis, [(i, i ^ turn) for i in range(count)])  14.2 us
    ppermute x18, waiting for transfers between devices, to_neighbour(): return lax.ppermute(face, ('gx', 'gy'), pairs)  12.5 us
    ppermute x8, starting transfers between devices, swap(): return lax.ppermute(array, axis, [(i, i ^ turn) for i in range(count)])  7 us
    ppermute x3, starting transfers between devices, local(): part = lax.ppermute(part, ('sta', 'gy'), pairs)  3.55 us
    ppermute x3, waiting for transfers between devices, local(): part = lax.ppermute(part, ('sta', 'gy'), pairs)  2.96 us
    add x1, other arithmetic, local(): combined + factor[:, None, None, None, None] * strains[turn].astype(F32)  2.91 us
  transfers between devices with their start and end apart: 29, of which 13 were waited for; matrix products, arithmetic and copies ran while one was open for 3% of the time, Pallas kernels for 14%

profile of v10, /device:TPU:0, one launch (start us, length us, event | category | flops | bytes accessed | tf_op | source)
XLA Modules:
  0.0 112.2 jit_solution(13363232772554877006)
XLA Ops:
  0.0 0.8 convert_bitcast_fusion
  0.8 1.3 %dynamic-slice_bitcast_fusion = (f32[9,8,8,128]{3,2,1,0:T(8,128)S(1)}, f32[9,8,8,128]{3,2,1,0:T(8,128)S(1)}, f32[9,8,8,128]{3,2,1,0:T(8,128)S(1)}, f32[9,8,8,128]{3,2,1,0:T(8,128)S(1)}) fusion(f32[1,4,9,8,8,128]{5,4,3,2,1,0:T(8,128)} %param.8, s32[]{:T(128)S(6)} %select_n.27, s32[]{:T(128)S(6)} %select_n.25, s32[]{:T(128)S(6)} %select_n.24, s32[]{:T(128)S(6)} %select_n.26), kind=kLoop, calls=%fused_computation.5 | loop fusion | bytes 2359312 | tf_op jit(solution)/shard_map/jit(dynamic_index_in_dim)/squeeze | solution.py:371
  2.2 2.5 %collective-permute-start.2 = (f32[10,8,8,128]{3,2,1,0:T(8,128)S(1)}, f32[10,8,8,128]{3,2,1,0:T(8,128)S(1)}, u32[]{:S(2)}, u32[]{:S(2)}) collective-permute-start(f32[10,8,8,128]{3,2,1,0:T(8,128)S(1)} %get-tuple-element.305), channel_id=1, source_target_pairs={{0,3},{1,2},{2,1},{3,0},{4,7},{5,6},{6,5},{7,4},{8,11},{9,10},{10,... | collective-permute-start | bytes 983048 | tf_op jit(solution)/shard_map/ppermute | solution.py:340
  4.7 0.7 collective-permute-start
  5.4 2.0 %collective-permute-start.3 = (bf16[8,6,8,8,128]{4,3,2,1,0:T(8,128)(2,1)}, bf16[8,6,8,8,128]{4,3,2,1,0:T(8,128)(2,1)}, u32[]{:S(2)}, u32[]{:S(2)}) collective-permute-start(bf16[8,6,8,8,128]{4,3,2,1,0:T(8,128)(2,1)} %bitcast), channel_id=1, source_target_pairs={{0,16},{16,0},{1,17},{17,1},{2,18},{18,2},{3,19},{19,3},{4,20},{20... | collective-permute-start | bytes 2359304 | tf_op jit(solution)/shard_map/ppermute | solution.py:340
  7.4 5.4 %collective-permute-done.2.refs_3_ = f32[10,8,8,128]{3,2,1,0:T(8,128)S(1)} collective-permute-done((f32[10,8,8,128]{3,2,1,0:T(8,128)S(1)}, f32[10,8,8,128]{3,2,1,0:T(8,128)S(1)}, u32[]{:S(2)}, u32[]{:S(2)}) %collective-permute-start.2) | collective-permute-done | bytes 327712 | tf_op jit(solution)/shard_map/ppermute | solution.py:340
  12.8 7.2 %collective-permute-done.1.refs_2_ = f32[10,8,8,128]{3,2,1,0:T(8,128)S(1)} collective-permute-done((f32[10,8,8,128]{3,2,1,0:T(8,128)S(1)}, f32[10,8,8,128]{3,2,1,0:T(8,128)S(1)}, u32[]{:S(2)}, u32[]{:S(2)}) %collective-permute-start.1) | collective-permute-done | bytes 327712 | tf_op jit(solution)/shard_map/ppermute | solution.py:340
  20.0 0.7 shard_map.82
  20.7 4.3 %collective-permute-start.4 = (f32[4,2,32,128]{3,2,1,0:T(8,128)S(1)}, f32[4,2,32,128]{3,2,1,0:T(8,128)S(1)}, u32[]{:S(2)}, u32[]{:S(2)}) collective-permute-start(f32[4,2,32,128]{3,2,1,0:T(8,128)S(1)} %get-tuple-element.161), channel_id=1, source_target_pairs={{0,4},{2,6},{4,0},{5,9},{6,2},{7,11},{8,12},{9,5},{10,14},{11,7},{... | collective-permute-start | bytes 393224 | tf_op jit(solution)/shard_map/ppermute | solution.py:356
  25.1 0.7 collective-permute-start.5
  25.8 2.1 %collective-permute-done.4.halo = f32[4,2,32,128]{3,2,1,0:T(8,128)S(1)} collective-permute-done((f32[4,2,32,128]{3,2,1,0:T(8,128)S(1)}, f32[4,2,32,128]{3,2,1,0:T(8,128)S(1)}, u32[]{:S(2)}, u32[]{:S(2)}) %collective-permute-start.4) | collective-permute-done | bytes 131104 | tf_op jit(solution)/shard_map/ppermute | solution.py:356
  27.9 1.1 %shard_map.83 = (f32[3,4,32,128]{3,2,1,0:T(8,128)S(1)}, bf16[15,32,128]{2,1,0:T(8,128)(2,1)S(1)}, f32[4,32,128]{2,1,0:T(8,128)S(1)}, f32[6,32,128]{2,1,0:T(8,128...) custom-call(f32[16,3]{1,0:T(8,128)S(1)} %copy.9.table, ...), custom_call_target="tpu_custom_call" | custom-call | flops 8000000000 | bytes 2000000 | tf_op jit(solution)/shard_map/pallas_call | solution.py:30
  29.1 4.2 %collective-permute-start.6 = (bf16[15,32,128]{2,1,0:T(8,128)(2,1)S(1)}, bf16[15,32,128]{2,1,0:T(8,128)(2,1)S(1)}, u32[]{:S(2)}, u32[]{:S(2)}) collective-permute-start(bf16[15,32,128]{2,1,0:T(8,128)(2,1)S(1)} %get-tuple-element.177), channel_id=1, source_target_pairs={{0,4},{2,6},{4,0},{5,9},{6,2},{7,11},{8,12},{9,5},{10,14},{11,7},{... | collective-permute-start | bytes 368648 | tf_op jit(solution)/shard_map/ppermute | solution.py:356
  33.3 1.1 %shard_map.84 = (f32[3,4,32,128]{3,2,1,0:T(8,128)S(1)}, bf16[15,32,128]{2,1,0:T(8,128)(2,1)S(1)}, f32[4,32,128]{2,1,0:T(8,128)S(1)}, f32[6,32,128]{2,1,0:T(8,128...) custom-call(f32[16,3]{1,0:T(8,128)S(1)} %copy.9.table, ...), custom_call_target="tpu_custom_call" | custom-call | flops 8000000000 | bytes 2000000 | tf_op jit(solution)/shard_map/pallas_call | solution.py:30
  34.5 0.7 collective-permute-start.7
  35.4 2.9 %multiply_add_fusion.refs_28_.refs_32_ = f32[8,6,8,8,128]{4,3,2,1,0:T(8,128)} fusion(bf16[8,6,8,8,128]{4,3,2,1,0:T(8,128)(2,1)} %collective-permute-done.3, bf16[8,6,8,8,128]{4,3,2,1,0:T(8,128)(2,1)} %bitcast, f32[8]{0:T(128)S(1)} %get-tuple-element.294, f32[8]{0:T(128)S(1)} %get-tuple-element.293), kind=kLoop, calls=%fused_computation | loop fusion | flops 1966080 | bytes 3145792 | tf_op jit(solution)/shard_map/add | solution.py:397
  38.3 1.5 %collective-permute-start.19 = (f32[8,6,8,8,128]{4,3,2,1,0:T(8,128)}, f32[8,6,8,8,128]{4,3,2,1,0:T(8,128)}, u32[]{:S(2)}, u32[]{:S(2)}) collective-permute-start(f32[8,6,8,8,128]{4,3,2,1,0:T(8,128)} %multiply_add_fusion.refs_28_.refs_32_), channel_id=1, source_target_pairs={{0,2},{1,3},{2,0},{3,1},{4,6},{5,7},{6,4},{7,5},{8,10},{9,11},{10,... | collective-permute-start | bytes 4718600 | tf_op jit(solution)/shard_map/ppermute | solution.py:340
  40.3 0.7 collective-permute-start.9
  41.5 8.7 %collective-permute-start.8 = (bf16[15,32,128]{2,1,0:T(8,128)(2,1)S(1)}, bf16[15,32,128]{2,1,0:T(8,128)(2,1)S(1)}, u32[]{:S(2)}, u32[]{:S(2)}) collective-permute-start(bf16[15,32,128]{2,1,0:T(8,128)(2,1)S(1)} %get-tuple-element.196), channel_id=1, source_target_pairs={{0,4},{2,6},{4,0},{5,9},{6,2},{7,11},{8,12},{9,5},{10,14},{11,7},{... | collective-permute-start | bytes 368648 | tf_op jit(solution)/shard_map/ppermute | solution.py:356
  51.0 0.7 collective-permute-start.11
  51.6 1.4 %collective-permute-done.8.halo = bf16[15,32,128]{2,1,0:T(8,128)(2,1)S(1)} collective-permute-done((bf16[15,32,128]{2,1,0:T(8,128)(2,1)S(1)}, bf16[15,32,128]{2,1,0:T(8,128)(2,1)S(1)}, u32[]{:S(2)}, u32[]{:S(2)}) %collective-permute-start.8) | collective-permute-done | bytes 122912 | tf_op jit(solution)/shard_map/ppermute | solution.py:356
  53.5 4.3 %collective-permute-start.10 = (bf16[15,32,128]{2,1,0:T(8,128)(2,1)S(1)}, bf16[15,32,128]{2,1,0:T(8,128)(2,1)S(1)}, u32[]{:S(2)}, u32[]{:S(2)}) collective-permute-start(bf16[15,32,128]{2,1,0:T(8,128)(2,1)S(1)} %get-tuple-element.210), channel_id=1, source_target_pairs={{0,4},{2,6},{4,0},{5,9},{6,2},{7,11},{8,12},{9,5},{10,14},{11,7},{... | collective-permute-start | bytes 368648 | tf_op jit(solution)/shard_map/ppermute | solution.py:356
  58.6 0.7 collective-permute-start.13
  59.2 1.4 %collective-permute-done.10.halo = bf16[15,32,128]{2,1,0:T(8,128)(2,1)S(1)} collective-permute-done((bf16[15,32,128]{2,1,0:T(8,128)(2,1)S(1)}, bf16[15,32,128]{2,1,0:T(8,128)(2,1)S(1)}, u32[]{:S(2)}, u32[]{:S(2)}) %collective-permute-start.10) | collective-permute-done | bytes 122912 | tf_op jit(solution)/shard_map/ppermute | solution.py:356
  61.1 3.9 %collective-permute-start.12 = (bf16[15,32,128]{2,1,0:T(8,128)(2,1)S(1)}, bf16[15,32,128]{2,1,0:T(8,128)(2,1)S(1)}, u32[]{:S(2)}, u32[]{:S(2)}) collective-permute-start(bf16[15,32,128]{2,1,0:T(8,128)(2,1)S(1)} %get-tuple-element.224), channel_id=1, source_target_pairs={{0,4},{2,6},{4,0},{5,9},{6,2},{7,11},{8,12},{9,5},{10,14},{11,7},{... | collective-permute-start | bytes 368648 | tf_op jit(solution)/shard_map/ppermute | solution.py:356
  65.8 0.7 collective-permute-start.15
  66.5 1.4 %collective-permute-done.12.halo = bf16[15,32,128]{2,1,0:T(8,128)(2,1)S(1)} collective-permute-done((bf16[15,32,128]{2,1,0:T(8,128)(2,1)S(1)}, bf16[15,32,128]{2,1,0:T(8,128)(2,1)S(1)}, u32[]{:S(2)}, u32[]{:S(2)}) %collective-permute-start.12) | collective-permute-done | bytes 122912 | tf_op jit(solution)/shard_map/ppermute | solution.py:356
  68.4 3.9 %collective-permute-start.14 = (bf16[15,32,128]{2,1,0:T(8,128)(2,1)S(1)}, bf16[15,32,128]{2,1,0:T(8,128)(2,1)S(1)}, u32[]{:S(2)}, u32[]{:S(2)}) collective-permute-start(bf16[15,32,128]{2,1,0:T(8,128)(2,1)S(1)} %get-tuple-element.238), channel_id=1, source_target_pairs={{0,4},{2,6},{4,0},{5,9},{6,2},{7,11},{8,12},{9,5},{10,14},{11,7},{... | collective-permute-start | bytes 368648 | tf_op jit(solution)/shard_map/ppermute | solution.py:356
  73.0 0.7 collective-permute-start.17
  73.7 1.4 %collective-permute-done.14.halo = bf16[15,32,128]{2,1,0:T(8,128)(2,1)S(1)} collective-permute-done((bf16[15,32,128]{2,1,0:T(8,128)(2,1)S(1)}, bf16[15,32,128]{2,1,0:T(8,128)(2,1)S(1)}, u32[]{:S(2)}, u32[]{:S(2)}) %collective-permute-start.14) | collective-permute-done | bytes 122912 | tf_op jit(solution)/shard_map/ppermute | solution.py:356
  75.6 5.1 %collective-permute-start.16 = (bf16[15,32,128]{2,1,0:T(8,128)(2,1)S(1)}, bf16[15,32,128]{2,1,0:T(8,128)(2,1)S(1)}, u32[]{:S(2)}, u32[]{:S(2)}) collective-permute-start(bf16[15,32,128]{2,1,0:T(8,128)(2,1)S(1)} %get-tuple-element.252), channel_id=1, source_target_pairs={{0,4},{2,6},{4,0},{5,9},{6,2},{7,11},{8,12},{9,5},{10,14},{11,7},{... | collective-permute-start | bytes 368648 | tf_op jit(solution)/shard_map/ppermute | solution.py:356
  81.0 0.5 shard_map.102
  81.5 0.7 collective-permute-start.21
  82.1 2.7 %collective-permute-done.16.halo = bf16[15,32,128]{2,1,0:T(8,128)(2,1)S(1)} collective-permute-done((bf16[15,32,128]{2,1,0:T(8,128)(2,1)S(1)}, bf16[15,32,128]{2,1,0:T(8,128)(2,1)S(1)}, u32[]{:S(2)}, u32[]{:S(2)}) %collective-permute-start.16) | collective-permute-done | bytes 122912 | tf_op jit(solution)/shard_map/ppermute | solution.py:356
  85.3 3.7 %collective-permute-start.20 = (bf16[15,32,128]{2,1,0:T(8,128)(2,1)S(1)}, bf16[15,32,128]{2,1,0:T(8,128)(2,1)S(1)}, u32[]{:S(2)}, u32[]{:S(2)}) collective-permute-start(bf16[15,32,128]{2,1,0:T(8,128)(2,1)S(1)} %get-tuple-element.269), channel_id=1, source_target_pairs={{0,4},{2,6},{4,0},{5,9},{6,2},{7,11},{8,12},{9,5},{10,14},{11,7},{... | collective-permute-start | bytes 368648 | tf_op jit(solution)/shard_map/ppermute | solution.py:356
  89.2 1.0 shard_map.105
  90.2 0.7 collective-permute-start.23
  90.8 2.1 %collective-permute-done.20.halo = bf16[15,32,128]{2,1,0:T(8,128)(2,1)S(1)} collective-permute-done((bf16[15,32,128]{2,1,0:T(8,128)(2,1)S(1)}, bf16[15,32,128]{2,1,0:T(8,128)(2,1)S(1)}, u32[]{:S(2)}, u32[]{:S(2)}) %collective-permute-start.20) | collective-permute-done | bytes 122912 | tf_op jit(solution)/shard_map/ppermute | solution.py:356
  92.9 0.9 shard_map.104
  93.8 3.5 %collective-permute-start.22 = (bf16[15,32,128]{2,1,0:T(8,128)(2,1)S(1)}, bf16[15,32,128]{2,1,0:T(8,128)(2,1)S(1)}, u32[]{:S(2)}, u32[]{:S(2)}) collective-permute-start(bf16[15,32,128]{2,1,0:T(8,128)(2,1)S(1)} %get-tuple-element.287), channel_id=1, source_target_pairs={{0,4},{2,6},{4,0},{5,9},{6,2},{7,11},{8,12},{9,5},{10,14},{11,7},{... | collective-permute-start | bytes 368648 | tf_op jit(solution)/shard_map/ppermute | solution.py:356
  97.6 2.8 %shard_map.107.refs_36_ = f32[3,2,8,8,128]{4,3,2,1,0:T(8,128)S(1)} custom-call(f32[1,4,8]{2,1,0:T(4,128)S(1)} %copy-done, f32[6,2,32,128]{3,2,1,0:T(8,128)S(1)} %get-tuple-element.172.refs_0_, f32[6,2,32,128]{3,2,1,0:T(8,128)S(1)} %get-tuple-element.176.refs_1_, f32[6,2,32,128]{3,2,1,0:T(8,128)S(1)} %get-tuple-element.184.refs_2_, ...), custom_call_target="tpu_custom_call" | custom-call | flops 8000000000 | bytes 2000000 | tf_op jit(solution)/shard_map/pallas_call | solution.py:30
  101.3 2.4 %shard_map.110 = f32[4,2,8,8,128]{4,3,2,1,0:T(8,128)S(1)} custom-call(f32[1,4,8]{2,1,0:T(4,128)S(1)} %copy-done, f32[6,2,32,128]{3,2,1,0:T(8,128)S(1)} %get-tuple-element.172.refs_0_, f32[6,2,32,128]{3,2,1,0:T(8,128)S(1)} %get-tuple-element.176.refs_1_, f32[6,2,32,128]{3,2,1,0:T(8,128)S(1)} %get-tuple-element.184.refs_2_, ...), custom_call_target="tpu_custom_call" | custom-call | flops 8000000000 | bytes 2000000 | tf_op jit(solution)/shard_map/pallas_call | solution.py:30
  103.8 1.2 %collective-permute-done.25 = f32[2,2,8,8,128]{4,3,2,1,0:T(8,128)S(1)} collective-permute-done((f32[2,2,8,8,128]{4,3,2,1,0:T(8,128)S(1)}, f32[2,2,8,8,128]{4,3,2,1,0:T(8,128)S(1)}, u32[]{:S(2)}, u32[]{:S(2)}) %collective-permute-start.25) | collective-permute-done | bytes 131104 | tf_op jit(solution)/shard_map/ppermute | solution.py:340
  105.1 1.5 %collective-permute-start.27 = (f32[2,4,8,128]{3,2,1,0:T(8,128)S(1)}, f32[2,4,8,128]{3,2,1,0:T(8,128)S(1)}, u32[]{:S(2)}, u32[]{:S(2)}) collective-permute-start(f32[2,4,8,128]{3,2,1,0:T(8,128)S(1)} %dynamic-slice_bitcast_fusion.5), channel_id=1, source_target_pairs={{0,16},{1,17},{2,18},{3,19},{16,0},{17,1},{18,2},{19,3},{4,20},{5,... | collective-permute-start | bytes 98312 | tf_op jit(solution)/shard_map/ppermute | solution.py:483
  106.7 0.7 collective-permute-start.26
  107.4 1.3 %collective-permute-start.28 = (f32[2,4,8,128]{3,2,1,0:T(8,128)S(1)}, f32[2,4,8,128]{3,2,1,0:T(8,128)S(1)}, u32[]{:S(2)}, u32[]{:S(2)}) collective-permute-start(f32[2,4,8,128]{3,2,1,0:T(8,128)S(1)} %get-tuple-element.304), channel_id=1, source_target_pairs={{0,2},{1,3},{2,0},{3,1},{16,18},{17,19},{18,16},{19,17},{4,6},{5,7... | collective-permute-start | bytes 98312 | tf_op jit(solution)/shard_map/ppermute | solution.py:483
  109.1 2.5 %collective-permute-done.26 = f32[2,4,8,128]{3,2,1,0:T(8,128)S(1)} collective-permute-done((f32[2,4,8,128]{3,2,1,0:T(8,128)S(1)}, f32[2,4,8,128]{3,2,1,0:T(8,128)S(1)}, u32[]{:S(2)}, u32[]{:S(2)}) %collective-permute-start.26) | collective-permute-done | bytes 32800 | tf_op jit(solution)/shard_map/ppermute | solution.py:483
  111.6 0.6 bitcast_add_fusion
  (62 shorter events, 9.0 us)
Async XLA Ops:
  2.2 10.6 %collective-permute-start.2 = (f32[10,8,8,128]{3,2,1,0:T(8,128)S(1)}, f32[10,8,8,128]{3,2,1,0:T(8,128)S(1)}, u32[]{:S(2)}, u32[]{:S(2)}) collective-permute-start(f32[10,8,8,128]{3,2,1,0:T(8,128)S(1)} %get-tuple-element.305), channel_id=1, source_target_pairs={{0,3},{1,2},{2,1},{3,0},{4,7},{5,6},{6,5},{7,4},{8,11},{9,10},{10,... | collective-permute-start | bytes 983048 | tf_op jit(solution)/shard_map/ppermute | solution.py:340
  4.7 8.1 %collective-permute-start = (f32[10,8,8,128]{3,2,1,0:T(8,128)S(1)}, f32[10,8,8,128]{3,2,1,0:T(8,128)S(1)}, u32[]{:S(2)}, u32[]{:S(2)}) collective-permute-start(f32[10,8,8,128]{3,2,1,0:T(8,128)S(1)} %get-tuple-element.306), channel_id=1, source_target_pairs={{0,1},{1,0},{2,3},{3,2},{4,5},{5,4},{6,7},{7,6},{8,9},{9,8},{10,11... | collective-permute-start | bytes 983048 | tf_op jit(solution)/shard_map/ppermute | solution.py:340
  5.4 14.6 %collective-permute-start.1 = (f32[10,8,8,128]{3,2,1,0:T(8,128)S(1)}, f32[10,8,8,128]{3,2,1,0:T(8,128)S(1)}, u32[]{:S(2)}, u32[]{:S(2)}) collective-permute-start(f32[10,8,8,128]{3,2,1,0:T(8,128)S(1)} %get-tuple-element.307), channel_id=1, source_target_pairs={{0,2},{1,3},{2,0},{3,1},{4,6},{5,7},{6,4},{7,5},{8,10},{9,11},{10,... | collective-permute-start | bytes 983048 | tf_op jit(solution)/shard_map/ppermute | solution.py:340
  5.4 20.4 %collective-permute-start.3 = (bf16[8,6,8,8,128]{4,3,2,1,0:T(8,128)(2,1)}, bf16[8,6,8,8,128]{4,3,2,1,0:T(8,128)(2,1)}, u32[]{:S(2)}, u32[]{:S(2)}) collective-permute-start(bf16[8,6,8,8,128]{4,3,2,1,0:T(8,128)(2,1)} %bitcast), channel_id=1, source_target_pairs={{0,16},{16,0},{1,17},{17,1},{2,18},{18,2},{3,19},{19,3},{4,20},{20... | collective-permute-start | bytes 2359304 | tf_op jit(solution)/shard_map/ppermute | solution.py:340
  20.0 5.0 %copy-start.4 = (s32[2,8,2]{1,2,0:T(2,128)S(1)}, s32[2,8,2]{1,2,0:T(2,128)}, u32[]{:S(2)}) copy-start(s32[2,8,2]{1,2,0:T(2,128)} %param.14) | copy-start | bytes 388
  20.0 5.0 %copy-start.2 = (f32[16,3]{0,1:T(4,128)S(1)}, f32[16,3]{0,1:T(4,128)}, u32[]{:S(2)}) copy-start(f32[16,3]{0,1:T(4,128)} %param.11) | copy-start | bytes 580
  20.0 5.1 %copy-start.3 = (s32[2,8]{1,0:T(2,128)S(1)}, s32[2,8]{1,0:T(2,128)}, u32[]{:S(2)}) copy-start(s32[2,8]{1,0:T(2,128)} %param.15) | copy-start | bytes 196
  20.0 7.9 %copy-start = (f32[1,4,8]{2,1,0:T(4,128)S(1)}, f32[1,4,8]{2,1,0:T(4,128)}, u32[]{:S(2)}) copy-start(f32[1,4,8]{2,1,0:T(4,128)} %residual.7) | copy-start | bytes 388
  20.0 7.9 %copy-start.1 = (s32[1,4]{1,0:T(1,128)S(1)}, s32[1,4]{1,0:T(1,128)}, u32[]{:S(2)}) copy-start(s32[1,4]{1,0:T(1,128)} %rec_cell.3) | copy-start | bytes 52
  20.7 7.2 %collective-permute-start.4 = (f32[4,2,32,128]{3,2,1,0:T(8,128)S(1)}, f32[4,2,32,128]{3,2,1,0:T(8,128)S(1)}, u32[]{:S(2)}, u32[]{:S(2)}) collective-permute-start(f32[4,2,32,128]{3,2,1,0:T(8,128)S(1)} %get-tuple-element.161), channel_id=1, source_target_pairs={{0,4},{2,6},{4,0},{5,9},{6,2},{7,11},{8,12},{9,5},{10,14},{11,7},{... | collective-permute-start | bytes 393224 | tf_op jit(solution)/shard_map/ppermute | solution.py:356
  25.1 8.2 %collective-permute-start.5 = (f32[4,2,32,128]{3,2,1,0:T(8,128)S(1)}, f32[4,2,32,128]{3,2,1,0:T(8,128)S(1)}, u32[]{:S(2)}, u32[]{:S(2)}) collective-permute-start(f32[4,2,32,128]{3,2,1,0:T(8,128)S(1)} %get-tuple-element.166), channel_id=1, source_target_pairs={{1,5},{3,7},{4,8},{5,1},{6,10},{7,3},{8,4},{9,13},{10,6},{11,15},{... | collective-permute-start | bytes 393224 | tf_op jit(solution)/shard_map/ppermute | solution.py:356
  29.1 11.9 %collective-permute-start.6 = (bf16[15,32,128]{2,1,0:T(8,128)(2,1)S(1)}, bf16[15,32,128]{2,1,0:T(8,128)(2,1)S(1)}, u32[]{:S(2)}, u32[]{:S(2)}) collective-permute-start(bf16[15,32,128]{2,1,0:T(8,128)(2,1)S(1)} %get-tuple-element.177), channel_id=1, source_target_pairs={{0,4},{2,6},{4,0},{5,9},{6,2},{7,11},{8,12},{9,5},{10,14},{11,7},{... | collective-permute-start | bytes 368648 | tf_op jit(solution)/shard_map/ppermute | solution.py:356
  34.5 5.4 %collective-permute-start.7 = (bf16[15,32,128]{2,1,0:T(8,128)(2,1)S(1)}, bf16[15,32,128]{2,1,0:T(8,128)(2,1)S(1)}, u32[]{:S(2)}, u32[]{:S(2)}) collective-permute-start(bf16[15,32,128]{2,1,0:T(8,128)(2,1)S(1)} %get-tuple-element.185), channel_id=1, source_target_pairs={{1,5},{3,7},{4,8},{5,1},{6,10},{7,3},{8,4},{9,13},{10,6},{11,15},{... | collective-permute-start | bytes 368648 | tf_op jit(solution)/shard_map/ppermute | solution.py:356
  38.3 59.2 %collective-permute-start.19 = (f32[8,6,8,8,128]{4,3,2,1,0:T(8,128)}, f32[8,6,8,8,128]{4,3,2,1,0:T(8,128)}, u32[]{:S(2)}, u32[]{:S(2)}) collective-permute-start(f32[8,6,8,8,128]{4,3,2,1,0:T(8,128)} %multiply_add_fusion.refs_28_.refs_32_), channel_id=1, source_target_pairs={{0,2},{1,3},{2,0},{3,1},{4,6},{5,7},{6,4},{7,5},{8,10},{9,11},{10,... | collective-permute-start | bytes 4718600 | tf_op jit(solution)/shard_map/ppermute | solution.py:340
  40.3 10.2 %collective-permute-start.9 = (bf16[15,32,128]{2,1,0:T(8,128)(2,1)S(1)}, bf16[15,32,128]{2,1,0:T(8,128)(2,1)S(1)}, u32[]{:S(2)}, u32[]{:S(2)}) collective-permute-start(bf16[15,32,128]{2,1,0:T(8,128)(2,1)S(1)} %get-tuple-element.202), channel_id=1, source_target_pairs={{1,5},{3,7},{4,8},{5,1},{6,10},{7,3},{8,4},{9,13},{10,6},{11,15},{... | collective-permute-start | bytes 368648 | tf_op jit(solution)/shard_map/ppermute | solution.py:356
  41.5 11.5 %collective-permute-start.8 = (bf16[15,32,128]{2,1,0:T(8,128)(2,1)S(1)}, bf16[15,32,128]{2,1,0:T(8,128)(2,1)S(1)}, u32[]{:S(2)}, u32[]{:S(2)}) collective-permute-start(bf16[15,32,128]{2,1,0:T(8,128)(2,1)S(1)} %get-tuple-element.196), channel_id=1, source_target_pairs={{0,4},{2,6},{4,0},{5,9},{6,2},{7,11},{8,12},{9,5},{10,14},{11,7},{... | collective-permute-start | bytes 368648 | tf_op jit(solution)/shard_map/ppermute | solution.py:356
  50.4 47.1 %collective-permute-start.18 = (f32[8,6,8,8,128]{4,3,2,1,0:T(8,128)}, f32[8,6,8,8,128]{4,3,2,1,0:T(8,128)S(1)}, u32[]{:S(2)}, u32[]{:S(2)}) collective-permute-start(f32[8,6,8,8,128]{4,3,2,1,0:T(8,128)} %multiply_add_fusion.refs_28_.refs_32_), channel_id=1, source_target_pairs={{0,1},{1,0},{2,3},{3,2},{4,5},{5,4},{6,7},{7,6},{8,9},{9,8},{10,11... | collective-permute-start | bytes 4718600 | tf_op jit(solution)/shard_map/ppermute | solution.py:340
  51.0 7.1 %collective-permute-start.11 = (bf16[15,32,128]{2,1,0:T(8,128)(2,1)S(1)}, bf16[15,32,128]{2,1,0:T(8,128)(2,1)S(1)}, u32[]{:S(2)}, u32[]{:S(2)}) collective-permute-start(bf16[15,32,128]{2,1,0:T(8,128)(2,1)S(1)} %get-tuple-element.216), channel_id=1, source_target_pairs={{1,5},{3,7},{4,8},{5,1},{6,10},{7,3},{8,4},{9,13},{10,6},{11,15},{... | collective-permute-start | bytes 368648 | tf_op jit(solution)/shard_map/ppermute | solution.py:356
  53.5 7.2 %collective-permute-start.10 = (bf16[15,32,128]{2,1,0:T(8,128)(2,1)S(1)}, bf16[15,32,128]{2,1,0:T(8,128)(2,1)S(1)}, u32[]{:S(2)}, u32[]{:S(2)}) collective-permute-start(bf16[15,32,128]{2,1,0:T(8,128)(2,1)S(1)} %get-tuple-element.210), channel_id=1, source_target_pairs={{0,4},{2,6},{4,0},{5,9},{6,2},{7,11},{8,12},{9,5},{10,14},{11,7},{... | collective-permute-start | bytes 368648 | tf_op jit(solution)/shard_map/ppermute | solution.py:356
  58.6 6.8 %collective-permute-start.13 = (bf16[15,32,128]{2,1,0:T(8,128)(2,1)S(1)}, bf16[15,32,128]{2,1,0:T(8,128)(2,1)S(1)}, u32[]{:S(2)}, u32[]{:S(2)}) collective-permute-start(bf16[15,32,128]{2,1,0:T(8,128)(2,1)S(1)} %get-tuple-element.230), channel_id=1, source_target_pairs={{1,5},{3,7},{4,8},{5,1},{6,10},{7,3},{8,4},{9,13},{10,6},{11,15},{... | collective-permute-start | bytes 368648 | tf_op jit(solution)/shard_map/ppermute | solution.py:356
  61.1 6.8 %collective-permute-start.12 = (bf16[15,32,128]{2,1,0:T(8,128)(2,1)S(1)}, bf16[15,32,128]{2,1,0:T(8,128)(2,1)S(1)}, u32[]{:S(2)}, u32[]{:S(2)}) collective-permute-start(bf16[15,32,128]{2,1,0:T(8,128)(2,1)S(1)} %get-tuple-element.224), channel_id=1, source_target_pairs={{0,4},{2,6},{4,0},{5,9},{6,2},{7,11},{8,12},{9,5},{10,14},{11,7},{... | collective-permute-start | bytes 368648 | tf_op jit(solution)/shard_map/ppermute | solution.py:356
  65.8 6.8 %collective-permute-start.15 = (bf16[15,32,128]{2,1,0:T(8,128)(2,1)S(1)}, bf16[15,32,128]{2,1,0:T(8,128)(2,1)S(1)}, u32[]{:S(2)}, u32[]{:S(2)}) collective-permute-start(bf16[15,32,128]{2,1,0:T(8,128)(2,1)S(1)} %get-tuple-element.244), channel_id=1, source_target_pairs={{1,5},{3,7},{4,8},{5,1},{6,10},{7,3},{8,4},{9,13},{10,6},{11,15},{... | collective-permute-start | bytes 368648 | tf_op jit(solution)/shard_map/ppermute | solution.py:356
  68.4 6.8 %collective-permute-start.14 = (bf16[15,32,128]{2,1,0:T(8,128)(2,1)S(1)}, bf16[15,32,128]{2,1,0:T(8,128)(2,1)S(1)}, u32[]{:S(2)}, u32[]{:S(2)}) collective-permute-start(bf16[15,32,128]{2,1,0:T(8,128)(2,1)S(1)} %get-tuple-element.238), channel_id=1, source_target_pairs={{0,4},{2,6},{4,0},{5,9},{6,2},{7,11},{8,12},{9,5},{10,14},{11,7},{... | collective-permute-start | bytes 368648 | tf_op jit(solution)/shard_map/ppermute | solution.py:356
  73.0 7.9 %collective-permute-start.17 = (bf16[15,32,128]{2,1,0:T(8,128)(2,1)S(1)}, bf16[15,32,128]{2,1,0:T(8,128)(2,1)S(1)}, u32[]{:S(2)}, u32[]{:S(2)}) collective-permute-start(bf16[15,32,128]{2,1,0:T(8,128)(2,1)S(1)} %get-tuple-element.258), channel_id=1, source_target_pairs={{1,5},{3,7},{4,8},{5,1},{6,10},{7,3},{8,4},{9,13},{10,6},{11,15},{... | collective-permute-start | bytes 368648 | tf_op jit(solution)/shard_map/ppermute | solution.py:356
  75.6 9.2 %collective-permute-start.16 = (bf16[15,32,128]{2,1,0:T(8,128)(2,1)S(1)}, bf16[15,32,128]{2,1,0:T(8,128)(2,1)S(1)}, u32[]{:S(2)}, u32[]{:S(2)}) collective-permute-start(bf16[15,32,128]{2,1,0:T(8,128)(2,1)S(1)} %get-tuple-element.252), channel_id=1, source_target_pairs={{0,4},{2,6},{4,0},{5,9},{6,2},{7,11},{8,12},{9,5},{10,14},{11,7},{... | collective-permute-start | bytes 368648 | tf_op jit(solution)/shard_map/ppermute | solution.py:356
  81.5 7.7 %collective-permute-start.21 = (bf16[15,32,128]{2,1,0:T(8,128)(2,1)S(1)}, bf16[15,32,128]{2,1,0:T(8,128)(2,1)S(1)}, u32[]{:S(2)}, u32[]{:S(2)}) collective-permute-start(bf16[15,32,128]{2,1,0:T(8,128)(2,1)S(1)} %get-tuple-element.275), channel_id=1, source_target_pairs={{1,5},{3,7},{4,8},{5,1},{6,10},{7,3},{8,4},{9,13},{10,6},{11,15},{... | collective-permute-start | bytes 368648 | tf_op jit(solution)/shard_map/ppermute | solution.py:356
  85.3 7.6 %collective-permute-start.20 = (bf16[15,32,128]{2,1,0:T(8,128)(2,1)S(1)}, bf16[15,32,128]{2,1,0:T(8,128)(2,1)S(1)}, u32[]{:S(2)}, u32[]{:S(2)}) collective-permute-start(bf16[15,32,128]{2,1,0:T(8,128)(2,1)S(1)} %get-tuple-element.269), channel_id=1, source_target_pairs={{0,4},{2,6},{4,0},{5,9},{6,2},{7,11},{8,12},{9,5},{10,14},{11,7},{... | collective-permute-start | bytes 368648 | tf_op jit(solution)/shard_map/ppermute | solution.py:356
  90.2 10.3 %collective-permute-start.23 = (bf16[15,32,128]{2,1,0:T(8,128)(2,1)S(1)}, bf16[15,32,128]{2,1,0:T(8,128)(2,1)S(1)}, u32[]{:S(2)}, u32[]{:S(2)}) collective-permute-start(bf16[15,32,128]{2,1,0:T(8,128)(2,1)S(1)} %get-tuple-element.290), channel_id=1, source_target_pairs={{1,5},{3,7},{4,8},{5,1},{6,10},{7,3},{8,4},{9,13},{10,6},{11,15},{... | collective-permute-start | bytes 368648 | tf_op jit(solution)/shard_map/ppermute | solution.py:356
  93.8 6.8 %collective-permute-start.22 = (bf16[15,32,128]{2,1,0:T(8,128)(2,1)S(1)}, bf16[15,32,128]{2,1,0:T(8,128)(2,1)S(1)}, u32[]{:S(2)}, u32[]{:S(2)}) collective-permute-start(bf16[15,32,128]{2,1,0:T(8,128)(2,1)S(1)} %get-tuple-element.287), channel_id=1, source_target_pairs={{0,4},{2,6},{4,0},{5,9},{6,2},{7,11},{8,12},{9,5},{10,14},{11,7},{... | collective-permute-start | bytes 368648 | tf_op jit(solution)/shard_map/ppermute | solution.py:356
  97.6 3.7 %collective-permute-start.24 = (f32[8,6,8,8,128]{4,3,2,1,0:T(8,128)}, f32[8,6,8,8,128]{4,3,2,1,0:T(8,128)S(1)}, u32[]{:S(2)}, u32[]{:S(2)}) collective-permute-start(f32[8,6,8,8,128]{4,3,2,1,0:T(8,128)} %collective-permute-done.19.refs_30_.refs_34_), channel_id=1, source_target_pairs={{0,1},{1,0},{2,3},{3,2},{4,5},{5,4},{6,7},{7,6},{8,9},{9,8},{10,11... | collective-permute-start | bytes 4718600 | tf_op jit(solution)/shard_map/ppermute | solution.py:340
  103.7 1.4 %collective-permute-start.25 = (f32[2,2,8,8,128]{4,3,2,1,0:T(8,128)S(1)}, f32[2,2,8,8,128]{4,3,2,1,0:T(8,128)S(1)}, u32[]{:S(2)}, u32[]{:S(2)}) collective-permute-start(f32[2,2,8,8,128]{4,3,2,1,0:T(8,128)S(1)} %pad_maximum_fusion.4), channel_id=1, source_target_pairs={{0,1},{1,0},{2,3},{3,2},{4,5},{5,4},{6,7},{7,6},{8,9},{9,8},{10,11... | collective-permute-start | bytes 393224 | tf_op jit(solution)/shard_map/ppermute | solution.py:340
  105.1 4.0 %collective-permute-start.27 = (f32[2,4,8,128]{3,2,1,0:T(8,128)S(1)}, f32[2,4,8,128]{3,2,1,0:T(8,128)S(1)}, u32[]{:S(2)}, u32[]{:S(2)}) collective-permute-start(f32[2,4,8,128]{3,2,1,0:T(8,128)S(1)} %dynamic-slice_bitcast_fusion.5), channel_id=1, source_target_pairs={{0,16},{1,17},{2,18},{3,19},{16,0},{17,1},{18,2},{19,3},{4,20},{5,... | collective-permute-start | bytes 98312 | tf_op jit(solution)/shard_map/ppermute | solution.py:483
  106.7 4.9 %collective-permute-start.26 = (f32[2,4,8,128]{3,2,1,0:T(8,128)S(1)}, f32[2,4,8,128]{3,2,1,0:T(8,128)S(1)}, u32[]{:S(2)}, u32[]{:S(2)}) collective-permute-start(f32[2,4,8,128]{3,2,1,0:T(8,128)S(1)} %get-tuple-element.303), channel_id=1, source_target_pairs={{0,18},{1,19},{2,16},{3,17},{16,2},{17,3},{18,0},{19,1},{4,22},{5,... | collective-permute-start | bytes 98312 | tf_op jit(solution)/shard_map/ppermute | solution.py:483
  107.4 4.3 %collective-permute-start.28 = (f32[2,4,8,128]{3,2,1,0:T(8,128)S(1)}, f32[2,4,8,128]{3,2,1,0:T(8,128)S(1)}, u32[]{:S(2)}, u32[]{:S(2)}) collective-permute-start(f32[2,4,8,128]{3,2,1,0:T(8,128)S(1)} %get-tuple-element.304), channel_id=1, source_target_pairs={{0,2},{1,3},{2,0},{3,1},{16,18},{17,19},{18,16},{19,17},{4,6},{5,7... | collective-permute-start | bytes 98312 | tf_op jit(solution)/shard_map/ppermute | solution.py:483

commit v11 on v9

--- a/solution.py
+++ b/solution.py
@@ -25,7 +25,7 @@
 F32, BF16 = jnp.float32, jnp.bfloat16
 
 
-def call(body, outs, ins, scratch=(), flops=1_000_000):
+def call(body, outs, ins, scratch=(), flops=8_000_000_000):
     scalars, arrays = ins
     return list(pl.pallas_call(
         body,
@@ -413,10 +413,6 @@
         functools.partial(combine, groups), [(own.shape, F32)], ([listed, src_pick], strains)
     )
     combined = combined.reshape(own.shape[:2] + (tile_x, tile_y, depth))
-    combined, halos = lax.optimization_barrier((combined, halos))
-    found = {turn: swap(combined, "gy", turn) for turn in range(pieces - 1, 0, -1) if turn & (turn - 1) == 0}
-    found[0] = combined
-
     sent, lights, lames, shears, old_halos, spots, amounts = ([None, None] for _ in range(7))
     fresh = [None, None]
     for side in range(2):
@@ -434,9 +430,13 @@
         sent[side] = to_neighbour(sent[side], side)
     vels = fresh
 
-    rates = []
+    found, rates = {0: combined}, []
+    exchanges = {0: [pieces // 2], 1: [w for w in range(1, pieces // 2) if w & (w - 1) == 0]}
+    rest = [turn for turn in range(pieces) if turn & (turn - 1)]
     for moment in range(moments):
         last = moment == moments - 1
+        if last:
+            found, vels = lax.optimization_barrier((found, vels))
         results = call(
             functools.partial(inner, last),
             [pair_shape] * (2 if last else 4),
@@ -445,12 +445,15 @@
         rates += results[:2]
         if not last:
             middles = results[2:]
-        if moment == 3 * moments // 4:
-            ready, rates[-1] = lax.optimization_barrier((found, rates[-1]))
-            for turn in range(pieces):
-                if turn not in found:
-                    low = turn & -turn
-                    found[turn] = swap(ready[turn ^ low], "gy", low)
+        if moment in exchanges:
+            ready, rates[-1] = lax.optimization_barrier((combined, rates[-1]))
+            for turn in exchanges[moment]:
+                found[turn] = swap(ready, "gy", turn)
+        if moment == 5 * moments // 8:
+            found, rates[-1] = lax.optimization_barrier((found, rates[-1]))
+            for turn in rest:
+                low = turn & -turn
+                found[turn] = swap(found[turn ^ low], "gy", low)
         if last:
             early, late = list(range(pieces)), []
             jobs = {turn: list(range(moment)) for turn in early}

time: 124 us -> 105 us (0.85)
  local copies, waits for them, and re-layouts: 12.4 us -> 1.54 us
  starting transfers between devices: 61.4 us -> 54.5 us
  Pallas kernels: 18.7 us -> 16.1 us
    unnamed x42 -> x16, local copies, waits for them, and re-layouts: 11 us -> 0.2 us
    ppermute x8, starting transfers between devices: 10.7 us -> 6.68 us  [swap(): return lax.ppermute(array, axis, [(i, i ^ turn) for i in range(count)])]
    ppermute x18, starting transfers between devices: 47.2 us -> 44.3 us  [to_neighbour(): return lax.ppermute(face, ('gx', 'gy'), pairs)]
    pallas_call x30, Pallas kernels: 18.7 us -> 16.1 us  [call(): pl.pallas_call(body, out_shape=[jax.ShapeDtypeStruct(shape, kind) for sha...]
    ppermute x18, waiting for transfers between devices: 10.9 us -> 12.4 us  [to_neighbour(): return lax.ppermute(face, ('gx', 'gy'), pairs)]
  transfers between devices with their start and end apart: 29 -> 29, of which waited for: 13 -> 14; matrix products, arithmetic and copies ran while one was open for 1% -> 0% of each run, Pallas kernels for 14% -> 15%
where the time goes in v11:
time: 105 us; the launch traced here: 104 us
  starting transfers between devices  54.5 us (52%)
  waiting for transfers between devices  30.4 us (29%)
  Pallas kernels  16.1 us (15%)
  local copies, waits for them, and re-layouts  1.54 us (1%)
    ppermute x18, starting transfers between devices, to_neighbour(): return lax.ppermute(face, ('gx', 'gy'), pairs)  44.3 us
    pallas_call x30, Pallas kernels, call(): pl.pallas_call(body, out_shape=[jax.ShapeDtypeStruct(shape, kind) for sha...  16.1 us
    ppermute x8, waiting for transfers between devices, swap(): return lax.ppermute(array, axis, [(i, i ^ turn) for i in range(count)])  14.6 us
    ppermute x18, waiting for transfers between devices, to_neighbour(): return lax.ppermute(face, ('gx', 'gy'), pairs)  12.4 us
    ppermute x8, starting transfers between devices, swap(): return lax.ppermute(array, axis, [(i, i ^ turn) for i in range(count)])  6.68 us
    ppermute x3, starting transfers between devices, local(): part = lax.ppermute(part, ('sta', 'gy'), pairs)  3.55 us
    ppermute x3, waiting for transfers between devices, local(): part = lax.ppermute(part, ('sta', 'gy'), pairs)  3.39 us
  transfers between devices with their start and end apart: 29, of which 14 were waited for; matrix products, arithmetic and copies ran while one was open for 0% of the time, Pallas kernels for 15%

profile of v11, /device:TPU:0, one launch (start us, length us, event | category | flops | bytes accessed | tf_op | source)
XLA Modules:
  0.0 104.0 jit_solution(12080207934100711966)
XLA Ops:
  0.0 1.3 %dynamic-slice_bitcast_fusion = (f32[9,8,8,128]{3,2,1,0:T(8,128)S(1)}, f32[9,8,8,128]{3,2,1,0:T(8,128)S(1)}, f32[9,8,8,128]{3,2,1,0:T(8,128)S(1)}, f32[9,8,8,128]{3,2,1,0:T(8,128)S(1)}) fusion(f32[1,4,9,8,8,128]{5,4,3,2,1,0:T(8,128)} %param.8, s32[]{:T(128)S(6)} %select_n.24, s32[]{:T(128)S(6)} %select_n.22, s32[]{:T(128)S(6)} %select_n.21, s32[]{:T(128)S(6)} %select_n.23), kind=kLoop, calls=%fused_computation.4 | loop fusion | bytes 2359312 | tf_op jit(solution)/shard_map/jit(dynamic_index_in_dim)/squeeze | solution.py:389
  2.0 2.6 %collective-permute-start.1 = (f32[10,8,8,128]{3,2,1,0:T(8,128)S(1)}, f32[10,8,8,128]{3,2,1,0:T(8,128)S(1)}, u32[]{:S(2)}, u32[]{:S(2)}) collective-permute-start(f32[10,8,8,128]{3,2,1,0:T(8,128)S(1)} %get-tuple-element.317), channel_id=1, source_target_pairs={{0,2},{1,3},{2,0},{3,1},{4,6},{5,7},{6,4},{7,5},{8,10},{9,11},{10,... | collective-permute-start | bytes 983048 | tf_op jit(solution)/shard_map/ppermute | solution.py:358
  4.7 1.7 %collective-permute-start.3 = (bf16[8,6,64,128]{3,2,1,0:T(8,128)(2,1)S(1)}, bf16[8,6,64,128]{3,2,1,0:T(8,128)(2,1)S(1)}, u32[]{:S(2)}, u32[]{:S(2)}) collective-permute-start(bf16[8,6,64,128]{3,2,1,0:T(8,128)(2,1)S(1)} %bitcast.24), channel_id=1, source_target_pairs={{0,16},{16,0},{1,17},{17,1},{2,18},{18,2},{3,19},{19,3},{4,20},{20... | collective-permute-start | bytes 2359304 | tf_op jit(solution)/shard_map/ppermute | solution.py:358
  6.4 6.8 %collective-permute-done.1.refs_2_ = f32[10,8,8,128]{3,2,1,0:T(8,128)S(1)} collective-permute-done((f32[10,8,8,128]{3,2,1,0:T(8,128)S(1)}, f32[10,8,8,128]{3,2,1,0:T(8,128)S(1)}, u32[]{:S(2)}, u32[]{:S(2)}) %collective-permute-start.1) | collective-permute-done | bytes 327712 | tf_op jit(solution)/shard_map/ppermute | solution.py:358
  13.2 6.5 %collective-permute-done.2.refs_3_ = f32[10,8,8,128]{3,2,1,0:T(8,128)S(1)} collective-permute-done((f32[10,8,8,128]{3,2,1,0:T(8,128)S(1)}, f32[10,8,8,128]{3,2,1,0:T(8,128)S(1)}, u32[]{:S(2)}, u32[]{:S(2)}) %collective-permute-start.2) | collective-permute-done | bytes 327712 | tf_op jit(solution)/shard_map/ppermute | solution.py:358
  19.7 0.7 shard_map.82
  20.4 0.7 collective-permute-start.5
  21.3 6.3 %collective-permute-start.4 = (f32[4,2,32,128]{3,2,1,0:T(8,128)S(1)}, f32[4,2,32,128]{3,2,1,0:T(8,128)S(1)}, u32[]{:S(2)}, u32[]{:S(2)}) collective-permute-start(f32[4,2,32,128]{3,2,1,0:T(8,128)S(1)} %get-tuple-element.167), channel_id=1, source_target_pairs={{0,4},{2,6},{4,0},{5,9},{6,2},{7,11},{8,12},{9,5},{10,14},{11,7},{... | collective-permute-start | bytes 393224 | tf_op jit(solution)/shard_map/ppermute | solution.py:374
  27.6 1.1 %shard_map.84 = (f32[3,4,32,128]{3,2,1,0:T(8,128)S(1)}, bf16[15,32,128]{2,1,0:T(8,128)(2,1)S(1)}, f32[4,32,128]{2,1,0:T(8,128)S(1)}, f32[6,32,128]{2,1,0:T(8,128...) custom-call(f32[16,3]{1,0:T(8,128)S(1)} %copy.9.table, ...), custom_call_target="tpu_custom_call" | custom-call | flops 8000000000 | bytes 2000000 | tf_op jit(solution)/shard_map/pallas_call | solution.py:30
  28.8 0.7 collective-permute-start.7
  29.5 1.1 %collective-permute-done.4.halo = f32[4,2,32,128]{3,2,1,0:T(8,128)S(1)} collective-permute-done((f32[4,2,32,128]{3,2,1,0:T(8,128)S(1)}, f32[4,2,32,128]{3,2,1,0:T(8,128)S(1)}, u32[]{:S(2)}, u32[]{:S(2)}) %collective-permute-start.4) | collective-permute-done | bytes 131104 | tf_op jit(solution)/shard_map/ppermute | solution.py:374
  30.5 1.1 %shard_map.83 = (f32[3,4,32,128]{3,2,1,0:T(8,128)S(1)}, bf16[15,32,128]{2,1,0:T(8,128)(2,1)S(1)}, f32[4,32,128]{2,1,0:T(8,128)S(1)}, f32[6,32,128]{2,1,0:T(8,128...) custom-call(f32[16,3]{1,0:T(8,128)S(1)} %copy.9.table, ...), custom_call_target="tpu_custom_call" | custom-call | flops 8000000000 | bytes 2000000 | tf_op jit(solution)/shard_map/pallas_call | solution.py:30
  31.7 4.9 %collective-permute-start.6 = (bf16[15,32,128]{2,1,0:T(8,128)(2,1)S(1)}, bf16[15,32,128]{2,1,0:T(8,128)(2,1)S(1)}, u32[]{:S(2)}, u32[]{:S(2)}) collective-permute-start(bf16[15,32,128]{2,1,0:T(8,128)(2,1)S(1)} %get-tuple-element.183), channel_id=1, source_target_pairs={{0,4},{2,6},{4,0},{5,9},{6,2},{7,11},{8,12},{9,5},{10,14},{11,7},{... | collective-permute-start | bytes 368648 | tf_op jit(solution)/shard_map/ppermute | solution.py:374
  36.6 1.0 shard_map.86
  37.8 1.6 %collective-permute-start.17 = (f32[8,6,8,8,128]{4,3,2,1,0:T(8,128)S(1)}, f32[8,6,8,8,128]{4,3,2,1,0:T(8,128)S(1)}, u32[]{:S(2)}, u32[]{:S(2)}) collective-permute-start(f32[8,6,8,8,128]{4,3,2,1,0:T(8,128)S(1)} %bitcast.20), channel_id=1, source_target_pairs={{0,2},{1,3},{2,0},{3,1},{4,6},{5,7},{6,4},{7,5},{8,10},{9,11},{10,... | collective-permute-start | bytes 4718600 | tf_op jit(solution)/shard_map/ppermute | solution.py:358
  39.9 0.7 collective-permute-start.9
  41.0 3.6 %collective-permute-start.8 = (bf16[15,32,128]{2,1,0:T(8,128)(2,1)S(1)}, bf16[15,32,128]{2,1,0:T(8,128)(2,1)S(1)}, u32[]{:S(2)}, u32[]{:S(2)}) collective-permute-start(bf16[15,32,128]{2,1,0:T(8,128)(2,1)S(1)} %get-tuple-element.202), channel_id=1, source_target_pairs={{0,4},{2,6},{4,0},{5,9},{6,2},{7,11},{8,12},{9,5},{10,14},{11,7},{... | collective-permute-start | bytes 368648 | tf_op jit(solution)/shard_map/ppermute | solution.py:374
  45.5 0.7 collective-permute-start.11
  46.1 1.7 %collective-permute-done.8.halo = bf16[15,32,128]{2,1,0:T(8,128)(2,1)S(1)} collective-permute-done((bf16[15,32,128]{2,1,0:T(8,128)(2,1)S(1)}, bf16[15,32,128]{2,1,0:T(8,128)(2,1)S(1)}, u32[]{:S(2)}, u32[]{:S(2)}) %collective-permute-start.8) | collective-permute-done | bytes 122912 | tf_op jit(solution)/shard_map/ppermute | solution.py:374
  48.3 3.6 %collective-permute-start.10 = (bf16[15,32,128]{2,1,0:T(8,128)(2,1)S(1)}, bf16[15,32,128]{2,1,0:T(8,128)(2,1)S(1)}, u32[]{:S(2)}, u32[]{:S(2)}) collective-permute-start(bf16[15,32,128]{2,1,0:T(8,128)(2,1)S(1)} %get-tuple-element.216), channel_id=1, source_target_pairs={{0,4},{2,6},{4,0},{5,9},{6,2},{7,11},{8,12},{9,5},{10,14},{11,7},{... | collective-permute-start | bytes 368648 | tf_op jit(solution)/shard_map/ppermute | solution.py:374
  52.6 0.7 collective-permute-start.13
  53.3 1.8 %collective-permute-done.10.halo = bf16[15,32,128]{2,1,0:T(8,128)(2,1)S(1)} collective-permute-done((bf16[15,32,128]{2,1,0:T(8,128)(2,1)S(1)}, bf16[15,32,128]{2,1,0:T(8,128)(2,1)S(1)}, u32[]{:S(2)}, u32[]{:S(2)}) %collective-permute-start.10) | collective-permute-done | bytes 122912 | tf_op jit(solution)/shard_map/ppermute | solution.py:374
  55.5 3.6 %collective-permute-start.12 = (bf16[15,32,128]{2,1,0:T(8,128)(2,1)S(1)}, bf16[15,32,128]{2,1,0:T(8,128)(2,1)S(1)}, u32[]{:S(2)}, u32[]{:S(2)}) collective-permute-start(bf16[15,32,128]{2,1,0:T(8,128)(2,1)S(1)} %get-tuple-element.230), channel_id=1, source_target_pairs={{0,4},{2,6},{4,0},{5,9},{6,2},{7,11},{8,12},{9,5},{10,14},{11,7},{... | collective-permute-start | bytes 368648 | tf_op jit(solution)/shard_map/ppermute | solution.py:374
  59.9 0.7 collective-permute-start.15
  60.5 1.7 %collective-permute-done.12.halo = bf16[15,32,128]{2,1,0:T(8,128)(2,1)S(1)} collective-permute-done((bf16[15,32,128]{2,1,0:T(8,128)(2,1)S(1)}, bf16[15,32,128]{2,1,0:T(8,128)(2,1)S(1)}, u32[]{:S(2)}, u32[]{:S(2)}) %collective-permute-start.12) | collective-permute-done | bytes 122912 | tf_op jit(solution)/shard_map/ppermute | solution.py:374
  62.7 3.6 %collective-permute-start.14 = (bf16[15,32,128]{2,1,0:T(8,128)(2,1)S(1)}, bf16[15,32,128]{2,1,0:T(8,128)(2,1)S(1)}, u32[]{:S(2)}, u32[]{:S(2)}) collective-permute-start(bf16[15,32,128]{2,1,0:T(8,128)(2,1)S(1)} %get-tuple-element.244), channel_id=1, source_target_pairs={{0,4},{2,6},{4,0},{5,9},{6,2},{7,11},{8,12},{9,5},{10,14},{11,7},{... | collective-permute-start | bytes 368648 | tf_op jit(solution)/shard_map/ppermute | solution.py:374
  67.1 0.7 collective-permute-start.19
  67.8 1.7 %collective-permute-done.14.halo = bf16[15,32,128]{2,1,0:T(8,128)(2,1)S(1)} collective-permute-done((bf16[15,32,128]{2,1,0:T(8,128)(2,1)S(1)}, bf16[15,32,128]{2,1,0:T(8,128)(2,1)S(1)}, u32[]{:S(2)}, u32[]{:S(2)}) %collective-permute-start.14) | collective-permute-done | bytes 122912 | tf_op jit(solution)/shard_map/ppermute | solution.py:374
  70.0 4.4 %collective-permute-start.18 = (bf16[15,32,128]{2,1,0:T(8,128)(2,1)S(1)}, bf16[15,32,128]{2,1,0:T(8,128)(2,1)S(1)}, u32[]{:S(2)}, u32[]{:S(2)}) collective-permute-start(bf16[15,32,128]{2,1,0:T(8,128)(2,1)S(1)} %get-tuple-element.261), channel_id=1, source_target_pairs={{0,4},{2,6},{4,0},{5,9},{6,2},{7,11},{8,12},{9,5},{10,14},{11,7},{... | collective-permute-start | bytes 368648 | tf_op jit(solution)/shard_map/ppermute | solution.py:374
  75.1 0.7 collective-permute-start.21
  75.8 2.7 %collective-permute-done.18.halo = bf16[15,32,128]{2,1,0:T(8,128)(2,1)S(1)} collective-permute-done((bf16[15,32,128]{2,1,0:T(8,128)(2,1)S(1)}, bf16[15,32,128]{2,1,0:T(8,128)(2,1)S(1)}, u32[]{:S(2)}, u32[]{:S(2)}) %collective-permute-start.18) | collective-permute-done | bytes 122912 | tf_op jit(solution)/shard_map/ppermute | solution.py:374
  79.0 3.8 %collective-permute-start.20 = (bf16[15,32,128]{2,1,0:T(8,128)(2,1)S(1)}, bf16[15,32,128]{2,1,0:T(8,128)(2,1)S(1)}, u32[]{:S(2)}, u32[]{:S(2)}) collective-permute-start(bf16[15,32,128]{2,1,0:T(8,128)(2,1)S(1)} %get-tuple-element.275), channel_id=1, source_target_pairs={{0,4},{2,6},{4,0},{5,9},{6,2},{7,11},{8,12},{9,5},{10,14},{11,7},{... | collective-permute-start | bytes 368648 | tf_op jit(solution)/shard_map/ppermute | solution.py:374
  83.1 0.9 shard_map.106
  84.0 0.7 collective-permute-start.24
  84.7 1.1 %collective-permute-done.20.halo = bf16[15,32,128]{2,1,0:T(8,128)(2,1)S(1)} collective-permute-done((bf16[15,32,128]{2,1,0:T(8,128)(2,1)S(1)}, bf16[15,32,128]{2,1,0:T(8,128)(2,1)S(1)}, u32[]{:S(2)}, u32[]{:S(2)}) %collective-permute-start.20) | collective-permute-done | bytes 122912 | tf_op jit(solution)/shard_map/ppermute | solution.py:374
  85.7 0.9 shard_map.105
  86.7 4.4 %collective-permute-start.23 = (bf16[15,32,128]{2,1,0:T(8,128)(2,1)S(1)}, bf16[15,32,128]{2,1,0:T(8,128)(2,1)S(1)}, u32[]{:S(2)}, u32[]{:S(2)}) collective-permute-start(bf16[15,32,128]{2,1,0:T(8,128)(2,1)S(1)} %get-tuple-element.299), channel_id=1, source_target_pairs={{0,4},{2,6},{4,0},{5,9},{6,2},{7,11},{8,12},{9,5},{10,14},{11,7},{... | collective-permute-start | bytes 368648 | tf_op jit(solution)/shard_map/ppermute | solution.py:374
  91.3 1.7 %shard_map.108.refs_36_ = f32[4,2,8,8,128]{4,3,2,1,0:T(8,128)S(1)} custom-call(f32[1,4,8]{2,1,0:T(4,128)S(1)} %copy-done.1, f32[6,2,32,128]{3,2,1,0:T(8,128)S(1)} %get-tuple-element.178.refs_0_, f32[6,2,32,128]{3,2,1,0:T(8,128)S(1)} %get-tuple-element.182.refs_1_, f32[6,2,32,128]{3,2,1,0:T(8,128)S(1)} %get-tuple-element.190.refs_2_, ...), custom_call_target="tpu_custom_call" | custom-call | flops 8000000000 | bytes 2000000 | tf_op jit(solution)/shard_map/pallas_call | solution.py:30
  93.3 0.7 collective-permute-done.23.halo
  94.1 0.8 shard_map.111
  95.0 1.3 %collective-permute-done.25 = f32[2,2,8,8,128]{4,3,2,1,0:T(8,128)S(1)} collective-permute-done((f32[2,2,8,8,128]{4,3,2,1,0:T(8,128)S(1)}, f32[2,2,8,8,128]{4,3,2,1,0:T(8,128)S(1)}, u32[]{:S(2)}, u32[]{:S(2)}) %collective-permute-start.25) | collective-permute-done | bytes 131104 | tf_op jit(solution)/shard_map/ppermute | solution.py:358
  96.4 1.6 %collective-permute-start.26 = (f32[2,4,8,128]{3,2,1,0:T(8,128)S(1)}, f32[2,4,8,128]{3,2,1,0:T(8,128)S(1)}, u32[]{:S(2)}, u32[]{:S(2)}) collective-permute-start(f32[2,4,8,128]{3,2,1,0:T(8,128)S(1)} %get-tuple-element.313), channel_id=1, source_target_pairs={{0,18},{1,19},{2,16},{3,17},{16,2},{17,3},{18,0},{19,1},{4,22},{5,... | collective-permute-start | bytes 98312 | tf_op jit(solution)/shard_map/ppermute | solution.py:503
  98.0 1.4 %collective-permute-start.28 = (f32[2,4,8,128]{3,2,1,0:T(8,128)S(1)}, f32[2,4,8,128]{3,2,1,0:T(8,128)S(1)}, u32[]{:S(2)}, u32[]{:S(2)}) collective-permute-start(f32[2,4,8,128]{3,2,1,0:T(8,128)S(1)} %get-tuple-element.314), channel_id=1, source_target_pairs={{0,2},{1,3},{2,0},{3,1},{16,18},{17,19},{18,16},{19,17},{4,6},{5,7... | collective-permute-start | bytes 98312 | tf_op jit(solution)/shard_map/ppermute | solution.py:503
  99.4 0.5 collective-permute-start.27
  100.0 1.3 %collective-permute-done.26 = f32[2,4,8,128]{3,2,1,0:T(8,128)S(1)} collective-permute-done((f32[2,4,8,128]{3,2,1,0:T(8,128)S(1)}, f32[2,4,8,128]{3,2,1,0:T(8,128)S(1)}, u32[]{:S(2)}, u32[]{:S(2)}) %collective-permute-start.26) | collective-permute-done | bytes 32800 | tf_op jit(solution)/shard_map/ppermute | solution.py:503
  101.3 0.7 collective-permute-done.28
  101.9 1.4 %collective-permute-done.27 = f32[2,4,8,128]{3,2,1,0:T(8,128)S(1)} collective-permute-done((f32[2,4,8,128]{3,2,1,0:T(8,128)S(1)}, f32[2,4,8,128]{3,2,1,0:T(8,128)S(1)}, u32[]{:S(2)}, u32[]{:S(2)}) %collective-permute-start.27) | collective-permute-done | bytes 32800 | tf_op jit(solution)/shard_map/ppermute | solution.py:503
  103.3 0.6 bitcast_add_fusion
  (65 shorter events, 9.1 us)
Async XLA Ops:
  0.0 1.3 %copy-start.4 = (s32[8,8,128]{2,1,0:T(8,128)S(1)}, s32[8,8,128]{2,1,0:T(8,128)}, u32[]{:S(2)}) copy-start(s32[8,8,128]{2,1,0:T(8,128)} %param.10) | copy-start | bytes 98308
  1.3 3.4 %copy-start = (bf16[1,8,6,8,8,128]{5,4,3,2,1,0:T(8,128)(2,1)S(1)}, bf16[1,8,6,8,8,128]{5,4,3,2,1,0:T(8,128)(2,1)}, u32[]{:S(2)}) copy-start(bf16[1,8,6,8,8,128]{5,4,3,2,1,0:T(8,128)(2,1)} %param.9) | copy-start | bytes 2359300
  1.5 4.9 %collective-permute-start = (f32[10,8,8,128]{3,2,1,0:T(8,128)S(1)}, f32[10,8,8,128]{3,2,1,0:T(8,128)S(1)}, u32[]{:S(2)}, u32[]{:S(2)}) collective-permute-start(f32[10,8,8,128]{3,2,1,0:T(8,128)S(1)} %get-tuple-element.316), channel_id=1, source_target_pairs={{0,1},{1,0},{2,3},{3,2},{4,5},{5,4},{6,7},{7,6},{8,9},{9,8},{10,11... | collective-permute-start | bytes 983048 | tf_op jit(solution)/shard_map/ppermute | solution.py:358
  2.0 11.2 %collective-permute-start.1 = (f32[10,8,8,128]{3,2,1,0:T(8,128)S(1)}, f32[10,8,8,128]{3,2,1,0:T(8,128)S(1)}, u32[]{:S(2)}, u32[]{:S(2)}) collective-permute-start(f32[10,8,8,128]{3,2,1,0:T(8,128)S(1)} %get-tuple-element.317), channel_id=1, source_target_pairs={{0,2},{1,3},{2,0},{3,1},{4,6},{5,7},{6,4},{7,5},{8,10},{9,11},{10,... | collective-permute-start | bytes 983048 | tf_op jit(solution)/shard_map/ppermute | solution.py:358
  4.6 15.1 %collective-permute-start.2 = (f32[10,8,8,128]{3,2,1,0:T(8,128)S(1)}, f32[10,8,8,128]{3,2,1,0:T(8,128)S(1)}, u32[]{:S(2)}, u32[]{:S(2)}) collective-permute-start(f32[10,8,8,128]{3,2,1,0:T(8,128)S(1)} %get-tuple-element.315), channel_id=1, source_target_pairs={{0,3},{1,2},{2,1},{3,0},{4,7},{5,6},{6,5},{7,4},{8,11},{9,10},{10,... | collective-permute-start | bytes 983048 | tf_op jit(solution)/shard_map/ppermute | solution.py:358
  4.7 22.9 %collective-permute-start.3 = (bf16[8,6,64,128]{3,2,1,0:T(8,128)(2,1)S(1)}, bf16[8,6,64,128]{3,2,1,0:T(8,128)(2,1)S(1)}, u32[]{:S(2)}, u32[]{:S(2)}) collective-permute-start(bf16[8,6,64,128]{3,2,1,0:T(8,128)(2,1)S(1)} %bitcast.24), channel_id=1, source_target_pairs={{0,16},{16,0},{1,17},{17,1},{2,18},{18,2},{3,19},{19,3},{4,20},{20... | collective-permute-start | bytes 2359304 | tf_op jit(solution)/shard_map/ppermute | solution.py:358
  19.7 1.4 %copy-start.5 = (f32[16,3]{0,1:T(4,128)S(1)}, f32[16,3]{0,1:T(4,128)}, u32[]{:S(2)}) copy-start(f32[16,3]{0,1:T(4,128)} %param.11) | copy-start | bytes 580
  19.7 1.5 %copy-start.6 = (s32[2,8,2]{1,2,0:T(2,128)S(1)}, s32[2,8,2]{1,2,0:T(2,128)}, u32[]{:S(2)}) copy-start(s32[2,8,2]{1,2,0:T(2,128)} %param.14) | copy-start | bytes 388
  19.7 7.9 %copy-start.1 = (f32[1,4,8]{2,1,0:T(4,128)S(1)}, f32[1,4,8]{2,1,0:T(4,128)}, u32[]{:S(2)}) copy-start(f32[1,4,8]{2,1,0:T(4,128)} %residual.7) | copy-start | bytes 388
  19.7 7.9 %copy-start.3 = (s32[1,4]{1,0:T(1,128)S(1)}, s32[1,4]{1,0:T(1,128)}, u32[]{:S(2)}) copy-start(s32[1,4]{1,0:T(1,128)} %rec_cell.3) | copy-start | bytes 52
  20.4 7.2 %collective-permute-start.5 = (f32[4,2,32,128]{3,2,1,0:T(8,128)S(1)}, f32[4,2,32,128]{3,2,1,0:T(8,128)S(1)}, u32[]{:S(2)}, u32[]{:S(2)}) collective-permute-start(f32[4,2,32,128]{3,2,1,0:T(8,128)S(1)} %get-tuple-element.172), channel_id=1, source_target_pairs={{1,5},{3,7},{4,8},{5,1},{6,10},{7,3},{8,4},{9,13},{10,6},{11,15},{... | collective-permute-start | bytes 393224 | tf_op jit(solution)/shard_map/ppermute | solution.py:374
  21.3 9.3 %collective-permute-start.4 = (f32[4,2,32,128]{3,2,1,0:T(8,128)S(1)}, f32[4,2,32,128]{3,2,1,0:T(8,128)S(1)}, u32[]{:S(2)}, u32[]{:S(2)}) collective-permute-start(f32[4,2,32,128]{3,2,1,0:T(8,128)S(1)} %get-tuple-element.167), channel_id=1, source_target_pairs={{0,4},{2,6},{4,0},{5,9},{6,2},{7,11},{8,12},{9,5},{10,14},{11,7},{... | collective-permute-start | bytes 393224 | tf_op jit(solution)/shard_map/ppermute | solution.py:374
  28.8 10.6 %collective-permute-start.7 = (bf16[15,32,128]{2,1,0:T(8,128)(2,1)S(1)}, bf16[15,32,128]{2,1,0:T(8,128)(2,1)S(1)}, u32[]{:S(2)}, u32[]{:S(2)}) collective-permute-start(bf16[15,32,128]{2,1,0:T(8,128)(2,1)S(1)} %get-tuple-element.191), channel_id=1, source_target_pairs={{1,5},{3,7},{4,8},{5,1},{6,10},{7,3},{8,4},{9,13},{10,6},{11,15},{... | collective-permute-start | bytes 368648 | tf_op jit(solution)/shard_map/ppermute | solution.py:374
  30.5 6.1 %copy-start.2 = (s32[2,8]{1,0:T(2,128)S(1)}, s32[2,8]{1,0:T(2,128)}, u32[]{:S(2)}) copy-start(s32[2,8]{1,0:T(2,128)} %src_pick.1) | copy-start | bytes 196
  31.7 8.9 %collective-permute-start.6 = (bf16[15,32,128]{2,1,0:T(8,128)(2,1)S(1)}, bf16[15,32,128]{2,1,0:T(8,128)(2,1)S(1)}, u32[]{:S(2)}, u32[]{:S(2)}) collective-permute-start(bf16[15,32,128]{2,1,0:T(8,128)(2,1)S(1)} %get-tuple-element.183), channel_id=1, source_target_pairs={{0,4},{2,6},{4,0},{5,9},{6,2},{7,11},{8,12},{9,5},{10,14},{11,7},{... | collective-permute-start | bytes 368648 | tf_op jit(solution)/shard_map/ppermute | solution.py:374
  37.8 44.9 %collective-permute-start.17 = (f32[8,6,8,8,128]{4,3,2,1,0:T(8,128)S(1)}, f32[8,6,8,8,128]{4,3,2,1,0:T(8,128)S(1)}, u32[]{:S(2)}, u32[]{:S(2)}) collective-permute-start(f32[8,6,8,8,128]{4,3,2,1,0:T(8,128)S(1)} %bitcast.20), channel_id=1, source_target_pairs={{0,2},{1,3},{2,0},{3,1},{4,6},{5,7},{6,4},{7,5},{8,10},{9,11},{10,... | collective-permute-start | bytes 4718600 | tf_op jit(solution)/shard_map/ppermute | solution.py:358
  39.9 5.1 %collective-permute-start.9 = (bf16[15,32,128]{2,1,0:T(8,128)(2,1)S(1)}, bf16[15,32,128]{2,1,0:T(8,128)(2,1)S(1)}, u32[]{:S(2)}, u32[]{:S(2)}) collective-permute-start(bf16[15,32,128]{2,1,0:T(8,128)(2,1)S(1)} %get-tuple-element.208), channel_id=1, source_target_pairs={{1,5},{3,7},{4,8},{5,1},{6,10},{7,3},{8,4},{9,13},{10,6},{11,15},{... | collective-permute-start | bytes 368648 | tf_op jit(solution)/shard_map/ppermute | solution.py:374
  41.0 6.8 %collective-permute-start.8 = (bf16[15,32,128]{2,1,0:T(8,128)(2,1)S(1)}, bf16[15,32,128]{2,1,0:T(8,128)(2,1)S(1)}, u32[]{:S(2)}, u32[]{:S(2)}) collective-permute-start(bf16[15,32,128]{2,1,0:T(8,128)(2,1)S(1)} %get-tuple-element.202), channel_id=1, source_target_pairs={{0,4},{2,6},{4,0},{5,9},{6,2},{7,11},{8,12},{9,5},{10,14},{11,7},{... | collective-permute-start | bytes 368648 | tf_op jit(solution)/shard_map/ppermute | solution.py:374
  44.9 37.8 %collective-permute-start.16 = (f32[8,6,8,8,128]{4,3,2,1,0:T(8,128)S(1)}, f32[8,6,8,8,128]{4,3,2,1,0:T(8,128)S(1)}, u32[]{:S(2)}, u32[]{:S(2)}) collective-permute-start(f32[8,6,8,8,128]{4,3,2,1,0:T(8,128)S(1)} %bitcast.21), channel_id=1, source_target_pairs={{0,1},{1,0},{2,3},{3,2},{4,5},{5,4},{6,7},{7,6},{8,9},{9,8},{10,11... | collective-permute-start | bytes 4718600 | tf_op jit(solution)/shard_map/ppermute | solution.py:358
  45.5 6.7 %collective-permute-start.11 = (bf16[15,32,128]{2,1,0:T(8,128)(2,1)S(1)}, bf16[15,32,128]{2,1,0:T(8,128)(2,1)S(1)}, u32[]{:S(2)}, u32[]{:S(2)}) collective-permute-start(bf16[15,32,128]{2,1,0:T(8,128)(2,1)S(1)} %get-tuple-element.222), channel_id=1, source_target_pairs={{1,5},{3,7},{4,8},{5,1},{6,10},{7,3},{8,4},{9,13},{10,6},{11,15},{... | collective-permute-start | bytes 368648 | tf_op jit(solution)/shard_map/ppermute | solution.py:374
  48.3 6.8 %collective-permute-start.10 = (bf16[15,32,128]{2,1,0:T(8,128)(2,1)S(1)}, bf16[15,32,128]{2,1,0:T(8,128)(2,1)S(1)}, u32[]{:S(2)}, u32[]{:S(2)}) collective-permute-start(bf16[15,32,128]{2,1,0:T(8,128)(2,1)S(1)} %get-tuple-element.216), channel_id=1, source_target_pairs={{0,4},{2,6},{4,0},{5,9},{6,2},{7,11},{8,12},{9,5},{10,14},{11,7},{... | collective-permute-start | bytes 368648 | tf_op jit(solution)/shard_map/ppermute | solution.py:374
  52.6 6.8 %collective-permute-start.13 = (bf16[15,32,128]{2,1,0:T(8,128)(2,1)S(1)}, bf16[15,32,128]{2,1,0:T(8,128)(2,1)S(1)}, u32[]{:S(2)}, u32[]{:S(2)}) collective-permute-start(bf16[15,32,128]{2,1,0:T(8,128)(2,1)S(1)} %get-tuple-element.236), channel_id=1, source_target_pairs={{1,5},{3,7},{4,8},{5,1},{6,10},{7,3},{8,4},{9,13},{10,6},{11,15},{... | collective-permute-start | bytes 368648 | tf_op jit(solution)/shard_map/ppermute | solution.py:374
  55.5 6.8 %collective-permute-start.12 = (bf16[15,32,128]{2,1,0:T(8,128)(2,1)S(1)}, bf16[15,32,128]{2,1,0:T(8,128)(2,1)S(1)}, u32[]{:S(2)}, u32[]{:S(2)}) collective-permute-start(bf16[15,32,128]{2,1,0:T(8,128)(2,1)S(1)} %get-tuple-element.230), channel_id=1, source_target_pairs={{0,4},{2,6},{4,0},{5,9},{6,2},{7,11},{8,12},{9,5},{10,14},{11,7},{... | collective-permute-start | bytes 368648 | tf_op jit(solution)/shard_map/ppermute | solution.py:374
  59.9 6.8 %collective-permute-start.15 = (bf16[15,32,128]{2,1,0:T(8,128)(2,1)S(1)}, bf16[15,32,128]{2,1,0:T(8,128)(2,1)S(1)}, u32[]{:S(2)}, u32[]{:S(2)}) collective-permute-start(bf16[15,32,128]{2,1,0:T(8,128)(2,1)S(1)} %get-tuple-element.250), channel_id=1, source_target_pairs={{1,5},{3,7},{4,8},{5,1},{6,10},{7,3},{8,4},{9,13},{10,6},{11,15},{... | collective-permute-start | bytes 368648 | tf_op jit(solution)/shard_map/ppermute | solution.py:374
  62.7 6.8 %collective-permute-start.14 = (bf16[15,32,128]{2,1,0:T(8,128)(2,1)S(1)}, bf16[15,32,128]{2,1,0:T(8,128)(2,1)S(1)}, u32[]{:S(2)}, u32[]{:S(2)}) collective-permute-start(bf16[15,32,128]{2,1,0:T(8,128)(2,1)S(1)} %get-tuple-element.244), channel_id=1, source_target_pairs={{0,4},{2,6},{4,0},{5,9},{6,2},{7,11},{8,12},{9,5},{10,14},{11,7},{... | collective-permute-start | bytes 368648 | tf_op jit(solution)/shard_map/ppermute | solution.py:374
  67.1 7.5 %collective-permute-start.19 = (bf16[15,32,128]{2,1,0:T(8,128)(2,1)S(1)}, bf16[15,32,128]{2,1,0:T(8,128)(2,1)S(1)}, u32[]{:S(2)}, u32[]{:S(2)}) collective-permute-start(bf16[15,32,128]{2,1,0:T(8,128)(2,1)S(1)} %get-tuple-element.267), channel_id=1, source_target_pairs={{1,5},{3,7},{4,8},{5,1},{6,10},{7,3},{8,4},{9,13},{10,6},{11,15},{... | collective-permute-start | bytes 368648 | tf_op jit(solution)/shard_map/ppermute | solution.py:374
  70.0 8.5 %collective-permute-start.18 = (bf16[15,32,128]{2,1,0:T(8,128)(2,1)S(1)}, bf16[15,32,128]{2,1,0:T(8,128)(2,1)S(1)}, u32[]{:S(2)}, u32[]{:S(2)}) collective-permute-start(bf16[15,32,128]{2,1,0:T(8,128)(2,1)S(1)} %get-tuple-element.261), channel_id=1, source_target_pairs={{0,4},{2,6},{4,0},{5,9},{6,2},{7,11},{8,12},{9,5},{10,14},{11,7},{... | collective-permute-start | bytes 368648 | tf_op jit(solution)/shard_map/ppermute | solution.py:374
  75.1 7.9 %collective-permute-start.21 = (bf16[15,32,128]{2,1,0:T(8,128)(2,1)S(1)}, bf16[15,32,128]{2,1,0:T(8,128)(2,1)S(1)}, u32[]{:S(2)}, u32[]{:S(2)}) collective-permute-start(bf16[15,32,128]{2,1,0:T(8,128)(2,1)S(1)} %get-tuple-element.281), channel_id=1, source_target_pairs={{1,5},{3,7},{4,8},{5,1},{6,10},{7,3},{8,4},{9,13},{10,6},{11,15},{... | collective-permute-start | bytes 368648 | tf_op jit(solution)/shard_map/ppermute | solution.py:374
  79.0 6.8 %collective-permute-start.20 = (bf16[15,32,128]{2,1,0:T(8,128)(2,1)S(1)}, bf16[15,32,128]{2,1,0:T(8,128)(2,1)S(1)}, u32[]{:S(2)}, u32[]{:S(2)}) collective-permute-start(bf16[15,32,128]{2,1,0:T(8,128)(2,1)S(1)} %get-tuple-element.275), channel_id=1, source_target_pairs={{0,4},{2,6},{4,0},{5,9},{6,2},{7,11},{8,12},{9,5},{10,14},{11,7},{... | collective-permute-start | bytes 368648 | tf_op jit(solution)/shard_map/ppermute | solution.py:374
  82.7 8.4 %collective-permute-start.22 = (f32[8,6,8,8,128]{4,3,2,1,0:T(8,128)S(1)}, f32[8,6,8,8,128]{4,3,2,1,0:T(8,128)S(1)}, u32[]{:S(2)}, u32[]{:S(2)}) collective-permute-start(f32[8,6,8,8,128]{4,3,2,1,0:T(8,128)S(1)} %collective-permute-done.17.refs_30_.refs_34_), channel_id=1, source_target_pairs={{0,1},{1,0},{2,3},{3,2},{4,5},{5,4},{6,7},{7,6},{8,9},{9,8},{10,11... | collective-permute-start | bytes 4718600 | tf_op jit(solution)/shard_map/ppermute | solution.py:358
  84.0 9.1 %collective-permute-start.24 = (bf16[15,32,128]{2,1,0:T(8,128)(2,1)S(1)}, bf16[15,32,128]{2,1,0:T(8,128)(2,1)S(1)}, u32[]{:S(2)}, u32[]{:S(2)}) collective-permute-start(bf16[15,32,128]{2,1,0:T(8,128)(2,1)S(1)} %get-tuple-element.302), channel_id=1, source_target_pairs={{1,5},{3,7},{4,8},{5,1},{6,10},{7,3},{8,4},{9,13},{10,6},{11,15},{... | collective-permute-start | bytes 368648 | tf_op jit(solution)/shard_map/ppermute | solution.py:374
  86.7 7.3 %collective-permute-start.23 = (bf16[15,32,128]{2,1,0:T(8,128)(2,1)S(1)}, bf16[15,32,128]{2,1,0:T(8,128)(2,1)S(1)}, u32[]{:S(2)}, u32[]{:S(2)}) collective-permute-start(bf16[15,32,128]{2,1,0:T(8,128)(2,1)S(1)} %get-tuple-element.299), channel_id=1, source_target_pairs={{0,4},{2,6},{4,0},{5,9},{6,2},{7,11},{8,12},{9,5},{10,14},{11,7},{... | collective-permute-start | bytes 368648 | tf_op jit(solution)/shard_map/ppermute | solution.py:374
  94.9 1.4 %collective-permute-start.25 = (f32[2,2,8,8,128]{4,3,2,1,0:T(8,128)S(1)}, f32[2,2,8,8,128]{4,3,2,1,0:T(8,128)S(1)}, u32[]{:S(2)}, u32[]{:S(2)}) collective-permute-start(f32[2,2,8,8,128]{4,3,2,1,0:T(8,128)S(1)} %pad_maximum_fusion.4), channel_id=1, source_target_pairs={{0,1},{1,0},{2,3},{3,2},{4,5},{5,4},{6,7},{7,6},{8,9},{9,8},{10,11... | collective-permute-start | bytes 393224 | tf_op jit(solution)/shard_map/ppermute | solution.py:358
  96.4 4.9 %collective-permute-start.26 = (f32[2,4,8,128]{3,2,1,0:T(8,128)S(1)}, f32[2,4,8,128]{3,2,1,0:T(8,128)S(1)}, u32[]{:S(2)}, u32[]{:S(2)}) collective-permute-start(f32[2,4,8,128]{3,2,1,0:T(8,128)S(1)} %get-tuple-element.313), channel_id=1, source_target_pairs={{0,18},{1,19},{2,16},{3,17},{16,2},{17,3},{18,0},{19,1},{4,22},{5,... | collective-permute-start | bytes 98312 | tf_op jit(solution)/shard_map/ppermute | solution.py:503
  98.0 3.9 %collective-permute-start.28 = (f32[2,4,8,128]{3,2,1,0:T(8,128)S(1)}, f32[2,4,8,128]{3,2,1,0:T(8,128)S(1)}, u32[]{:S(2)}, u32[]{:S(2)}) collective-permute-start(f32[2,4,8,128]{3,2,1,0:T(8,128)S(1)} %get-tuple-element.314), channel_id=1, source_target_pairs={{0,2},{1,3},{2,0},{3,1},{16,18},{17,19},{18,16},{19,17},{4,6},{5,7... | collective-permute-start | bytes 98312 | tf_op jit(solution)/shard_map/ppermute | solution.py:503
  99.4 3.9 %collective-permute-start.27 = (f32[2,4,8,128]{3,2,1,0:T(8,128)S(1)}, f32[2,4,8,128]{3,2,1,0:T(8,128)S(1)}, u32[]{:S(2)}, u32[]{:S(2)}) collective-permute-start(f32[2,4,8,128]{3,2,1,0:T(8,128)S(1)} %dynamic-slice_bitcast_fusion.5), channel_id=1, source_target_pairs={{0,16},{1,17},{2,18},{3,19},{16,0},{17,1},{18,2},{19,3},{4,20},{5,... | collective-permute-start | bytes 98312 | tf_op jit(solution)/shard_map/ppermute | solution.py:503

commit v12 on v11

--- a/solution.py
+++ b/solution.py
@@ -168,8 +168,25 @@
     return halo[comp * PACKED + NEAR_ROWS + near].astype(F32)
 
 
-def first(side, table, residual, rec_cell, vel, middle, other, edge, cells, halo, *outs):
-    vel_out, sent, light, lame, shear, halo_out, spots, amounts = outs
+def properties(table, number):
+    parts = [jnp.full(number.shape, table[0, c], F32) for c in range(3)]
+    for m in range(1, table.shape[0]):
+        hit = number == float(m)
+        parts = [jnp.where(hit, table[m, c], parts[c]) for c in range(3)]
+    return parts
+
+
+def materials(table, *refs):
+    for cells, (light, lame, shear) in zip(refs[:2], (refs[2:5], refs[5:])):
+        for out in range(DEEP):
+            parts = properties(table, cells[out])
+            light[out] = (TIME_STEP / UNIT) / parts[0]
+            lame[out] = (TIME_STEP * STIFFNESS / UNIT) * parts[1]
+            shear[out] = (TIME_STEP * STIFFNESS / UNIT) * parts[2]
+
+
+def first(side, table, residual, rec_cell, vel, middle, other, edge, light, lame_own, shear_own, halo, *outs):
+    vel_out, sent, lame, shear, halo_out, spots, amounts = outs
     size_y, depth = vel.shape[2:]
     planes = size_y // SUBLANES
     slab, me, flip = position()
@@ -186,21 +203,14 @@
     for moment in range(residual.shape[2]):
         amounts[moment] = jnp.full((size_y, depth), residual[0, me, moment], F32)
     _, inside = partner(slab, me, lax.axis_size("gx"), side)
-    count = table.shape[0]
-    for out in range(DEEP + REACH):
-        if out < DEEP:
-            number, share = cells[out], 1.0
-        else:
-            number = halo[len(ALONG_X), REACH - 1 - (out - DEEP)]
-            share = jnp.where(inside, 1.0, 0.0)
-        parts = [jnp.full(number.shape, table[0, c], F32) for c in range(3)]
-        for m in range(1, count):
-            hit = number == float(m)
-            parts = [jnp.where(hit, table[m, c], parts[c]) for c in range(3)]
-        lame[out] = (TIME_STEP * STIFFNESS / UNIT * share) * parts[1]
-        shear[out] = (TIME_STEP * STIFFNESS / UNIT * share) * parts[2]
-        if out < DEEP:
-            light[out] = (TIME_STEP / UNIT) / parts[0]
+    share = jnp.where(inside, TIME_STEP * STIFFNESS / UNIT, 0.0)
+    for out in range(DEEP):
+        lame[out] = lame_own[out]
+        shear[out] = shear_own[out]
+    for out in range(DEEP, DEEP + REACH):
+        parts = properties(table, halo[len(ALONG_X), REACH - 1 - (out - DEEP)])
+        lame[out] = share * parts[1]
+        shear[out] = share * parts[2]
     for at in range(len(ALONG_X)):
         for near in range(REACH):
             value = halo[at, REACH - 1 - near]
@@ -413,20 +423,23 @@
         functools.partial(combine, groups), [(own.shape, F32)], ([listed, src_pick], strains)
     )
     combined = combined.reshape(own.shape[:2] + (tile_x, tile_y, depth))
+    own_rows = call(materials, [shape(DEEP)] * 6, ([material_table], cells))
+    own_rows = (own_rows[:3], own_rows[3:])
     sent, lights, lames, shears, old_halos, spots, amounts = ([None, None] for _ in range(7))
     fresh = [None, None]
     for side in range(2):
         results = call(
             functools.partial(first, side),
-            [vel_shape, sent_shape, shape(DEEP), shape(DEEP + REACH), shape(DEEP + REACH), halo_shape]
+            [vel_shape, sent_shape, shape(DEEP + REACH), shape(DEEP + REACH), halo_shape]
             + [shape(DEEP), shape(moments)],
             (
                 [material_table, residual, rec_cell],
-                [vels[side], middles[side], middles[1 - side], edges[side], cells[side], halos[side]],
+                [vels[side], middles[side], middles[1 - side], edges[side], *own_rows[side], halos[side]],
             ),
         )
-        fresh[side], sent[side], lights[side], lames[side], shears[side], old_halos[side] = results[:6]
-        spots[side], amounts[side] = results[6:]
+        fresh[side], sent[side], lames[side], shears[side], old_halos[side] = results[:5]
+        spots[side], amounts[side] = results[5:]
+        lights[side] = own_rows[side][0]
         sent[side] = to_neighbour(sent[side], side)
     vels = fresh
 

time: 105 us -> 105 us (level)
  waiting for transfers between devices: 30.4 us -> 28 us
  local copies, waits for them, and re-layouts: 1.54 us -> 2.66 us
    ppermute x18, waiting for transfers between devices: 12.4 us -> 10.8 us  [to_neighbour(): return lax.ppermute(face, ('gx', 'gy'), pairs)]
    unnamed x16, local copies, waits for them, and re-layouts: 0.2 us -> 1.32 us
    pallas_call x30 -> x31, Pallas kernels: 16.1 us -> 17 us  [call(): pl.pallas_call(body, out_shape=[jax.ShapeDtypeStruct(shape, kind) for sha...]
  transfers between devices with their start and end apart: 29 -> 29, of which waited for: 14 -> 14; matrix products, arithmetic and copies ran while one was open for 0% -> 1% of each run, Pallas kernels for 15% -> 15%
where the time goes in v12:
time: 105 us; the launch traced here: 104 us
  starting transfers between devices  54.8 us (52%)
  waiting for transfers between devices  28 us (27%)
  Pallas kernels  17 us (16%)
  local copies, waits for them, and re-layouts  2.66 us (3%)
  other arithmetic  1.51 us (1%)
    ppermute x18, starting transfers between devices, to_neighbour(): return lax.ppermute(face, ('gx', 'gy'), pairs)  44.6 us
    pallas_call x31, Pallas kernels, call(): pl.pallas_call(body, out_shape=[jax.ShapeDtypeStruct(shape, kind) for sha...  17 us
    ppermute x8, waiting for transfers between devices, swap(): return lax.ppermute(array, axis, [(i, i ^ turn) for i in range(count)])  13.9 us
    ppermute x18, waiting for transfers between devices, to_neighbour(): return lax.ppermute(face, ('gx', 'gy'), pairs)  10.8 us
    ppermute x8, starting transfers between devices, swap(): return lax.ppermute(array, axis, [(i, i ^ turn) for i in range(count)])  6.6 us
    ppermute x3, starting transfers between devices, local(): part = lax.ppermute(part, ('sta', 'gy'), pairs)  3.55 us
    ppermute x3, waiting for transfers between devices, local(): part = lax.ppermute(part, ('sta', 'gy'), pairs)  3.37 us
  transfers between devices with their start and end apart: 29, of which 14 were waited for; matrix products, arithmetic and copies ran while one was open for 1% of the time, Pallas kernels for 15%

profile of v12, /device:TPU:0, one launch (start us, length us, event | category | flops | bytes accessed | tf_op | source)
XLA Modules:
  0.0 104.5 jit_solution(15117833579451931571)
XLA Ops:
  0.0 1.3 %dynamic-slice_bitcast_fusion = (f32[9,8,8,128]{3,2,1,0:T(8,128)S(1)}, f32[9,8,8,128]{3,2,1,0:T(8,128)S(1)}, f32[9,8,8,128]{3,2,1,0:T(8,128)S(1)}, f32[9,8,8,128]{3,2,1,0:T(8,128)S(1)}) fusion(f32[1,4,9,8,8,128]{5,4,3,2,1,0:T(8,128)} %param.8, s32[]{:T(128)S(6)} %select_n.24, s32[]{:T(128)S(6)} %select_n.22, s32[]{:T(128)S(6)} %select_n.21, s32[]{:T(128)S(6)} %select_n.23), kind=kLoop, calls=%fused_computation.4 | loop fusion | bytes 2359312 | tf_op jit(solution)/shard_map/jit(dynamic_index_in_dim)/squeeze | solution.py:399
  1.4 0.9 pad_maximum_fusion
  2.7 2.5 %collective-permute-start.1 = (f32[10,8,8,128]{3,2,1,0:T(8,128)S(1)}, f32[10,8,8,128]{3,2,1,0:T(8,128)S(1)}, u32[]{:S(2)}, u32[]{:S(2)}) collective-permute-start(f32[10,8,8,128]{3,2,1,0:T(8,128)S(1)} %get-tuple-element.325), channel_id=1, source_target_pairs={{0,2},{1,3},{2,0},{3,1},{4,6},{5,7},{6,4},{7,5},{8,10},{9,11},{10,... | collective-permute-start | bytes 983048 | tf_op jit(solution)/shard_map/ppermute | solution.py:368
  5.3 1.7 %collective-permute-start.3 = (bf16[8,6,64,128]{3,2,1,0:T(8,128)(2,1)S(1)}, bf16[8,6,64,128]{3,2,1,0:T(8,128)(2,1)S(1)}, u32[]{:S(2)}, u32[]{:S(2)}) collective-permute-start(bf16[8,6,64,128]{3,2,1,0:T(8,128)(2,1)S(1)} %bitcast.24), channel_id=1, source_target_pairs={{0,16},{16,0},{1,17},{17,1},{2,18},{18,2},{3,19},{19,3},{4,20},{20... | collective-permute-start | bytes 2359304 | tf_op jit(solution)/shard_map/ppermute | solution.py:368
  7.1 0.8 copy.12.listed
  7.9 5.9 %collective-permute-done.1.refs_2_ = f32[10,8,8,128]{3,2,1,0:T(8,128)S(1)} collective-permute-done((f32[10,8,8,128]{3,2,1,0:T(8,128)S(1)}, f32[10,8,8,128]{3,2,1,0:T(8,128)S(1)}, u32[]{:S(2)}, u32[]{:S(2)}) %collective-permute-start.1) | collective-permute-done | bytes 327712 | tf_op jit(solution)/shard_map/ppermute | solution.py:368
  13.7 6.7 %collective-permute-done.2.refs_3_ = f32[10,8,8,128]{3,2,1,0:T(8,128)S(1)} collective-permute-done((f32[10,8,8,128]{3,2,1,0:T(8,128)S(1)}, f32[10,8,8,128]{3,2,1,0:T(8,128)S(1)}, u32[]{:S(2)}, u32[]{:S(2)}) %collective-permute-start.2) | collective-permute-done | bytes 327712 | tf_op jit(solution)/shard_map/ppermute | solution.py:368
  20.4 0.7 shard_map.82
  21.1 0.7 collective-permute-start.5
  21.8 6.3 %collective-permute-start.4 = (f32[4,2,32,128]{3,2,1,0:T(8,128)S(1)}, f32[4,2,32,128]{3,2,1,0:T(8,128)S(1)}, u32[]{:S(2)}, u32[]{:S(2)}) collective-permute-start(f32[4,2,32,128]{3,2,1,0:T(8,128)S(1)} %get-tuple-element.175), channel_id=1, source_target_pairs={{0,4},{2,6},{4,0},{5,9},{6,2},{7,11},{8,12},{9,5},{10,14},{11,7},{... | collective-permute-start | bytes 393224 | tf_op jit(solution)/shard_map/ppermute | solution.py:384
  28.1 1.1 %shard_map.83 = (f32[4,32,128]{2,1,0:T(8,128)S(1)}, f32[4,32,128]{2,1,0:T(8,128)S(1)}, f32[4,32,128]{2,1,0:T(8,128)S(1)}, f32[4,32,128]{2,1,0:T(8,128)S(1)}, f32...) custom-call(f32[16,3]{1,0:T(8,128)S(1)} %copy.10.table, f32[4,32,128]{2,1,0:T(8,128)S(1)} %get-tuple-element.170.refs_0_, ...), custom_call_target="tpu_custom_call" | custom-call | flops 8000000000 | bytes 2000000 | tf_op jit(solution)/shard_map/pallas_call | solution.py:30
  29.2 1.0 shard_map.85
  30.3 0.7 collective-permute-start.7
  31.0 1.0 shard_map.84
  32.0 5.0 %collective-permute-start.6 = (bf16[15,32,128]{2,1,0:T(8,128)(2,1)S(1)}, bf16[15,32,128]{2,1,0:T(8,128)(2,1)S(1)}, u32[]{:S(2)}, u32[]{:S(2)}) collective-permute-start(bf16[15,32,128]{2,1,0:T(8,128)(2,1)S(1)} %get-tuple-element.193), channel_id=1, source_target_pairs={{0,4},{2,6},{4,0},{5,9},{6,2},{7,11},{8,12},{9,5},{10,14},{11,7},{... | collective-permute-start | bytes 368648 | tf_op jit(solution)/shard_map/ppermute | solution.py:384
  37.0 1.0 shard_map.87
  38.2 1.6 %collective-permute-start.17 = (f32[8,6,8,8,128]{4,3,2,1,0:T(8,128)S(1)}, f32[8,6,8,8,128]{4,3,2,1,0:T(8,128)S(1)}, u32[]{:S(2)}, u32[]{:S(2)}) collective-permute-start(f32[8,6,8,8,128]{4,3,2,1,0:T(8,128)S(1)} %bitcast.20), channel_id=1, source_target_pairs={{0,2},{1,3},{2,0},{3,1},{4,6},{5,7},{6,4},{7,5},{8,10},{9,11},{10,... | collective-permute-start | bytes 4718600 | tf_op jit(solution)/shard_map/ppermute | solution.py:368
  40.3 0.7 collective-permute-start.9
  41.5 3.6 %collective-permute-start.8 = (bf16[15,32,128]{2,1,0:T(8,128)(2,1)S(1)}, bf16[15,32,128]{2,1,0:T(8,128)(2,1)S(1)}, u32[]{:S(2)}, u32[]{:S(2)}) collective-permute-start(bf16[15,32,128]{2,1,0:T(8,128)(2,1)S(1)} %get-tuple-element.210), channel_id=1, source_target_pairs={{0,4},{2,6},{4,0},{5,9},{6,2},{7,11},{8,12},{9,5},{10,14},{11,7},{... | collective-permute-start | bytes 368648 | tf_op jit(solution)/shard_map/ppermute | solution.py:384
  45.9 0.7 collective-permute-start.11
  46.6 1.7 %collective-permute-done.8.halo = bf16[15,32,128]{2,1,0:T(8,128)(2,1)S(1)} collective-permute-done((bf16[15,32,128]{2,1,0:T(8,128)(2,1)S(1)}, bf16[15,32,128]{2,1,0:T(8,128)(2,1)S(1)}, u32[]{:S(2)}, u32[]{:S(2)}) %collective-permute-start.8) | collective-permute-done | bytes 122912 | tf_op jit(solution)/shard_map/ppermute | solution.py:384
  48.7 3.6 %collective-permute-start.10 = (bf16[15,32,128]{2,1,0:T(8,128)(2,1)S(1)}, bf16[15,32,128]{2,1,0:T(8,128)(2,1)S(1)}, u32[]{:S(2)}, u32[]{:S(2)}) collective-permute-start(bf16[15,32,128]{2,1,0:T(8,128)(2,1)S(1)} %get-tuple-element.224), channel_id=1, source_target_pairs={{0,4},{2,6},{4,0},{5,9},{6,2},{7,11},{8,12},{9,5},{10,14},{11,7},{... | collective-permute-start | bytes 368648 | tf_op jit(solution)/shard_map/ppermute | solution.py:384
  53.1 0.7 collective-permute-start.13
  53.7 1.7 %collective-permute-done.10.halo = bf16[15,32,128]{2,1,0:T(8,128)(2,1)S(1)} collective-permute-done((bf16[15,32,128]{2,1,0:T(8,128)(2,1)S(1)}, bf16[15,32,128]{2,1,0:T(8,128)(2,1)S(1)}, u32[]{:S(2)}, u32[]{:S(2)}) %collective-permute-start.10) | collective-permute-done | bytes 122912 | tf_op jit(solution)/shard_map/ppermute | solution.py:384
  55.9 3.6 %collective-permute-start.12 = (bf16[15,32,128]{2,1,0:T(8,128)(2,1)S(1)}, bf16[15,32,128]{2,1,0:T(8,128)(2,1)S(1)}, u32[]{:S(2)}, u32[]{:S(2)}) collective-permute-start(bf16[15,32,128]{2,1,0:T(8,128)(2,1)S(1)} %get-tuple-element.238), channel_id=1, source_target_pairs={{0,4},{2,6},{4,0},{5,9},{6,2},{7,11},{8,12},{9,5},{10,14},{11,7},{... | collective-permute-start | bytes 368648 | tf_op jit(solution)/shard_map/ppermute | solution.py:384
  60.3 0.7 collective-permute-start.15
  61.0 1.7 %collective-permute-done.12.halo = bf16[15,32,128]{2,1,0:T(8,128)(2,1)S(1)} collective-permute-done((bf16[15,32,128]{2,1,0:T(8,128)(2,1)S(1)}, bf16[15,32,128]{2,1,0:T(8,128)(2,1)S(1)}, u32[]{:S(2)}, u32[]{:S(2)}) %collective-permute-start.12) | collective-permute-done | bytes 122912 | tf_op jit(solution)/shard_map/ppermute | solution.py:384
  63.2 3.6 %collective-permute-start.14 = (bf16[15,32,128]{2,1,0:T(8,128)(2,1)S(1)}, bf16[15,32,128]{2,1,0:T(8,128)(2,1)S(1)}, u32[]{:S(2)}, u32[]{:S(2)}) collective-permute-start(bf16[15,32,128]{2,1,0:T(8,128)(2,1)S(1)} %get-tuple-element.252), channel_id=1, source_target_pairs={{0,4},{2,6},{4,0},{5,9},{6,2},{7,11},{8,12},{9,5},{10,14},{11,7},{... | collective-permute-start | bytes 368648 | tf_op jit(solution)/shard_map/ppermute | solution.py:384
  67.5 0.7 collective-permute-start.19
  68.2 1.7 %collective-permute-done.14.halo = bf16[15,32,128]{2,1,0:T(8,128)(2,1)S(1)} collective-permute-done((bf16[15,32,128]{2,1,0:T(8,128)(2,1)S(1)}, bf16[15,32,128]{2,1,0:T(8,128)(2,1)S(1)}, u32[]{:S(2)}, u32[]{:S(2)}) %collective-permute-start.14) | collective-permute-done | bytes 122912 | tf_op jit(solution)/shard_map/ppermute | solution.py:384
  70.4 4.4 %collective-permute-start.18 = (bf16[15,32,128]{2,1,0:T(8,128)(2,1)S(1)}, bf16[15,32,128]{2,1,0:T(8,128)(2,1)S(1)}, u32[]{:S(2)}, u32[]{:S(2)}) collective-permute-start(bf16[15,32,128]{2,1,0:T(8,128)(2,1)S(1)} %get-tuple-element.269), channel_id=1, source_target_pairs={{0,4},{2,6},{4,0},{5,9},{6,2},{7,11},{8,12},{9,5},{10,14},{11,7},{... | collective-permute-start | bytes 368648 | tf_op jit(solution)/shard_map/ppermute | solution.py:384
  75.5 0.7 collective-permute-start.21
  76.2 2.6 %collective-permute-done.18.halo = bf16[15,32,128]{2,1,0:T(8,128)(2,1)S(1)} collective-permute-done((bf16[15,32,128]{2,1,0:T(8,128)(2,1)S(1)}, bf16[15,32,128]{2,1,0:T(8,128)(2,1)S(1)}, u32[]{:S(2)}, u32[]{:S(2)}) %collective-permute-start.18) | collective-permute-done | bytes 122912 | tf_op jit(solution)/shard_map/ppermute | solution.py:384
  79.3 3.9 %collective-permute-start.20 = (bf16[15,32,128]{2,1,0:T(8,128)(2,1)S(1)}, bf16[15,32,128]{2,1,0:T(8,128)(2,1)S(1)}, u32[]{:S(2)}, u32[]{:S(2)}) collective-permute-start(bf16[15,32,128]{2,1,0:T(8,128)(2,1)S(1)} %get-tuple-element.283), channel_id=1, source_target_pairs={{0,4},{2,6},{4,0},{5,9},{6,2},{7,11},{8,12},{9,5},{10,14},{11,7},{... | collective-permute-start | bytes 368648 | tf_op jit(solution)/shard_map/ppermute | solution.py:384
  83.5 1.0 shard_map.107
  84.5 0.7 collective-permute-start.24
  85.2 0.9 collective-permute-done.20.halo
  86.1 0.9 shard_map.106
  87.0 4.6 %collective-permute-start.23 = (bf16[15,32,128]{2,1,0:T(8,128)(2,1)S(1)}, bf16[15,32,128]{2,1,0:T(8,128)(2,1)S(1)}, u32[]{:S(2)}, u32[]{:S(2)}) collective-permute-start(bf16[15,32,128]{2,1,0:T(8,128)(2,1)S(1)} %get-tuple-element.307), channel_id=1, source_target_pairs={{0,4},{2,6},{4,0},{5,9},{6,2},{7,11},{8,12},{9,5},{10,14},{11,7},{... | collective-permute-start | bytes 368648 | tf_op jit(solution)/shard_map/ppermute | solution.py:384
  92.3 1.7 %shard_map.109.refs_36_ = f32[4,2,8,8,128]{4,3,2,1,0:T(8,128)S(1)} custom-call(f32[1,4,8]{2,1,0:T(4,128)S(1)} %copy-done.2, f32[6,2,32,128]{3,2,1,0:T(8,128)S(1)} %get-tuple-element.188.refs_0_, f32[6,2,32,128]{3,2,1,0:T(8,128)S(1)} %get-tuple-element.192.refs_1_, f32[6,2,32,128]{3,2,1,0:T(8,128)S(1)} %get-tuple-element.199.refs_2_, ...), custom_call_target="tpu_custom_call" | custom-call | flops 8000000000 | bytes 2000000 | tf_op jit(solution)/shard_map/pallas_call | solution.py:30
  94.7 0.8 shard_map.112
  95.6 1.3 %collective-permute-done.25 = f32[2,2,8,8,128]{4,3,2,1,0:T(8,128)S(1)} collective-permute-done((f32[2,2,8,8,128]{4,3,2,1,0:T(8,128)S(1)}, f32[2,2,8,8,128]{4,3,2,1,0:T(8,128)S(1)}, u32[]{:S(2)}, u32[]{:S(2)}) %collective-permute-start.25) | collective-permute-done | bytes 131104 | tf_op jit(solution)/shard_map/ppermute | solution.py:368
  96.9 1.5 %collective-permute-start.26 = (f32[2,4,8,128]{3,2,1,0:T(8,128)S(1)}, f32[2,4,8,128]{3,2,1,0:T(8,128)S(1)}, u32[]{:S(2)}, u32[]{:S(2)}) collective-permute-start(f32[2,4,8,128]{3,2,1,0:T(8,128)S(1)} %get-tuple-element.321), channel_id=1, source_target_pairs={{0,18},{1,19},{2,16},{3,17},{16,2},{17,3},{18,0},{19,1},{4,22},{5,... | collective-permute-start | bytes 98312 | tf_op jit(solution)/shard_map/ppermute | solution.py:516
  98.5 1.5 %collective-permute-start.28 = (f32[2,4,8,128]{3,2,1,0:T(8,128)S(1)}, f32[2,4,8,128]{3,2,1,0:T(8,128)S(1)}, u32[]{:S(2)}, u32[]{:S(2)}) collective-permute-start(f32[2,4,8,128]{3,2,1,0:T(8,128)S(1)} %get-tuple-element.322), channel_id=1, source_target_pairs={{0,2},{1,3},{2,0},{3,1},{16,18},{17,19},{18,16},{19,17},{4,6},{5,7... | collective-permute-start | bytes 98312 | tf_op jit(solution)/shard_map/ppermute | solution.py:516
  100.5 1.3 %collective-permute-done.26 = f32[2,4,8,128]{3,2,1,0:T(8,128)S(1)} collective-permute-done((f32[2,4,8,128]{3,2,1,0:T(8,128)S(1)}, f32[2,4,8,128]{3,2,1,0:T(8,128)S(1)}, u32[]{:S(2)}, u32[]{:S(2)}) %collective-permute-start.26) | collective-permute-done | bytes 32800 | tf_op jit(solution)/shard_map/ppermute | solution.py:516
  101.8 0.6 collective-permute-done.28
  102.4 1.5 %collective-permute-done.27 = f32[2,4,8,128]{3,2,1,0:T(8,128)S(1)} collective-permute-done((f32[2,4,8,128]{3,2,1,0:T(8,128)S(1)}, f32[2,4,8,128]{3,2,1,0:T(8,128)S(1)}, u32[]{:S(2)}, u32[]{:S(2)}) %collective-permute-start.27) | collective-permute-done | bytes 32800 | tf_op jit(solution)/shard_map/ppermute | solution.py:516
  103.9 0.6 bitcast_add_fusion
  (66 shorter events, 10.3 us)
Async XLA Ops:
  0.0 1.3 %copy-start.5 = (s32[8,8,128]{2,1,0:T(8,128)S(1)}, s32[8,8,128]{2,1,0:T(8,128)}, u32[]{:S(2)}) copy-start(s32[8,8,128]{2,1,0:T(8,128)} %param.10) | copy-start | bytes 98308
  1.3 4.0 %copy-start = (bf16[1,8,6,8,8,128]{5,4,3,2,1,0:T(8,128)(2,1)S(1)}, bf16[1,8,6,8,8,128]{5,4,3,2,1,0:T(8,128)(2,1)}, u32[]{:S(2)}) copy-start(bf16[1,8,6,8,8,128]{5,4,3,2,1,0:T(8,128)(2,1)} %param.9) | copy-start | bytes 2359300
  1.3 5.7 %copy-start.6 = (f32[16,3]{0,1:T(4,128)S(1)}, f32[16,3]{0,1:T(4,128)}, u32[]{:S(2)}) copy-start(f32[16,3]{0,1:T(4,128)} %param.11) | copy-start | bytes 580
  2.2 5.7 %collective-permute-start = (f32[10,8,8,128]{3,2,1,0:T(8,128)}, f32[10,8,8,128]{3,2,1,0:T(8,128)S(1)}, u32[]{:S(2)}, u32[]{:S(2)}) collective-permute-start(f32[10,8,8,128]{3,2,1,0:T(8,128)} %get-tuple-element.324), channel_id=1, source_target_pairs={{0,1},{1,0},{2,3},{3,2},{4,5},{5,4},{6,7},{7,6},{8,9},{9,8},{10,11... | collective-permute-start | bytes 983048 | tf_op jit(solution)/shard_map/ppermute | solution.py:368
  2.7 11.1 %collective-permute-start.1 = (f32[10,8,8,128]{3,2,1,0:T(8,128)S(1)}, f32[10,8,8,128]{3,2,1,0:T(8,128)S(1)}, u32[]{:S(2)}, u32[]{:S(2)}) collective-permute-start(f32[10,8,8,128]{3,2,1,0:T(8,128)S(1)} %get-tuple-element.325), channel_id=1, source_target_pairs={{0,2},{1,3},{2,0},{3,1},{4,6},{5,7},{6,4},{7,5},{8,10},{9,11},{10,... | collective-permute-start | bytes 983048 | tf_op jit(solution)/shard_map/ppermute | solution.py:368
  5.2 15.2 %collective-permute-start.2 = (f32[10,8,8,128]{3,2,1,0:T(8,128)S(1)}, f32[10,8,8,128]{3,2,1,0:T(8,128)S(1)}, u32[]{:S(2)}, u32[]{:S(2)}) collective-permute-start(f32[10,8,8,128]{3,2,1,0:T(8,128)S(1)} %get-tuple-element.323), channel_id=1, source_target_pairs={{0,3},{1,2},{2,1},{3,0},{4,7},{5,6},{6,5},{7,4},{8,11},{9,10},{10,... | collective-permute-start | bytes 983048 | tf_op jit(solution)/shard_map/ppermute | solution.py:368
  5.3 22.8 %collective-permute-start.3 = (bf16[8,6,64,128]{3,2,1,0:T(8,128)(2,1)S(1)}, bf16[8,6,64,128]{3,2,1,0:T(8,128)(2,1)S(1)}, u32[]{:S(2)}, u32[]{:S(2)}) collective-permute-start(bf16[8,6,64,128]{3,2,1,0:T(8,128)(2,1)S(1)} %bitcast.24), channel_id=1, source_target_pairs={{0,16},{16,0},{1,17},{17,1},{2,18},{18,2},{3,19},{19,3},{4,20},{20... | collective-permute-start | bytes 2359304 | tf_op jit(solution)/shard_map/ppermute | solution.py:368
  21.1 8.1 %collective-permute-start.5 = (f32[4,2,32,128]{3,2,1,0:T(8,128)S(1)}, f32[4,2,32,128]{3,2,1,0:T(8,128)S(1)}, u32[]{:S(2)}, u32[]{:S(2)}) collective-permute-start(f32[4,2,32,128]{3,2,1,0:T(8,128)S(1)} %get-tuple-element.182), channel_id=1, source_target_pairs={{1,5},{3,7},{4,8},{5,1},{6,10},{7,3},{8,4},{9,13},{10,6},{11,15},{... | collective-permute-start | bytes 393224 | tf_op jit(solution)/shard_map/ppermute | solution.py:384
  21.8 9.3 %collective-permute-start.4 = (f32[4,2,32,128]{3,2,1,0:T(8,128)S(1)}, f32[4,2,32,128]{3,2,1,0:T(8,128)S(1)}, u32[]{:S(2)}, u32[]{:S(2)}) collective-permute-start(f32[4,2,32,128]{3,2,1,0:T(8,128)S(1)} %get-tuple-element.175), channel_id=1, source_target_pairs={{0,4},{2,6},{4,0},{5,9},{6,2},{7,11},{8,12},{9,5},{10,14},{11,7},{... | collective-permute-start | bytes 393224 | tf_op jit(solution)/shard_map/ppermute | solution.py:384
  28.1 1.1 %copy-start.1 = (f32[1,4,8]{2,1,0:T(4,128)S(1)}, f32[1,4,8]{2,1,0:T(4,128)}, u32[]{:S(2)}) copy-start(f32[1,4,8]{2,1,0:T(4,128)} %residual.7) | copy-start | bytes 388
  28.1 1.1 %copy-start.4 = (s32[1,4]{1,0:T(1,128)S(1)}, s32[1,4]{1,0:T(1,128)}, u32[]{:S(2)}) copy-start(s32[1,4]{1,0:T(1,128)} %rec_cell.3) | copy-start | bytes 52
  30.3 9.6 %collective-permute-start.7 = (bf16[15,32,128]{2,1,0:T(8,128)(2,1)S(1)}, bf16[15,32,128]{2,1,0:T(8,128)(2,1)S(1)}, u32[]{:S(2)}, u32[]{:S(2)}) collective-permute-start(bf16[15,32,128]{2,1,0:T(8,128)(2,1)S(1)} %get-tuple-element.200), channel_id=1, source_target_pairs={{1,5},{3,7},{4,8},{5,1},{6,10},{7,3},{8,4},{9,13},{10,6},{11,15},{... | collective-permute-start | bytes 368648 | tf_op jit(solution)/shard_map/ppermute | solution.py:384
  31.0 6.0 %copy-start.3 = (s32[2,8]{1,0:T(2,128)S(1)}, s32[2,8]{1,0:T(2,128)}, u32[]{:S(2)}) copy-start(s32[2,8]{1,0:T(2,128)} %src_pick.1) | copy-start | bytes 196
  32.0 8.9 %collective-permute-start.6 = (bf16[15,32,128]{2,1,0:T(8,128)(2,1)S(1)}, bf16[15,32,128]{2,1,0:T(8,128)(2,1)S(1)}, u32[]{:S(2)}, u32[]{:S(2)}) collective-permute-start(bf16[15,32,128]{2,1,0:T(8,128)(2,1)S(1)} %get-tuple-element.193), channel_id=1, source_target_pairs={{0,4},{2,6},{4,0},{5,9},{6,2},{7,11},{8,12},{9,5},{10,14},{11,7},{... | collective-permute-start | bytes 368648 | tf_op jit(solution)/shard_map/ppermute | solution.py:384
  38.2 44.9 %collective-permute-start.17 = (f32[8,6,8,8,128]{4,3,2,1,0:T(8,128)S(1)}, f32[8,6,8,8,128]{4,3,2,1,0:T(8,128)S(1)}, u32[]{:S(2)}, u32[]{:S(2)}) collective-permute-start(f32[8,6,8,8,128]{4,3,2,1,0:T(8,128)S(1)} %bitcast.20), channel_id=1, source_target_pairs={{0,2},{1,3},{2,0},{3,1},{4,6},{5,7},{6,4},{7,5},{8,10},{9,11},{10,... | collective-permute-start | bytes 4718600 | tf_op jit(solution)/shard_map/ppermute | solution.py:368
  40.3 5.1 %collective-permute-start.9 = (bf16[15,32,128]{2,1,0:T(8,128)(2,1)S(1)}, bf16[15,32,128]{2,1,0:T(8,128)(2,1)S(1)}, u32[]{:S(2)}, u32[]{:S(2)}) collective-permute-start(bf16[15,32,128]{2,1,0:T(8,128)(2,1)S(1)} %get-tuple-element.216), channel_id=1, source_target_pairs={{1,5},{3,7},{4,8},{5,1},{6,10},{7,3},{8,4},{9,13},{10,6},{11,15},{... | collective-permute-start | bytes 368648 | tf_op jit(solution)/shard_map/ppermute | solution.py:384
  41.5 6.8 %collective-permute-start.8 = (bf16[15,32,128]{2,1,0:T(8,128)(2,1)S(1)}, bf16[15,32,128]{2,1,0:T(8,128)(2,1)S(1)}, u32[]{:S(2)}, u32[]{:S(2)}) collective-permute-start(bf16[15,32,128]{2,1,0:T(8,128)(2,1)S(1)} %get-tuple-element.210), channel_id=1, source_target_pairs={{0,4},{2,6},{4,0},{5,9},{6,2},{7,11},{8,12},{9,5},{10,14},{11,7},{... | collective-permute-start | bytes 368648 | tf_op jit(solution)/shard_map/ppermute | solution.py:384
  45.3 37.9 %collective-permute-start.16 = (f32[8,6,8,8,128]{4,3,2,1,0:T(8,128)S(1)}, f32[8,6,8,8,128]{4,3,2,1,0:T(8,128)S(1)}, u32[]{:S(2)}, u32[]{:S(2)}) collective-permute-start(f32[8,6,8,8,128]{4,3,2,1,0:T(8,128)S(1)} %bitcast.21), channel_id=1, source_target_pairs={{0,1},{1,0},{2,3},{3,2},{4,5},{5,4},{6,7},{7,6},{8,9},{9,8},{10,11... | collective-permute-start | bytes 4718600 | tf_op jit(solution)/shard_map/ppermute | solution.py:368
  45.9 6.7 %collective-permute-start.11 = (bf16[15,32,128]{2,1,0:T(8,128)(2,1)S(1)}, bf16[15,32,128]{2,1,0:T(8,128)(2,1)S(1)}, u32[]{:S(2)}, u32[]{:S(2)}) collective-permute-start(bf16[15,32,128]{2,1,0:T(8,128)(2,1)S(1)} %get-tuple-element.230), channel_id=1, source_target_pairs={{1,5},{3,7},{4,8},{5,1},{6,10},{7,3},{8,4},{9,13},{10,6},{11,15},{... | collective-permute-start | bytes 368648 | tf_op jit(solution)/shard_map/ppermute | solution.py:384
  48.7 6.8 %collective-permute-start.10 = (bf16[15,32,128]{2,1,0:T(8,128)(2,1)S(1)}, bf16[15,32,128]{2,1,0:T(8,128)(2,1)S(1)}, u32[]{:S(2)}, u32[]{:S(2)}) collective-permute-start(bf16[15,32,128]{2,1,0:T(8,128)(2,1)S(1)} %get-tuple-element.224), channel_id=1, source_target_pairs={{0,4},{2,6},{4,0},{5,9},{6,2},{7,11},{8,12},{9,5},{10,14},{11,7},{... | collective-permute-start | bytes 368648 | tf_op jit(solution)/shard_map/ppermute | solution.py:384
  53.1 6.8 %collective-permute-start.13 = (bf16[15,32,128]{2,1,0:T(8,128)(2,1)S(1)}, bf16[15,32,128]{2,1,0:T(8,128)(2,1)S(1)}, u32[]{:S(2)}, u32[]{:S(2)}) collective-permute-start(bf16[15,32,128]{2,1,0:T(8,128)(2,1)S(1)} %get-tuple-element.244), channel_id=1, source_target_pairs={{1,5},{3,7},{4,8},{5,1},{6,10},{7,3},{8,4},{9,13},{10,6},{11,15},{... | collective-permute-start | bytes 368648 | tf_op jit(solution)/shard_map/ppermute | solution.py:384
  55.9 6.8 %collective-permute-start.12 = (bf16[15,32,128]{2,1,0:T(8,128)(2,1)S(1)}, bf16[15,32,128]{2,1,0:T(8,128)(2,1)S(1)}, u32[]{:S(2)}, u32[]{:S(2)}) collective-permute-start(bf16[15,32,128]{2,1,0:T(8,128)(2,1)S(1)} %get-tuple-element.238), channel_id=1, source_target_pairs={{0,4},{2,6},{4,0},{5,9},{6,2},{7,11},{8,12},{9,5},{10,14},{11,7},{... | collective-permute-start | bytes 368648 | tf_op jit(solution)/shard_map/ppermute | solution.py:384
  60.3 6.8 %collective-permute-start.15 = (bf16[15,32,128]{2,1,0:T(8,128)(2,1)S(1)}, bf16[15,32,128]{2,1,0:T(8,128)(2,1)S(1)}, u32[]{:S(2)}, u32[]{:S(2)}) collective-permute-start(bf16[15,32,128]{2,1,0:T(8,128)(2,1)S(1)} %get-tuple-element.258), channel_id=1, source_target_pairs={{1,5},{3,7},{4,8},{5,1},{6,10},{7,3},{8,4},{9,13},{10,6},{11,15},{... | collective-permute-start | bytes 368648 | tf_op jit(solution)/shard_map/ppermute | solution.py:384
  63.2 6.8 %collective-permute-start.14 = (bf16[15,32,128]{2,1,0:T(8,128)(2,1)S(1)}, bf16[15,32,128]{2,1,0:T(8,128)(2,1)S(1)}, u32[]{:S(2)}, u32[]{:S(2)}) collective-permute-start(bf16[15,32,128]{2,1,0:T(8,128)(2,1)S(1)} %get-tuple-element.252), channel_id=1, source_target_pairs={{0,4},{2,6},{4,0},{5,9},{6,2},{7,11},{8,12},{9,5},{10,14},{11,7},{... | collective-permute-start | bytes 368648 | tf_op jit(solution)/shard_map/ppermute | solution.py:384
  67.5 7.5 %collective-permute-start.19 = (bf16[15,32,128]{2,1,0:T(8,128)(2,1)S(1)}, bf16[15,32,128]{2,1,0:T(8,128)(2,1)S(1)}, u32[]{:S(2)}, u32[]{:S(2)}) collective-permute-start(bf16[15,32,128]{2,1,0:T(8,128)(2,1)S(1)} %get-tuple-element.275), channel_id=1, source_target_pairs={{1,5},{3,7},{4,8},{5,1},{6,10},{7,3},{8,4},{9,13},{10,6},{11,15},{... | collective-permute-start | bytes 368648 | tf_op jit(solution)/shard_map/ppermute | solution.py:384
  70.4 8.4 %collective-permute-start.18 = (bf16[15,32,128]{2,1,0:T(8,128)(2,1)S(1)}, bf16[15,32,128]{2,1,0:T(8,128)(2,1)S(1)}, u32[]{:S(2)}, u32[]{:S(2)}) collective-permute-start(bf16[15,32,128]{2,1,0:T(8,128)(2,1)S(1)} %get-tuple-element.269), channel_id=1, source_target_pairs={{0,4},{2,6},{4,0},{5,9},{6,2},{7,11},{8,12},{9,5},{10,14},{11,7},{... | collective-permute-start | bytes 368648 | tf_op jit(solution)/shard_map/ppermute | solution.py:384
  75.5 8.0 %collective-permute-start.21 = (bf16[15,32,128]{2,1,0:T(8,128)(2,1)S(1)}, bf16[15,32,128]{2,1,0:T(8,128)(2,1)S(1)}, u32[]{:S(2)}, u32[]{:S(2)}) collective-permute-start(bf16[15,32,128]{2,1,0:T(8,128)(2,1)S(1)} %get-tuple-element.289), channel_id=1, source_target_pairs={{1,5},{3,7},{4,8},{5,1},{6,10},{7,3},{8,4},{9,13},{10,6},{11,15},{... | collective-permute-start | bytes 368648 | tf_op jit(solution)/shard_map/ppermute | solution.py:384
  79.3 6.8 %collective-permute-start.20 = (bf16[15,32,128]{2,1,0:T(8,128)(2,1)S(1)}, bf16[15,32,128]{2,1,0:T(8,128)(2,1)S(1)}, u32[]{:S(2)}, u32[]{:S(2)}) collective-permute-start(bf16[15,32,128]{2,1,0:T(8,128)(2,1)S(1)} %get-tuple-element.283), channel_id=1, source_target_pairs={{0,4},{2,6},{4,0},{5,9},{6,2},{7,11},{8,12},{9,5},{10,14},{11,7},{... | collective-permute-start | bytes 368648 | tf_op jit(solution)/shard_map/ppermute | solution.py:384
  83.2 8.4 %collective-permute-start.22 = (f32[8,6,8,8,128]{4,3,2,1,0:T(8,128)S(1)}, f32[8,6,8,8,128]{4,3,2,1,0:T(8,128)S(1)}, u32[]{:S(2)}, u32[]{:S(2)}) collective-permute-start(f32[8,6,8,8,128]{4,3,2,1,0:T(8,128)S(1)} %collective-permute-done.17.refs_30_.refs_34_), channel_id=1, source_target_pairs={{0,1},{1,0},{2,3},{3,2},{4,5},{5,4},{6,7},{7,6},{8,9},{9,8},{10,11... | collective-permute-start | bytes 4718600 | tf_op jit(solution)/shard_map/ppermute | solution.py:368
  84.5 9.5 %collective-permute-start.24 = (bf16[15,32,128]{2,1,0:T(8,128)(2,1)S(1)}, bf16[15,32,128]{2,1,0:T(8,128)(2,1)S(1)}, u32[]{:S(2)}, u32[]{:S(2)}) collective-permute-start(bf16[15,32,128]{2,1,0:T(8,128)(2,1)S(1)} %get-tuple-element.310), channel_id=1, source_target_pairs={{1,5},{3,7},{4,8},{5,1},{6,10},{7,3},{8,4},{9,13},{10,6},{11,15},{... | collective-permute-start | bytes 368648 | tf_op jit(solution)/shard_map/ppermute | solution.py:384
  87.0 7.4 %collective-permute-start.23 = (bf16[15,32,128]{2,1,0:T(8,128)(2,1)S(1)}, bf16[15,32,128]{2,1,0:T(8,128)(2,1)S(1)}, u32[]{:S(2)}, u32[]{:S(2)}) collective-permute-start(bf16[15,32,128]{2,1,0:T(8,128)(2,1)S(1)} %get-tuple-element.307), channel_id=1, source_target_pairs={{0,4},{2,6},{4,0},{5,9},{6,2},{7,11},{8,12},{9,5},{10,14},{11,7},{... | collective-permute-start | bytes 368648 | tf_op jit(solution)/shard_map/ppermute | solution.py:384
  91.6 0.7 copy-start.2
  95.5 1.4 %collective-permute-start.25 = (f32[2,2,8,8,128]{4,3,2,1,0:T(8,128)S(1)}, f32[2,2,8,8,128]{4,3,2,1,0:T(8,128)S(1)}, u32[]{:S(2)}, u32[]{:S(2)}) collective-permute-start(f32[2,2,8,8,128]{4,3,2,1,0:T(8,128)S(1)} %pad_maximum_fusion.4), channel_id=1, source_target_pairs={{0,1},{1,0},{2,3},{3,2},{4,5},{5,4},{6,7},{7,6},{8,9},{9,8},{10,11... | collective-permute-start | bytes 393224 | tf_op jit(solution)/shard_map/ppermute | solution.py:368
  96.9 4.9 %collective-permute-start.26 = (f32[2,4,8,128]{3,2,1,0:T(8,128)S(1)}, f32[2,4,8,128]{3,2,1,0:T(8,128)S(1)}, u32[]{:S(2)}, u32[]{:S(2)}) collective-permute-start(f32[2,4,8,128]{3,2,1,0:T(8,128)S(1)} %get-tuple-element.321), channel_id=1, source_target_pairs={{0,18},{1,19},{2,16},{3,17},{16,2},{17,3},{18,0},{19,1},{4,22},{5,... | collective-permute-start | bytes 98312 | tf_op jit(solution)/shard_map/ppermute | solution.py:516
  98.5 3.9 %collective-permute-start.28 = (f32[2,4,8,128]{3,2,1,0:T(8,128)S(1)}, f32[2,4,8,128]{3,2,1,0:T(8,128)S(1)}, u32[]{:S(2)}, u32[]{:S(2)}) collective-permute-start(f32[2,4,8,128]{3,2,1,0:T(8,128)S(1)} %get-tuple-element.322), channel_id=1, source_target_pairs={{0,2},{1,3},{2,0},{3,1},{16,18},{17,19},{18,16},{19,17},{4,6},{5,7... | collective-permute-start | bytes 98312 | tf_op jit(solution)/shard_map/ppermute | solution.py:516
  99.9 3.9 %collective-permute-start.27 = (f32[2,4,8,128]{3,2,1,0:T(8,128)S(1)}, f32[2,4,8,128]{3,2,1,0:T(8,128)S(1)}, u32[]{:S(2)}, u32[]{:S(2)}) collective-permute-start(f32[2,4,8,128]{3,2,1,0:T(8,128)S(1)} %dynamic-slice_bitcast_fusion.5), channel_id=1, source_target_pairs={{0,16},{1,17},{2,18},{3,19},{16,0},{17,1},{18,2},{19,3},{4,20},{5,... | collective-permute-start | bytes 98312 | tf_op jit(solution)/shard_map/ppermute | solution.py:516
